TPU v7x, 512 devices: a whole 4x4x16 slice. The times are simulated.
512 devices in a mesh: group: 16 (over x, z_lo), mp: 32 (over z_hi, y, core).
Axes of the slice: x: 4, y: 4, z: 16 (z_hi: 4, z_lo: 4; z = z_hi * 4 + z_lo), core: 2. Of those that a mesh axis runs over, the one named last changes fastest.
Arguments:
- inputs: bfloat16 [2, 12288, 8192], P(None, 'group', 'mp'), may hold values from -6 to 6
- targets: bfloat16 [2, 12288, 1024], P(None, ('group', 'mp')), may hold values from -6 to 6
- numerator: bfloat16 [16, 8192, 1024], P('group', 'mp'), may hold values from -6 to 6
- momentum: float32 [16, 8192, 1024], P('group', 'mp'), may hold values from -4 to 4
- received: bfloat16 [16, 8192, 1024], P('group', 'mp'), may hold values from -6 to 6
- push_weight: float32 [16], P('group'), may hold values from 0.5 to 2
- received_weight: float32 [16], P('group'), may hold values from 0.5 to 2
- mix_share: int32 [16, 2], P('group'), may hold values from 1 to 7
Outputs:
- final_numerator: bfloat16 [16, 8192, 1024], P('group', 'mp')
- final_weight: float32 [16], P('group')
- final_received: bfloat16 [16, 8192, 1024], P('group', 'mp')
- final_received_weight: float32 [16], P('group')
- value_rows: bfloat16 [2, 12288, 1024], P(None, ('group', 'mp'))
All inputs are finite; a program needn't handle non-finite values.
Results may differ from a plain program's by a relative error of at most 0.02.
Values may be sent and summed in bfloat16 or wider, within the bound.
No kernel may reach another device: no remote copies, remote signals or barrier semaphores. Data moves between devices by JAX's collectives and lax.ppermute only.
A program may use at most 64 MiB of HBM per device.

v0:
```python
import math

import jax
import jax.numpy as jnp
from jax import lax
from jax.sharding import PartitionSpec as P

D = 8192
TOK_GRP = 768


momentum_decay = 0.9
step_size = 0.5


def from_behind(value, axis, steps):
    count = lax.axis_size(axis)
    pairs = [(source, (source + steps) % count) for source in range(count)]
    return lax.ppermute(value, axis, pairs)


def local(inputs, targets, numerator, momentum, received, push_weight, received_weight, mix_share):
    row_scale = 1.0 / math.sqrt(D)
    grad_scale = 1.0 / math.sqrt(TOK_GRP)
    steps_count = inputs.shape[0]
    own_rows = targets.shape[1]
    current = numerator[0]
    velocity = momentum[0]
    arrived = received[0]
    arrived_weight = received_weight
    weight = push_weight
    value_steps = []
    for step_index in range(steps_count):
        tokens = inputs[step_index]
        scaled = (current.astype(jnp.float32) / weight[0]).astype(jnp.bfloat16)

        def row_term(first_row, row_count, tokens=tokens, scaled=scaled):
            product = jnp.dot(tokens, scaled, preferred_element_type=jnp.float32) * row_scale
            return lax.optimization_barrier(product.astype(jnp.bfloat16)).astype(jnp.float32)

        values = lax.psum_scatter(
            row_term(jnp.int32(0), lax.axis_size("mp") * own_rows).astype(jnp.bfloat16),
            "mp",
            scatter_dimension=0,
            tiled=True,
        )
        residual = (values.astype(jnp.float32) - targets[step_index].astype(jnp.float32)).astype(
            jnp.bfloat16
        )

        def add_rows(running, piece_rows, first_row, tokens=tokens):
            return lax.dot_general(
                tokens, piece_rows, (((0,), (0,)), ((), ())), preferred_element_type=jnp.float32
            )

        gradient = (
            add_rows(
                jnp.zeros(current.shape, jnp.float32),
                lax.all_gather(residual, "mp", axis=0, tiled=True),
                jnp.int32(0),
            )
            * grad_scale
        )
        velocity = momentum_decay * velocity + gradient
        half_step = current.astype(jnp.float32) - step_size * velocity
        kept_share = mix_share[0, step_index].astype(jnp.float32) / 8.0
        outgoing = ((1.0 - kept_share) * half_step).astype(jnp.bfloat16)
        outgoing_weight = ((1.0 - kept_share) * weight).astype(jnp.bfloat16)
        current = (kept_share * half_step + arrived.astype(jnp.float32)).astype(jnp.bfloat16)
        weight = kept_share * weight + arrived_weight
        message = (outgoing, outgoing_weight)
        if step_index == 0:
            message = from_behind((outgoing, outgoing_weight), "group", 1)
        else:
            message = from_behind((outgoing, outgoing_weight), "group", 2)
        arrived = message[0]
        arrived_weight = message[1].astype(jnp.float32)
        value_steps.append(values)
    return (current[None], weight, arrived[None], arrived_weight, jnp.stack(value_steps))


def solution(mesh):
    placed = (
        P(None, "group", "mp"),
        P(None, ("group", "mp"), None),
        P("group", "mp", None),
        P("group", "mp", None),
        P("group", "mp", None),
        P("group"),
        P("group"),
        P("group", None),
    )
    return jax.shard_map(
        local,
        mesh=mesh,
        in_specs=placed,
        out_specs=(
            P("group", "mp", None),
            P("group"),
            P("group", "mp", None),
            P("group"),
            P(None, ("group", "mp"), None),
        ),
        check_vma=False,
    )
```

profile of v0, /device:TPU:1, one launch (start us, length us, event | category | flops | bytes accessed | tf_op | source)
XLA Modules:
  0.0 448.1 jit_solution(8477593004699742631)
XLA Ops:
  7.9 1.2 copy.32
  9.1 1.6 fusion
  10.7 1.7 copy.41
  12.5 121.7 %reduce-scatter.7.cloned.1.call-done = bf16[24,1024]{1,0:T(8,128)(2,1)} async-done(((bf16[768,1024]{1,0:T(8,128)(2,1)}), bf16[24,1024]{1,0:T(8,128)(2,1)}) %reduce-scatter.7.cloned.1.call-update) | async-done | bytes 49168 | tf_op jit(solution)/shard_map/reduce_scatter | solution.py:41
  134.2 1.4 fusion.27
  136.3 0.6 fusion.30
  137.8 0.3 copy.33
  138.1 72.2 %all-gather.3.cloned.1.call-done = bf16[768,1024]{1,0:T(8,128)(2,1)} async-done(((bf16[24,1024]{1,0:T(8,128)(2,1)}), bf16[768,1024]{1,0:T(8,128)(2,1)}) %all-gather.3.cloned.1.call-update) | async-done | bytes 1572880 | tf_op jit(solution)/shard_map/all_gather | solution.py:59
  210.3 3.1 multiply_convert_fusion.3
  213.4 1.0 copy-done.9
  214.4 0.7 fusion.1
  215.1 1.7 copy.43
  216.9 110.8 %reduce-scatter.9.cloned.1.call-done = bf16[24,1024]{1,0:T(8,128)(2,1)} async-done(((bf16[768,1024]{1,0:T(8,128)(2,1)}), bf16[24,1024]{1,0:T(8,128)(2,1)}) %reduce-scatter.9.cloned.1.call-update) | async-done | bytes 49168 | tf_op jit(solution)/shard_map/reduce_scatter | solution.py:41
  327.7 1.4 fusion.26
  329.1 2.1 collective-permute-start
  331.9 13.9 %collective-permute-done = bf16[256,1024]{0,1:T(8,128)(2,1)S(1)} collective-permute-done((bf16[256,1024]{0,1:T(8,128)(2,1)S(1)}, bf16[256,1024]{0,1:T(8,128)(2,1)S(1)}, u32[]{:S(2)}, u32[]{:S(2)}) %collective-permute-start) | collective-permute-done | bytes 524320 | tf_op jit(solution)/shard_map/ppermute | solution.py:19
  345.8 57.9 %all-gather.5.cloned.1.call-done = bf16[768,1024]{1,0:T(8,128)(2,1)} async-done(((bf16[24,1024]{1,0:T(8,128)(2,1)}), bf16[768,1024]{1,0:T(8,128)(2,1)}) %all-gather.5.cloned.1.call-update) | async-done | bytes 1572880 | tf_op jit(solution)/shard_map/all_gather | solution.py:59
  403.7 2.7 multiply_convert_fusion.2
  406.4 1.9 collective-permute-start.2
  408.3 11.5 %collective-permute-start.3 = (bf16[1]{0:T(256)(128)(2,1)}, bf16[1]{0:T(256)(128)(2,1)}, u32[]{:S(2)}, u32[]{:S(2)}) collective-permute-start(bf16[1]{0:T(256)(128)(2,1)} %mul.109), channel_id=1, source_target_pairs={{0,64},{32,96},{64,128},{96,160},{128,192},{160,224},{192,256},{22... | collective-permute-start | bytes 14 | tf_op jit(solution)/shard_map/ppermute | solution.py:19
  419.8 15.0 %collective-permute-start.1 = (bf16[1]{0:T(256)(128)(2,1)}, bf16[1]{0:T(256)(128)(2,1)}, u32[]{:S(2)}, u32[]{:S(2)}) collective-permute-start(bf16[1]{0:T(256)(128)(2,1)} %mul.105), channel_id=1, source_target_pairs={{0,32},{32,64},{64,96},{96,128},{128,160},{160,192},{192,224},{224... | collective-permute-start | bytes 14 | tf_op jit(solution)/shard_map/ppermute | solution.py:19
  436.7 0.7 pad_maximum_fusion
  437.3 1.0 copy.39
  438.3 1.0 copy.40
  (35 shorter events, 1.1 us)
Async XLA Ops:
  7.2 127.0 %reduce-scatter.7.cloned.1.call-start = ((), (), s32[]{:S(2)}) async-start(), calls=%async_computation.4 | async-start | bytes 1622016 | tf_op jit(solution)/shard_map/reduce_scatter | solution.py:41
  10.7 123.4 %copy-start.4 = (bf16[2,24,1024]{2,1,0:T(8,128)(2,1)S(1)}, bf16[2,24,1024]{2,1,0:T(8,128)(2,1)}, u32[]{:S(2)}) copy-start(bf16[2,24,1024]{2,1,0:T(8,128)(2,1)} %param.9) | copy-start | bytes 294916
  12.4 123.9 %copy-start.5 = (s32[1,2]{1,0:T(1,128)S(1)}, s32[1,2]{1,0:T(1,128)}, u32[]{:S(2)}) copy-start(s32[1,2]{1,0:T(1,128)} %param.15) | copy-start | bytes 28
  12.4 125.1 %copy-start.1 = (bf16[1,256,1024]{2,1,0:T(8,128)(2,1)S(1)}, bf16[1,256,1024]{2,1,0:T(8,128)(2,1)}, u32[]{:S(2)}) copy-start(bf16[1,256,1024]{2,1,0:T(8,128)(2,1)} %param.12) | copy-start | bytes 1572868
  12.4 125.4 %copy-start = (f32[1,256,1024]{2,1,0:T(8,128)S(1)}, f32[1,256,1024]{2,1,0:T(8,128)}, u32[]{:S(2)}) copy-start(f32[1,256,1024]{2,1,0:T(8,128)} %param.11) | copy-start | bytes 3145732
  12.4 197.9 %all-gather.3.cloned.1.call-start = ((), (), s32[]{:S(2)}) async-start(), calls=%async_computation.2 | async-start | bytes 1622016 | tf_op jit(solution)/shard_map/all_gather | solution.py:59
  135.6 192.0 %reduce-scatter.9.cloned.1.call-start = ((), (), s32[]{:S(2)}) async-start(), calls=%async_computation.5 | async-start | bytes 1622016 | tf_op jit(solution)/shard_map/reduce_scatter | solution.py:41
  210.3 4.0 copy-start.6
  213.4 1.0 copy-start.9
  216.8 112.3 %copy-start.8 = (bf16[256,1024]{0,1:T(8,128)(2,1)S(1)}, bf16[256,1024]{0,1:T(8,128)(2,1)}, u32[]{:S(2)}) copy-start(bf16[256,1024]{0,1:T(8,128)(2,1)} %get-tuple-element.24) | copy-start | bytes 1572868
  216.8 186.9 %copy-start.7 = (bf16[2,768,256]{2,1,0:T(8,128)(2,1)S(1)}, bf16[2,768,256]{2,1,0:T(8,128)(2,1)}, u32[]{:S(2)}) copy-start(bf16[2,768,256]{2,1,0:T(8,128)(2,1)} %param.8) | copy-start | bytes 2359300
  216.8 186.9 %all-gather.5.cloned.1.call-start = ((), (), s32[]{:S(2)}) async-start(), calls=%async_computation.3 | async-start | bytes 1622016 | tf_op jit(solution)/shard_map/all_gather | solution.py:59
  329.1 16.7 %collective-permute-start = (bf16[256,1024]{0,1:T(8,128)(2,1)S(1)}, bf16[256,1024]{0,1:T(8,128)(2,1)S(1)}, u32[]{:S(2)}, u32[]{:S(2)}) collective-permute-start(bf16[256,1024]{0,1:T(8,128)(2,1)S(1)} %copy-done.8), channel_id=1, source_target_pairs={{0,32},{32,64},{64,96},{96,128},{128,160},{160,192},{192,224},{224... | collective-permute-start | bytes 1572872 | tf_op jit(solution)/shard_map/ppermute | solution.py:19
  331.9 104.2 %copy-start.2 = (bf16[24,1024]{1,0:T(8,128)(2,1)S(1)}, bf16[24,1024]{1,0:T(8,128)(2,1)}, u32[]{:S(2)}) copy-start(bf16[24,1024]{1,0:T(8,128)(2,1)} %reduce-scatter.7.cloned.1.call-done) | copy-start | bytes 147460
  331.9 104.5 %copy-start.3 = (bf16[24,1024]{1,0:T(8,128)(2,1)S(1)}, bf16[24,1024]{1,0:T(8,128)(2,1)}, u32[]{:S(2)}) copy-start(bf16[24,1024]{1,0:T(8,128)(2,1)} %reduce-scatter.9.cloned.1.call-done) | copy-start | bytes 147460
  406.4 32.0 %collective-permute-start.2 = (bf16[256,1024]{0,1:T(8,128)(2,1)S(1)}, bf16[256,1024]{0,1:T(8,128)(2,1)S(1)}, u32[]{:S(2)}, u32[]{:S(2)}) collective-permute-start(bf16[256,1024]{0,1:T(8,128)(2,1)S(1)} %get-tuple-element.20), channel_id=1, source_target_pairs={{0,64},{32,96},{64,128},{96,160},{128,192},{160,224},{192,256},{22... | collective-permute-start | bytes 1572872 | tf_op jit(solution)/shard_map/ppermute | solution.py:19
  408.3 26.4 %collective-permute-start.3 = (bf16[1]{0:T(256)(128)(2,1)}, bf16[1]{0:T(256)(128)(2,1)}, u32[]{:S(2)}, u32[]{:S(2)}) collective-permute-start(bf16[1]{0:T(256)(128)(2,1)} %mul.109), channel_id=1, source_target_pairs={{0,64},{32,96},{64,128},{96,160},{128,192},{160,224},{192,256},{22... | collective-permute-start | bytes 14 | tf_op jit(solution)/shard_map/ppermute | solution.py:19
  419.8 15.6 %collective-permute-start.1 = (bf16[1]{0:T(256)(128)(2,1)}, bf16[1]{0:T(256)(128)(2,1)}, u32[]{:S(2)}, u32[]{:S(2)}) collective-permute-start(bf16[1]{0:T(256)(128)(2,1)} %mul.105), channel_id=1, source_target_pairs={{0,32},{32,64},{64,96},{96,128},{128,160},{160,192},{192,224},{224... | collective-permute-start | bytes 14 | tf_op jit(solution)/shard_map/ppermute | solution.py:19
Sparse Core Ops, SparseCore 0:
  12.6 121.5 reduce-scatter.6
  137.9 72.4 all-gather.2
  216.9 110.6 reduce-scatter.8
  331.2 72.4 all-gather.4
where the time goes:
time: 449 us; the launch traced here: 448 us
  waiting for transfers between devices  377 us (84%)
  starting transfers between devices  30.6 us (7%)
  between operations  20.1 us (4%)
  local copies, waits for them, and re-layouts  9.29 us (2%)
  matrix products  8.1 us (2%)
    reduce_scatter x2, waiting for transfers between devices, local(): lax.psum_scatter(row_term(jnp.int32(0), lax.axis_size('mp') * own_rows).a...  232 us
    all_gather x2, waiting for transfers between devices, local(): lax.all_gather(residual, 'mp', axis=0, tiled=True)  130 us
    ppermute x4, starting transfers between devices, from_behind(): return lax.ppermute(value, axis, pairs)  30.4 us
    ppermute x4, waiting for transfers between devices, from_behind(): return lax.ppermute(value, axis, pairs)  14 us
  transfers between devices with their start and end apart: 8, of which 5 were waited for; matrix products, arithmetic and copies ran while one was open for 1% of the time, Pallas kernels for 0%

commit v1 on v0

v1 whole, which is shorter than its diff:
```python
import math

import jax
import jax.numpy as jnp
import numpy as np
from jax import lax
from jax.sharding import PartitionSpec as P

D = 8192
TOK_GRP = 768
N_MP = 32
ROWS = TOK_GRP // N_MP

momentum_decay = 0.9
step_size = 0.5


def turns(core):
    return (1, 3) if core == 0 else (3, 1)


def partner(index, step):
    zh, y, core = index // 8, index // 2 % 4, index % 2
    if step == 0:
        core ^= 1
    elif step <= 2:
        y ^= turns(core)[step - 1]
    else:
        zh ^= turns(core)[step - 3]
    return zh * 8 + y * 2 + core


def block_order():
    table = np.zeros((N_MP, N_MP), np.int32)
    for index in range(N_MP):
        zh, y, core = index // 8, index // 2 % 4, index % 2
        for place in range(N_MP):
            bits = [place >> (4 - k) & 1 for k in range(5)]
            owner = core ^ bits[0]
            t0, t1 = turns(owner)
            dy = (bits[1] * t0) ^ (bits[2] * t1)
            dz = (bits[3] * t0) ^ (bits[4] * t1)
            table[index, place] = (zh ^ dz) * 8 + (y ^ dy) * 2 + owner
    return table


PAIRS = [[(i, partner(i, step)) for i in range(N_MP)] for step in range(5)]


def reduce_scatter(part):
    for step in range(5):
        half = part.shape[0] // 2
        got = lax.ppermute(part[half:], "mp", PAIRS[step])
        part = (part[:half].astype(jnp.float32) + got.astype(jnp.float32)).astype(jnp.bfloat16)
    return part


def all_gather(own):
    for step in (4, 3, 2, 1):
        own = jnp.concatenate([own, lax.ppermute(own, "mp", PAIRS[step])], axis=0)
    return own, lax.ppermute(own, "mp", PAIRS[0])


def local(inputs, targets, numerator, momentum, received, push_weight, received_weight, mix_share):
    row_scale = 1.0 / math.sqrt(D)
    grad_scale = 1.0 / math.sqrt(TOK_GRP)
    count = lax.axis_size("group")
    me = lax.axis_index("group")
    current = numerator[0]
    velocity = momentum[0]
    arrived = received[0]

    kept = mix_share[0].astype(jnp.float32) / 8.0
    weight0 = push_weight[0]
    weight1 = kept[0] * weight0 + received_weight[0]
    sent = jnp.stack([(1.0 - kept[0]) * weight0, (1.0 - kept[1]) * weight1]).astype(jnp.bfloat16)
    all_sent = lax.all_gather(sent, "group", axis=0).astype(jnp.float32)
    arrived0 = lax.dynamic_index_in_dim(all_sent, lax.rem(me + count - 1, count), 0, False)[0]
    arrived1 = lax.dynamic_index_in_dim(all_sent, lax.rem(me + count - 2, count), 0, False)[1]
    weight2 = kept[1] * weight1 + arrived0
    weights = (weight0, weight1)

    order = jnp.asarray(block_order())[lax.axis_index("mp")]
    place = lax.broadcasted_iota(jnp.int32, (N_MP, ROWS, TOK_GRP), 2)
    want = order[:, None, None] * ROWS + lax.broadcasted_iota(jnp.int32, (N_MP, ROWS, TOK_GRP), 1)
    pick = (place == want).astype(jnp.bfloat16).reshape(TOK_GRP, TOK_GRP)

    value_steps = []
    for step in range(2):
        tokens = jnp.dot(pick, inputs[step], preferred_element_type=jnp.float32).astype(jnp.bfloat16)
        scaled = (current.astype(jnp.float32) / weights[step]).astype(jnp.bfloat16)
        product = jnp.dot(tokens, scaled, preferred_element_type=jnp.float32) * row_scale
        values = reduce_scatter(product.astype(jnp.bfloat16))
        residual = (
            values.astype(jnp.float32) - targets[step].astype(jnp.float32)
        ).astype(jnp.bfloat16)
        near, far = all_gather(residual)
        half = near.shape[0]
        dims = (((0,), (0,)), ((), ()))
        gradient = (
            lax.dot_general(tokens[:half], near, dims, preferred_element_type=jnp.float32)
            + lax.dot_general(tokens[half:], far, dims, preferred_element_type=jnp.float32)
        ) * grad_scale
        velocity = momentum_decay * velocity + gradient
        half_step = current.astype(jnp.float32) - step_size * velocity
        outgoing = ((1.0 - kept[step]) * half_step).astype(jnp.bfloat16)
        current = (kept[step] * half_step + arrived.astype(jnp.float32)).astype(jnp.bfloat16)
        hop = 2**step
        arrived = lax.ppermute(outgoing, "group", [(i, (i + hop) % count) for i in range(count)])
        value_steps.append(values)
    return (
        current[None],
        weight2[None],
        arrived[None],
        arrived1[None],
        jnp.stack(value_steps),
    )


def solution(mesh):
    placed = (
        P(None, "group", "mp"),
        P(None, ("group", "mp"), None),
        P("group", "mp", None),
        P("group", "mp", None),
        P("group", "mp", None),
        P("group"),
        P("group"),
        P("group", None),
    )
    return jax.shard_map(
        local,
        mesh=mesh,
        in_specs=placed,
        out_specs=(
            P("group", "mp", None),
            P("group"),
            P("group", "mp", None),
            P("group"),
            P(None, ("group", "mp"), None),
        ),
        check_vma=False,
    )
```

time: 449 us -> 279 us (0.62)
  waiting for transfers between devices: 377 us -> 90.1 us
  starting transfers between devices: 30.6 us -> 123 us
  blocking collectives: 0 us -> 39.2 us
  between operations: 20.1 us -> 6.33 us
  local copies, waits for them, and re-layouts: 9.29 us -> 3.44 us
    reduce_scatter x2 -> x0, waiting for transfers between devices: 232 us -> none  [local(): lax.psum_scatter(row_term(jnp.int32(0), lax.axis_size('mp') * own_rows).a...]
    all_gather x2 -> x0, waiting for transfers between devices: 130 us -> none  [local(): lax.all_gather(residual, 'mp', axis=0, tiled=True)]
    ppermute x4 -> x22, starting transfers between devices: 30.4 us -> 123 us  [the longest x10 52.6 us: reduce_scatter(): got = lax.ppermute(part[half:], 'mp', PAIRS[step])]
    ppermute x4 -> x22, waiting for transfers between devices: 14 us -> 90.1 us  [the longest x10 36.3 us: reduce_scatter(): got = lax.ppermute(part[half:], 'mp', PAIRS[step])]
    all_gather x0 -> x1, blocking collectives: none -> 39.2 us  [local(): all_sent = lax.all_gather(sent, 'group', axis=0).astype(jnp.float32)]
    unnamed x29, local copies, waits for them, and re-layouts: 8.46 us -> 2 us
    dot_general x4 -> x8, matrix products: 8.1 us -> 12.3 us  [the longest x2 5.46 us: local(): lax.dot_general(tokens[:half], near, dims, preferred_element_type=jnp.flo...]
  transfers between devices with their start and end apart: 8 -> 22, of which waited for: 5 -> 19; matrix products, arithmetic and copies ran while one was open for 1% -> 2% of each run, Pallas kernels for 0% -> 0%
where the time goes in v1:
time: 279 us; the launch traced here: 278 us
  starting transfers between devices  123 us (44%)
  waiting for transfers between devices  90.1 us (32%)
  blocking collectives  39.2 us (14%)
  matrix products  12.3 us (4%)
  between operations  6.33 us (2%)
  local copies, waits for them, and re-layouts  3.44 us (1%)
  other arithmetic  3.11 us (1%)
    ppermute x10, starting transfers between devices, reduce_scatter(): got = lax.ppermute(part[half:], 'mp', PAIRS[step])  52.6 us
    ppermute x8, starting transfers between devices, all_gather(): own = jnp.concatenate([own, lax.ppermute(own, 'mp', PAIRS[step])], axis=0)  42.1 us
    all_gather x1, blocking collectives, local(): all_sent = lax.all_gather(sent, 'group', axis=0).astype(jnp.float32)  39.2 us
    ppermute x10, waiting for transfers between devices, reduce_scatter(): got = lax.ppermute(part[half:], 'mp', PAIRS[step])  36.3 us
    ppermute x8, waiting for transfers between devices, all_gather(): own = jnp.concatenate([own, lax.ppermute(own, 'mp', PAIRS[step])], axis=0)  31.4 us
    ppermute x2, waiting for transfers between devices, local(): lax.ppermute(outgoing, 'group', [(i, (i + hop) % count) for i in range(co...  22.3 us
    ppermute x2, starting transfers between devices, all_gather(): return (own, lax.ppermute(own, 'mp', PAIRS[0]))  19.9 us
    ppermute x2, starting transfers between devices, local(): lax.ppermute(outgoing, 'group', [(i, (i + hop) % count) for i in range(co...  8.6 us
  transfers between devices with their start and end apart: 22, of which 19 were waited for; matrix products, arithmetic and copies ran while one was open for 2% of the time, Pallas kernels for 0%

profile of v1, /device:TPU:1, one launch (start us, length us, event | category | flops | bytes accessed | tf_op | source)
XLA Modules:
  0.0 277.7 jit_solution(3352316616193696978)
XLA Ops:
  4.8 8.8 %collective-permute-start = (bf16[384,1024]{1,0:T(8,128)(2,1)S(1)}, bf16[384,1024]{1,0:T(8,128)(2,1)S(1)}, u32[]{:S(2)}, u32[]{:S(2)}) collective-permute-start(bf16[384,1024]{1,0:T(8,128)(2,1)S(1)} %slice.143), channel_id=1, source_target_pairs={{0,1},{1,0},{2,3},{3,2},{4,5},{5,4},{6,7},{7,6},{8,9},{9,8},{10,11... | collective-permute-start | bytes 2359304 | tf_op jit(solution)/shard_map/ppermute | solution.py:53
  17.9 7.8 %collective-permute-done.1 = bf16[192,1024]{1,0:T(8,128)(2,1)S(1)} collective-permute-done((bf16[192,1024]{1,0:T(8,128)(2,1)S(1)}, bf16[192,1024]{1,0:T(8,128)(2,1)S(1)}, u32[]{:S(2)}, u32[]{:S(2)}) %collective-permute-start.1) | collective-permute-done | bytes 393248 | tf_op jit(solution)/shard_map/ppermute | solution.py:53
  27.8 4.8 %collective-permute-done.2 = bf16[96,1024]{1,0:T(8,128)(2,1)S(1)} collective-permute-done((bf16[96,1024]{1,0:T(8,128)(2,1)S(1)}, bf16[96,1024]{1,0:T(8,128)(2,1)S(1)}, u32[]{:S(2)}, u32[]{:S(2)}) %collective-permute-start.2) | collective-permute-done | bytes 196640 | tf_op jit(solution)/shard_map/ppermute | solution.py:53
  32.7 7.2 %collective-permute-start.3 = (bf16[48,1024]{1,0:T(8,128)(2,1)S(1)}, bf16[48,1024]{1,0:T(8,128)(2,1)S(1)}, u32[]{:S(2)}, u32[]{:S(2)}) collective-permute-start(bf16[48,1024]{1,0:T(8,128)(2,1)S(1)} %slice.149), channel_id=1, source_target_pairs={{0,8},{1,25},{2,10},{3,27},{4,12},{5,29},{6,14},{7,31},{8,0},{9,17... | collective-permute-start | bytes 294920 | tf_op jit(solution)/shard_map/ppermute | solution.py:53
  43.7 6.5 %collective-permute-start.4 = (bf16[24,1024]{1,0:T(8,128)(2,1)S(1)}, bf16[24,1024]{1,0:T(8,128)(2,1)S(1)}, u32[]{:S(2)}, u32[]{:S(2)}) collective-permute-start(bf16[24,1024]{1,0:T(8,128)(2,1)S(1)} %slice.151), channel_id=1, source_target_pairs={{0,24},{1,9},{2,26},{3,11},{4,28},{5,13},{6,30},{7,15},{8,16},{9,1... | collective-permute-start | bytes 147464 | tf_op jit(solution)/shard_map/ppermute | solution.py:53
  52.5 6.5 %collective-permute-start.5 = (bf16[24,1024]{1,0:T(8,128)(2,1)S(1)}, bf16[24,1024]{1,0:T(8,128)(2,1)S(1)}, u32[]{:S(2)}, u32[]{:S(2)}) collective-permute-start(bf16[24,1024]{1,0:T(8,128)(2,1)S(1)} %get-tuple-element.8), channel_id=1, source_target_pairs={{0,24},{1,9},{2,26},{3,11},{4,28},{5,13},{6,30},{7,15},{8,16},{9,1... | collective-permute-start | bytes 147464 | tf_op jit(solution)/shard_map/ppermute | solution.py:60
  61.3 8.0 %collective-permute-start.6 = (bf16[48,1024]{1,0:T(8,128)(2,1)S(1)}, bf16[48,1024]{1,0:T(8,128)(2,1)S(1)}, u32[]{:S(2)}, u32[]{:S(2)}) collective-permute-start(bf16[48,1024]{1,0:T(8,128)(2,1)S(1)} %pad_maximum_fusion.4), channel_id=1, source_target_pairs={{0,8},{1,25},{2,10},{3,27},{4,12},{5,29},{6,14},{7,31},{8,0},{9,17... | collective-permute-start | bytes 294920 | tf_op jit(solution)/shard_map/ppermute | solution.py:60
  73.4 4.4 %collective-permute-done.7 = bf16[96,1024]{1,0:T(8,128)(2,1)S(1)} collective-permute-done((bf16[96,1024]{1,0:T(8,128)(2,1)S(1)}, bf16[96,1024]{1,0:T(8,128)(2,1)S(1)}, u32[]{:S(2)}, u32[]{:S(2)}) %collective-permute-start.7) | collective-permute-done | bytes 196640 | tf_op jit(solution)/shard_map/ppermute | solution.py:60
  77.8 5.8 %collective-permute-start.8 = (bf16[192,1024]{1,0:T(8,128)(2,1)S(1)}, bf16[192,1024]{1,0:T(8,128)(2,1)S(1)}, u32[]{:S(2)}, u32[]{:S(2)}) collective-permute-start(bf16[192,1024]{1,0:T(8,128)(2,1)S(1)} %pad_maximum_fusion), channel_id=1, source_target_pairs={{0,2},{1,7},{2,0},{3,5},{4,6},{5,3},{6,4},{7,1},{8,10},{9,15},{10,... | collective-permute-start | bytes 1179656 | tf_op jit(solution)/shard_map/ppermute | solution.py:60
  83.7 5.8 %collective-permute-done.8 = bf16[192,1024]{1,0:T(8,128)(2,1)S(1)} collective-permute-done((bf16[192,1024]{1,0:T(8,128)(2,1)S(1)}, bf16[192,1024]{1,0:T(8,128)(2,1)S(1)}, u32[]{:S(2)}, u32[]{:S(2)}) %collective-permute-start.8) | collective-permute-done | bytes 393248 | tf_op jit(solution)/shard_map/ppermute | solution.py:60
  89.5 8.9 %collective-permute-start.9 = (bf16[384,1024]{1,0:T(8,128)(2,1)S(1)}, bf16[384,1024]{1,0:T(8,128)(2,1)S(1)}, u32[]{:S(2)}, u32[]{:S(2)}) collective-permute-start(bf16[384,1024]{1,0:T(8,128)(2,1)S(1)} %constant_dynamic-update-slice_fusion), channel_id=1, source_target_pairs={{0,1},{1,0},{2,3},{3,2},{4,5},{5,4},{6,7},{7,6},{8,9},{9,8},{10,11... | collective-permute-start | bytes 2359304 | tf_op jit(solution)/shard_map/ppermute | solution.py:61
  111.3 4.6 %collective-permute-start.11 = (bf16[192,1024]{1,0:T(8,128)(2,1)S(1)}, bf16[192,1024]{1,0:T(8,128)(2,1)S(1)}, u32[]{:S(2)}, u32[]{:S(2)}) collective-permute-start(bf16[192,1024]{1,0:T(8,128)(2,1)S(1)} %slice.157), channel_id=1, source_target_pairs={{0,2},{1,7},{2,0},{3,5},{4,6},{5,3},{6,4},{7,1},{8,10},{9,15},{10,... | collective-permute-start | bytes 1179656 | tf_op jit(solution)/shard_map/ppermute | solution.py:53
  115.9 5.2 %collective-permute-done.11 = bf16[192,1024]{1,0:T(8,128)(2,1)S(1)} collective-permute-done((bf16[192,1024]{1,0:T(8,128)(2,1)S(1)}, bf16[192,1024]{1,0:T(8,128)(2,1)S(1)}, u32[]{:S(2)}, u32[]{:S(2)}) %collective-permute-start.11) | collective-permute-done | bytes 393248 | tf_op jit(solution)/shard_map/ppermute | solution.py:53
  123.1 4.8 %collective-permute-done.12 = bf16[96,1024]{1,0:T(8,128)(2,1)S(1)} collective-permute-done((bf16[96,1024]{1,0:T(8,128)(2,1)S(1)}, bf16[96,1024]{1,0:T(8,128)(2,1)S(1)}, u32[]{:S(2)}, u32[]{:S(2)}) %collective-permute-start.12) | collective-permute-done | bytes 196640 | tf_op jit(solution)/shard_map/ppermute | solution.py:53
  128.0 7.6 %collective-permute-start.13 = (bf16[48,1024]{1,0:T(8,128)(2,1)S(1)}, bf16[48,1024]{1,0:T(8,128)(2,1)S(1)}, u32[]{:S(2)}, u32[]{:S(2)}) collective-permute-start(bf16[48,1024]{1,0:T(8,128)(2,1)S(1)} %slice.161), channel_id=1, source_target_pairs={{0,8},{1,25},{2,10},{3,27},{4,12},{5,29},{6,14},{7,31},{8,0},{9,17... | collective-permute-start | bytes 294920 | tf_op jit(solution)/shard_map/ppermute | solution.py:53
  137.6 10.3 %collective-permute-start.14 = (bf16[24,1024]{1,0:T(8,128)(2,1)S(1)}, bf16[24,1024]{1,0:T(8,128)(2,1)S(1)}, u32[]{:S(2)}, u32[]{:S(2)}) collective-permute-start(bf16[24,1024]{1,0:T(8,128)(2,1)S(1)} %slice.163), channel_id=1, source_target_pairs={{0,24},{1,9},{2,26},{3,11},{4,28},{5,13},{6,30},{7,15},{8,16},{9,1... | collective-permute-start | bytes 147464 | tf_op jit(solution)/shard_map/ppermute | solution.py:53
  149.4 7.3 %collective-permute-start.15 = (bf16[24,1024]{1,0:T(8,128)(2,1)S(1)}, bf16[24,1024]{1,0:T(8,128)(2,1)S(1)}, u32[]{:S(2)}, u32[]{:S(2)}) collective-permute-start(bf16[24,1024]{1,0:T(8,128)(2,1)S(1)} %get-tuple-element.6), channel_id=1, source_target_pairs={{0,24},{1,9},{2,26},{3,11},{4,28},{5,13},{6,30},{7,15},{8,16},{9,1... | collective-permute-start | bytes 147464 | tf_op jit(solution)/shard_map/ppermute | solution.py:60
  158.2 6.3 %collective-permute-start.16 = (bf16[48,1024]{1,0:T(8,128)(2,1)S(1)}, bf16[48,1024]{1,0:T(8,128)(2,1)S(1)}, u32[]{:S(2)}, u32[]{:S(2)}) collective-permute-start(bf16[48,1024]{1,0:T(8,128)(2,1)S(1)} %pad_maximum_fusion.5), channel_id=1, source_target_pairs={{0,8},{1,25},{2,10},{3,27},{4,12},{5,29},{6,14},{7,31},{8,0},{9,17... | collective-permute-start | bytes 294920 | tf_op jit(solution)/shard_map/ppermute | solution.py:60
  169.6 4.8 %collective-permute-done.17 = bf16[96,1024]{1,0:T(8,128)(2,1)S(1)} collective-permute-done((bf16[96,1024]{1,0:T(8,128)(2,1)S(1)}, bf16[96,1024]{1,0:T(8,128)(2,1)S(1)}, u32[]{:S(2)}, u32[]{:S(2)}) %collective-permute-start.17) | collective-permute-done | bytes 196640 | tf_op jit(solution)/shard_map/ppermute | solution.py:60
  178.8 7.5 %collective-permute-done.18 = bf16[192,1024]{1,0:T(8,128)(2,1)S(1)} collective-permute-done((bf16[192,1024]{1,0:T(8,128)(2,1)S(1)}, bf16[192,1024]{1,0:T(8,128)(2,1)S(1)}, u32[]{:S(2)}, u32[]{:S(2)}) %collective-permute-start.18) | collective-permute-done | bytes 393248 | tf_op jit(solution)/shard_map/ppermute | solution.py:60
  186.3 11.0 %collective-permute-start.19 = (bf16[384,1024]{1,0:T(8,128)(2,1)S(1)}, bf16[384,1024]{1,0:T(8,128)(2,1)S(1)}, u32[]{:S(2)}, u32[]{:S(2)}) collective-permute-start(bf16[384,1024]{1,0:T(8,128)(2,1)S(1)} %constant_dynamic-update-slice_fusion.5), channel_id=1, source_target_pairs={{0,1},{1,0},{2,3},{3,2},{4,5},{5,4},{6,7},{7,6},{8,9},{9,8},{10,11... | collective-permute-start | bytes 2359304 | tf_op jit(solution)/shard_map/ppermute | solution.py:61
  197.3 6.7 %collective-permute-start.20 = (bf16[256,1024]{1,0:T(8,128)(2,1)}, bf16[256,1024]{1,0:T(8,128)(2,1)}, u32[]{:S(2)}, u32[]{:S(2)}) collective-permute-start(bf16[256,1024]{1,0:T(8,128)(2,1)} %get-tuple-element.15), channel_id=1, source_target_pairs={{0,32},{32,64},{64,96},{96,128},{128,160},{160,192},{192,224},{224... | collective-permute-start | bytes 1572872 | tf_op jit(solution)/shard_map/ppermute | solution.py:109
  204.8 39.2 %all-gather = bf16[16,1,2]{2,1,0:T(2,128)(2,1)S(1)} all-gather(bf16[1,1,2]{2,1,0:T(2,128)(2,1)S(1)} %maximum_bitcast_fusion), channel_id=1, replica_groups=mesh['group'=16,'mp'=32] {'group'}, dimensions={0}, use_global_device_ids=true | all-gather | bytes 68 | tf_op jit(solution)/shard_map/all_gather | solution.py:77
  253.4 22.3 %collective-permute-done.21 = bf16[256,1024]{1,0:T(8,128)(2,1)S(1)} collective-permute-done((bf16[256,1024]{1,0:T(8,128)(2,1)S(1)}, bf16[256,1024]{1,0:T(8,128)(2,1)S(1)}, u32[]{:S(2)}, u32[]{:S(2)}) %collective-permute-start.21) | collective-permute-done | bytes 524320 | tf_op jit(solution)/shard_map/ppermute | solution.py:109
  (98 shorter events, 59.6 us)
Async XLA Ops:
  4.8 10.7 %collective-permute-start = (bf16[384,1024]{1,0:T(8,128)(2,1)S(1)}, bf16[384,1024]{1,0:T(8,128)(2,1)S(1)}, u32[]{:S(2)}, u32[]{:S(2)}) collective-permute-start(bf16[384,1024]{1,0:T(8,128)(2,1)S(1)} %slice.143), channel_id=1, source_target_pairs={{0,1},{1,0},{2,3},{3,2},{4,5},{5,4},{6,7},{7,6},{8,9},{9,8},{10,11... | collective-permute-start | bytes 2359304 | tf_op jit(solution)/shard_map/ppermute | solution.py:53
  15.8 36.6 %copy-start.9 = (bf16[2,24,1024]{2,1,0:T(8,128)(2,1)S(1)}, bf16[2,24,1024]{2,1,0:T(8,128)(2,1)}, u32[]{:S(2)}) copy-start(bf16[2,24,1024]{2,1,0:T(8,128)(2,1)} %param.10) | copy-start | bytes 294916
  15.9 9.9 %collective-permute-start.1 = (bf16[192,1024]{1,0:T(8,128)(2,1)S(1)}, bf16[192,1024]{1,0:T(8,128)(2,1)S(1)}, u32[]{:S(2)}, u32[]{:S(2)}) collective-permute-start(bf16[192,1024]{1,0:T(8,128)(2,1)S(1)} %slice.145), channel_id=1, source_target_pairs={{0,2},{1,7},{2,0},{3,5},{4,6},{5,3},{6,4},{7,1},{8,10},{9,15},{10,... | collective-permute-start | bytes 1179656 | tf_op jit(solution)/shard_map/ppermute | solution.py:53
  25.9 6.7 %collective-permute-start.2 = (bf16[96,1024]{1,0:T(8,128)(2,1)S(1)}, bf16[96,1024]{1,0:T(8,128)(2,1)S(1)}, u32[]{:S(2)}, u32[]{:S(2)}) collective-permute-start(bf16[96,1024]{1,0:T(8,128)(2,1)S(1)} %slice.147), channel_id=1, source_target_pairs={{0,6},{1,3},{2,4},{3,1},{4,2},{5,7},{6,0},{7,5},{8,14},{9,11},{10,... | collective-permute-start | bytes 589832 | tf_op jit(solution)/shard_map/ppermute | solution.py:53
  32.7 11.0 %collective-permute-start.3 = (bf16[48,1024]{1,0:T(8,128)(2,1)S(1)}, bf16[48,1024]{1,0:T(8,128)(2,1)S(1)}, u32[]{:S(2)}, u32[]{:S(2)}) collective-permute-start(bf16[48,1024]{1,0:T(8,128)(2,1)S(1)} %slice.149), channel_id=1, source_target_pairs={{0,8},{1,25},{2,10},{3,27},{4,12},{5,29},{6,14},{7,31},{8,0},{9,17... | collective-permute-start | bytes 294920 | tf_op jit(solution)/shard_map/ppermute | solution.py:53
  43.7 55.4 %copy-start.10 = (s32[1,2]{1,0:T(1,128)S(1)}, s32[1,2]{1,0:T(1,128)}, u32[]{:S(2)}) copy-start(s32[1,2]{1,0:T(1,128)} %param.16) | copy-start | bytes 28
  43.7 8.7 %collective-permute-start.4 = (bf16[24,1024]{1,0:T(8,128)(2,1)S(1)}, bf16[24,1024]{1,0:T(8,128)(2,1)S(1)}, u32[]{:S(2)}, u32[]{:S(2)}) collective-permute-start(bf16[24,1024]{1,0:T(8,128)(2,1)S(1)} %slice.151), channel_id=1, source_target_pairs={{0,24},{1,9},{2,26},{3,11},{4,28},{5,13},{6,30},{7,15},{8,16},{9,1... | collective-permute-start | bytes 147464 | tf_op jit(solution)/shard_map/ppermute | solution.py:53
  52.5 8.7 %collective-permute-start.5 = (bf16[24,1024]{1,0:T(8,128)(2,1)S(1)}, bf16[24,1024]{1,0:T(8,128)(2,1)S(1)}, u32[]{:S(2)}, u32[]{:S(2)}) collective-permute-start(bf16[24,1024]{1,0:T(8,128)(2,1)S(1)} %get-tuple-element.8), channel_id=1, source_target_pairs={{0,24},{1,9},{2,26},{3,11},{4,28},{5,13},{6,30},{7,15},{8,16},{9,1... | collective-permute-start | bytes 147464 | tf_op jit(solution)/shard_map/ppermute | solution.py:60
  61.3 10.1 %collective-permute-start.6 = (bf16[48,1024]{1,0:T(8,128)(2,1)S(1)}, bf16[48,1024]{1,0:T(8,128)(2,1)S(1)}, u32[]{:S(2)}, u32[]{:S(2)}) collective-permute-start(bf16[48,1024]{1,0:T(8,128)(2,1)S(1)} %pad_maximum_fusion.4), channel_id=1, source_target_pairs={{0,8},{1,25},{2,10},{3,27},{4,12},{5,29},{6,14},{7,31},{8,0},{9,17... | collective-permute-start | bytes 294920 | tf_op jit(solution)/shard_map/ppermute | solution.py:60
  71.4 6.4 %collective-permute-start.7 = (bf16[96,1024]{1,0:T(8,128)(2,1)S(1)}, bf16[96,1024]{1,0:T(8,128)(2,1)S(1)}, u32[]{:S(2)}, u32[]{:S(2)}) collective-permute-start(bf16[96,1024]{1,0:T(8,128)(2,1)S(1)} %pad_maximum_fusion.2), channel_id=1, source_target_pairs={{0,6},{1,3},{2,4},{3,1},{4,2},{5,7},{6,0},{7,5},{8,14},{9,11},{10,... | collective-permute-start | bytes 589832 | tf_op jit(solution)/shard_map/ppermute | solution.py:60
  77.8 11.7 %collective-permute-start.8 = (bf16[192,1024]{1,0:T(8,128)(2,1)S(1)}, bf16[192,1024]{1,0:T(8,128)(2,1)S(1)}, u32[]{:S(2)}, u32[]{:S(2)}) collective-permute-start(bf16[192,1024]{1,0:T(8,128)(2,1)S(1)} %pad_maximum_fusion), channel_id=1, source_target_pairs={{0,2},{1,7},{2,0},{3,5},{4,6},{5,3},{6,4},{7,1},{8,10},{9,15},{10,... | collective-permute-start | bytes 1179656 | tf_op jit(solution)/shard_map/ppermute | solution.py:60
  89.5 13.0 %collective-permute-start.9 = (bf16[384,1024]{1,0:T(8,128)(2,1)S(1)}, bf16[384,1024]{1,0:T(8,128)(2,1)S(1)}, u32[]{:S(2)}, u32[]{:S(2)}) collective-permute-start(bf16[384,1024]{1,0:T(8,128)(2,1)S(1)} %constant_dynamic-update-slice_fusion), channel_id=1, source_target_pairs={{0,1},{1,0},{2,3},{3,2},{4,5},{5,4},{6,7},{7,6},{8,9},{9,8},{10,11... | collective-permute-start | bytes 2359304 | tf_op jit(solution)/shard_map/ppermute | solution.py:61
  106.8 4.2 %collective-permute-start.10 = (bf16[384,1024]{1,0:T(8,128)(2,1)S(1)}, bf16[384,1024]{1,0:T(8,128)(2,1)S(1)}, u32[]{:S(2)}, u32[]{:S(2)}) collective-permute-start(bf16[384,1024]{1,0:T(8,128)(2,1)S(1)} %slice.155), channel_id=1, source_target_pairs={{0,1},{1,0},{2,3},{3,2},{4,5},{5,4},{6,7},{7,6},{8,9},{9,8},{10,11... | collective-permute-start | bytes 2359304 | tf_op jit(solution)/shard_map/ppermute | solution.py:53
  111.3 9.7 %collective-permute-start.11 = (bf16[192,1024]{1,0:T(8,128)(2,1)S(1)}, bf16[192,1024]{1,0:T(8,128)(2,1)S(1)}, u32[]{:S(2)}, u32[]{:S(2)}) collective-permute-start(bf16[192,1024]{1,0:T(8,128)(2,1)S(1)} %slice.157), channel_id=1, source_target_pairs={{0,2},{1,7},{2,0},{3,5},{4,6},{5,3},{6,4},{7,1},{8,10},{9,15},{10,... | collective-permute-start | bytes 1179656 | tf_op jit(solution)/shard_map/ppermute | solution.py:53
  121.2 6.7 %collective-permute-start.12 = (bf16[96,1024]{1,0:T(8,128)(2,1)S(1)}, bf16[96,1024]{1,0:T(8,128)(2,1)S(1)}, u32[]{:S(2)}, u32[]{:S(2)}) collective-permute-start(bf16[96,1024]{1,0:T(8,128)(2,1)S(1)} %slice.159), channel_id=1, source_target_pairs={{0,6},{1,3},{2,4},{3,1},{4,2},{5,7},{6,0},{7,5},{8,14},{9,11},{10,... | collective-permute-start | bytes 589832 | tf_op jit(solution)/shard_map/ppermute | solution.py:53
  128.0 9.6 %collective-permute-start.13 = (bf16[48,1024]{1,0:T(8,128)(2,1)S(1)}, bf16[48,1024]{1,0:T(8,128)(2,1)S(1)}, u32[]{:S(2)}, u32[]{:S(2)}) collective-permute-start(bf16[48,1024]{1,0:T(8,128)(2,1)S(1)} %slice.161), channel_id=1, source_target_pairs={{0,8},{1,25},{2,10},{3,27},{4,12},{5,29},{6,14},{7,31},{8,0},{9,17... | collective-permute-start | bytes 294920 | tf_op jit(solution)/shard_map/ppermute | solution.py:53
  137.6 11.8 %collective-permute-start.14 = (bf16[24,1024]{1,0:T(8,128)(2,1)S(1)}, bf16[24,1024]{1,0:T(8,128)(2,1)S(1)}, u32[]{:S(2)}, u32[]{:S(2)}) collective-permute-start(bf16[24,1024]{1,0:T(8,128)(2,1)S(1)} %slice.163), channel_id=1, source_target_pairs={{0,24},{1,9},{2,26},{3,11},{4,28},{5,13},{6,30},{7,15},{8,16},{9,1... | collective-permute-start | bytes 147464 | tf_op jit(solution)/shard_map/ppermute | solution.py:53
  149.4 8.7 %collective-permute-start.15 = (bf16[24,1024]{1,0:T(8,128)(2,1)S(1)}, bf16[24,1024]{1,0:T(8,128)(2,1)S(1)}, u32[]{:S(2)}, u32[]{:S(2)}) collective-permute-start(bf16[24,1024]{1,0:T(8,128)(2,1)S(1)} %get-tuple-element.6), channel_id=1, source_target_pairs={{0,24},{1,9},{2,26},{3,11},{4,28},{5,13},{6,30},{7,15},{8,16},{9,1... | collective-permute-start | bytes 147464 | tf_op jit(solution)/shard_map/ppermute | solution.py:60
  158.2 9.5 %collective-permute-start.16 = (bf16[48,1024]{1,0:T(8,128)(2,1)S(1)}, bf16[48,1024]{1,0:T(8,128)(2,1)S(1)}, u32[]{:S(2)}, u32[]{:S(2)}) collective-permute-start(bf16[48,1024]{1,0:T(8,128)(2,1)S(1)} %pad_maximum_fusion.5), channel_id=1, source_target_pairs={{0,8},{1,25},{2,10},{3,27},{4,12},{5,29},{6,14},{7,31},{8,0},{9,17... | collective-permute-start | bytes 294920 | tf_op jit(solution)/shard_map/ppermute | solution.py:60
  167.7 6.7 %collective-permute-start.17 = (bf16[96,1024]{1,0:T(8,128)(2,1)S(1)}, bf16[96,1024]{1,0:T(8,128)(2,1)S(1)}, u32[]{:S(2)}, u32[]{:S(2)}) collective-permute-start(bf16[96,1024]{1,0:T(8,128)(2,1)S(1)} %pad_maximum_fusion.3), channel_id=1, source_target_pairs={{0,6},{1,3},{2,4},{3,1},{4,2},{5,7},{6,0},{7,5},{8,14},{9,11},{10,... | collective-permute-start | bytes 589832 | tf_op jit(solution)/shard_map/ppermute | solution.py:60
  174.4 11.8 %collective-permute-start.18 = (bf16[192,1024]{1,0:T(8,128)(2,1)S(1)}, bf16[192,1024]{1,0:T(8,128)(2,1)S(1)}, u32[]{:S(2)}, u32[]{:S(2)}) collective-permute-start(bf16[192,1024]{1,0:T(8,128)(2,1)S(1)} %pad_maximum_fusion.1), channel_id=1, source_target_pairs={{0,2},{1,7},{2,0},{3,5},{4,6},{5,3},{6,4},{7,1},{8,10},{9,15},{10,... | collective-permute-start | bytes 1179656 | tf_op jit(solution)/shard_map/ppermute | solution.py:60
  186.3 59.0 %collective-permute-start.19 = (bf16[384,1024]{1,0:T(8,128)(2,1)S(1)}, bf16[384,1024]{1,0:T(8,128)(2,1)S(1)}, u32[]{:S(2)}, u32[]{:S(2)}) collective-permute-start(bf16[384,1024]{1,0:T(8,128)(2,1)S(1)} %constant_dynamic-update-slice_fusion.5), channel_id=1, source_target_pairs={{0,1},{1,0},{2,3},{3,2},{4,5},{5,4},{6,7},{7,6},{8,9},{9,8},{10,11... | collective-permute-start | bytes 2359304 | tf_op jit(solution)/shard_map/ppermute | solution.py:61
  197.3 49.5 %collective-permute-start.20 = (bf16[256,1024]{1,0:T(8,128)(2,1)}, bf16[256,1024]{1,0:T(8,128)(2,1)}, u32[]{:S(2)}, u32[]{:S(2)}) collective-permute-start(bf16[256,1024]{1,0:T(8,128)(2,1)} %get-tuple-element.15), channel_id=1, source_target_pairs={{0,32},{32,64},{64,96},{96,128},{128,160},{160,192},{192,224},{224... | collective-permute-start | bytes 1572872 | tf_op jit(solution)/shard_map/ppermute | solution.py:109
  250.8 25.0 %collective-permute-start.21 = (bf16[256,1024]{1,0:T(8,128)(2,1)S(1)}, bf16[256,1024]{1,0:T(8,128)(2,1)S(1)}, u32[]{:S(2)}, u32[]{:S(2)}) collective-permute-start(bf16[256,1024]{1,0:T(8,128)(2,1)S(1)} %get-tuple-element.9), channel_id=1, source_target_pairs={{0,64},{32,96},{64,128},{96,160},{128,192},{160,224},{192,256},{22... | collective-permute-start | bytes 1572872 | tf_op jit(solution)/shard_map/ppermute | solution.py:109
  (9 other events, 25.5 us)

commit v2 on v0

v2 whole, which is shorter than its diff:
```python
import math

import jax
import jax.numpy as jnp
from jax import lax
from jax.sharding import Mesh
from jax.sharding import PartitionSpec as P

GROUP = ("x", "z_lo")
MP = ("z_hi", "y", "core")
SIZES = (4, 4, 4, 4, 2)

momentum_decay = 0.9
step_size = 0.5


def f32(value):
    return value.astype(jnp.float32)


def bf16(value):
    return value.astype(jnp.bfloat16)


def pick(first, when_true, when_false):
    return jnp.where(first, when_true, when_false)


def z_pairs(step):
    pairs = []
    for zh in range(SIZES[2]):
        for core in range(2):
            turn = (1, 3)[step ^ core]
            pairs.append((zh * 2 + core, (zh ^ turn) * 2 + core))
    return pairs


def reduce_y(part):
    count = SIZES[3]
    rows = part.shape[0] // count
    got = lax.all_to_all(part, "y", 0, 0, tiled=True).reshape(count, rows, part.shape[1])
    return bf16(jnp.sum(f32(got), axis=0))


def reduce_z(part):
    for step in range(2):
        part = bf16(f32(part) + f32(lax.ppermute(part, ("z_hi", "core"), z_pairs(step))))
    return part


def swap_core(value):
    return lax.ppermute(value, "core", [(0, 1), (1, 0)])


def to_group(value, hop):
    count = SIZES[0] * SIZES[1]
    return lax.ppermute(value, GROUP, [(i, (i + hop) % count) for i in range(count)])


def dot(a, b, dims):
    return lax.dot_general(a, b, (dims, ((), ())), preferred_element_type=jnp.float32)


def local(inputs, targets, numerator, momentum, received, push_weight, received_weight, mix_share):
    tokens_count, width = inputs.shape[1:]
    value_count = numerator.shape[2]
    row_scale = 1.0 / math.sqrt(width * SIZES[2] * SIZES[3] * SIZES[4])
    grad_scale = 1.0 / math.sqrt(tokens_count)
    core = lax.axis_index("core")
    first = core == 0
    cols = value_count // 2
    own_rows = targets.shape[1]

    def own_half(value):
        return pick(first, value[..., :cols], value[..., cols:])

    def other_half(value):
        return pick(first, value[..., cols:], value[..., :cols])

    kept = f32(mix_share[0]) / 8.0
    weight0 = push_weight[0]
    weight1 = kept[0] * weight0 + received_weight[0]
    arrived0 = f32(to_group(bf16((1.0 - kept[0]) * weight0)[None], 1))
    arrived1 = f32(to_group(bf16((1.0 - kept[1]) * weight1)[None], 2))
    weight2 = kept[1] * weight1 + arrived0

    slab = inputs.reshape(2, SIZES[2], SIZES[3], 2 * own_rows, width)
    tokens = slab.transpose(0, 2, 1, 3, 4).reshape(2, tokens_count, width)

    split = cols // 2
    away = other_half(numerator[0])
    got = swap_core(jnp.concatenate([tokens[0], away[:, :split], away[:, split:]], axis=0))
    tokens1 = jnp.concatenate([tokens[0], got[:tokens_count]], axis=1)
    far = got[tokens_count:]
    start = jnp.concatenate(
        [own_half(numerator[0]), jnp.concatenate([far[:width], far[width:]], axis=1)], axis=0
    )
    scaled = bf16(f32(start) / weight0)
    part1 = bf16(dot(tokens1, scaled, ((1,), (0,))) * row_scale)
    values1 = reduce_z(reduce_y(part1))

    away = other_half(received[0])
    got = swap_core(jnp.concatenate([tokens[1], away[:, :split], away[:, split:]], axis=0))
    tokens2 = jnp.concatenate([tokens[1], got[:tokens_count]], axis=1)
    far = got[tokens_count:]
    arrived = jnp.concatenate(
        [own_half(received[0]), jnp.concatenate([far[:width], far[width:]], axis=1)], axis=0
    )
    velocity = jnp.concatenate(
        [own_half(momentum[0]), swap_core(other_half(momentum[0]))], axis=0
    )

    ahead = f32(start) - (step_size * momentum_decay) * velocity
    base = kept[0] * ahead + f32(arrived)
    part2 = bf16(dot(tokens2, bf16(base / weight1), ((1,), (0,))) * row_scale)
    gram_cols = tokens_count // 2
    mine = lax.dynamic_slice_in_dim(tokens1, core * gram_cols, gram_cols, 0)
    gram_part = bf16(dot(tokens2, mine, ((1,), (1,))))
    second = reduce_z(reduce_y(jnp.concatenate([part2, gram_part], axis=1)))
    values2, gram = second[:, :cols], second[:, cols:]
    gram_far = swap_core(gram)

    taught = lax.all_gather(targets, ("z_hi", "core"), axis=1)
    taught = own_half(taught.reshape(2, -1, value_count))

    residual1 = bf16(f32(values1) - f32(taught[0]))
    all1 = lax.all_gather(residual1, "y", axis=0, tiled=True)
    rows_mine = lax.dynamic_slice_in_dim(all1, core * gram_cols, gram_cols, 0)
    rows_far = lax.dynamic_slice_in_dim(all1, (1 - core) * gram_cols, gram_cols, 0)
    turned = dot(gram, rows_mine, ((1,), (0,))) + dot(gram_far, rows_far, ((1,), (0,)))
    values2 = bf16(
        f32(values2) - (step_size * grad_scale * row_scale * kept[0] / weight1) * turned
    )
    residual2 = bf16(f32(values2) - f32(taught[1]))
    all2 = lax.all_gather(residual2, "y", axis=0, tiled=True)

    gradient1 = dot(tokens1, all1, ((0,), (0,))) * grad_scale
    current = bf16(base - (step_size * kept[0]) * gradient1)
    outgoing = bf16((1.0 - kept[0]) * (ahead - step_size * gradient1))
    arrived = to_group(outgoing, 1)
    velocity = momentum_decay * velocity + gradient1

    gradient2 = dot(tokens2, all2, ((0,), (0,))) * grad_scale
    half_step = f32(current) - step_size * (momentum_decay * velocity + gradient2)
    outgoing = bf16((1.0 - kept[1]) * half_step)
    current = bf16(kept[1] * half_step + f32(arrived))

    count = SIZES[0] * SIZES[1]
    hop = [((i * 2 + c), ((i + 2) % count) * 2 + (1 - c)) for i in range(count) for c in range(2)]
    sent_far = lax.ppermute(outgoing[width:], GROUP + ("core",), hop)
    sent_own = to_group(outgoing[:width], 2)

    both = jnp.stack([values1, values2])
    at = lax.axis_index("z_hi") * (2 * own_rows)
    mine = lax.dynamic_slice_in_dim(both, at + core * own_rows, own_rows, 1)
    theirs = lax.dynamic_slice_in_dim(both, at + (1 - core) * own_rows, own_rows, 1)
    got = swap_core(jnp.concatenate([current[width:], theirs.reshape(2 * own_rows, cols)], axis=0))

    def whole(near, far):
        return jnp.concatenate([pick(first, near, far), pick(first, far, near)], axis=-1)

    return (
        whole(current[:width], got[:width])[None],
        weight2,
        whole(sent_own, sent_far)[None],
        arrived1,
        whole(mine, got[width:].reshape(2, own_rows, cols)),
    )


def solution(mesh):
    fine = Mesh(mesh.devices.reshape(SIZES), GROUP + MP)
    placed = (
        P(None, GROUP, MP),
        P(None, GROUP + MP, None),
        P(GROUP, MP, None),
        P(GROUP, MP, None),
        P(GROUP, MP, None),
        P(GROUP),
        P(GROUP),
        P(GROUP, None),
    )
    return jax.shard_map(
        local,
        mesh=fine,
        in_specs=placed,
        out_specs=(
            P(GROUP, MP, None),
            P(GROUP),
            P(GROUP, MP, None),
            P(GROUP),
            P(None, GROUP + MP, None),
        ),
        check_vma=False,
    )
```

time: 449 us -> 205 us (0.46)
  the two profiles are of different devices: /device:TPU:1 before, /device:TPU:35 now
where the time goes in v2:
time: 205 us; the launch traced here: 204 us
  starting transfers between devices  81.7 us (40%)
  blocking collectives  54.3 us (26%)
  waiting for transfers between devices  33.4 us (16%)
  matrix products  12.1 us (6%)
  between operations  10.2 us (5%)
  other arithmetic  9.23 us (5%)
  local copies, waits for them, and re-layouts  2.68 us (1%)
    all_gather x1, blocking collectives, local(): taught = lax.all_gather(targets, ('z_hi', 'core'), axis=1)  31.7 us
    ppermute x5, starting transfers between devices, swap_core(): return lax.ppermute(value, 'core', [(0, 1), (1, 0)])  26.4 us
    ppermute x4, starting transfers between devices, to_group(): lax.ppermute(value, GROUP, [(i, (i + hop) % count) for i in range(count)])  24.7 us
    ppermute x4, waiting for transfers between devices, reduce_z(): lax.ppermute(part, ('z_hi', 'core'), z_pairs(step))  21.8 us
    ppermute x4, starting transfers between devices, reduce_z(): lax.ppermute(part, ('z_hi', 'core'), z_pairs(step))  19.2 us
    dot_general x7, matrix products, dot(): lax.dot_general(a, b, (dims, ((), ())), preferred_element_type=jnp.float32)  12.1 us
    all_gather x1, blocking collectives, local(): all2 = lax.all_gather(residual2, 'y', axis=0, tiled=True)  11.5 us
    all_gather x1, blocking collectives, local(): all1 = lax.all_gather(residual1, 'y', axis=0, tiled=True)  11.1 us
  transfers between devices with their start and end apart: 16, of which 7 were waited for; matrix products, arithmetic and copies ran while one was open for 7% of the time, Pallas kernels for 0%

profile of v2, /device:TPU:35, one launch (start us, length us, event | category | flops | bytes accessed | tf_op | source)
XLA Modules:
  0.0 203.6 jit_solution(4670441185623530880)
XLA Ops:
  2.8 2.7 %collective-permute-start = (bf16[1280,256]{1,0:T(8,128)(2,1)S(1)}, bf16[1280,256]{1,0:T(8,128)(2,1)S(1)}, u32[]{:S(2)}, u32[]{:S(2)}) collective-permute-start(bf16[1280,256]{1,0:T(8,128)(2,1)S(1)} %pad_maximum_fusion.4), channel_id=1, source_target_pairs={{0,1},{1,0},{2,3},{3,2},{4,5},{5,4},{6,7},{7,6},{8,9},{9,8},{10,11... | collective-permute-start | bytes 1966088 | tf_op jit(solution)/shard_map/ppermute | solution.py:52
  7.2 2.0 %collective-permute-start.2 = (bf16[1280,256]{1,0:T(8,128)(2,1)}, bf16[1280,256]{1,0:T(8,128)(2,1)S(1)}, u32[]{:S(2)}, u32[]{:S(2)}) collective-permute-start(bf16[1280,256]{1,0:T(8,128)(2,1)} %pad_maximum_fusion.5), channel_id=1, source_target_pairs={{0,1},{1,0},{2,3},{3,2},{4,5},{5,4},{6,7},{7,6},{8,9},{9,8},{10,11... | collective-permute-start | bytes 1966088 | tf_op jit(solution)/shard_map/ppermute | solution.py:52
  10.3 2.4 %collective-permute-start.1 = (f32[256,512]{1,0:T(8,128)}, f32[256,512]{1,0:T(8,128)}, u32[]{:S(2)}, u32[]{:S(2)}) collective-permute-start(f32[256,512]{1,0:T(8,128)} %get-tuple-element.10), channel_id=1, source_target_pairs={{0,1},{1,0},{2,3},{3,2},{4,5},{5,4},{6,7},{7,6},{8,9},{9,8},{10,11... | collective-permute-start | bytes 1572872 | tf_op jit(solution)/shard_map/ppermute | solution.py:52
  15.4 2.6 %multiply_convert_fusion.1 = bf16[768,512]{1,0:T(8,128)(2,1)} fusion(f32[]{:T(128)} %bitcast.40, bf16[768,256]{1,0:T(8,128)(2,1)S(1)} %slice.170, bf16[768,256]{1,0:T(8,128)(2,1)S(1)} %bitcast.52, bf16[256,256]{1,0:T(8,128)(2,1)S(1)} %get-tuple-element.18, bf16[256,256]{1,0:T(8,128)(2,1)S(1)} %get-tuple-element.17, bf16[256,512]{1,0:T(8,128)(2,1)} %get-tuple-element.25), kind=kOutput, calls=%fused_computation.1 | convolution fusion | flops 407109632 | bytes 2097156 | tf_op jit(solution)/shard_map/dot_general | solution.py:61
  18.0 4.2 %all-to-all-start = ((bf16[4,192,512]{2,1,0:T(8,128)(2,1)}), bf16[4,192,512]{2,1,0:T(8,128)(2,1)S(1)}, u32[]{:S(2)}, u32[]{:S(2)}) async-start(bf16[4,192,512]{2,1,0:T(8,128)(2,1)} %bitcast.10), calls=%async_computation | async-start | bytes 1572864 | tf_op jit(solution)/shard_map/all_to_all | solution.py:41
  23.7 2.4 %multiply_convert_fusion = bf16[768,512]{1,0:T(8,128)(2,1)S(1)} fusion(f32[]{:T(128)S(6)} %add.59, f32[]{:T(128)} %bitcast.1, f32[256,512]{1,0:T(8,128)} %collective-permute-done.1, f32[256,512]{1,0:T(8,128)S(1)} %copy-done.4, bf16[768,256]{1,0:T(8,128)(2,1)S(1)} %slice.174, bf16[768,256]{1,0:T(8,128)(2,1)S(1)} %bitcast.49, ...), kind=kOutput, calls=%fused_computation | convolution fusion | flops 409993216 | bytes 3670024 | tf_op jit(solution)/shard_map/dot_general | solution.py:61
  27.3 7.0 %all-to-all-done = bf16[4,192,512]{2,1,0:T(8,128)(2,1)S(1)} async-done(((bf16[4,192,512]{2,1,0:T(8,128)(2,1)}), bf16[4,192,512]{2,1,0:T(8,128)(2,1)S(1)}, u32[]{:S(2)}, u32[]{:S(2)}) %all-to-all-start) | async-done | bytes 786464 | tf_op jit(solution)/shard_map/all_to_all | solution.py:41
  34.3 3.7 %all-to-all-start.1 = ((bf16[4,192,896]{2,1,0:T(8,128)(2,1)}), bf16[4,192,896]{2,1,0:T(8,128)(2,1)S(1)}, u32[]{:S(2)}, u32[]{:S(2)}) async-start(bf16[4,192,896]{2,1,0:T(8,128)(2,1)} %bitcast.13), calls=%async_computation.1 | async-start | bytes 2752512 | tf_op jit(solution)/shard_map/all_to_all | solution.py:41
  38.0 31.7 %all-gather = bf16[2,192,1024]{2,1,0:T(8,128)(2,1)S(1)} all-gather(bf16[2,24,1024]{2,1,0:T(8,128)(2,1)S(1)} %copy-done.25), channel_id=2, replica_groups=mesh['x'=4,'z_lo'=4,'z_hi'=4,'y'=4,'core'=2] {'z_hi','core'}, dimensions={1}, use_global_device_ids=true | all-gather | bytes 884736 | tf_op jit(solution)/shard_map/all_gather | solution.py:123
  69.9 1.9 collective-permute-start.3
  72.1 7.3 %collective-permute-start.5 = (bf16[192,896]{1,0:T(8,128)(2,1)S(1)}, bf16[192,896]{1,0:T(8,128)(2,1)S(1)}, u32[]{:S(2)}, u32[]{:S(2)}) collective-permute-start(bf16[192,896]{1,0:T(8,128)(2,1)S(1)} %reduce_sum.25), channel_id=1, source_target_pairs={{0,8},{1,25},{8,0},{9,17},{16,24},{17,9},{24,16},{25,1},{2,10},{3,... | collective-permute-start | bytes 1032200 | tf_op jit(solution)/shard_map/ppermute | solution.py:47
  82.1 2.2 %collective-permute-done.3 = bf16[192,512]{1,0:T(8,128)(2,1)S(1)} collective-permute-done((bf16[192,512]{1,0:T(8,128)(2,1)S(1)}, bf16[192,512]{1,0:T(8,128)(2,1)S(1)}, u32[]{:S(2)}, u32[]{:S(2)}) %collective-permute-start.3) | collective-permute-done | bytes 196640 | tf_op jit(solution)/shard_map/ppermute | solution.py:47
  84.4 8.1 %collective-permute-start.4 = (bf16[192,512]{1,0:T(8,128)(2,1)S(1)}, bf16[192,512]{1,0:T(8,128)(2,1)S(1)}, u32[]{:S(2)}, u32[]{:S(2)}) collective-permute-start(bf16[192,512]{1,0:T(8,128)(2,1)S(1)} %add_convert_fusion.4), channel_id=1, source_target_pairs={{0,24},{1,9},{8,16},{9,1},{16,8},{17,25},{24,0},{25,17},{2,26},{3,... | collective-permute-start | bytes 589832 | tf_op jit(solution)/shard_map/ppermute | solution.py:47
  92.5 17.2 %collective-permute-done.5 = bf16[192,896]{1,0:T(8,128)(2,1)S(1)} collective-permute-done((bf16[192,896]{1,0:T(8,128)(2,1)S(1)}, bf16[192,896]{1,0:T(8,128)(2,1)S(1)}, u32[]{:S(2)}, u32[]{:S(2)}) %collective-permute-start.5) | collective-permute-done | bytes 344096 | tf_op jit(solution)/shard_map/ppermute | solution.py:47
  111.8 11.1 %all_gather.14 = bf16[768,512]{1,0:T(8,128)(2,1)S(1)} all-gather(bf16[192,512]{1,0:T(8,128)(2,1)S(1)} %get-tuple-element.27), channel_id=1, replica_groups=mesh['x'=4,'z_lo'=4,'z_hi'=4,'y'=4,'core'=2] {'y'}, dimensions={0}, use_global_device_ids=true | all-gather | bytes 983040 | tf_op jit(solution)/shard_map/all_gather | solution.py:127
  122.9 2.4 %collective-permute-done.6 = bf16[192,896]{1,0:T(8,128)(2,1)S(1)} collective-permute-done((bf16[192,896]{1,0:T(8,128)(2,1)S(1)}, bf16[192,896]{1,0:T(8,128)(2,1)S(1)}, u32[]{:S(2)}, u32[]{:S(2)}) %collective-permute-start.6) | collective-permute-done | bytes 344096 | tf_op jit(solution)/shard_map/ppermute | solution.py:47
  125.5 14.5 %collective-permute-start.7 = (bf16[192,384]{1,0:T(8,128)(2,1)S(1)}, bf16[192,384]{1,0:T(8,128)(2,1)S(1)}, u32[]{:S(2)}, u32[]{:S(2)}) collective-permute-start(bf16[192,384]{1,0:T(8,128)(2,1)S(1)} %slice.176), channel_id=1, source_target_pairs={{0,1},{1,0},{2,3},{3,2},{4,5},{5,4},{6,7},{7,6},{8,9},{9,8},{10,11... | collective-permute-start | bytes 442376 | tf_op jit(solution)/shard_map/ppermute | solution.py:52
  144.4 11.5 %all_gather.15 = bf16[768,512]{1,0:T(8,128)(2,1)S(1)} all-gather(bf16[192,512]{1,0:T(8,128)(2,1)S(1)} %get-tuple-element.35), channel_id=1, replica_groups=mesh['x'=4,'z_lo'=4,'z_hi'=4,'y'=4,'core'=2] {'y'}, dimensions={0}, use_global_device_ids=true | all-gather | bytes 983040 | tf_op jit(solution)/shard_map/all_gather | solution.py:135
  157.2 4.3 %multiply_convert_fusion.2 = (bf16[512,512]{1,0:T(8,128)(2,1)S(1)}, bf16[512,512]{1,0:T(8,128)(2,1)}) fusion(f32[]{:T(128)S(6)} %sub.42, bf16[512,512]{1,0:T(8,128)(2,1)S(1)} %collective-permute-done.8, f32[]{:T(128)} %bitcast, bf16[768,512]{1,0:T(8,128)(2,1)S(1)} %all_gather.15, bf16[768,256]{1,0:T(8,128)(2,1)S(1)} %copy-done.9, ...), kind=kOutput, calls=%fused_computation.11 | convolution fusion | flops 413401088 | bytes 6291472 | tf_op jit(solution)/shard_map/dot_general | solution.py:61
  163.5 3.5 %collective-permute-start.12 = (bf16[256,512]{1,0:T(8,128)(2,1)S(1)}, bf16[256,512]{1,0:T(8,128)(2,1)S(1)}, u32[]{:S(2)}, u32[]{:S(2)}) collective-permute-start(bf16[256,512]{1,0:T(8,128)(2,1)S(1)} %get-tuple-element.22), channel_id=1, source_target_pairs={{0,65},{1,64},{32,97},{33,96},{64,129},{65,128},{96,161},{97,160},... | collective-permute-start | bytes 786440 | tf_op jit(solution)/shard_map/ppermute | solution.py:150
  167.0 18.3 %collective-permute-start.10 = (bf16[1]{0:T(256)(128)(2,1)}, bf16[1]{0:T(256)(128)(2,1)}, u32[]{:S(2)}, u32[]{:S(2)}) collective-permute-start(bf16[1]{0:T(256)(128)(2,1)} %bitcast.20), channel_id=1, source_target_pairs={{0,32},{32,64},{64,96},{96,128},{128,160},{160,192},{192,224},{224... | collective-permute-start | bytes 14 | tf_op jit(solution)/shard_map/ppermute | solution.py:57
  185.2 2.6 %collective-permute-start.13 = (bf16[1]{0:T(256)(128)(2,1)}, bf16[1]{0:T(256)(128)(2,1)}, u32[]{:S(2)}, u32[]{:S(2)}) collective-permute-start(bf16[1]{0:T(256)(128)(2,1)} %bitcast.22), channel_id=1, source_target_pairs={{0,64},{32,96},{64,128},{96,160},{128,192},{160,224},{192,256},{22... | collective-permute-start | bytes 14 | tf_op jit(solution)/shard_map/ppermute | solution.py:57
  188.5 2.9 %collective-permute-done.13 = bf16[1]{0:T(256)(128)(2,1)} collective-permute-done((bf16[1]{0:T(256)(128)(2,1)}, bf16[1]{0:T(256)(128)(2,1)}, u32[]{:S(2)}, u32[]{:S(2)}) %collective-permute-start.13) | collective-permute-done | bytes 34 | tf_op jit(solution)/shard_map/ppermute | solution.py:57
  193.8 4.7 %collective-permute-start.9 = (bf16[304,512]{1,0:T(8,128)(2,1)S(1)}, bf16[304,512]{1,0:T(8,128)(2,1)S(1)}, u32[]{:S(2)}, u32[]{:S(2)}) collective-permute-start(bf16[304,512]{1,0:T(8,128)(2,1)S(1)} %pad_maximum_fusion.8), channel_id=1, source_target_pairs={{0,1},{1,0},{2,3},{3,2},{4,5},{5,4},{6,7},{7,6},{8,9},{9,8},{10,11... | collective-permute-start | bytes 933896 | tf_op jit(solution)/shard_map/ppermute | solution.py:52
  (108 shorter events, 22.2 us)
Async XLA Ops:
  2.7 19.6 %copy-start = (bf16[1,4,4,48,256]{4,3,2,1,0:T(8,128)(2,1)}, bf16[1,4,4,48,256]{4,3,2,1,0:T(8,128)(2,1)S(1)}, u32[]{:S(2)}) copy-start(bf16[1,4,4,48,256]{4,3,2,1,0:T(8,128)(2,1)S(1)} %get-tuple-element.14) | copy-start | bytes 1179652
  2.8 12.5 %collective-permute-start = (bf16[1280,256]{1,0:T(8,128)(2,1)S(1)}, bf16[1280,256]{1,0:T(8,128)(2,1)S(1)}, u32[]{:S(2)}, u32[]{:S(2)}) collective-permute-start(bf16[1280,256]{1,0:T(8,128)(2,1)S(1)} %pad_maximum_fusion.4), channel_id=1, source_target_pairs={{0,1},{1,0},{2,3},{3,2},{4,5},{5,4},{6,7},{7,6},{8,9},{9,8},{10,11... | collective-permute-start | bytes 1966088 | tf_op jit(solution)/shard_map/ppermute | solution.py:52
  7.2 15.0 %collective-permute-start.2 = (bf16[1280,256]{1,0:T(8,128)(2,1)}, bf16[1280,256]{1,0:T(8,128)(2,1)S(1)}, u32[]{:S(2)}, u32[]{:S(2)}) collective-permute-start(bf16[1280,256]{1,0:T(8,128)(2,1)} %pad_maximum_fusion.5), channel_id=1, source_target_pairs={{0,1},{1,0},{2,3},{3,2},{4,5},{5,4},{6,7},{7,6},{8,9},{9,8},{10,11... | collective-permute-start | bytes 1966088 | tf_op jit(solution)/shard_map/ppermute | solution.py:52
  10.3 12.6 %collective-permute-start.1 = (f32[256,512]{1,0:T(8,128)}, f32[256,512]{1,0:T(8,128)}, u32[]{:S(2)}, u32[]{:S(2)}) collective-permute-start(f32[256,512]{1,0:T(8,128)} %get-tuple-element.10), channel_id=1, source_target_pairs={{0,1},{1,0},{2,3},{3,2},{4,5},{5,4},{6,7},{7,6},{8,9},{9,8},{10,11... | collective-permute-start | bytes 1572872 | tf_op jit(solution)/shard_map/ppermute | solution.py:52
  18.0 16.3 %all-to-all-start = ((bf16[4,192,512]{2,1,0:T(8,128)(2,1)}), bf16[4,192,512]{2,1,0:T(8,128)(2,1)S(1)}, u32[]{:S(2)}, u32[]{:S(2)}) async-start(bf16[4,192,512]{2,1,0:T(8,128)(2,1)} %bitcast.10), calls=%async_computation | async-start | bytes 1572864 | tf_op jit(solution)/shard_map/all_to_all | solution.py:41
  34.3 37.4 %all-to-all-start.1 = ((bf16[4,192,896]{2,1,0:T(8,128)(2,1)}), bf16[4,192,896]{2,1,0:T(8,128)(2,1)S(1)}, u32[]{:S(2)}, u32[]{:S(2)}) async-start(bf16[4,192,896]{2,1,0:T(8,128)(2,1)} %bitcast.13), calls=%async_computation.1 | async-start | bytes 2752512 | tf_op jit(solution)/shard_map/all_to_all | solution.py:41
  69.9 14.4 %collective-permute-start.3 = (bf16[192,512]{1,0:T(8,128)(2,1)S(1)}, bf16[192,512]{1,0:T(8,128)(2,1)S(1)}, u32[]{:S(2)}, u32[]{:S(2)}) collective-permute-start(bf16[192,512]{1,0:T(8,128)(2,1)S(1)} %reduce_sum.24), channel_id=1, source_target_pairs={{0,8},{1,25},{8,0},{9,17},{16,24},{17,9},{24,16},{25,1},{2,10},{3,... | collective-permute-start | bytes 589832 | tf_op jit(solution)/shard_map/ppermute | solution.py:47
  72.1 37.5 %collective-permute-start.5 = (bf16[192,896]{1,0:T(8,128)(2,1)S(1)}, bf16[192,896]{1,0:T(8,128)(2,1)S(1)}, u32[]{:S(2)}, u32[]{:S(2)}) collective-permute-start(bf16[192,896]{1,0:T(8,128)(2,1)S(1)} %reduce_sum.25), channel_id=1, source_target_pairs={{0,8},{1,25},{8,0},{9,17},{16,24},{17,9},{24,16},{25,1},{2,10},{3,... | collective-permute-start | bytes 1032200 | tf_op jit(solution)/shard_map/ppermute | solution.py:47
  84.4 27.3 %collective-permute-start.4 = (bf16[192,512]{1,0:T(8,128)(2,1)S(1)}, bf16[192,512]{1,0:T(8,128)(2,1)S(1)}, u32[]{:S(2)}, u32[]{:S(2)}) collective-permute-start(bf16[192,512]{1,0:T(8,128)(2,1)S(1)} %add_convert_fusion.4), channel_id=1, source_target_pairs={{0,24},{1,9},{8,16},{9,1},{16,8},{17,25},{24,0},{25,17},{2,26},{3,... | collective-permute-start | bytes 589832 | tf_op jit(solution)/shard_map/ppermute | solution.py:47
  109.7 15.7 %collective-permute-start.6 = (bf16[192,896]{1,0:T(8,128)(2,1)S(1)}, bf16[192,896]{1,0:T(8,128)(2,1)S(1)}, u32[]{:S(2)}, u32[]{:S(2)}) collective-permute-start(bf16[192,896]{1,0:T(8,128)(2,1)S(1)} %add_convert_fusion.2), channel_id=1, source_target_pairs={{0,24},{1,9},{8,16},{9,1},{16,8},{17,25},{24,0},{25,17},{2,26},{3,... | collective-permute-start | bytes 1032200 | tf_op jit(solution)/shard_map/ppermute | solution.py:47
  111.7 28.3 %copy-start.1 = (bf16[1,4,4,48,256]{4,3,2,1,0:T(8,128)(2,1)S(1)}, bf16[1,4,4,48,256]{4,3,2,1,0:T(8,128)(2,1)}, u32[]{:S(2)}) copy-start(bf16[1,4,4,48,256]{4,3,2,1,0:T(8,128)(2,1)} %copy-done) | copy-start | bytes 1179652
  111.7 28.3 %copy-start.5 = (f32[256,512]{1,0:T(8,128)S(1)}, f32[256,512]{1,0:T(8,128)}, u32[]{:S(2)}) copy-start(f32[256,512]{1,0:T(8,128)} %get-tuple-element.9) | copy-start | bytes 1572868
  111.8 28.3 %copy-start.11 = (bf16[768,256]{1,0:T(8,128)(2,1)S(1)}, bf16[768,256]{1,0:T(8,128)(2,1)}, u32[]{:S(2)}) copy-start(bf16[768,256]{1,0:T(8,128)(2,1)} %copy-done.10) | copy-start | bytes 1179652
  111.8 28.3 %copy-start.13 = (bf16[256,512]{1,0:T(8,128)(2,1)S(1)}, bf16[256,512]{1,0:T(8,128)(2,1)}, u32[]{:S(2)}) copy-start(bf16[256,512]{1,0:T(8,128)(2,1)} %get-tuple-element.25) | copy-start | bytes 786436
  111.8 28.3 %copy-start.17 = (bf16[256,256]{1,0:T(8,128)(2,1)S(1)}, bf16[256,256]{1,0:T(8,128)(2,1)}, u32[]{:S(2)}) copy-start(bf16[256,256]{1,0:T(8,128)(2,1)} %copy-done.16) | copy-start | bytes 393220
  111.8 28.3 %copy-start.20 = (bf16[256,256]{1,0:T(8,128)(2,1)S(1)}, bf16[256,256]{1,0:T(8,128)(2,1)}, u32[]{:S(2)}) copy-start(bf16[256,256]{1,0:T(8,128)(2,1)} %copy-done.18) | copy-start | bytes 393220
  125.5 18.2 %collective-permute-start.7 = (bf16[192,384]{1,0:T(8,128)(2,1)S(1)}, bf16[192,384]{1,0:T(8,128)(2,1)S(1)}, u32[]{:S(2)}, u32[]{:S(2)}) collective-permute-start(bf16[192,384]{1,0:T(8,128)(2,1)S(1)} %slice.176), channel_id=1, source_target_pairs={{0,1},{1,0},{2,3},{3,2},{4,5},{5,4},{6,7},{7,6},{8,9},{9,8},{10,11... | collective-permute-start | bytes 442376 | tf_op jit(solution)/shard_map/ppermute | solution.py:52
  141.8 15.4 %collective-permute-start.8 = (bf16[512,512]{1,0:T(8,128)(2,1)S(1)}, bf16[512,512]{1,0:T(8,128)(2,1)S(1)}, u32[]{:S(2)}, u32[]{:S(2)}) collective-permute-start(bf16[512,512]{1,0:T(8,128)(2,1)S(1)} %get-tuple-element.37), channel_id=1, source_target_pairs={{0,32},{32,64},{64,96},{96,128},{128,160},{160,192},{192,224},{224... | collective-permute-start | bytes 1572872 | tf_op jit(solution)/shard_map/ppermute | solution.py:57
  144.0 13.2 %copy-start.9 = (bf16[768,256]{1,0:T(8,128)(2,1)S(1)}, bf16[768,256]{1,0:T(8,128)(2,1)}, u32[]{:S(2)}) copy-start(bf16[768,256]{1,0:T(8,128)(2,1)} %copy-done.8) | copy-start | bytes 1179652
  161.6 36.9 %collective-permute-start.11 = (bf16[256,512]{1,0:T(8,128)(2,1)S(1)}, bf16[256,512]{1,0:T(8,128)(2,1)S(1)}, u32[]{:S(2)}, u32[]{:S(2)}) collective-permute-start(bf16[256,512]{1,0:T(8,128)(2,1)S(1)} %get-tuple-element.21), channel_id=1, source_target_pairs={{0,64},{32,96},{64,128},{96,160},{128,192},{160,224},{192,256},{22... | collective-permute-start | bytes 786440 | tf_op jit(solution)/shard_map/ppermute | solution.py:57
  163.5 35.0 %collective-permute-start.12 = (bf16[256,512]{1,0:T(8,128)(2,1)S(1)}, bf16[256,512]{1,0:T(8,128)(2,1)S(1)}, u32[]{:S(2)}, u32[]{:S(2)}) collective-permute-start(bf16[256,512]{1,0:T(8,128)(2,1)S(1)} %get-tuple-element.22), channel_id=1, source_target_pairs={{0,65},{1,64},{32,97},{33,96},{64,129},{65,128},{96,161},{97,160},... | collective-permute-start | bytes 786440 | tf_op jit(solution)/shard_map/ppermute | solution.py:150
  167.0 25.1 %collective-permute-start.10 = (bf16[1]{0:T(256)(128)(2,1)}, bf16[1]{0:T(256)(128)(2,1)}, u32[]{:S(2)}, u32[]{:S(2)}) collective-permute-start(bf16[1]{0:T(256)(128)(2,1)} %bitcast.20), channel_id=1, source_target_pairs={{0,32},{32,64},{64,96},{96,128},{128,160},{160,192},{192,224},{224... | collective-permute-start | bytes 14 | tf_op jit(solution)/shard_map/ppermute | solution.py:57
  185.2 6.2 %collective-permute-start.13 = (bf16[1]{0:T(256)(128)(2,1)}, bf16[1]{0:T(256)(128)(2,1)}, u32[]{:S(2)}, u32[]{:S(2)}) collective-permute-start(bf16[1]{0:T(256)(128)(2,1)} %bitcast.22), channel_id=1, source_target_pairs={{0,64},{32,96},{64,128},{96,160},{128,192},{160,224},{192,256},{22... | collective-permute-start | bytes 14 | tf_op jit(solution)/shard_map/ppermute | solution.py:57
  193.8 5.9 %collective-permute-start.9 = (bf16[304,512]{1,0:T(8,128)(2,1)S(1)}, bf16[304,512]{1,0:T(8,128)(2,1)S(1)}, u32[]{:S(2)}, u32[]{:S(2)}) collective-permute-start(bf16[304,512]{1,0:T(8,128)(2,1)S(1)} %pad_maximum_fusion.8), channel_id=1, source_target_pairs={{0,1},{1,0},{2,3},{3,2},{4,5},{5,4},{6,7},{7,6},{8,9},{9,8},{10,11... | collective-permute-start | bytes 933896 | tf_op jit(solution)/shard_map/ppermute | solution.py:52
  (19 other events, 89.3 us)

commit v3 on v2

v3 whole, which is shorter than its diff:
```python
import functools
import math

import jax
import jax.numpy as jnp
from jax import lax
from jax.experimental import pallas as pl
from jax.experimental.pallas import tpu as pltpu
from jax.sharding import Mesh
from jax.sharding import PartitionSpec as P

GROUP = ("x", "z_lo")
MP = ("z_hi", "y", "core")
SIZES = (4, 4, 4, 4, 2)
N_Z, N_Y = SIZES[2], SIZES[3]

momentum_decay = 0.9
step_size = 0.5

ROWS = 24
BLOCK = 2 * ROWS
SLAB = N_Z * BLOCK
TOKENS = N_Y * SLAB
WIDTH = 256
VALUES = 1024
COLS = VALUES // 2
HALF = TOKENS // 2
PADDED = 32
ROW_SCALE = 1.0 / math.sqrt(WIDTH * N_Z * N_Y * 2)
GRAD_SCALE = 1.0 / math.sqrt(TOKENS)

X2_AT = TOKENS
W_AT = 2 * TOKENS
REC_AT = W_AT + 2 * WIDTH
T_AT = REC_AT + 2 * WIDTH
MESSAGE = T_AT + 4 * PADDED


def f32(value):
    return value.astype(jnp.float32)


def bf16(value):
    return value.astype(jnp.bfloat16)


def dot(a, b, dims=((1,), (0,))):
    return lax.dot_general(a, b, (dims, ((), ())), preferred_element_type=jnp.float32)


def cols_of(core):
    return pl.ds(pl.multiple_of(core * COLS, COLS), COLS)


def block_of(index):
    return pl.ds(pl.multiple_of(index * BLOCK, 16), BLOCK)


def by_y():
    return [((zh * N_Y + y) * BLOCK, (y * N_Z + zh) * BLOCK) for zh in range(N_Z) for y in range(N_Y)]


def first_values(ids, facts, x, w, far, own):
    core = ids[0]
    for out, side in ((far, 1 - core), (own, core)):
        scaled = bf16(f32(w[0, :, cols_of(side)]) / facts[0])
        part = bf16(dot(x[0], scaled) * ROW_SCALE)
        for at, to in by_y():
            out[to : to + BLOCK] = part[at : at + BLOCK]


def make_message(ids, x, w, rec, targets, velocity, message, velocity_far):
    far = 1 - ids[0]
    for step in range(2):
        for at, to in by_y():
            message[step * TOKENS + to : step * TOKENS + to + BLOCK] = x[step, at : at + BLOCK]
    for ref, row in ((w, W_AT), (rec, REC_AT)):
        half = ref[0, :, cols_of(far)]
        message[row : row + WIDTH] = half[:, :WIDTH]
        message[row + WIDTH : row + 2 * WIDTH] = half[:, WIDTH:]
    for step in range(2):
        half = targets[step, :, cols_of(far)]
        row = T_AT + 2 * step * PADDED
        message[row : row + PADDED] = half[:, :WIDTH]
        message[row + PADDED : row + 2 * PADDED] = half[:, WIDTH:]
    velocity_far[...] = velocity[0, :, cols_of(far)]


def second_values(ids, facts, mine, got, w, rec, velocity, velocity_got, out, ahead, base):
    core = ids[0]
    keep, weight = facts[2], facts[1]
    side = cols_of(core)
    decayed = step_size * momentum_decay
    ahead[:WIDTH] = f32(w[0, :, side]) - decayed * velocity[0, :, side]
    base[:WIDTH] = keep * ahead[:WIDTH] + f32(rec[0, :, side])
    for k in range(2):
        part = slice(k * WIDTH, (k + 1) * WIDTH)
        ahead[WIDTH:, part] = (
            f32(got[W_AT + k * WIDTH : W_AT + (k + 1) * WIDTH]) - decayed * velocity_got[:, part]
        )
        base[WIDTH:, part] = keep * ahead[WIDTH:, part] + f32(
            got[REC_AT + k * WIDTH : REC_AT + (k + 1) * WIDTH]
        )
    scaled = bf16(base[...] / weight)
    near, far = mine[X2_AT : X2_AT + TOKENS], got[X2_AT : X2_AT + TOKENS]
    out[:, :COLS] = bf16((dot(near, scaled[:WIDTH]) + dot(far, scaled[WIDTH:])) * ROW_SCALE)
    rows = pl.ds(pl.multiple_of(core * HALF, 16), HALF)
    across = ((1,), (1,))
    out[:, COLS:] = bf16(dot(near, mine[rows], across) + dot(far, got[rows], across))


def sum_and_split(ids, parts, keep, send):
    for out, first in ((keep, 1), (send, 3)):
        for k in range(2):
            rows = block_of(ids[first + k])
            total = f32(parts[0, rows])
            for y in range(1, N_Y):
                total = total + f32(parts[y, rows])
            out[k * BLOCK : (k + 1) * BLOCK] = bf16(total)


def spread(ids, mine, got, out):
    for ref, first in ((mine, 1), (got, 3)):
        for k in range(2):
            rows = block_of(ids[first + k])
            for y in range(N_Y):
                out[y, rows] = ref[k * BLOCK : (k + 1) * BLOCK]


def merge_gram(ids, mine, got, gram):
    for ref, first in ((mine, 1), (got, 3)):
        for k in range(2):
            gram[block_of(ids[first + k])] = ref[k * BLOCK : (k + 1) * BLOCK, COLS:]


def second_residual(ids, facts, gram, gram_got, all1, mine, got, values, out, own_values, turned):
    core = ids[0]
    near = all1[pl.ds(pl.multiple_of(core * HALF, 16), HALF)]
    far = all1[pl.ds(pl.multiple_of((1 - core) * HALF, 16), HALF)]
    turned[...] = (dot(gram[...], near) + dot(gram_got[...], far)) * facts[4]
    for ref, first in ((mine, 1), (got, 3)):
        for k in range(2):
            rows = block_of(ids[first + k])
            block = bf16(f32(ref[k * BLOCK : (k + 1) * BLOCK, :COLS]) - turned[rows])
            for y in range(N_Y):
                out[y, rows] = block
    own_values[...] = bf16(f32(values[block_of(ids[6])]) - turned[block_of(ids[5])])


def first_gradient(ids, facts, mine, got, all1, ahead, base, velocity, velocity_got, out, ready):
    side = cols_of(ids[0])
    keep = facts[2]
    down = ((0,), (0,))
    for k, x, old in ((0, mine, velocity[0, :, side]), (1, got, velocity_got[...])):
        rows = slice(k * WIDTH, (k + 1) * WIDTH)
        gradient = dot(x[:TOKENS], all1[...], down) * GRAD_SCALE
        out[rows] = bf16((1.0 - keep) * (ahead[rows] - step_size * gradient))
        current = bf16(base[rows] - (step_size * keep) * gradient)
        moved = momentum_decay * old + gradient
        ready[rows] = f32(current) - (step_size * momentum_decay) * moved


def second_gradient(facts, mine, got, all2, ready, near, far, half):
    keep = facts[3]
    down = ((0,), (0,))
    for k, x, out in ((1, got, far), (0, mine, near)):
        rows = slice(k * WIDTH, (k + 1) * WIDTH)
        gradient = dot(x[X2_AT : X2_AT + TOKENS], all2[...], down) * GRAD_SCALE
        moved = ready[rows] - step_size * gradient
        out[...] = bf16((1.0 - keep) * moved)
        half[rows] = keep * moved


def add_arrived(half, arrived, near, far):
    near[...] = bf16(half[:WIDTH] + f32(arrived[:WIDTH]))
    far[...] = bf16(half[WIDTH:] + f32(arrived[WIDTH:]))


def join(ids, near, far, out):
    core = ids[0]
    out[0, :, cols_of(core)] = near[...]
    out[0, :, cols_of(1 - core)] = far[...]


SMEM = pl.BlockSpec(memory_space=pltpu.SMEM)
VMEM = pl.BlockSpec(memory_space=pltpu.VMEM)


def call(body, scalars, arrays, outs, scratch=(), flops=0):
    result = [jax.ShapeDtypeStruct(shape, kind) for shape, kind in outs]
    moved = sum(a.size * a.dtype.itemsize for a in list(arrays) + result)
    got = pl.pallas_call(
        body,
        out_shape=result,
        in_specs=[SMEM] * len(scalars) + [VMEM] * len(arrays),
        out_specs=[VMEM] * len(outs),
        scratch_shapes=[pltpu.VMEM(shape, kind) for shape, kind in scratch],
        compiler_params=pltpu.CompilerParams(vmem_limit_bytes=28 * 2**20),
        cost_estimate=pl.CostEstimate(flops=flops, bytes_accessed=moved, transcendentals=0),
        name=body.__name__,
    )(*scalars, *arrays)
    return got


B16, F32 = jnp.bfloat16, jnp.float32


def z_pairs(step):
    pairs = []
    for zh in range(N_Z):
        for core in range(2):
            turn = (1, 3)[step ^ core]
            pairs.append((zh * 2 + core, (zh ^ turn) * 2 + core))
    return pairs


def over_z(value, step):
    return lax.ppermute(value, ("z_hi", "core"), z_pairs(step))


def over_y(value):
    return lax.all_to_all(value, "y", 0, 0, tiled=True)


def swap_core(value):
    return lax.ppermute(value, "core", [(0, 1), (1, 0)])


def to_group(value, hop):
    count = SIZES[0] * SIZES[1]
    return lax.ppermute(value, GROUP, [(i, (i + hop) % count) for i in range(count)])


def reduce_slab(ids, part):
    columns = part.shape[1]
    got = over_y(part.reshape(N_Y, SLAB, columns))
    keep, send = call(
        sum_and_split, [ids], [got], [((2 * BLOCK, columns), B16), ((2 * BLOCK, columns), B16)]
    )
    mine = bf16(f32(keep) + f32(over_z(send, 0)))
    return f32(mine) + f32(over_z(mine, 1))


def local(inputs, targets, numerator, momentum, received, push_weight, received_weight, mix_share):
    core = lax.axis_index("core")
    zh = lax.axis_index("z_hi")
    first = core == 0
    pick = functools.partial(jnp.where, first)

    kept = f32(mix_share[0]) / 8.0
    weight0 = push_weight[0]
    weight1 = kept[0] * weight0 + received_weight[0]
    arrived0 = f32(to_group(bf16((1.0 - kept[0]) * weight0)[None], 1))
    arrived1 = f32(to_group(bf16((1.0 - kept[1]) * weight1)[None], 2))
    weight2 = kept[1] * weight1 + arrived0

    step0 = jnp.where(first, 1, 3)
    step1 = jnp.where(first, 3, 1)
    meet, away = zh ^ step1, zh ^ step0
    across = away ^ step1
    low, high = jnp.minimum(zh, meet), jnp.maximum(zh, meet)
    ids = jnp.stack(
        [core, low, high, jnp.minimum(away, across), jnp.maximum(away, across), zh, (zh == high) * 1, core]
    ).astype(jnp.int32)
    back = step_size * GRAD_SCALE * ROW_SCALE * kept[0] / weight1
    facts = jnp.stack([weight0, weight1, kept[0], kept[1], back, back, back, back])

    part = [((TOKENS, COLS), B16)] * 2
    part_far, part_own = call(first_values, [ids, facts], [inputs, numerator], part)
    part_got = swap_core(part_far)
    part1 = bf16(f32(part_own) + f32(part_got))

    padded = jnp.pad(targets, ((0, 0), (0, PADDED - ROWS), (0, 0)))
    padded, part_far = lax.optimization_barrier((padded, part_far))
    mine, velocity_far = call(
        make_message,
        [ids],
        [inputs, numerator, received, padded, momentum],
        [((MESSAGE, WIDTH), B16), ((WIDTH, COLS), F32)],
    )
    got = swap_core(mine)
    velocity_got = swap_core(velocity_far)

    near_rows = pick(targets[..., :COLS], targets[..., COLS:])
    far_rows = got[T_AT:].reshape(2, 2, PADDED, WIDTH)[:, :, :ROWS].transpose(0, 2, 1, 3)
    far_rows = far_rows.reshape(2, ROWS, COLS)
    chip = jnp.concatenate([pick(near_rows, far_rows), pick(far_rows, near_rows)], axis=1)
    chip_met = over_z(chip, 1)
    is_low = zh == low
    taught = jnp.concatenate(
        [jnp.where(is_low, chip, chip_met), jnp.where(is_low, chip_met, chip)], axis=1
    )

    part2, ahead, base = call(
        second_values,
        [ids, facts],
        [mine, got, numerator, received, momentum, velocity_got],
        [((TOKENS, COLS + HALF), B16), ((2 * WIDTH, COLS), F32), ((2 * WIDTH, COLS), F32)],
    )

    values1 = bf16(reduce_slab(ids, part1))
    residual1 = bf16(f32(values1) - f32(taught[0]))
    slab = [((N_Y, SLAB, COLS), B16)]
    (sent,) = call(spread, [ids], [residual1, over_z(residual1, 0)], slab)
    all1 = over_y(sent).reshape(TOKENS, COLS)

    second = reduce_slab(ids, part2)
    values2 = second[:, :COLS]
    second = jnp.concatenate([values2 - f32(taught[1]), second[:, COLS:]], axis=1)
    second = bf16(second)
    second_got = over_z(second, 0)
    (gram,) = call(merge_gram, [ids], [second, second_got], [((SLAB, HALF), B16)])
    gram_got = swap_core(gram)

    outgoing, ready = call(
        first_gradient,
        [ids, facts],
        [mine, got, all1, ahead, base, momentum, velocity_got],
        [((2 * WIDTH, COLS), B16), ((2 * WIDTH, COLS), F32)],
    )
    arrived = to_group(outgoing, 1)

    sent, own2 = call(
        second_residual,
        [ids, facts],
        [gram, gram_got, all1, second, second_got, values2],
        slab + [((BLOCK, COLS), B16)],
        [((SLAB, COLS), F32)],
    )
    all2 = over_y(sent).reshape(TOKENS, COLS)

    near, far, half = call(
        second_gradient,
        [facts],
        [mine, got, all2, ready],
        [((WIDTH, COLS), B16), ((WIDTH, COLS), B16), ((2 * WIDTH, COLS), F32)],
    )

    count = SIZES[0] * SIZES[1]
    hop = [(i * 2 + c, (i + 2) % count * 2 + 1 - c) for i in range(count) for c in range(2)]
    sent_far = lax.ppermute(far, GROUP + ("core",), hop)
    sent_own = to_group(near, 2)

    current, current_far = call(add_arrived, [], [half, arrived], [((WIDTH, COLS), B16)] * 2)
    own1 = lax.dynamic_slice_in_dim(values1, (zh == high) * BLOCK, BLOCK, 0)
    both = jnp.stack([own1, own2]).reshape(2, 2, ROWS, COLS)
    values_near = pick(both[:, 0], both[:, 1])
    values_far = pick(both[:, 1], both[:, 0])
    values_got = swap_core(values_far)
    current_got = swap_core(current_far)
    whole = [((1, WIDTH, VALUES), B16)]
    (final_numerator,) = call(join, [ids], [current, current_got], whole)
    (final_received,) = call(join, [ids], [sent_own, sent_far], whole)
    value_rows = jnp.concatenate(
        [pick(values_near, values_got), pick(values_got, values_near)], axis=-1
    )
    return final_numerator, weight2, final_received, arrived1, value_rows


def solution(mesh):
    fine = Mesh(mesh.devices.reshape(SIZES), GROUP + MP)
    placed = (
        P(None, GROUP, MP),
        P(None, GROUP + MP, None),
        P(GROUP, MP, None),
        P(GROUP, MP, None),
        P(GROUP, MP, None),
        P(GROUP),
        P(GROUP),
        P(GROUP, None),
    )
    return jax.shard_map(
        local,
        mesh=fine,
        in_specs=placed,
        out_specs=(
            P(GROUP, MP, None),
            P(GROUP),
            P(GROUP, MP, None),
            P(GROUP),
            P(None, GROUP + MP, None),
        ),
        check_vma=False,
    )
```

time: 205 us -> 220 us (1.073)
  the two profiles are of different devices: /device:TPU:35 before, /device:TPU:1 now
where the time goes in v3:
time: 220 us; the launch traced here: 218 us
  starting transfers between devices  111 us (50%)
  waiting for transfers between devices  46 us (21%)
  local copies, waits for them, and re-layouts  28.2 us (13%)
  Pallas kernels  15.1 us (7%)
  between operations  9.4 us (4%)
  other arithmetic  8.07 us (4%)
    ppermute x7, starting transfers between devices, over_z(): return lax.ppermute(value, ('z_hi', 'core'), z_pairs(step))  44.4 us
    ppermute x6, starting transfers between devices, swap_core(): return lax.ppermute(value, 'core', [(0, 1), (1, 0)])  32.8 us
    unnamed x73, local copies, waits for them, and re-layouts  24.8 us
    ppermute x7, waiting for transfers between devices, over_z(): return lax.ppermute(value, ('z_hi', 'core'), z_pairs(step))  19.7 us
    all_to_all x4, starting transfers between devices, over_y(): return lax.all_to_all(value, 'y', 0, 0, tiled=True)  16.6 us
    ppermute x4, waiting for transfers between devices, to_group(): lax.ppermute(value, GROUP, [(i, (i + hop) % count) for i in range(count)])  15.5 us
    pallas_call x13, Pallas kernels, call(): pl.pallas_call(body, out_shape=result, in_specs=[SMEM] * len(scalars) + [...  15.1 us
    ppermute x4, starting transfers between devices, to_group(): lax.ppermute(value, GROUP, [(i, (i + hop) % count) for i in range(count)])  12.4 us
  transfers between devices with their start and end apart: 22, of which 10 were waited for; matrix products, arithmetic and copies ran while one was open for 4% of the time, Pallas kernels for 5%

profile of v3, /device:TPU:1, one launch (start us, length us, event | category | flops | bytes accessed | tf_op | source)
XLA Modules:
  0.0 217.8 jit_solution(1559226557937499981)
XLA Ops:
  8.1 8.8 %collective-permute-start.7 = (bf16[768,512]{1,0:T(8,128)(2,1)S(1)}, bf16[768,512]{1,0:T(8,128)(2,1)S(1)}, u32[]{:S(2)}, u32[]{:S(2)}) collective-permute-start(bf16[768,512]{1,0:T(8,128)(2,1)S(1)} %get-tuple-element.26), channel_id=1, source_target_pairs={{0,1},{1,0},{2,3},{3,2},{4,5},{5,4},{6,7},{7,6},{8,9},{9,8},{10,11... | collective-permute-start | bytes 2359304 | tf_op jit(solution)/shard_map/ppermute | solution.py:226
  22.7 4.3 %all-to-all-start.1 = ((bf16[4,192,512]{2,1,0:T(8,128)(2,1)}), bf16[4,192,512]{2,1,0:T(8,128)(2,1)}, u32[]{:S(2)}, u32[]{:S(2)}) async-start(bf16[4,192,512]{2,1,0:T(8,128)(2,1)} %bitcast.52), calls=%async_computation.1 | async-start | bytes 1572864 | tf_op jit(solution)/shard_map/all_to_all | solution.py:222
  27.1 2.4 %collective-permute-start.1 = (f32[256,512]{1,0:T(8,128)}, f32[256,512]{1,0:T(8,128)S(1)}, u32[]{:S(2)}, u32[]{:S(2)}) collective-permute-start(f32[256,512]{1,0:T(8,128)} %copy-done.31), channel_id=1, source_target_pairs={{0,1},{1,0},{2,3},{3,2},{4,5},{5,4},{6,7},{7,6},{8,9},{9,8},{10,11... | collective-permute-start | bytes 1572872 | tf_op jit(solution)/shard_map/ppermute | solution.py:226
  39.0 4.6 %all-to-all-start = ((bf16[4,192,896]{2,1,0:T(8,128)(2,1)}), bf16[4,192,896]{2,1,0:T(8,128)(2,1)}, u32[]{:S(2)}, u32[]{:S(2)}) async-start(bf16[4,192,896]{2,1,0:T(8,128)(2,1)} %bitcast.49), calls=%async_computation | async-start | bytes 2752512 | tf_op jit(solution)/shard_map/all_to_all | solution.py:222
  44.9 7.4 %collective-permute-start.8 = (bf16[96,512]{1,0:T(8,128)(2,1)S(1)}, bf16[96,512]{1,0:T(8,128)(2,1)S(1)}, u32[]{:S(2)}, u32[]{:S(2)}) collective-permute-start(bf16[96,512]{1,0:T(8,128)(2,1)S(1)} %get-tuple-element.35), channel_id=1, source_target_pairs={{0,8},{1,25},{8,0},{9,17},{16,24},{17,9},{24,16},{25,1},{2,10},{3,... | collective-permute-start | bytes 294920 | tf_op jit(solution)/shard_map/ppermute | solution.py:218
  53.0 5.2 %collective-permute-start.4 = (bf16[2,48,512]{2,1,0:T(8,128)(2,1)}, bf16[2,48,512]{2,1,0:T(8,128)(2,1)}, u32[]{:S(2)}, u32[]{:S(2)}) collective-permute-start(bf16[2,48,512]{2,1,0:T(8,128)(2,1)} %pad_maximum_fusion.2), channel_id=1, source_target_pairs={{0,24},{1,9},{8,16},{9,1},{16,8},{17,25},{24,0},{25,17},{2,26},{3,... | collective-permute-start | bytes 294920 | tf_op jit(solution)/shard_map/ppermute | solution.py:218
  58.2 3.1 %all-to-all-done.parts = bf16[4,192,896]{2,1,0:T(8,128)(2,1)} async-done(((bf16[4,192,896]{2,1,0:T(8,128)(2,1)}), bf16[4,192,896]{2,1,0:T(8,128)(2,1)}, u32[]{:S(2)}, u32[]{:S(2)}) %all-to-all-start) | async-done | bytes 1376288 | tf_op jit(solution)/shard_map/all_to_all | solution.py:222
  62.8 7.7 %collective-permute-start.2 = (bf16[96,896]{1,0:T(8,128)(2,1)S(1)}, bf16[96,896]{1,0:T(8,128)(2,1)S(1)}, u32[]{:S(2)}, u32[]{:S(2)}) collective-permute-start(bf16[96,896]{1,0:T(8,128)(2,1)S(1)} %get-tuple-element.32), channel_id=1, source_target_pairs={{0,8},{1,25},{8,0},{9,17},{16,24},{17,9},{24,16},{25,1},{2,10},{3,... | collective-permute-start | bytes 516104 | tf_op jit(solution)/shard_map/ppermute | solution.py:218
  70.6 5.2 %collective-permute-start.9 = (bf16[96,512]{1,0:T(8,128)(2,1)S(1)}, bf16[96,512]{1,0:T(8,128)(2,1)S(1)}, u32[]{:S(2)}, u32[]{:S(2)}) collective-permute-start(bf16[96,512]{1,0:T(8,128)(2,1)S(1)} %add_convert_fusion.3), channel_id=1, source_target_pairs={{0,24},{1,9},{8,16},{9,1},{16,8},{17,25},{24,0},{25,17},{2,26},{3,... | collective-permute-start | bytes 294920 | tf_op jit(solution)/shard_map/ppermute | solution.py:218
  76.2 12.0 %collective-permute-start.3 = (bf16[96,896]{1,0:T(8,128)(2,1)S(1)}, bf16[96,896]{1,0:T(8,128)(2,1)S(1)}, u32[]{:S(2)}, u32[]{:S(2)}) collective-permute-start(bf16[96,896]{1,0:T(8,128)(2,1)S(1)} %add_convert_fusion.1), channel_id=1, source_target_pairs={{0,24},{1,9},{8,16},{9,1},{16,8},{17,25},{24,0},{25,17},{2,26},{3,... | collective-permute-start | bytes 516104 | tf_op jit(solution)/shard_map/ppermute | solution.py:218
  89.1 6.4 %collective-permute-done.3 = bf16[96,896]{1,0:T(8,128)(2,1)S(1)} collective-permute-done((bf16[96,896]{1,0:T(8,128)(2,1)S(1)}, bf16[96,896]{1,0:T(8,128)(2,1)S(1)}, u32[]{:S(2)}, u32[]{:S(2)}) %collective-permute-start.3) | collective-permute-done | bytes 172064 | tf_op jit(solution)/shard_map/ppermute | solution.py:218
  98.3 7.3 %collective-permute-done.10.got = bf16[96,512]{1,0:T(8,128)(2,1)S(1)} collective-permute-done((bf16[96,512]{1,0:T(8,128)(2,1)S(1)}, bf16[96,512]{1,0:T(8,128)(2,1)S(1)}, u32[]{:S(2)}, u32[]{:S(2)}) %collective-permute-start.10) | collective-permute-done | bytes 98336 | tf_op jit(solution)/shard_map/ppermute | solution.py:218
  107.2 3.5 %all-to-all-start.2 = ((bf16[4,192,512]{2,1,0:T(8,128)(2,1)}), bf16[4,192,512]{2,1,0:T(8,128)(2,1)S(1)}, u32[]{:S(2)}, u32[]{:S(2)}) async-start(bf16[4,192,512]{2,1,0:T(8,128)(2,1)} %copy-done.5), calls=%async_computation.2 | async-start | bytes 1572864 | tf_op jit(solution)/shard_map/all_to_all | solution.py:222
  112.5 5.1 %collective-permute-start.5 = (bf16[96,896]{1,0:T(8,128)(2,1)S(1)}, bf16[96,896]{1,0:T(8,128)(2,1)S(1)}, u32[]{:S(2)}, u32[]{:S(2)}) collective-permute-start(bf16[96,896]{1,0:T(8,128)(2,1)S(1)} %pad_maximum_fusion.mine), channel_id=1, source_target_pairs={{0,8},{1,25},{8,0},{9,17},{16,24},{17,9},{24,16},{25,1},{2,10},{3,... | collective-permute-start | bytes 516104 | tf_op jit(solution)/shard_map/ppermute | solution.py:218
  117.6 5.6 %collective-permute-done.5.got = bf16[96,896]{1,0:T(8,128)(2,1)S(1)} collective-permute-done((bf16[96,896]{1,0:T(8,128)(2,1)S(1)}, bf16[96,896]{1,0:T(8,128)(2,1)S(1)}, u32[]{:S(2)}, u32[]{:S(2)}) %collective-permute-start.5) | collective-permute-done | bytes 172064 | tf_op jit(solution)/shard_map/ppermute | solution.py:218
  123.8 15.2 %collective-permute-start.6 = (bf16[192,384]{1,0:T(8,128)(2,1)S(1)}, bf16[192,384]{1,0:T(8,128)(2,1)S(1)}, u32[]{:S(2)}, u32[]{:S(2)}) collective-permute-start(bf16[192,384]{1,0:T(8,128)(2,1)S(1)} %merge_gram.1.gram), channel_id=1, source_target_pairs={{0,1},{1,0},{2,3},{3,2},{4,5},{5,4},{6,7},{7,6},{8,9},{9,8},{10,11... | collective-permute-start | bytes 442376 | tf_op jit(solution)/shard_map/ppermute | solution.py:226
  147.7 4.2 %all-to-all-start.3 = ((bf16[4,192,512]{2,1,0:T(8,128)(2,1)}), bf16[4,192,512]{2,1,0:T(8,128)(2,1)}, u32[]{:S(2)}, u32[]{:S(2)}) async-start(bf16[4,192,512]{2,1,0:T(8,128)(2,1)} %copy-done.21), calls=%async_computation.3 | async-start | bytes 1572864 | tf_op jit(solution)/shard_map/all_to_all | solution.py:222
  163.9 2.6 %collective-permute-start.17 = (bf16[2,24,512]{2,1,0:T(8,128)(2,1)}, bf16[2,24,512]{2,1,0:T(8,128)(2,1)}, u32[]{:S(2)}, u32[]{:S(2)}) collective-permute-start(bf16[2,24,512]{2,1,0:T(8,128)(2,1)} %select_bitcast_fusion), channel_id=1, source_target_pairs={{0,1},{1,0},{2,3},{3,2},{4,5},{5,4},{6,7},{7,6},{8,9},{9,8},{10,11... | collective-permute-start | bytes 147464 | tf_op jit(solution)/shard_map/ppermute | solution.py:226
  167.2 5.8 %collective-permute-start.16 = (bf16[1]{0:T(256)(128)(2,1)}, bf16[1]{0:T(256)(128)(2,1)}, u32[]{:S(2)}, u32[]{:S(2)}) collective-permute-start(bf16[1]{0:T(256)(128)(2,1)} %bitcast.24), channel_id=1, source_target_pairs={{0,64},{32,96},{64,128},{96,160},{128,192},{160,224},{192,256},{22... | collective-permute-start | bytes 14 | tf_op jit(solution)/shard_map/ppermute | solution.py:231
  173.6 2.7 %collective-permute-start.13 = (bf16[1]{0:T(256)(128)(2,1)}, bf16[1]{0:T(256)(128)(2,1)}, u32[]{:S(2)}, u32[]{:S(2)}) collective-permute-start(bf16[1]{0:T(256)(128)(2,1)} %bitcast.23), channel_id=1, source_target_pairs={{0,32},{32,64},{64,96},{96,128},{128,160},{160,192},{192,224},{224... | collective-permute-start | bytes 14 | tf_op jit(solution)/shard_map/ppermute | solution.py:231
  177.6 4.3 %collective-permute-done.13 = bf16[1]{0:T(256)(128)(2,1)} collective-permute-done((bf16[1]{0:T(256)(128)(2,1)}, bf16[1]{0:T(256)(128)(2,1)}, u32[]{:S(2)}, u32[]{:S(2)}) %collective-permute-start.13) | collective-permute-done | bytes 34 | tf_op jit(solution)/shard_map/ppermute | solution.py:231
  187.6 4.9 %collective-permute-start.15 = (bf16[256,512]{1,0:T(8,128)(2,1)S(1)}, bf16[256,512]{1,0:T(8,128)(2,1)S(1)}, u32[]{:S(2)}, u32[]{:S(2)}) collective-permute-start(bf16[256,512]{1,0:T(8,128)(2,1)S(1)} %get-tuple-element.45), channel_id=1, source_target_pairs={{0,65},{1,64},{32,97},{33,96},{64,129},{65,128},{96,161},{97,160},... | collective-permute-start | bytes 786440 | tf_op jit(solution)/shard_map/ppermute | solution.py:341
  196.0 11.2 %collective-permute-done.14.near = bf16[256,512]{1,0:T(8,128)(2,1)S(1)} collective-permute-done((bf16[256,512]{1,0:T(8,128)(2,1)S(1)}, bf16[256,512]{1,0:T(8,128)(2,1)S(1)}, u32[]{:S(2)}, u32[]{:S(2)}) %collective-permute-start.14) | collective-permute-done | bytes 262176 | tf_op jit(solution)/shard_map/ppermute | solution.py:231
  207.2 5.6 %collective-permute-done.15.far = bf16[256,512]{1,0:T(8,128)(2,1)S(1)} collective-permute-done((bf16[256,512]{1,0:T(8,128)(2,1)S(1)}, bf16[256,512]{1,0:T(8,128)(2,1)S(1)}, u32[]{:S(2)}, u32[]{:S(2)}) %collective-permute-start.15) | collective-permute-done | bytes 262176 | tf_op jit(solution)/shard_map/ppermute | solution.py:341
  (127 shorter events, 63.6 us)
Async XLA Ops:
  8.1 13.5 %collective-permute-start.7 = (bf16[768,512]{1,0:T(8,128)(2,1)S(1)}, bf16[768,512]{1,0:T(8,128)(2,1)S(1)}, u32[]{:S(2)}, u32[]{:S(2)}) collective-permute-start(bf16[768,512]{1,0:T(8,128)(2,1)S(1)} %get-tuple-element.26), channel_id=1, source_target_pairs={{0,1},{1,0},{2,3},{3,2},{4,5},{5,4},{6,7},{7,6},{8,9},{9,8},{10,11... | collective-permute-start | bytes 2359304 | tf_op jit(solution)/shard_map/ppermute | solution.py:226
  19.7 11.5 %collective-permute-start = (bf16[2688,256]{1,0:T(8,128)(2,1)S(1)}, bf16[2688,256]{1,0:T(8,128)(2,1)S(1)}, u32[]{:S(2)}, u32[]{:S(2)}) collective-permute-start(bf16[2688,256]{1,0:T(8,128)(2,1)S(1)} %get-tuple-element.28.mine), channel_id=1, source_target_pairs={{0,1},{1,0},{2,3},{3,2},{4,5},{5,4},{6,7},{7,6},{8,9},{9,8},{10,11... | collective-permute-start | bytes 4128776 | tf_op jit(solution)/shard_map/ppermute | solution.py:226
  22.7 16.3 %all-to-all-start.1 = ((bf16[4,192,512]{2,1,0:T(8,128)(2,1)}), bf16[4,192,512]{2,1,0:T(8,128)(2,1)}, u32[]{:S(2)}, u32[]{:S(2)}) async-start(bf16[4,192,512]{2,1,0:T(8,128)(2,1)} %bitcast.52), calls=%async_computation.1 | async-start | bytes 1572864 | tf_op jit(solution)/shard_map/all_to_all | solution.py:222
  27.1 4.1 %collective-permute-start.1 = (f32[256,512]{1,0:T(8,128)}, f32[256,512]{1,0:T(8,128)S(1)}, u32[]{:S(2)}, u32[]{:S(2)}) collective-permute-start(f32[256,512]{1,0:T(8,128)} %copy-done.31), channel_id=1, source_target_pairs={{0,1},{1,0},{2,3},{3,2},{4,5},{5,4},{6,7},{7,6},{8,9},{9,8},{10,11... | collective-permute-start | bytes 1572872 | tf_op jit(solution)/shard_map/ppermute | solution.py:226
  39.0 22.2 %all-to-all-start = ((bf16[4,192,896]{2,1,0:T(8,128)(2,1)}), bf16[4,192,896]{2,1,0:T(8,128)(2,1)}, u32[]{:S(2)}, u32[]{:S(2)}) async-start(bf16[4,192,896]{2,1,0:T(8,128)(2,1)} %bitcast.49), calls=%async_computation | async-start | bytes 2752512 | tf_op jit(solution)/shard_map/all_to_all | solution.py:222
  44.9 25.6 %collective-permute-start.8 = (bf16[96,512]{1,0:T(8,128)(2,1)S(1)}, bf16[96,512]{1,0:T(8,128)(2,1)S(1)}, u32[]{:S(2)}, u32[]{:S(2)}) collective-permute-start(bf16[96,512]{1,0:T(8,128)(2,1)S(1)} %get-tuple-element.35), channel_id=1, source_target_pairs={{0,8},{1,25},{8,0},{9,17},{16,24},{17,9},{24,16},{25,1},{2,10},{3,... | collective-permute-start | bytes 294920 | tf_op jit(solution)/shard_map/ppermute | solution.py:218
  53.0 35.2 %collective-permute-start.4 = (bf16[2,48,512]{2,1,0:T(8,128)(2,1)}, bf16[2,48,512]{2,1,0:T(8,128)(2,1)}, u32[]{:S(2)}, u32[]{:S(2)}) collective-permute-start(bf16[2,48,512]{2,1,0:T(8,128)(2,1)} %pad_maximum_fusion.2), channel_id=1, source_target_pairs={{0,24},{1,9},{8,16},{9,1},{16,8},{17,25},{24,0},{25,17},{2,26},{3,... | collective-permute-start | bytes 294920 | tf_op jit(solution)/shard_map/ppermute | solution.py:218
  62.8 13.3 %collective-permute-start.2 = (bf16[96,896]{1,0:T(8,128)(2,1)S(1)}, bf16[96,896]{1,0:T(8,128)(2,1)S(1)}, u32[]{:S(2)}, u32[]{:S(2)}) collective-permute-start(bf16[96,896]{1,0:T(8,128)(2,1)S(1)} %get-tuple-element.32), channel_id=1, source_target_pairs={{0,8},{1,25},{8,0},{9,17},{16,24},{17,9},{24,16},{25,1},{2,10},{3,... | collective-permute-start | bytes 516104 | tf_op jit(solution)/shard_map/ppermute | solution.py:218
  70.6 25.0 %collective-permute-start.9 = (bf16[96,512]{1,0:T(8,128)(2,1)S(1)}, bf16[96,512]{1,0:T(8,128)(2,1)S(1)}, u32[]{:S(2)}, u32[]{:S(2)}) collective-permute-start(bf16[96,512]{1,0:T(8,128)(2,1)S(1)} %add_convert_fusion.3), channel_id=1, source_target_pairs={{0,24},{1,9},{8,16},{9,1},{16,8},{17,25},{24,0},{25,17},{2,26},{3,... | collective-permute-start | bytes 294920 | tf_op jit(solution)/shard_map/ppermute | solution.py:218
  76.2 19.3 %collective-permute-start.3 = (bf16[96,896]{1,0:T(8,128)(2,1)S(1)}, bf16[96,896]{1,0:T(8,128)(2,1)S(1)}, u32[]{:S(2)}, u32[]{:S(2)}) collective-permute-start(bf16[96,896]{1,0:T(8,128)(2,1)S(1)} %add_convert_fusion.1), channel_id=1, source_target_pairs={{0,24},{1,9},{8,16},{9,1},{16,8},{17,25},{24,0},{25,17},{2,26},{3,... | collective-permute-start | bytes 516104 | tf_op jit(solution)/shard_map/ppermute | solution.py:218
  96.4 9.3 %collective-permute-start.10 = (bf16[96,512]{1,0:T(8,128)(2,1)S(1)}, bf16[96,512]{1,0:T(8,128)(2,1)S(1)}, u32[]{:S(2)}, u32[]{:S(2)}) collective-permute-start(bf16[96,512]{1,0:T(8,128)(2,1)S(1)} %get-tuple-element.51.mine), channel_id=1, source_target_pairs={{0,8},{1,25},{8,0},{9,17},{16,24},{17,9},{24,16},{25,1},{2,10},{3,... | collective-permute-start | bytes 294920 | tf_op jit(solution)/shard_map/ppermute | solution.py:218
  107.2 33.4 %all-to-all-start.2 = ((bf16[4,192,512]{2,1,0:T(8,128)(2,1)}), bf16[4,192,512]{2,1,0:T(8,128)(2,1)S(1)}, u32[]{:S(2)}, u32[]{:S(2)}) async-start(bf16[4,192,512]{2,1,0:T(8,128)(2,1)} %copy-done.5), calls=%async_computation.2 | async-start | bytes 1572864 | tf_op jit(solution)/shard_map/all_to_all | solution.py:222
  112.5 26.5 %copy-start.12 = (bf16[96,896]{1,0:T(8,128)(2,1)}, bf16[96,896]{1,0:T(8,128)(2,1)S(1)}, u32[]{:S(2)}) copy-start(bf16[96,896]{1,0:T(8,128)(2,1)S(1)} %pad_maximum_fusion.mine) | copy-start | bytes 516100
  112.5 10.7 %collective-permute-start.5 = (bf16[96,896]{1,0:T(8,128)(2,1)S(1)}, bf16[96,896]{1,0:T(8,128)(2,1)S(1)}, u32[]{:S(2)}, u32[]{:S(2)}) collective-permute-start(bf16[96,896]{1,0:T(8,128)(2,1)S(1)} %pad_maximum_fusion.mine), channel_id=1, source_target_pairs={{0,8},{1,25},{8,0},{9,17},{16,24},{17,9},{24,16},{25,1},{2,10},{3,... | collective-permute-start | bytes 516104 | tf_op jit(solution)/shard_map/ppermute | solution.py:218
  123.8 16.2 %collective-permute-start.6 = (bf16[192,384]{1,0:T(8,128)(2,1)S(1)}, bf16[192,384]{1,0:T(8,128)(2,1)S(1)}, u32[]{:S(2)}, u32[]{:S(2)}) collective-permute-start(bf16[192,384]{1,0:T(8,128)(2,1)S(1)} %merge_gram.1.gram), channel_id=1, source_target_pairs={{0,1},{1,0},{2,3},{3,2},{4,5},{5,4},{6,7},{7,6},{8,9},{9,8},{10,11... | collective-permute-start | bytes 442376 | tf_op jit(solution)/shard_map/ppermute | solution.py:226
  147.7 34.8 %all-to-all-start.3 = ((bf16[4,192,512]{2,1,0:T(8,128)(2,1)}), bf16[4,192,512]{2,1,0:T(8,128)(2,1)}, u32[]{:S(2)}, u32[]{:S(2)}) async-start(bf16[4,192,512]{2,1,0:T(8,128)(2,1)} %copy-done.21), calls=%async_computation.3 | async-start | bytes 1572864 | tf_op jit(solution)/shard_map/all_to_all | solution.py:222
  159.8 32.7 %collective-permute-start.11 = (bf16[512,512]{1,0:T(8,128)(2,1)}, bf16[512,512]{1,0:T(8,128)(2,1)S(1)}, u32[]{:S(2)}, u32[]{:S(2)}) collective-permute-start(bf16[512,512]{1,0:T(8,128)(2,1)} %get-tuple-element.41), channel_id=1, source_target_pairs={{0,32},{32,64},{64,96},{96,128},{128,160},{160,192},{192,224},{224... | collective-permute-start | bytes 1572872 | tf_op jit(solution)/shard_map/ppermute | solution.py:231
  162.5 20.0 %copy-start.33 = (bf16[48,512]{1,0:T(8,128)(2,1)}, bf16[48,512]{1,0:T(8,128)(2,1)S(1)}, u32[]{:S(2)}) copy-start(bf16[48,512]{1,0:T(8,128)(2,1)S(1)} %constant_dynamic-slice_fusion) | copy-start | bytes 147460
  163.9 30.6 %collective-permute-start.17 = (bf16[2,24,512]{2,1,0:T(8,128)(2,1)}, bf16[2,24,512]{2,1,0:T(8,128)(2,1)}, u32[]{:S(2)}, u32[]{:S(2)}) collective-permute-start(bf16[2,24,512]{2,1,0:T(8,128)(2,1)} %select_bitcast_fusion), channel_id=1, source_target_pairs={{0,1},{1,0},{2,3},{3,2},{4,5},{5,4},{6,7},{7,6},{8,9},{9,8},{10,11... | collective-permute-start | bytes 147464 | tf_op jit(solution)/shard_map/ppermute | solution.py:226
  167.2 9.8 %collective-permute-start.16 = (bf16[1]{0:T(256)(128)(2,1)}, bf16[1]{0:T(256)(128)(2,1)}, u32[]{:S(2)}, u32[]{:S(2)}) collective-permute-start(bf16[1]{0:T(256)(128)(2,1)} %bitcast.24), channel_id=1, source_target_pairs={{0,64},{32,96},{64,128},{96,160},{128,192},{160,224},{192,256},{22... | collective-permute-start | bytes 14 | tf_op jit(solution)/shard_map/ppermute | solution.py:231
  173.6 8.3 %collective-permute-start.13 = (bf16[1]{0:T(256)(128)(2,1)}, bf16[1]{0:T(256)(128)(2,1)}, u32[]{:S(2)}, u32[]{:S(2)}) collective-permute-start(bf16[1]{0:T(256)(128)(2,1)} %bitcast.23), channel_id=1, source_target_pairs={{0,32},{32,64},{64,96},{96,128},{128,160},{160,192},{192,224},{224... | collective-permute-start | bytes 14 | tf_op jit(solution)/shard_map/ppermute | solution.py:231
  185.6 21.6 %collective-permute-start.14 = (bf16[256,512]{1,0:T(8,128)(2,1)S(1)}, bf16[256,512]{1,0:T(8,128)(2,1)S(1)}, u32[]{:S(2)}, u32[]{:S(2)}) collective-permute-start(bf16[256,512]{1,0:T(8,128)(2,1)S(1)} %get-tuple-element.44), channel_id=1, source_target_pairs={{0,64},{32,96},{64,128},{96,160},{128,192},{160,224},{192,256},{22... | collective-permute-start | bytes 786440 | tf_op jit(solution)/shard_map/ppermute | solution.py:231
  187.6 25.2 %collective-permute-start.15 = (bf16[256,512]{1,0:T(8,128)(2,1)S(1)}, bf16[256,512]{1,0:T(8,128)(2,1)S(1)}, u32[]{:S(2)}, u32[]{:S(2)}) collective-permute-start(bf16[256,512]{1,0:T(8,128)(2,1)S(1)} %get-tuple-element.45), channel_id=1, source_target_pairs={{0,65},{1,64},{32,97},{33,96},{64,129},{65,128},{96,161},{97,160},... | collective-permute-start | bytes 786440 | tf_op jit(solution)/shard_map/ppermute | solution.py:341
  192.6 21.6 %collective-permute-start.12 = (bf16[256,512]{1,0:T(8,128)(2,1)S(1)}, bf16[256,512]{1,0:T(8,128)(2,1)S(1)}, u32[]{:S(2)}, u32[]{:S(2)}) collective-permute-start(bf16[256,512]{1,0:T(8,128)(2,1)S(1)} %get-tuple-element.43), channel_id=1, source_target_pairs={{0,1},{1,0},{2,3},{3,2},{4,5},{5,4},{6,7},{7,6},{8,9},{9,8},{10,11... | collective-permute-start | bytes 786440 | tf_op jit(solution)/shard_map/ppermute | solution.py:226
  (34 other events, 114.2 us)

commit v4 on v3

v4 whole, which is shorter than its diff:
```python
import functools
import math

import jax
import jax.numpy as jnp
from jax import lax
from jax.experimental import pallas as pl
from jax.experimental.pallas import tpu as pltpu
from jax.sharding import Mesh
from jax.sharding import PartitionSpec as P

GROUP = ("x", "z_lo")
MP = ("z_hi", "y", "core")
SIZES = (4, 4, 4, 4, 2)
N_Z, N_Y = SIZES[2], SIZES[3]

momentum_decay = 0.9
step_size = 0.5

ROWS = 24
BLOCK = 2 * ROWS
SLAB = N_Z * BLOCK
TOKENS = N_Y * SLAB
WIDTH = 256
VALUES = 1024
COLS = VALUES // 2
HALF = TOKENS // 2
PADDED = 32
EXTRA = 16
ROW_SCALE = 1.0 / math.sqrt(WIDTH * N_Z * N_Y * 2)
GRAD_SCALE = 1.0 / math.sqrt(TOKENS)

X2_AT = TOKENS
W_AT = 2 * TOKENS
REC_AT = W_AT + 2 * WIDTH
T_AT = REC_AT + 2 * WIDTH
MESSAGE = T_AT + 4 * PADDED

B16, F32 = jnp.bfloat16, jnp.float32


def f32(value):
    return value.astype(jnp.float32)


def bf16(value):
    return value.astype(jnp.bfloat16)


def dot(a, b, dims=((1,), (0,))):
    return lax.dot_general(a, b, (dims, ((), ())), preferred_element_type=jnp.float32)


def cols_of(core):
    return pl.ds(pl.multiple_of(core * COLS, COLS), COLS)


def half_of(core):
    return pl.ds(pl.multiple_of(core * HALF, 16), HALF)


def own_block():
    return pl.ds(pl.multiple_of(lax.axis_index("z_hi") * BLOCK, 16), BLOCK)


def kept(mix, step):
    return mix[0, step].astype(jnp.float32) * 0.125


def by_y():
    return [((zh * N_Y + y) * BLOCK, (y * N_Z + zh) * BLOCK) for zh in range(N_Z) for y in range(N_Y)]


def first_values(push, x, w, far, own):
    core = lax.axis_index("core")
    for out, side in ((far, 1 - core), (own, core)):
        scaled = bf16(f32(w[:, cols_of(side)]) / push[0])
        part = bf16(dot(x[...], scaled) * ROW_SCALE)
        for at, to in by_y():
            out[to : to + BLOCK] = part[at : at + BLOCK]


def make_message(x, w, rec, targets, velocity, message, velocity_far):
    far = 1 - lax.axis_index("core")
    for step in range(2):
        for at, to in by_y():
            message[step * TOKENS + to : step * TOKENS + to + BLOCK] = x[step, at : at + BLOCK]
    for ref, row in ((w, W_AT), (rec, REC_AT)):
        half = ref[:, cols_of(far)]
        message[row : row + WIDTH] = half[:, :WIDTH]
        message[row + WIDTH : row + 2 * WIDTH] = half[:, WIDTH:]
    spare = jnp.zeros((PADDED - ROWS, COLS), jnp.float32)
    for step in range(2):
        half = bf16(jnp.concatenate([f32(targets[step, :, cols_of(far)]), spare], axis=0))
        row = T_AT + 2 * step * PADDED
        message[row : row + PADDED] = half[:, :WIDTH]
        message[row + PADDED : row + 2 * PADDED] = half[:, WIDTH:]
    velocity_far[...] = velocity[:, cols_of(far)]


def second_values(
    push, push_got, mix, w, rec, velocity, targets, mine, got, velocity_got, out, ahead, base, taught
):
    core = lax.axis_index("core")
    keep = kept(mix, 0)
    weight = keep * push[0] + push_got[0]
    side = cols_of(core)
    decayed = step_size * momentum_decay
    ahead[:WIDTH] = f32(w[:, side]) - decayed * velocity[:, side]
    base[:WIDTH] = keep * ahead[:WIDTH] + f32(rec[:, side])
    for k in range(2):
        part = slice(k * WIDTH, (k + 1) * WIDTH)
        ahead[WIDTH:, part] = (
            f32(got[W_AT + k * WIDTH : W_AT + (k + 1) * WIDTH]) - decayed * velocity_got[:, part]
        )
        base[WIDTH:, part] = keep * ahead[WIDTH:, part] + f32(
            got[REC_AT + k * WIDTH : REC_AT + (k + 1) * WIDTH]
        )
    scaled = bf16(base[...] / weight)
    near, far = mine[X2_AT : X2_AT + TOKENS], got[X2_AT : X2_AT + TOKENS]
    out[:, :COLS] = bf16((dot(near, scaled[:WIDTH]) + dot(far, scaled[WIDTH:])) * ROW_SCALE)
    rows = half_of(core)
    across = ((1,), (1,))
    out[:, COLS:] = bf16(dot(near, mine[rows], across) + dot(far, got[rows], across))
    for step in range(2):
        own = f32(targets[step, :, side])
        row = T_AT + 2 * step * PADDED
        other = jnp.concatenate(
            [f32(got[row : row + PADDED]), f32(got[row + PADDED : row + 2 * PADDED])], axis=1
        )[:ROWS]
        taught[step, :ROWS] = jnp.where(core == 0, own, other)
        taught[step, ROWS:] = jnp.where(core == 0, other, own)


def sum_over_y(step, parts, taught, slab, own):
    total = f32(parts[0])
    for y in range(1, N_Y):
        total = total + f32(parts[y])
    slab[...] = bf16(total)
    rows = own_block()
    total = f32(parts[0, rows, :COLS])
    for y in range(1, N_Y):
        total = total + f32(parts[y, rows, :COLS])
    own[...] = total
    slab[rows, :COLS] = bf16(total - taught[step])


def add_slab(mine, got, own, out, own_out):
    out[...] = bf16(f32(mine[...]) + f32(got[...]))
    own_out[...] = own[...] + f32(got[own_block(), :COLS])


def add_and_spread(mine, got, own, out, own_out):
    total = bf16(f32(mine[...]) + f32(got[...]))
    for y in range(N_Y):
        out[y] = total
    own_out[...] = own[...] + f32(got[own_block()])


def add_and_part(mine, got, own, out, gram, own_out):
    out[...] = bf16(f32(mine[:, :COLS]) + f32(got[:, :COLS]))
    gram[...] = bf16(f32(mine[:, COLS:]) + f32(got[:, COLS:]))
    own_out[...] = own[...] + f32(got[own_block(), :COLS])


def second_residual(push, push_got, mix, all1, gram, gram_got, base, own, out, own_out, turned):
    core = lax.axis_index("core")
    keep = kept(mix, 0)
    back = step_size * GRAD_SCALE * ROW_SCALE * keep / (keep * push[0] + push_got[0])
    near, far = all1[half_of(core)], all1[half_of(1 - core)]
    turned[...] = (dot(gram[...], near) + dot(gram_got[...], far)) * back
    residual = bf16(f32(base[...]) - turned[...])
    for y in range(N_Y):
        out[y] = residual
    own_out[...] = own[...] - turned[own_block()]


def first_gradient(push, mix, all1, mine, got, ahead, base, velocity, velocity_got, out, ready):
    side = cols_of(lax.axis_index("core"))
    keep = kept(mix, 0)
    down = ((0,), (0,))
    for k, x, old in ((0, mine, velocity[:, side]), (1, got, velocity_got[...])):
        rows = slice(k * WIDTH, (k + 1) * WIDTH)
        gradient = dot(x[:TOKENS], all1[...], down) * GRAD_SCALE
        out[rows] = bf16((1.0 - keep) * (ahead[rows] - step_size * gradient))
        current = bf16(base[rows] - (step_size * keep) * gradient)
        moved = momentum_decay * old + gradient
        ready[rows] = f32(current) - (step_size * momentum_decay) * moved
    out[2 * WIDTH :] = bf16(jnp.full((EXTRA, COLS), (1.0 - keep) * push[0], jnp.float32))


def second_gradient(push, push_got, mix, all2, mine, got, ready, far, near, half):
    keep = kept(mix, 1)
    down = ((0,), (0,))
    for k, x, out in ((1, got, far), (0, mine, near)):
        rows = slice(k * WIDTH, (k + 1) * WIDTH)
        gradient = dot(x[...], all2[...], down) * GRAD_SCALE
        moved = ready[rows] - step_size * gradient
        out[:WIDTH] = bf16((1.0 - keep) * moved)
        half[rows] = keep * moved
    first = kept(mix, 0)
    weight = first * push[0] + push_got[0]
    near[WIDTH:] = bf16(jnp.full((EXTRA, COLS), (1.0 - keep) * weight, jnp.float32))


def add_arrived(half, arrived, own1, own2, near, far, values):
    core = lax.axis_index("core")
    near[...] = bf16(half[:WIDTH] + f32(arrived[:WIDTH]))
    far[:WIDTH] = bf16(half[WIDTH:] + f32(arrived[WIDTH : 2 * WIDTH]))
    spare = jnp.zeros((PADDED - ROWS, COLS), jnp.float32)
    for step, own in ((0, own1), (1, own2)):
        low, high = own[:ROWS], own[ROWS:]
        values[step] = bf16(jnp.where(core == 0, low, high))
        row = WIDTH + step * PADDED
        far[row : row + PADDED] = bf16(
            jnp.concatenate([jnp.where(core == 0, high, low), spare], axis=0)
        )


def join_numerator(near, far, values, out, rows_out):
    core = lax.axis_index("core")
    out[0, :, cols_of(core)] = near[...]
    out[0, :, cols_of(1 - core)] = far[:WIDTH]
    for step in range(2):
        row = WIDTH + step * PADDED
        rows_out[step, :, cols_of(core)] = values[step]
        rows_out[step, :, cols_of(1 - core)] = bf16(f32(far[row : row + PADDED])[:ROWS])


def join_received(near, far, out):
    core = lax.axis_index("core")
    out[0, :, cols_of(core)] = near[:WIDTH]
    out[0, :, cols_of(1 - core)] = far[...]


SMEM = pl.BlockSpec(memory_space=pltpu.SMEM)
VMEM = pl.BlockSpec(memory_space=pltpu.VMEM)
ANY = pl.BlockSpec(memory_space=pl.ANY)


def call(body, scalars, fetched, arrays, outs, scratch=(), flops=0):
    fetched = [f if isinstance(f, tuple) else (f, None) for f in fetched]
    result = [jax.ShapeDtypeStruct(shape, kind) for shape, kind in outs]
    n, first, last = len(fetched), len(scalars), len(scalars) + len(fetched)

    def view(ref, where):
        return ref if where is None else ref.at[where]

    def shape(value, where):
        if where is None:
            return value.shape
        if isinstance(where, int):
            return value.shape[1:]
        return (where.size,) + value.shape[1:]

    def kernel(*refs):
        count = last + len(arrays) + len(outs)
        buffers = refs[count : count + n]
        rest = refs[count + n :]
        if n:
            sems, rest = rest[0], rest[1:]
            copies = [
                pltpu.make_async_copy(view(refs[first + i], fetched[i][1]), buffers[i], sems.at[i])
                for i in range(n)
            ]
            for copy in copies:
                copy.start()
            for copy in copies:
                copy.wait()
        body(*refs[:first], *buffers, *refs[last:count], *rest)

    held = [pltpu.VMEM(shape(value, where), value.dtype) for value, where in fetched]
    if n:
        held.append(pltpu.SemaphoreType.DMA((n,)))
    moved = sum(a.size * a.dtype.itemsize for a in [f[0] for f in fetched] + list(arrays) + result)
    return pl.pallas_call(
        kernel,
        out_shape=result,
        in_specs=[SMEM] * len(scalars) + [ANY] * n + [VMEM] * len(arrays),
        out_specs=[VMEM] * len(outs),
        scratch_shapes=held + [pltpu.VMEM(size, kind) for size, kind in scratch],
        compiler_params=pltpu.CompilerParams(vmem_limit_bytes=20 * 2**20),
        cost_estimate=pl.CostEstimate(flops=flops, bytes_accessed=moved, transcendentals=0),
        name=body.func.__name__ if isinstance(body, functools.partial) else body.__name__,
    )(*scalars, *[f[0] for f in fetched], *arrays)


def z_pairs(step):
    pairs = []
    for zh in range(N_Z):
        for core in range(2):
            turn = (1, 3)[step ^ core]
            pairs.append((zh * 2 + core, (zh ^ turn) * 2 + core))
    return pairs


def over_z(value, step):
    return lax.ppermute(value, ("z_hi", "core"), z_pairs(step))


def over_y(value):
    return lax.all_to_all(value, "y", 0, 0, tiled=True)


def swap_core(value):
    return lax.ppermute(value, "core", [(0, 1), (1, 0)])


def to_group(value, hop):
    count = SIZES[0] * SIZES[1]
    return lax.ppermute(value, GROUP, [(i, (i + hop) % count) for i in range(count)])


def reduce_slab(step, part, taught):
    columns = part.shape[1]
    parts = over_y(part.reshape(N_Y, SLAB, columns))
    own = ((BLOCK, COLS), F32)
    whole = ((SLAB, columns), B16)
    slab, values = call(functools.partial(sum_over_y, step), [], [parts], [taught], [whole, own])
    return call(add_slab, [], [], [slab, over_z(slab, 0), values], [whole, own])


def local(inputs, targets, numerator, momentum, received, push_weight, received_weight, mix_share):
    push, push_got, mix = push_weight, received_weight, mix_share

    part = [((TOKENS, COLS), B16)] * 2
    part_far, part_own = call(first_values, [push], [(inputs, 0), (numerator, 0)], [], part)
    part1 = bf16(f32(part_own) + f32(swap_core(part_far)))

    targets, part_far = lax.optimization_barrier((targets, part_far))
    mine, velocity_far = call(
        make_message,
        [],
        [inputs, (numerator, 0), (received, 0), targets, (momentum, 0)],
        [],
        [((MESSAGE, WIDTH), B16), ((WIDTH, COLS), F32)],
    )
    got = swap_core(mine)
    velocity_got = swap_core(velocity_far)

    tile = ((2 * WIDTH, COLS), F32)
    part2, ahead, base, taught = call(
        second_values,
        [push, push_got, mix],
        [(numerator, 0), (received, 0), (momentum, 0), targets],
        [mine, got, velocity_got],
        [((TOKENS, COLS + HALF), B16), tile, tile, ((2, BLOCK, COLS), F32)],
    )

    spread = ((N_Y, SLAB, COLS), B16)
    own = ((BLOCK, COLS), F32)
    slab1, own1 = reduce_slab(0, part1, taught)
    sent, own1 = call(add_and_spread, [], [], [slab1, over_z(slab1, 1), own1], [spread, own])
    all1 = over_y(sent).reshape(TOKENS, COLS)

    slab2, own2 = reduce_slab(1, part2, taught)
    ahead2, gram, own2 = call(
        add_and_part,
        [],
        [],
        [slab2, over_z(slab2, 1), own2],
        [((SLAB, COLS), B16), ((SLAB, HALF), B16), own],
    )
    gram_got = swap_core(gram)
    sent, own2 = call(
        second_residual,
        [push, push_got, mix],
        [all1],
        [gram, gram_got, ahead2, own2],
        [spread, own],
        [((SLAB, COLS), F32)],
    )
    all2 = over_y(sent).reshape(TOKENS, COLS)

    outgoing, ready = call(
        first_gradient,
        [push, mix],
        [
            all1,
            (mine, pl.ds(0, TOKENS)),
            (got, pl.ds(0, TOKENS)),
            ahead,
            base,
            (momentum, 0),
            velocity_got,
        ],
        [],
        [((2 * WIDTH + EXTRA, COLS), B16), tile],
    )
    arrived = to_group(outgoing, 1)

    far, near, half = call(
        second_gradient,
        [push, push_got, mix],
        [all2, (mine, pl.ds(X2_AT, TOKENS)), (got, pl.ds(X2_AT, TOKENS)), ready],
        [],
        [((WIDTH, COLS), B16), ((WIDTH + EXTRA, COLS), B16), tile],
    )

    count = SIZES[0] * SIZES[1]
    hop = [(i * 2 + c, (i + 2) % count * 2 + 1 - c) for i in range(count) for c in range(2)]
    sent_far = lax.ppermute(far, GROUP + ("core",), hop)
    sent_own = to_group(near, 2)

    current, current_far, values = call(
        add_arrived,
        [],
        [half, arrived, own1, own2],
        [],
        [((WIDTH, COLS), B16), ((WIDTH + 2 * PADDED, COLS), B16), ((2, ROWS, COLS), B16)],
    )
    whole = ((1, WIDTH, VALUES), B16)
    final_numerator, value_rows = call(
        join_numerator,
        [],
        [],
        [current, swap_core(current_far), values],
        [whole, ((2, ROWS, VALUES), B16)],
    )
    arrived_weight = f32(arrived[2 * WIDTH, :1])
    keep = f32(mix[0]) / 8.0
    final_weight = keep[1] * (keep[0] * push + push_got) + arrived_weight
    sent_far, final_numerator, final_weight = lax.optimization_barrier(
        (sent_far, final_numerator, final_weight)
    )
    (final_received,) = call(join_received, [], [], [sent_own, sent_far], [whole])
    return final_numerator, final_weight, final_received, f32(sent_own[WIDTH, :1]), value_rows


def solution(mesh):
    fine = Mesh(mesh.devices.reshape(SIZES), GROUP + MP)
    placed = (
        P(None, GROUP, MP),
        P(None, GROUP + MP, None),
        P(GROUP, MP, None),
        P(GROUP, MP, None),
        P(GROUP, MP, None),
        P(GROUP),
        P(GROUP),
        P(GROUP, None),
    )
    return jax.shard_map(
        local,
        mesh=fine,
        in_specs=placed,
        out_specs=(
            P(GROUP, MP, None),
            P(GROUP),
            P(GROUP, MP, None),
            P(GROUP),
            P(None, GROUP + MP, None),
        ),
        check_vma=False,
    )
```

time: 220 us -> 195 us (0.89)
  starting transfers between devices: 111 us -> 76.5 us
  waiting for transfers between devices: 46 us -> 64.7 us
  other arithmetic: 8.07 us -> 1.1 us
  Pallas kernels: 15.1 us -> 17.8 us
    ppermute x7 -> x4, starting transfers between devices: 44.4 us -> 21.9 us  [over_z(): return lax.ppermute(value, ('z_hi', 'core'), z_pairs(step))]
    ppermute x7 -> x4, waiting for transfers between devices: 19.7 us -> 32.1 us  [over_z(): return lax.ppermute(value, ('z_hi', 'core'), z_pairs(step))]
    all_to_all x4, waiting for transfers between devices: 3.13 us -> 8.94 us  [over_y(): return lax.all_to_all(value, 'y', 0, 0, tiled=True)]
    ppermute x4 -> x2, waiting for transfers between devices: 15.5 us -> 21.3 us  [to_group(): lax.ppermute(value, GROUP, [(i, (i + hop) % count) for i in range(count)])]
    ppermute x6 -> x5, starting transfers between devices: 32.8 us -> 27.1 us  [swap_core(): return lax.ppermute(value, 'core', [(0, 1), (1, 0)])]
    ppermute x1, waiting for transfers between devices: 5.62 us -> 0.01 us  [local(): sent_far = lax.ppermute(far, GROUP + ('core',), hop)]
    ppermute x4 -> x2, starting transfers between devices: 12.4 us -> 9.07 us  [to_group(): lax.ppermute(value, GROUP, [(i, (i + hop) % count) for i in range(count)])]
    select_n x4 -> x0, other arithmetic: 3.17 us -> none  [the longest x1 1.4 us: local(): values_far = pick(both[:, 1], both[:, 0])]
  transfers between devices with their start and end apart: 22 -> 16, of which waited for: 10 -> 7; matrix products, arithmetic and copies ran while one was open for 4% -> 1% of each run, Pallas kernels for 5% -> 8%
where the time goes in v4:
time: 195 us; the launch traced here: 194 us
  starting transfers between devices  76.5 us (39%)
  waiting for transfers between devices  64.7 us (33%)
  local copies, waits for them, and re-layouts  26.5 us (14%)
  Pallas kernels  17.8 us (9%)
  between operations  7.32 us (4%)
    ppermute x4, waiting for transfers between devices, over_z(): return lax.ppermute(value, ('z_hi', 'core'), z_pairs(step))  32.1 us
    ppermute x5, starting transfers between devices, swap_core(): return lax.ppermute(value, 'core', [(0, 1), (1, 0)])  27.1 us
    unnamed x70, local copies, waits for them, and re-layouts  24.9 us
    ppermute x4, starting transfers between devices, over_z(): return lax.ppermute(value, ('z_hi', 'core'), z_pairs(step))  21.9 us
    ppermute x2, waiting for transfers between devices, to_group(): lax.ppermute(value, GROUP, [(i, (i + hop) % count) for i in range(count)])  21.3 us
    pallas_call x15, Pallas kernels, call(): pl.pallas_call(kernel, out_shape=result, in_specs=[SMEM] * len(scalars) +...  17.8 us
    all_to_all x4, starting transfers between devices, over_y(): return lax.all_to_all(value, 'y', 0, 0, tiled=True)  16.5 us
    ppermute x2, starting transfers between devices, to_group(): lax.ppermute(value, GROUP, [(i, (i + hop) % count) for i in range(count)])  9.07 us
  transfers between devices with their start and end apart: 16, of which 7 were waited for; matrix products, arithmetic and copies ran while one was open for 1% of the time, Pallas kernels for 8%

profile of v4, /device:TPU:1, one launch (start us, length us, event | category | flops | bytes accessed | tf_op | source)
XLA Modules:
  0.0 193.9 jit_solution(17595575717057940764)
XLA Ops:
  4.4 8.8 %collective-permute-start = (bf16[768,512]{1,0:T(8,128)(2,1)S(1)}, bf16[768,512]{1,0:T(8,128)(2,1)S(1)}, u32[]{:S(2)}, u32[]{:S(2)}) collective-permute-start(bf16[768,512]{1,0:T(8,128)(2,1)S(1)} %get-tuple-element.43), channel_id=1, source_target_pairs={{0,1},{1,0},{2,3},{3,2},{4,5},{5,4},{6,7},{7,6},{8,9},{9,8},{10,11... | collective-permute-start | bytes 2359304 | tf_op jit(solution)/shard_map/ppermute | solution.py:306
  14.8 1.9 collective-permute-start.1
  17.8 4.3 %all-to-all-start = ((bf16[4,192,512]{2,1,0:T(8,128)(2,1)}), bf16[4,192,512]{2,1,0:T(8,128)(2,1)}, u32[]{:S(2)}, u32[]{:S(2)}) async-start(bf16[4,192,512]{2,1,0:T(8,128)(2,1)} %bitcast.13), calls=%async_computation | async-start | bytes 1572864 | tf_op jit(solution)/shard_map/all_to_all | solution.py:302
  22.1 2.4 %collective-permute-start.2 = (f32[256,512]{1,0:T(8,128)}, f32[256,512]{1,0:T(8,128)S(1)}, u32[]{:S(2)}, u32[]{:S(2)}) collective-permute-start(f32[256,512]{1,0:T(8,128)} %copy-done.34), channel_id=1, source_target_pairs={{0,1},{1,0},{2,3},{3,2},{4,5},{5,4},{6,7},{7,6},{8,9},{9,8},{10,11... | collective-permute-start | bytes 1572872 | tf_op jit(solution)/shard_map/ppermute | solution.py:306
  29.5 2.0 %second_values.1 = (bf16[768,896]{1,0:T(8,128)(2,1)S(1)}, f32[512,512]{1,0:T(8,128)S(1)}, f32[512,512]{1,0:T(8,128)S(1)}, f32[2,48,512]{2,1,0:T(8,128)S(1)}) custom-call(f32[1]{0:T(128)S(6)} %copy.13.refs_0_, f32[1]{0:T(128)S(6)} %copy.14.refs_1_, s32[1,2]{1,0:T(1,128)S(1)} %copy-done.33, bf16[1,256,1024]{2,1,0:T(8,128)(2,1)S(1)} %copy-done.4, ...), custom_call_target="tpu_custom_call" | custom-call | bytes 9142272 | tf_op jit(solution)/shard_map/second_values/pallas_call | solution.py:276
  35.3 4.5 %all-to-all-start.2 = ((bf16[4,192,896]{2,1,0:T(8,128)(2,1)}), bf16[4,192,896]{2,1,0:T(8,128)(2,1)}, u32[]{:S(2)}, u32[]{:S(2)}) async-start(bf16[4,192,896]{2,1,0:T(8,128)(2,1)} %bitcast.12), calls=%async_computation.2 | async-start | bytes 2752512 | tf_op jit(solution)/shard_map/all_to_all | solution.py:302
  41.7 7.4 %collective-permute-start.3 = (bf16[192,512]{1,0:T(8,128)(2,1)S(1)}, bf16[192,512]{1,0:T(8,128)(2,1)S(1)}, u32[]{:S(2)}, u32[]{:S(2)}) collective-permute-start(bf16[192,512]{1,0:T(8,128)(2,1)S(1)} %get-tuple-element.48.refs_0_), channel_id=1, source_target_pairs={{0,8},{1,25},{8,0},{9,17},{16,24},{17,9},{24,16},{25,1},{2,10},{3,... | collective-permute-start | bytes 589832 | tf_op jit(solution)/shard_map/ppermute | solution.py:298
  49.1 8.9 %all-to-all-done.2.refs_0_ = bf16[4,192,896]{2,1,0:T(8,128)(2,1)} async-done(((bf16[4,192,896]{2,1,0:T(8,128)(2,1)}), bf16[4,192,896]{2,1,0:T(8,128)(2,1)}, u32[]{:S(2)}, u32[]{:S(2)}) %all-to-all-start.2) | async-done | bytes 1376288 | tf_op jit(solution)/shard_map/all_to_all | solution.py:302
  58.0 2.3 %sum_over_y.3 = (bf16[192,896]{1,0:T(8,128)(2,1)}, f32[48,512]{1,0:T(8,128)S(1)}) custom-call(bf16[4,192,896]{2,1,0:T(8,128)(2,1)} %all-to-all-done.2.refs_0_, f32[2,48,512]{2,1,0:T(8,128)S(1)} %get-tuple-element.47.refs_1_), custom_call_target="tpu_custom_call" | custom-call | bytes 2015232 | tf_op jit(solution)/shard_map/sum_over_y/pallas_call | solution.py:276
  60.3 7.4 %collective-permute-start.5 = (bf16[192,896]{1,0:T(8,128)(2,1)}, bf16[192,896]{1,0:T(8,128)(2,1)}, u32[]{:S(2)}, u32[]{:S(2)}) collective-permute-start(bf16[192,896]{1,0:T(8,128)(2,1)} %get-tuple-element.54.refs_0_), channel_id=1, source_target_pairs={{0,8},{1,25},{8,0},{9,17},{16,24},{17,9},{24,16},{25,1},{2,10},{3,... | collective-permute-start | bytes 1032200 | tf_op jit(solution)/shard_map/ppermute | solution.py:298
  67.8 5.2 %collective-permute-start.4 = (bf16[192,512]{1,0:T(8,128)(2,1)S(1)}, bf16[192,512]{1,0:T(8,128)(2,1)S(1)}, u32[]{:S(2)}, u32[]{:S(2)}) collective-permute-start(bf16[192,512]{1,0:T(8,128)(2,1)S(1)} %get-tuple-element.50.refs_0_), channel_id=1, source_target_pairs={{0,24},{1,9},{8,16},{9,1},{16,8},{17,25},{24,0},{25,17},{2,26},{3,... | collective-permute-start | bytes 589832 | tf_op jit(solution)/shard_map/ppermute | solution.py:298
  73.0 17.9 %collective-permute-done.4.refs_1_ = bf16[192,512]{1,0:T(8,128)(2,1)S(1)} collective-permute-done((bf16[192,512]{1,0:T(8,128)(2,1)S(1)}, bf16[192,512]{1,0:T(8,128)(2,1)S(1)}, u32[]{:S(2)}, u32[]{:S(2)}) %collective-permute-start.4) | collective-permute-done | bytes 196640 | tf_op jit(solution)/shard_map/ppermute | solution.py:298
  92.5 3.5 %all-to-all-start.1 = ((bf16[4,192,512]{2,1,0:T(8,128)(2,1)}), bf16[4,192,512]{2,1,0:T(8,128)(2,1)S(1)}, u32[]{:S(2)}, u32[]{:S(2)}) async-start(bf16[4,192,512]{2,1,0:T(8,128)(2,1)} %copy-done.17), calls=%async_computation.1 | async-start | bytes 1572864 | tf_op jit(solution)/shard_map/all_to_all | solution.py:302
  98.1 1.9 collective-permute-start.6
  100.1 14.1 %collective-permute-done.6.refs_1_ = bf16[192,896]{1,0:T(8,128)(2,1)S(1)} collective-permute-done((bf16[192,896]{1,0:T(8,128)(2,1)S(1)}, bf16[192,896]{1,0:T(8,128)(2,1)S(1)}, u32[]{:S(2)}, u32[]{:S(2)}) %collective-permute-start.6) | collective-permute-done | bytes 344096 | tf_op jit(solution)/shard_map/ppermute | solution.py:298
  116.2 10.1 %collective-permute-start.7 = (bf16[192,384]{1,0:T(8,128)(2,1)}, bf16[192,384]{1,0:T(8,128)(2,1)}, u32[]{:S(2)}, u32[]{:S(2)}) collective-permute-start(bf16[192,384]{1,0:T(8,128)(2,1)} %get-tuple-element.58.refs_4_), channel_id=1, source_target_pairs={{0,1},{1,0},{2,3},{3,2},{4,5},{5,4},{6,7},{7,6},{8,9},{9,8},{10,11... | collective-permute-start | bytes 442376 | tf_op jit(solution)/shard_map/ppermute | solution.py:306
  132.5 4.2 %all-to-all-start.3 = ((bf16[4,192,512]{2,1,0:T(8,128)(2,1)}), bf16[4,192,512]{2,1,0:T(8,128)(2,1)}, u32[]{:S(2)}, u32[]{:S(2)}) async-start(bf16[4,192,512]{2,1,0:T(8,128)(2,1)} %copy-done.18), calls=%async_computation.3 | async-start | bytes 1572864 | tf_op jit(solution)/shard_map/all_to_all | solution.py:302
  141.4 2.9 %first_gradient.1 = (bf16[528,512]{1,0:T(8,128)(2,1)}, f32[512,512]{1,0:T(8,128)S(1)}) custom-call(f32[1]{0:T(128)S(6)} %copy.13.refs_0_, s32[1,2]{1,0:T(1,128)S(1)} %copy-done.33, bf16[768,512]{1,0:T(8,128)(2,1)S(1)} %bitcast.11, bf16[2688,256]{1,0:T(8,128)(2,1)S(1)} %get-tuple-element.45.refs_7_.refs_3_.refs_4_, ...), custom_call_target="tpu_custom_call" | custom-call | bytes 8798208 | tf_op jit(solution)/shard_map/first_gradient/pallas_call | solution.py:276
  145.3 4.2 %collective-permute-start.9 = (bf16[528,512]{1,0:T(8,128)(2,1)}, bf16[528,512]{1,0:T(8,128)(2,1)S(1)}, u32[]{:S(2)}, u32[]{:S(2)}) collective-permute-start(bf16[528,512]{1,0:T(8,128)(2,1)} %get-tuple-element.67), channel_id=1, source_target_pairs={{0,32},{32,64},{64,96},{96,128},{128,160},{160,192},{192,224},{224... | collective-permute-start | bytes 1622024 | tf_op jit(solution)/shard_map/ppermute | solution.py:311
  150.8 2.4 %second_gradient.1 = (bf16[256,512]{1,0:T(8,128)(2,1)S(1)}, bf16[272,512]{1,0:T(8,128)(2,1)S(1)}, f32[512,512]{1,0:T(8,128)S(1)}) custom-call(f32[1]{0:T(128)S(6)} %copy.13.refs_0_, f32[1]{0:T(128)S(6)} %copy.14.refs_1_, s32[1,2]{1,0:T(1,128)S(1)} %copy-done.33, bf16[768,512]{1,0:T(8,128)(2,1)} %bitcast.3.refs_3_, ...), custom_call_target="tpu_custom_call" | custom-call | bytes 6176768 | tf_op jit(solution)/shard_map/second_gradient/pallas_call | solution.py:276
  155.1 4.9 %collective-permute-start.11 = (bf16[272,512]{1,0:T(8,128)(2,1)S(1)}, bf16[272,512]{1,0:T(8,128)(2,1)S(1)}, u32[]{:S(2)}, u32[]{:S(2)}) collective-permute-start(bf16[272,512]{1,0:T(8,128)(2,1)S(1)} %get-tuple-element.76), channel_id=1, source_target_pairs={{0,64},{32,96},{64,128},{96,160},{128,192},{160,224},{192,256},{22... | collective-permute-start | bytes 835592 | tf_op jit(solution)/shard_map/ppermute | solution.py:311
  159.9 4.9 %collective-permute-done.9.refs_1_ = bf16[528,512]{1,0:T(8,128)(2,1)S(1)} collective-permute-done((bf16[528,512]{1,0:T(8,128)(2,1)}, bf16[528,512]{1,0:T(8,128)(2,1)S(1)}, u32[]{:S(2)}, u32[]{:S(2)}) %collective-permute-start.9) | collective-permute-done | bytes 540704 | tf_op jit(solution)/shard_map/ppermute | solution.py:311
  165.4 3.9 %collective-permute-start.10 = (bf16[320,512]{1,0:T(8,128)(2,1)S(1)}, bf16[320,512]{1,0:T(8,128)(2,1)S(1)}, u32[]{:S(2)}, u32[]{:S(2)}) collective-permute-start(bf16[320,512]{1,0:T(8,128)(2,1)S(1)} %get-tuple-element.71), channel_id=1, source_target_pairs={{0,1},{1,0},{2,3},{3,2},{4,5},{5,4},{6,7},{7,6},{8,9},{9,8},{10,11... | collective-permute-start | bytes 983048 | tf_op jit(solution)/shard_map/ppermute | solution.py:306
  172.4 16.4 %collective-permute-done.11.refs_0_ = bf16[272,512]{1,0:T(8,128)(2,1)S(1)} collective-permute-done((bf16[272,512]{1,0:T(8,128)(2,1)S(1)}, bf16[272,512]{1,0:T(8,128)(2,1)S(1)}, u32[]{:S(2)}, u32[]{:S(2)}) %collective-permute-start.11) | collective-permute-done | bytes 278560 | tf_op jit(solution)/shard_map/ppermute | solution.py:311
  (98 shorter events, 40.3 us)
Async XLA Ops:
  0.6 12.6 %copy-start = (f32[1,256,1024]{2,1,0:T(8,128)S(1)}, f32[1,256,1024]{2,1,0:T(8,128)}, u32[]{:S(2)}) copy-start(f32[1,256,1024]{2,1,0:T(8,128)} %refs_7_.1) | copy-start | bytes 3145732
  3.6 9.7 %copy-start.19 = (bf16[2,24,1024]{2,1,0:T(8,128)(2,1)S(1)}, bf16[2,24,1024]{2,1,0:T(8,128)(2,1)}, u32[]{:S(2)}) copy-start(bf16[2,24,1024]{2,1,0:T(8,128)(2,1)} %refs_6_) | copy-start | bytes 294916
  4.4 12.3 %collective-permute-start = (bf16[768,512]{1,0:T(8,128)(2,1)S(1)}, bf16[768,512]{1,0:T(8,128)(2,1)S(1)}, u32[]{:S(2)}, u32[]{:S(2)}) collective-permute-start(bf16[768,512]{1,0:T(8,128)(2,1)S(1)} %get-tuple-element.43), channel_id=1, source_target_pairs={{0,1},{1,0},{2,3},{3,2},{4,5},{5,4},{6,7},{7,6},{8,9},{9,8},{10,11... | collective-permute-start | bytes 2359304 | tf_op jit(solution)/shard_map/ppermute | solution.py:306
  14.8 11.5 %collective-permute-start.1 = (bf16[2688,256]{1,0:T(8,128)(2,1)S(1)}, bf16[2688,256]{1,0:T(8,128)(2,1)S(1)}, u32[]{:S(2)}, u32[]{:S(2)}) collective-permute-start(bf16[2688,256]{1,0:T(8,128)(2,1)S(1)} %get-tuple-element.45.refs_7_.refs_3_.refs_4_), channel_id=1, source_target_pairs={{0,1},{1,0},{2,3},{3,2},{4,5},{5,4},{6,7},{7,6},{8,9},{9,8},{10,11... | collective-permute-start | bytes 4128776 | tf_op jit(solution)/shard_map/ppermute | solution.py:306
  17.8 8.5 %copy-start.4 = (bf16[1,256,1024]{2,1,0:T(8,128)(2,1)S(1)}, bf16[1,256,1024]{2,1,0:T(8,128)(2,1)}, u32[]{:S(2)}) copy-start(bf16[1,256,1024]{2,1,0:T(8,128)(2,1)} %refs_3_.2) | copy-start | bytes 1572868
  17.8 8.5 %copy-start.33 = (s32[1,2]{1,0:T(1,128)S(1)}, s32[1,2]{1,0:T(1,128)}, u32[]{:S(2)}) copy-start(s32[1,2]{1,0:T(1,128)} %refs_2_.9) | copy-start | bytes 28
  17.8 17.5 %all-to-all-start = ((bf16[4,192,512]{2,1,0:T(8,128)(2,1)}), bf16[4,192,512]{2,1,0:T(8,128)(2,1)}, u32[]{:S(2)}, u32[]{:S(2)}) async-start(bf16[4,192,512]{2,1,0:T(8,128)(2,1)} %bitcast.13), calls=%async_computation | async-start | bytes 1572864 | tf_op jit(solution)/shard_map/all_to_all | solution.py:302
  22.1 4.1 %collective-permute-start.2 = (f32[256,512]{1,0:T(8,128)}, f32[256,512]{1,0:T(8,128)S(1)}, u32[]{:S(2)}, u32[]{:S(2)}) collective-permute-start(f32[256,512]{1,0:T(8,128)} %copy-done.34), channel_id=1, source_target_pairs={{0,1},{1,0},{2,3},{3,2},{4,5},{5,4},{6,7},{7,6},{8,9},{9,8},{10,11... | collective-permute-start | bytes 1572872 | tf_op jit(solution)/shard_map/ppermute | solution.py:306
  35.3 22.7 %all-to-all-start.2 = ((bf16[4,192,896]{2,1,0:T(8,128)(2,1)}), bf16[4,192,896]{2,1,0:T(8,128)(2,1)}, u32[]{:S(2)}, u32[]{:S(2)}) async-start(bf16[4,192,896]{2,1,0:T(8,128)(2,1)} %bitcast.12), calls=%async_computation.2 | async-start | bytes 2752512 | tf_op jit(solution)/shard_map/all_to_all | solution.py:302
  41.7 26.1 %collective-permute-start.3 = (bf16[192,512]{1,0:T(8,128)(2,1)S(1)}, bf16[192,512]{1,0:T(8,128)(2,1)S(1)}, u32[]{:S(2)}, u32[]{:S(2)}) collective-permute-start(bf16[192,512]{1,0:T(8,128)(2,1)S(1)} %get-tuple-element.48.refs_0_), channel_id=1, source_target_pairs={{0,8},{1,25},{8,0},{9,17},{16,24},{17,9},{24,16},{25,1},{2,10},{3,... | collective-permute-start | bytes 589832 | tf_op jit(solution)/shard_map/ppermute | solution.py:298
  58.0 9.7 %copy-start.32 = (f32[48,512]{1,0:T(8,128)S(1)}, f32[48,512]{1,0:T(8,128)}, u32[]{:S(2)}) copy-start(f32[48,512]{1,0:T(8,128)} %copy-done.31) | copy-start | bytes 294916
  60.3 32.2 %copy-start.27 = (f32[48,512]{1,0:T(8,128)}, f32[48,512]{1,0:T(8,128)S(1)}, u32[]{:S(2)}) copy-start(f32[48,512]{1,0:T(8,128)S(1)} %get-tuple-element.55.refs_2_) | copy-start | bytes 294916
  60.3 35.7 %collective-permute-start.5 = (bf16[192,896]{1,0:T(8,128)(2,1)}, bf16[192,896]{1,0:T(8,128)(2,1)}, u32[]{:S(2)}, u32[]{:S(2)}) collective-permute-start(bf16[192,896]{1,0:T(8,128)(2,1)} %get-tuple-element.54.refs_0_), channel_id=1, source_target_pairs={{0,8},{1,25},{8,0},{9,17},{16,24},{17,9},{24,16},{25,1},{2,10},{3,... | collective-permute-start | bytes 1032200 | tf_op jit(solution)/shard_map/ppermute | solution.py:298
  67.8 23.1 %collective-permute-start.4 = (bf16[192,512]{1,0:T(8,128)(2,1)S(1)}, bf16[192,512]{1,0:T(8,128)(2,1)S(1)}, u32[]{:S(2)}, u32[]{:S(2)}) collective-permute-start(bf16[192,512]{1,0:T(8,128)(2,1)S(1)} %get-tuple-element.50.refs_0_), channel_id=1, source_target_pairs={{0,24},{1,9},{8,16},{9,1},{16,8},{17,25},{24,0},{25,17},{2,26},{3,... | collective-permute-start | bytes 589832 | tf_op jit(solution)/shard_map/ppermute | solution.py:298
  92.5 33.8 %all-to-all-start.1 = ((bf16[4,192,512]{2,1,0:T(8,128)(2,1)}), bf16[4,192,512]{2,1,0:T(8,128)(2,1)S(1)}, u32[]{:S(2)}, u32[]{:S(2)}) async-start(bf16[4,192,512]{2,1,0:T(8,128)(2,1)} %copy-done.17), calls=%async_computation.1 | async-start | bytes 1572864 | tf_op jit(solution)/shard_map/all_to_all | solution.py:302
  98.1 16.1 %collective-permute-start.6 = (bf16[192,896]{1,0:T(8,128)(2,1)S(1)}, bf16[192,896]{1,0:T(8,128)(2,1)S(1)}, u32[]{:S(2)}, u32[]{:S(2)}) collective-permute-start(bf16[192,896]{1,0:T(8,128)(2,1)S(1)} %get-tuple-element.56.refs_0_), channel_id=1, source_target_pairs={{0,24},{1,9},{8,16},{9,1},{16,8},{17,25},{24,0},{25,17},{2,26},{3,... | collective-permute-start | bytes 1032200 | tf_op jit(solution)/shard_map/ppermute | solution.py:298
  116.2 11.4 %collective-permute-start.7 = (bf16[192,384]{1,0:T(8,128)(2,1)}, bf16[192,384]{1,0:T(8,128)(2,1)}, u32[]{:S(2)}, u32[]{:S(2)}) collective-permute-start(bf16[192,384]{1,0:T(8,128)(2,1)} %get-tuple-element.58.refs_4_), channel_id=1, source_target_pairs={{0,1},{1,0},{2,3},{3,2},{4,5},{5,4},{6,7},{7,6},{8,9},{9,8},{10,11... | collective-permute-start | bytes 442376 | tf_op jit(solution)/shard_map/ppermute | solution.py:306
  132.5 17.1 %all-to-all-start.3 = ((bf16[4,192,512]{2,1,0:T(8,128)(2,1)}), bf16[4,192,512]{2,1,0:T(8,128)(2,1)}, u32[]{:S(2)}, u32[]{:S(2)}) async-start(bf16[4,192,512]{2,1,0:T(8,128)(2,1)} %copy-done.18), calls=%async_computation.3 | async-start | bytes 1572864 | tf_op jit(solution)/shard_map/all_to_all | solution.py:302
  145.3 19.5 %collective-permute-start.9 = (bf16[528,512]{1,0:T(8,128)(2,1)}, bf16[528,512]{1,0:T(8,128)(2,1)S(1)}, u32[]{:S(2)}, u32[]{:S(2)}) collective-permute-start(bf16[528,512]{1,0:T(8,128)(2,1)} %get-tuple-element.67), channel_id=1, source_target_pairs={{0,32},{32,64},{64,96},{96,128},{128,160},{160,192},{192,224},{224... | collective-permute-start | bytes 1622024 | tf_op jit(solution)/shard_map/ppermute | solution.py:311
  150.8 14.1 %copy-start.24 = (f32[48,512]{1,0:T(8,128)S(1)}, f32[48,512]{1,0:T(8,128)}, u32[]{:S(2)}) copy-start(f32[48,512]{1,0:T(8,128)} %copy-done.23) | copy-start | bytes 294916
  150.8 14.1 %copy-start.26 = (f32[48,512]{1,0:T(8,128)S(1)}, f32[48,512]{1,0:T(8,128)}, u32[]{:S(2)}) copy-start(f32[48,512]{1,0:T(8,128)} %copy-done.25) | copy-start | bytes 294916
  153.2 37.7 %collective-permute-start.8 = (bf16[256,512]{1,0:T(8,128)(2,1)S(1)}, bf16[256,512]{1,0:T(8,128)(2,1)S(1)}, u32[]{:S(2)}, u32[]{:S(2)}) collective-permute-start(bf16[256,512]{1,0:T(8,128)(2,1)S(1)} %get-tuple-element.65), channel_id=1, source_target_pairs={{0,65},{1,64},{32,97},{33,96},{64,129},{65,128},{96,161},{97,160},... | collective-permute-start | bytes 786440 | tf_op jit(solution)/shard_map/ppermute | solution.py:402
  155.1 33.7 %collective-permute-start.11 = (bf16[272,512]{1,0:T(8,128)(2,1)S(1)}, bf16[272,512]{1,0:T(8,128)(2,1)S(1)}, u32[]{:S(2)}, u32[]{:S(2)}) collective-permute-start(bf16[272,512]{1,0:T(8,128)(2,1)S(1)} %get-tuple-element.76), channel_id=1, source_target_pairs={{0,64},{32,96},{64,128},{96,160},{128,192},{160,224},{192,256},{22... | collective-permute-start | bytes 835592 | tf_op jit(solution)/shard_map/ppermute | solution.py:311
  165.4 24.5 %collective-permute-start.10 = (bf16[320,512]{1,0:T(8,128)(2,1)S(1)}, bf16[320,512]{1,0:T(8,128)(2,1)S(1)}, u32[]{:S(2)}, u32[]{:S(2)}) collective-permute-start(bf16[320,512]{1,0:T(8,128)(2,1)S(1)} %get-tuple-element.71), channel_id=1, source_target_pairs={{0,1},{1,0},{2,3},{3,2},{4,5},{5,4},{6,7},{7,6},{8,9},{9,8},{10,11... | collective-permute-start | bytes 983048 | tf_op jit(solution)/shard_map/ppermute | solution.py:306
  (27 other events, 28.0 us)

commit v5 on v4

--- a/solution.py
+++ b/solution.py
@@ -175,67 +175,60 @@
     own_out[...] = own[...] - turned[own_block()]
 
 
-def first_gradient(push, mix, all1, mine, got, ahead, base, velocity, velocity_got, out, ready):
+def first_gradient(push, mix, all1, mine, got, ahead, base, velocity, velocity_got, near, far, ready):
     side = cols_of(lax.axis_index("core"))
     keep = kept(mix, 0)
     down = ((0,), (0,))
-    for k, x, old in ((0, mine, velocity[:, side]), (1, got, velocity_got[...])):
+    for k, x, old, out in ((0, mine, velocity[:, side], near), (1, got, velocity_got[...], far)):
         rows = slice(k * WIDTH, (k + 1) * WIDTH)
         gradient = dot(x[:TOKENS], all1[...], down) * GRAD_SCALE
-        out[rows] = bf16((1.0 - keep) * (ahead[rows] - step_size * gradient))
+        out[:WIDTH] = bf16((1.0 - keep) * (ahead[rows] - step_size * gradient))
         current = bf16(base[rows] - (step_size * keep) * gradient)
         moved = momentum_decay * old + gradient
         ready[rows] = f32(current) - (step_size * momentum_decay) * moved
-    out[2 * WIDTH :] = bf16(jnp.full((EXTRA, COLS), (1.0 - keep) * push[0], jnp.float32))
-
-
-def second_gradient(push, push_got, mix, all2, mine, got, ready, far, near, half):
+    near[WIDTH:] = bf16(jnp.full((EXTRA, COLS), (1.0 - keep) * push[0], jnp.float32))
+
+
+def second_gradient(push, push_got, mix, mine, got, ready, all2, own1, own2, far, near, half, message):
+    core = lax.axis_index("core")
     keep = kept(mix, 1)
     down = ((0,), (0,))
-    for k, x, out in ((1, got, far), (0, mine, near)):
-        rows = slice(k * WIDTH, (k + 1) * WIDTH)
+    for k, x, out, held in ((1, got, far, message), (0, mine, near, half)):
         gradient = dot(x[...], all2[...], down) * GRAD_SCALE
-        moved = ready[rows] - step_size * gradient
+        moved = ready[k * WIDTH : (k + 1) * WIDTH] - step_size * gradient
         out[:WIDTH] = bf16((1.0 - keep) * moved)
-        half[rows] = keep * moved
-    first = kept(mix, 0)
-    weight = first * push[0] + push_got[0]
+        held[:WIDTH] = keep * moved
+    weight = kept(mix, 0) * push[0] + push_got[0]
     near[WIDTH:] = bf16(jnp.full((EXTRA, COLS), (1.0 - keep) * weight, jnp.float32))
-
-
-def add_arrived(half, arrived, own1, own2, near, far, values):
-    core = lax.axis_index("core")
-    near[...] = bf16(half[:WIDTH] + f32(arrived[:WIDTH]))
-    far[:WIDTH] = bf16(half[WIDTH:] + f32(arrived[WIDTH : 2 * WIDTH]))
-    spare = jnp.zeros((PADDED - ROWS, COLS), jnp.float32)
     for step, own in ((0, own1), (1, own2)):
-        low, high = own[:ROWS], own[ROWS:]
-        values[step] = bf16(jnp.where(core == 0, low, high))
-        row = WIDTH + step * PADDED
-        far[row : row + PADDED] = bf16(
-            jnp.concatenate([jnp.where(core == 0, high, low), spare], axis=0)
-        )
-
-
-def join_numerator(near, far, values, out, rows_out):
-    core = lax.axis_index("core")
-    out[0, :, cols_of(core)] = near[...]
-    out[0, :, cols_of(1 - core)] = far[:WIDTH]
-    for step in range(2):
-        row = WIDTH + step * PADDED
-        rows_out[step, :, cols_of(core)] = values[step]
-        rows_out[step, :, cols_of(1 - core)] = bf16(f32(far[row : row + PADDED])[:ROWS])
-
-
-def join_received(near, far, out):
+        row = WIDTH + step * ROWS
+        message[row : row + ROWS] = jnp.where(core == 0, own[ROWS:], own[:ROWS])
+
+
+def join_numerator(
+    push, push_got, mix, half, message, own1, own2, arrived, arrived_far, out, rows_out, weight
+):
+    core = lax.axis_index("core")
+    out[0, :, cols_of(core)] = bf16(half[...] + f32(arrived[:WIDTH]))
+    out[0, :, cols_of(1 - core)] = bf16(message[:WIDTH] + f32(arrived_far[...]))
+    for step, own in ((0, own1), (1, own2)):
+        row = WIDTH + step * ROWS
+        rows_out[step, :, cols_of(core)] = bf16(jnp.where(core == 0, own[:ROWS], own[ROWS:]))
+        rows_out[step, :, cols_of(1 - core)] = bf16(message[row : row + ROWS])
+    last = kept(mix, 0) * push[0] + push_got[0]
+    weight[0] = kept(mix, 1) * last + jnp.max(f32(arrived[WIDTH:]))
+
+
+def join_received(near, far, out, weight):
     core = lax.axis_index("core")
     out[0, :, cols_of(core)] = near[:WIDTH]
     out[0, :, cols_of(1 - core)] = far[...]
+    weight[0] = jnp.max(f32(near[WIDTH:]))
 
 
 SMEM = pl.BlockSpec(memory_space=pltpu.SMEM)
 VMEM = pl.BlockSpec(memory_space=pltpu.VMEM)
-ANY = pl.BlockSpec(memory_space=pl.ANY)
+HBM = pl.BlockSpec(memory_space=pltpu.HBM)
 
 
 def call(body, scalars, fetched, arrays, outs, scratch=(), flops=0):
@@ -276,8 +269,8 @@
     return pl.pallas_call(
         kernel,
         out_shape=result,
-        in_specs=[SMEM] * len(scalars) + [ANY] * n + [VMEM] * len(arrays),
-        out_specs=[VMEM] * len(outs),
+        in_specs=[SMEM] * len(scalars) + [HBM] * n + [VMEM] * len(arrays),
+        out_specs=[SMEM if shape == (1,) else VMEM for shape, _ in outs],
         scratch_shapes=held + [pltpu.VMEM(size, kind) for size, kind in scratch],
         compiler_params=pltpu.CompilerParams(vmem_limit_bytes=20 * 2**20),
         cost_estimate=pl.CostEstimate(flops=flops, bytes_accessed=moved, transcendentals=0),
@@ -311,11 +304,15 @@
     return lax.ppermute(value, GROUP, [(i, (i + hop) % count) for i in range(count)])
 
 
-def reduce_slab(step, part, taught):
-    columns = part.shape[1]
-    parts = over_y(part.reshape(N_Y, SLAB, columns))
+def to_group_other(value, hop):
+    count = SIZES[0] * SIZES[1]
+    pairs = [(i * 2 + c, (i + hop) % count * 2 + 1 - c) for i in range(count) for c in range(2)]
+    return lax.ppermute(value, GROUP + ("core",), pairs)
+
+
+def sum_slab(step, parts, taught):
     own = ((BLOCK, COLS), F32)
-    whole = ((SLAB, columns), B16)
+    whole = ((SLAB, parts.shape[2]), B16)
     slab, values = call(functools.partial(sum_over_y, step), [], [parts], [taught], [whole, own])
     return call(add_slab, [], [], [slab, over_z(slab, 0), values], [whole, own])
 
@@ -349,30 +346,14 @@
 
     spread = ((N_Y, SLAB, COLS), B16)
     own = ((BLOCK, COLS), F32)
-    slab1, own1 = reduce_slab(0, part1, taught)
+    parts2 = over_y(part2.reshape(N_Y, SLAB, COLS + HALF))
+    slab1, own1 = sum_slab(0, over_y(part1.reshape(N_Y, SLAB, COLS)), taught)
+    parts2, _ = lax.optimization_barrier((parts2, slab1))
     sent, own1 = call(add_and_spread, [], [], [slab1, over_z(slab1, 1), own1], [spread, own])
     all1 = over_y(sent).reshape(TOKENS, COLS)
 
-    slab2, own2 = reduce_slab(1, part2, taught)
-    ahead2, gram, own2 = call(
-        add_and_part,
-        [],
-        [],
-        [slab2, over_z(slab2, 1), own2],
-        [((SLAB, COLS), B16), ((SLAB, HALF), B16), own],
-    )
-    gram_got = swap_core(gram)
-    sent, own2 = call(
-        second_residual,
-        [push, push_got, mix],
-        [all1],
-        [gram, gram_got, ahead2, own2],
-        [spread, own],
-        [((SLAB, COLS), F32)],
-    )
-    all2 = over_y(sent).reshape(TOKENS, COLS)
-
-    outgoing, ready = call(
+    slab2, own2 = sum_slab(1, parts2, taught)
+    near, far, ready = call(
         first_gradient,
         [push, mix],
         [
@@ -385,46 +366,55 @@
             velocity_got,
         ],
         [],
-        [((2 * WIDTH + EXTRA, COLS), B16), tile],
-    )
-    arrived = to_group(outgoing, 1)
-
-    far, near, half = call(
+        [((WIDTH + EXTRA, COLS), B16), ((WIDTH, COLS), B16), tile],
+    )
+    slab2_got, _ = lax.optimization_barrier((over_z(slab2, 1), far))
+    arrived, arrived_far = to_group(near, 1), to_group_other(far, 1)
+    ahead2, gram, own2 = call(
+        add_and_part,
+        [],
+        [],
+        [slab2, slab2_got, own2],
+        [((SLAB, COLS), B16), ((SLAB, HALF), B16), own],
+    )
+    gram_got = swap_core(gram)
+    sent, own2 = call(
+        second_residual,
+        [push, push_got, mix],
+        [],
+        [all1, gram, gram_got, ahead2, own2],
+        [spread, own],
+        [((SLAB, COLS), F32)],
+    )
+    all2 = over_y(sent).reshape(TOKENS, COLS)
+    all2, arrived, arrived_far = lax.optimization_barrier((all2, arrived, arrived_far))
+
+    far, near, half, message = call(
         second_gradient,
         [push, push_got, mix],
-        [all2, (mine, pl.ds(X2_AT, TOKENS)), (got, pl.ds(X2_AT, TOKENS)), ready],
-        [],
-        [((WIDTH, COLS), B16), ((WIDTH + EXTRA, COLS), B16), tile],
-    )
-
-    count = SIZES[0] * SIZES[1]
-    hop = [(i * 2 + c, (i + 2) % count * 2 + 1 - c) for i in range(count) for c in range(2)]
-    sent_far = lax.ppermute(far, GROUP + ("core",), hop)
-    sent_own = to_group(near, 2)
-
-    current, current_far, values = call(
-        add_arrived,
-        [],
-        [half, arrived, own1, own2],
-        [],
-        [((WIDTH, COLS), B16), ((WIDTH + 2 * PADDED, COLS), B16), ((2, ROWS, COLS), B16)],
-    )
+        [(mine, pl.ds(X2_AT, TOKENS)), (got, pl.ds(X2_AT, TOKENS)), ready],
+        [all2, own1, own2],
+        [
+            ((WIDTH, COLS), B16),
+            ((WIDTH + EXTRA, COLS), B16),
+            ((WIDTH, COLS), F32),
+            ((WIDTH + 2 * ROWS, COLS), F32),
+        ],
+    )
+
+    sent_far, sent_own = to_group_other(far, 2), to_group(near, 2)
     whole = ((1, WIDTH, VALUES), B16)
-    final_numerator, value_rows = call(
+    number = ((1,), F32)
+    final_numerator, value_rows, final_weight = call(
         join_numerator,
-        [],
-        [],
-        [current, swap_core(current_far), values],
-        [whole, ((2, ROWS, VALUES), B16)],
-    )
-    arrived_weight = f32(arrived[2 * WIDTH, :1])
-    keep = f32(mix[0]) / 8.0
-    final_weight = keep[1] * (keep[0] * push + push_got) + arrived_weight
-    sent_far, final_numerator, final_weight = lax.optimization_barrier(
-        (sent_far, final_numerator, final_weight)
-    )
-    (final_received,) = call(join_received, [], [], [sent_own, sent_far], [whole])
-    return final_numerator, final_weight, final_received, f32(sent_own[WIDTH, :1]), value_rows
+        [push, push_got, mix],
+        [],
+        [half, swap_core(message), own1, own2, arrived, arrived_far],
+        [whole, ((2, ROWS, VALUES), B16), number],
+    )
+    sent_far, final_numerator = lax.optimization_barrier((sent_far, final_numerator))
+    final_received, got_weight = call(join_received, [], [], [sent_own, sent_far], [whole, number])
+    return final_numerator, final_weight, final_received, got_weight, value_rows
 
 
 def solution(mesh):

time: 195 us -> 188 us (0.964)
  between operations: 7.32 us -> 2.45 us
  waiting for transfers between devices: 64.7 us -> 62.4 us
    ppermute x1 -> x2, waiting for transfers between devices: 0.01 us -> 33 us  [to_group_other(): return lax.ppermute(value, GROUP + ('core',), pairs)]
    ppermute x2, waiting for transfers between devices: 21.3 us -> 0.01 us  [to_group(): lax.ppermute(value, GROUP, [(i, (i + hop) % count) for i in range(count)])]
    ppermute x5, starting transfers between devices: 27.1 us -> 17 us  [swap_core(): return lax.ppermute(value, 'core', [(0, 1), (1, 0)])]
    all_to_all x4, waiting for transfers between devices: 8.94 us -> 0.01 us  [over_y(): return lax.all_to_all(value, 'y', 0, 0, tiled=True)]
    ppermute x1 -> x2, starting transfers between devices: 1.92 us -> 8 us  [to_group_other(): return lax.ppermute(value, GROUP + ('core',), pairs)]
    ppermute x4, waiting for transfers between devices: 32.1 us -> 27 us  [over_z(): return lax.ppermute(value, ('z_hi', 'core'), z_pairs(step))]
    all_to_all x4, starting transfers between devices: 16.5 us -> 21 us  [over_y(): return lax.all_to_all(value, 'y', 0, 0, tiled=True)]
    ppermute x4, starting transfers between devices: 21.9 us -> 25.5 us  [over_z(): return lax.ppermute(value, ('z_hi', 'core'), z_pairs(step))]
  transfers between devices with their start and end apart: 16 -> 17, of which waited for: 7 -> 7; matrix products, arithmetic and copies ran while one was open for 1% -> 1% of each run, Pallas kernels for 8% -> 6%
where the time goes in v5:
time: 188 us; the launch traced here: 186 us
  starting transfers between devices  77.9 us (41%)
  waiting for transfers between devices  62.4 us (33%)
  local copies, waits for them, and re-layouts  25.3 us (13%)
  Pallas kernels  17.2 us (9%)
  between operations  2.45 us (1%)
    ppermute x2, waiting for transfers between devices, to_group_other(): return lax.ppermute(value, GROUP + ('core',), pairs)  33 us
    ppermute x4, waiting for transfers between devices, over_z(): return lax.ppermute(value, ('z_hi', 'core'), z_pairs(step))  27 us
    ppermute x4, starting transfers between devices, over_z(): return lax.ppermute(value, ('z_hi', 'core'), z_pairs(step))  25.5 us
    unnamed x78, local copies, waits for them, and re-layouts  25.3 us
    all_to_all x4, starting transfers between devices, over_y(): return lax.all_to_all(value, 'y', 0, 0, tiled=True)  21 us
    pallas_call x14, Pallas kernels, call(): pl.pallas_call(kernel, out_shape=result, in_specs=[SMEM] * len(scalars) +...  17.2 us
    ppermute x5, starting transfers between devices, swap_core(): return lax.ppermute(value, 'core', [(0, 1), (1, 0)])  17 us
    ppermute x2, starting transfers between devices, to_group_other(): return lax.ppermute(value, GROUP + ('core',), pairs)  8 us
  transfers between devices with their start and end apart: 17, of which 7 were waited for; matrix products, arithmetic and copies ran while one was open for 1% of the time, Pallas kernels for 6%

profile of v5, /device:TPU:1, one launch (start us, length us, event | category | flops | bytes accessed | tf_op | source)
XLA Modules:
  0.0 186.4 jit_solution(10975147103394022024)
XLA Ops:
  4.4 8.8 %collective-permute-start.1 = (bf16[768,512]{1,0:T(8,128)(2,1)S(1)}, bf16[768,512]{1,0:T(8,128)(2,1)S(1)}, u32[]{:S(2)}, u32[]{:S(2)}) collective-permute-start(bf16[768,512]{1,0:T(8,128)(2,1)S(1)} %get-tuple-element.48), channel_id=1, source_target_pairs={{0,1},{1,0},{2,3},{3,2},{4,5},{5,4},{6,7},{7,6},{8,9},{9,8},{10,11... | collective-permute-start | bytes 2359304 | tf_op jit(solution)/shard_map/ppermute | solution.py:299
  14.8 1.9 %collective-permute-start = (bf16[2688,256]{1,0:T(8,128)(2,1)S(1)}, bf16[2688,256]{1,0:T(8,128)(2,1)S(1)}, u32[]{:S(2)}, u32[]{:S(2)}) collective-permute-start(bf16[2688,256]{1,0:T(8,128)(2,1)S(1)} %get-tuple-element.50.refs_7_.refs_3_), channel_id=1, source_target_pairs={{0,1},{1,0},{2,3},{3,2},{4,5},{5,4},{6,7},{7,6},{8,9},{9,8},{10,11... | collective-permute-start | bytes 4128776 | tf_op jit(solution)/shard_map/ppermute | solution.py:299
  17.8 4.3 %all-to-all-start = ((bf16[4,192,512]{2,1,0:T(8,128)(2,1)}), bf16[4,192,512]{2,1,0:T(8,128)(2,1)}, u32[]{:S(2)}, u32[]{:S(2)}) async-start(bf16[4,192,512]{2,1,0:T(8,128)(2,1)} %bitcast.8), calls=%async_computation | async-start | bytes 1572864 | tf_op jit(solution)/shard_map/all_to_all | solution.py:295
  22.2 2.4 %collective-permute-start.2 = (f32[256,512]{1,0:T(8,128)}, f32[256,512]{1,0:T(8,128)S(1)}, u32[]{:S(2)}, u32[]{:S(2)}) collective-permute-start(f32[256,512]{1,0:T(8,128)} %copy-done.36), channel_id=1, source_target_pairs={{0,1},{1,0},{2,3},{3,2},{4,5},{5,4},{6,7},{7,6},{8,9},{9,8},{10,11... | collective-permute-start | bytes 1572872 | tf_op jit(solution)/shard_map/ppermute | solution.py:299
  29.5 1.9 %second_values.1 = (bf16[768,896]{1,0:T(8,128)(2,1)S(1)}, f32[512,512]{1,0:T(8,128)S(1)}, f32[512,512]{1,0:T(8,128)S(1)}, f32[2,48,512]{2,1,0:T(8,128)S(1)}) custom-call(f32[1]{0:T(128)S(6)} %copy.13.refs_0_, f32[1]{0:T(128)S(6)} %copy.14.refs_1_, s32[1,2]{1,0:T(1,128)S(1)} %copy-done.35, bf16[1,256,1024]{2,1,0:T(8,128)(2,1)S(1)} %copy-done.4, ...), custom_call_target="tpu_custom_call" | custom-call | bytes 9142272 | tf_op jit(solution)/shard_map/second_values/pallas_call | solution.py:269
  35.3 4.5 %all-to-all-start.2 = ((bf16[4,192,896]{2,1,0:T(8,128)(2,1)}), bf16[4,192,896]{2,1,0:T(8,128)(2,1)}, u32[]{:S(2)}, u32[]{:S(2)}) async-start(bf16[4,192,896]{2,1,0:T(8,128)(2,1)} %bitcast.7), calls=%async_computation.2 | async-start | bytes 2752512 | tf_op jit(solution)/shard_map/all_to_all | solution.py:295
  41.1 7.4 %collective-permute-start.3 = (bf16[192,512]{1,0:T(8,128)(2,1)S(1)}, bf16[192,512]{1,0:T(8,128)(2,1)S(1)}, u32[]{:S(2)}, u32[]{:S(2)}) collective-permute-start(bf16[192,512]{1,0:T(8,128)(2,1)S(1)} %get-tuple-element.54.refs_0_), channel_id=1, source_target_pairs={{0,8},{1,25},{8,0},{9,17},{16,24},{17,9},{24,16},{25,1},{2,10},{3,... | collective-permute-start | bytes 589832 | tf_op jit(solution)/shard_map/ppermute | solution.py:291
  48.5 7.0 %collective-permute-done.3.refs_1_ = bf16[192,512]{1,0:T(8,128)(2,1)S(1)} collective-permute-done((bf16[192,512]{1,0:T(8,128)(2,1)S(1)}, bf16[192,512]{1,0:T(8,128)(2,1)S(1)}, u32[]{:S(2)}, u32[]{:S(2)}) %collective-permute-start.3) | collective-permute-done | bytes 196640 | tf_op jit(solution)/shard_map/ppermute | solution.py:291
  56.1 7.6 %collective-permute-start.4 = (bf16[192,512]{1,0:T(8,128)(2,1)S(1)}, bf16[192,512]{1,0:T(8,128)(2,1)S(1)}, u32[]{:S(2)}, u32[]{:S(2)}) collective-permute-start(bf16[192,512]{1,0:T(8,128)(2,1)S(1)} %get-tuple-element.56.refs_0_), channel_id=1, source_target_pairs={{0,24},{1,9},{8,16},{9,1},{16,8},{17,25},{24,0},{25,17},{2,26},{3,... | collective-permute-start | bytes 589832 | tf_op jit(solution)/shard_map/ppermute | solution.py:291
  63.7 2.3 %sum_over_y.3 = (bf16[192,896]{1,0:T(8,128)(2,1)}, f32[48,512]{1,0:T(8,128)S(1)}) custom-call(bf16[4,192,896]{2,1,0:T(8,128)(2,1)} %all-to-all-done.2.refs_0_, f32[2,48,512]{2,1,0:T(8,128)S(1)} %get-tuple-element.53.refs_1_), custom_call_target="tpu_custom_call" | custom-call | bytes 2015232 | tf_op jit(solution)/shard_map/sum_over_y/pallas_call | solution.py:269
  66.0 7.3 %collective-permute-start.5 = (bf16[192,896]{1,0:T(8,128)(2,1)}, bf16[192,896]{1,0:T(8,128)(2,1)}, u32[]{:S(2)}, u32[]{:S(2)}) collective-permute-start(bf16[192,896]{1,0:T(8,128)(2,1)} %get-tuple-element.64.refs_0_), channel_id=1, source_target_pairs={{0,8},{1,25},{8,0},{9,17},{16,24},{17,9},{24,16},{25,1},{2,10},{3,... | collective-permute-start | bytes 1032200 | tf_op jit(solution)/shard_map/ppermute | solution.py:291
  75.0 3.5 %all-to-all-start.1 = ((bf16[4,192,512]{2,1,0:T(8,128)(2,1)}), bf16[4,192,512]{2,1,0:T(8,128)(2,1)S(1)}, u32[]{:S(2)}, u32[]{:S(2)}) async-start(bf16[4,192,512]{2,1,0:T(8,128)(2,1)} %copy-done.18), calls=%async_computation.1 | async-start | bytes 1572864 | tf_op jit(solution)/shard_map/all_to_all | solution.py:295
  78.5 7.7 %collective-permute-done.5.refs_1_ = bf16[192,896]{1,0:T(8,128)(2,1)} collective-permute-done((bf16[192,896]{1,0:T(8,128)(2,1)}, bf16[192,896]{1,0:T(8,128)(2,1)}, u32[]{:S(2)}, u32[]{:S(2)}) %collective-permute-start.5) | collective-permute-done | bytes 344096 | tf_op jit(solution)/shard_map/ppermute | solution.py:291
  89.5 3.4 %collective-permute-start.6 = (bf16[192,896]{1,0:T(8,128)(2,1)}, bf16[192,896]{1,0:T(8,128)(2,1)}, u32[]{:S(2)}, u32[]{:S(2)}) collective-permute-start(bf16[192,896]{1,0:T(8,128)(2,1)} %get-tuple-element.66.refs_0_), channel_id=1, source_target_pairs={{0,24},{1,9},{8,16},{9,1},{16,8},{17,25},{24,0},{25,17},{2,26},{3,... | collective-permute-start | bytes 1032200 | tf_op jit(solution)/shard_map/ppermute | solution.py:291
  97.7 2.1 %first_gradient.1 = (bf16[272,512]{1,0:T(8,128)(2,1)S(1)}, bf16[256,512]{1,0:T(8,128)(2,1)S(1)}, f32[512,512]{1,0:T(8,128)S(1)}) custom-call(f32[1]{0:T(128)S(6)} %copy.13.refs_0_, s32[1,2]{1,0:T(1,128)S(1)} %copy-done.35, bf16[768,512]{1,0:T(8,128)(2,1)S(1)} %bitcast.4, bf16[2688,256]{1,0:T(8,128)(2,1)S(1)} %get-tuple-element.50.refs_7_.refs_3_, ...), custom_call_target="tpu_custom_call" | custom-call | bytes 8798208 | tf_op jit(solution)/shard_map/first_gradient/pallas_call | solution.py:269
  100.5 12.3 %collective-permute-done.6.refs_1_ = bf16[192,896]{1,0:T(8,128)(2,1)} collective-permute-done((bf16[192,896]{1,0:T(8,128)(2,1)}, bf16[192,896]{1,0:T(8,128)(2,1)}, u32[]{:S(2)}, u32[]{:S(2)}) %collective-permute-start.6) | collective-permute-done | bytes 344096 | tf_op jit(solution)/shard_map/ppermute | solution.py:291
  114.0 1.9 %collective-permute-start.7 = (bf16[192,384]{1,0:T(8,128)(2,1)S(1)}, bf16[192,384]{1,0:T(8,128)(2,1)S(1)}, u32[]{:S(2)}, u32[]{:S(2)}) collective-permute-start(bf16[192,384]{1,0:T(8,128)(2,1)S(1)} %get-tuple-element.70.refs_4_), channel_id=1, source_target_pairs={{0,1},{1,0},{2,3},{3,2},{4,5},{5,4},{6,7},{7,6},{8,9},{9,8},{10,11... | collective-permute-start | bytes 442376 | tf_op jit(solution)/shard_map/ppermute | solution.py:299
  119.8 8.7 %all-to-all-start.3 = ((bf16[4,192,512]{2,1,0:T(8,128)(2,1)}), bf16[4,192,512]{2,1,0:T(8,128)(2,1)S(1)}, u32[]{:S(2)}, u32[]{:S(2)}) async-start(bf16[4,192,512]{2,1,0:T(8,128)(2,1)} %copy-done.17), calls=%async_computation.3 | async-start | bytes 1572864 | tf_op jit(solution)/shard_map/all_to_all | solution.py:295
  128.5 4.5 %collective-permute-start.8 = (bf16[272,512]{1,0:T(8,128)(2,1)}, bf16[272,512]{1,0:T(8,128)(2,1)S(1)}, u32[]{:S(2)}, u32[]{:S(2)}) collective-permute-start(bf16[272,512]{1,0:T(8,128)(2,1)} %copy-done.37), channel_id=1, source_target_pairs={{0,32},{32,64},{64,96},{96,128},{128,160},{160,192},{192,224},{224... | collective-permute-start | bytes 835592 | tf_op jit(solution)/shard_map/ppermute | solution.py:304
  132.9 2.7 %collective-permute-start.9 = (bf16[256,512]{1,0:T(8,128)(2,1)}, bf16[256,512]{1,0:T(8,128)(2,1)S(1)}, u32[]{:S(2)}, u32[]{:S(2)}) collective-permute-start(bf16[256,512]{1,0:T(8,128)(2,1)} %copy-done.38), channel_id=1, source_target_pairs={{0,33},{1,32},{32,65},{33,64},{64,97},{65,96},{96,129},{97,128},{1... | collective-permute-start | bytes 786440 | tf_op jit(solution)/shard_map/ppermute | solution.py:310
  135.6 12.9 %collective-permute-done.9.refs_8_ = bf16[256,512]{1,0:T(8,128)(2,1)S(1)} collective-permute-done((bf16[256,512]{1,0:T(8,128)(2,1)}, bf16[256,512]{1,0:T(8,128)(2,1)S(1)}, u32[]{:S(2)}, u32[]{:S(2)}) %collective-permute-start.9) | collective-permute-done | bytes 262176 | tf_op jit(solution)/shard_map/ppermute | solution.py:310
  154.6 2.0 %collective-permute-start.11 = (f32[304,512]{1,0:T(8,128)S(1)}, f32[304,512]{1,0:T(8,128)S(1)}, u32[]{:S(2)}, u32[]{:S(2)}) collective-permute-start(f32[304,512]{1,0:T(8,128)S(1)} %get-tuple-element.80), channel_id=1, source_target_pairs={{0,1},{1,0},{2,3},{3,2},{4,5},{5,4},{6,7},{7,6},{8,9},{9,8},{10,11... | collective-permute-start | bytes 1867784 | tf_op jit(solution)/shard_map/ppermute | solution.py:299
  158.5 5.3 %collective-permute-start.10 = (bf16[256,512]{1,0:T(8,128)(2,1)S(1)}, bf16[256,512]{1,0:T(8,128)(2,1)S(1)}, u32[]{:S(2)}, u32[]{:S(2)}) collective-permute-start(bf16[256,512]{1,0:T(8,128)(2,1)S(1)} %get-tuple-element.78), channel_id=1, source_target_pairs={{0,65},{1,64},{32,97},{33,96},{64,129},{65,128},{96,161},{97,160},... | collective-permute-start | bytes 786440 | tf_op jit(solution)/shard_map/ppermute | solution.py:310
  165.4 20.1 %collective-permute-done.10.refs_1_ = bf16[256,512]{1,0:T(8,128)(2,1)S(1)} collective-permute-done((bf16[256,512]{1,0:T(8,128)(2,1)S(1)}, bf16[256,512]{1,0:T(8,128)(2,1)S(1)}, u32[]{:S(2)}, u32[]{:S(2)}) %collective-permute-start.10) | collective-permute-done | bytes 262176 | tf_op jit(solution)/shard_map/ppermute | solution.py:310
  (103 shorter events, 41.6 us)
Async XLA Ops:
  0.6 12.6 %copy-start = (f32[1,256,1024]{2,1,0:T(8,128)S(1)}, f32[1,256,1024]{2,1,0:T(8,128)}, u32[]{:S(2)}) copy-start(f32[1,256,1024]{2,1,0:T(8,128)} %refs_7_.1) | copy-start | bytes 3145732
  3.6 9.7 %copy-start.19 = (bf16[2,24,1024]{2,1,0:T(8,128)(2,1)S(1)}, bf16[2,24,1024]{2,1,0:T(8,128)(2,1)}, u32[]{:S(2)}) copy-start(bf16[2,24,1024]{2,1,0:T(8,128)(2,1)} %refs_6_) | copy-start | bytes 294916
  4.4 12.3 %collective-permute-start.1 = (bf16[768,512]{1,0:T(8,128)(2,1)S(1)}, bf16[768,512]{1,0:T(8,128)(2,1)S(1)}, u32[]{:S(2)}, u32[]{:S(2)}) collective-permute-start(bf16[768,512]{1,0:T(8,128)(2,1)S(1)} %get-tuple-element.48), channel_id=1, source_target_pairs={{0,1},{1,0},{2,3},{3,2},{4,5},{5,4},{6,7},{7,6},{8,9},{9,8},{10,11... | collective-permute-start | bytes 2359304 | tf_op jit(solution)/shard_map/ppermute | solution.py:299
  14.8 11.6 %collective-permute-start = (bf16[2688,256]{1,0:T(8,128)(2,1)S(1)}, bf16[2688,256]{1,0:T(8,128)(2,1)S(1)}, u32[]{:S(2)}, u32[]{:S(2)}) collective-permute-start(bf16[2688,256]{1,0:T(8,128)(2,1)S(1)} %get-tuple-element.50.refs_7_.refs_3_), channel_id=1, source_target_pairs={{0,1},{1,0},{2,3},{3,2},{4,5},{5,4},{6,7},{7,6},{8,9},{9,8},{10,11... | collective-permute-start | bytes 4128776 | tf_op jit(solution)/shard_map/ppermute | solution.py:299
  17.8 17.5 %all-to-all-start = ((bf16[4,192,512]{2,1,0:T(8,128)(2,1)}), bf16[4,192,512]{2,1,0:T(8,128)(2,1)}, u32[]{:S(2)}, u32[]{:S(2)}) async-start(bf16[4,192,512]{2,1,0:T(8,128)(2,1)} %bitcast.8), calls=%async_computation | async-start | bytes 1572864 | tf_op jit(solution)/shard_map/all_to_all | solution.py:295
  22.2 4.1 %collective-permute-start.2 = (f32[256,512]{1,0:T(8,128)}, f32[256,512]{1,0:T(8,128)S(1)}, u32[]{:S(2)}, u32[]{:S(2)}) collective-permute-start(f32[256,512]{1,0:T(8,128)} %copy-done.36), channel_id=1, source_target_pairs={{0,1},{1,0},{2,3},{3,2},{4,5},{5,4},{6,7},{7,6},{8,9},{9,8},{10,11... | collective-permute-start | bytes 1572872 | tf_op jit(solution)/shard_map/ppermute | solution.py:299
  35.3 28.4 %all-to-all-start.2 = ((bf16[4,192,896]{2,1,0:T(8,128)(2,1)}), bf16[4,192,896]{2,1,0:T(8,128)(2,1)}, u32[]{:S(2)}, u32[]{:S(2)}) async-start(bf16[4,192,896]{2,1,0:T(8,128)(2,1)} %bitcast.7), calls=%async_computation.2 | async-start | bytes 2752512 | tf_op jit(solution)/shard_map/all_to_all | solution.py:295
  41.1 14.3 %collective-permute-start.3 = (bf16[192,512]{1,0:T(8,128)(2,1)S(1)}, bf16[192,512]{1,0:T(8,128)(2,1)S(1)}, u32[]{:S(2)}, u32[]{:S(2)}) collective-permute-start(bf16[192,512]{1,0:T(8,128)(2,1)S(1)} %get-tuple-element.54.refs_0_), channel_id=1, source_target_pairs={{0,8},{1,25},{8,0},{9,17},{16,24},{17,9},{24,16},{25,1},{2,10},{3,... | collective-permute-start | bytes 589832 | tf_op jit(solution)/shard_map/ppermute | solution.py:291
  56.1 17.2 %collective-permute-start.4 = (bf16[192,512]{1,0:T(8,128)(2,1)S(1)}, bf16[192,512]{1,0:T(8,128)(2,1)S(1)}, u32[]{:S(2)}, u32[]{:S(2)}) collective-permute-start(bf16[192,512]{1,0:T(8,128)(2,1)S(1)} %get-tuple-element.56.refs_0_), channel_id=1, source_target_pairs={{0,24},{1,9},{8,16},{9,1},{16,8},{17,25},{24,0},{25,17},{2,26},{3,... | collective-permute-start | bytes 589832 | tf_op jit(solution)/shard_map/ppermute | solution.py:291
  66.0 20.1 %collective-permute-start.5 = (bf16[192,896]{1,0:T(8,128)(2,1)}, bf16[192,896]{1,0:T(8,128)(2,1)}, u32[]{:S(2)}, u32[]{:S(2)}) collective-permute-start(bf16[192,896]{1,0:T(8,128)(2,1)} %get-tuple-element.64.refs_0_), channel_id=1, source_target_pairs={{0,8},{1,25},{8,0},{9,17},{16,24},{17,9},{24,16},{25,1},{2,10},{3,... | collective-permute-start | bytes 1032200 | tf_op jit(solution)/shard_map/ppermute | solution.py:291
  75.0 18.0 %all-to-all-start.1 = ((bf16[4,192,512]{2,1,0:T(8,128)(2,1)}), bf16[4,192,512]{2,1,0:T(8,128)(2,1)S(1)}, u32[]{:S(2)}, u32[]{:S(2)}) async-start(bf16[4,192,512]{2,1,0:T(8,128)(2,1)} %copy-done.18), calls=%async_computation.1 | async-start | bytes 1572864 | tf_op jit(solution)/shard_map/all_to_all | solution.py:295
  89.5 23.3 %collective-permute-start.6 = (bf16[192,896]{1,0:T(8,128)(2,1)}, bf16[192,896]{1,0:T(8,128)(2,1)}, u32[]{:S(2)}, u32[]{:S(2)}) collective-permute-start(bf16[192,896]{1,0:T(8,128)(2,1)} %get-tuple-element.66.refs_0_), channel_id=1, source_target_pairs={{0,24},{1,9},{8,16},{9,1},{16,8},{17,25},{24,0},{25,17},{2,26},{3,... | collective-permute-start | bytes 1032200 | tf_op jit(solution)/shard_map/ppermute | solution.py:291
  97.7 15.2 %copy-start.32 = (f32[48,512]{1,0:T(8,128)S(1)}, f32[48,512]{1,0:T(8,128)}, u32[]{:S(2)}) copy-start(f32[48,512]{1,0:T(8,128)} %copy-done.31) | copy-start | bytes 294916
  100.5 17.7 %copy-start.11 = (f32[512,512]{1,0:T(8,128)}, f32[512,512]{1,0:T(8,128)S(1)}, u32[]{:S(2)}) copy-start(f32[512,512]{1,0:T(8,128)S(1)} %get-tuple-element.61.refs_5_) | copy-start | bytes 3145732
  100.5 17.8 %copy-start.38 = (bf16[256,512]{1,0:T(8,128)(2,1)}, bf16[256,512]{1,0:T(8,128)(2,1)S(1)}, u32[]{:S(2)}) copy-start(bf16[256,512]{1,0:T(8,128)(2,1)S(1)} %get-tuple-element.67) | copy-start | bytes 786436
  114.0 3.3 %collective-permute-start.7 = (bf16[192,384]{1,0:T(8,128)(2,1)S(1)}, bf16[192,384]{1,0:T(8,128)(2,1)S(1)}, u32[]{:S(2)}, u32[]{:S(2)}) collective-permute-start(bf16[192,384]{1,0:T(8,128)(2,1)S(1)} %get-tuple-element.70.refs_4_), channel_id=1, source_target_pairs={{0,1},{1,0},{2,3},{3,2},{4,5},{5,4},{6,7},{7,6},{8,9},{9,8},{10,11... | collective-permute-start | bytes 442376 | tf_op jit(solution)/shard_map/ppermute | solution.py:299
  119.8 30.1 %all-to-all-start.3 = ((bf16[4,192,512]{2,1,0:T(8,128)(2,1)}), bf16[4,192,512]{2,1,0:T(8,128)(2,1)S(1)}, u32[]{:S(2)}, u32[]{:S(2)}) async-start(bf16[4,192,512]{2,1,0:T(8,128)(2,1)} %copy-done.17), calls=%async_computation.3 | async-start | bytes 1572864 | tf_op jit(solution)/shard_map/all_to_all | solution.py:295
  128.5 20.7 %collective-permute-start.8 = (bf16[272,512]{1,0:T(8,128)(2,1)}, bf16[272,512]{1,0:T(8,128)(2,1)S(1)}, u32[]{:S(2)}, u32[]{:S(2)}) collective-permute-start(bf16[272,512]{1,0:T(8,128)(2,1)} %copy-done.37), channel_id=1, source_target_pairs={{0,32},{32,64},{64,96},{96,128},{128,160},{160,192},{192,224},{224... | collective-permute-start | bytes 835592 | tf_op jit(solution)/shard_map/ppermute | solution.py:304
  132.9 15.5 %collective-permute-start.9 = (bf16[256,512]{1,0:T(8,128)(2,1)}, bf16[256,512]{1,0:T(8,128)(2,1)S(1)}, u32[]{:S(2)}, u32[]{:S(2)}) collective-permute-start(bf16[256,512]{1,0:T(8,128)(2,1)} %copy-done.38), channel_id=1, source_target_pairs={{0,33},{1,32},{32,65},{33,64},{64,97},{65,96},{96,129},{97,128},{1... | collective-permute-start | bytes 786440 | tf_op jit(solution)/shard_map/ppermute | solution.py:310
  152.9 10.9 %copy-start.26 = (bf16[272,512]{1,0:T(8,128)(2,1)S(1)}, bf16[272,512]{1,0:T(8,128)(2,1)}, u32[]{:S(2)}) copy-start(bf16[272,512]{1,0:T(8,128)(2,1)} %copy-done.25) | copy-start | bytes 835588
  152.9 11.0 %copy-start.28 = (bf16[256,512]{1,0:T(8,128)(2,1)S(1)}, bf16[256,512]{1,0:T(8,128)(2,1)}, u32[]{:S(2)}) copy-start(bf16[256,512]{1,0:T(8,128)(2,1)} %copy-done.27) | copy-start | bytes 786436
  154.6 9.3 %collective-permute-start.11 = (f32[304,512]{1,0:T(8,128)S(1)}, f32[304,512]{1,0:T(8,128)S(1)}, u32[]{:S(2)}, u32[]{:S(2)}) collective-permute-start(f32[304,512]{1,0:T(8,128)S(1)} %get-tuple-element.80), channel_id=1, source_target_pairs={{0,1},{1,0},{2,3},{3,2},{4,5},{5,4},{6,7},{7,6},{8,9},{9,8},{10,11... | collective-permute-start | bytes 1867784 | tf_op jit(solution)/shard_map/ppermute | solution.py:299
  156.6 29.0 %collective-permute-start.12 = (bf16[272,512]{1,0:T(8,128)(2,1)S(1)}, bf16[272,512]{1,0:T(8,128)(2,1)S(1)}, u32[]{:S(2)}, u32[]{:S(2)}) collective-permute-start(bf16[272,512]{1,0:T(8,128)(2,1)S(1)} %get-tuple-element.86), channel_id=1, source_target_pairs={{0,64},{32,96},{64,128},{96,160},{128,192},{160,224},{192,256},{22... | collective-permute-start | bytes 835592 | tf_op jit(solution)/shard_map/ppermute | solution.py:304
  158.5 27.1 %collective-permute-start.10 = (bf16[256,512]{1,0:T(8,128)(2,1)S(1)}, bf16[256,512]{1,0:T(8,128)(2,1)S(1)}, u32[]{:S(2)}, u32[]{:S(2)}) collective-permute-start(bf16[256,512]{1,0:T(8,128)(2,1)S(1)} %get-tuple-element.78), channel_id=1, source_target_pairs={{0,65},{1,64},{32,97},{33,96},{64,129},{65,128},{96,161},{97,160},... | collective-permute-start | bytes 786440 | tf_op jit(solution)/shard_map/ppermute | solution.py:310
  (32 other events, 64.0 us)

commit v6 on v5

v6 whole, which is shorter than its diff:
```python
import functools
import math

import jax
import jax.numpy as jnp
from jax import lax
from jax.experimental import pallas as pl
from jax.experimental.pallas import tpu as pltpu
from jax.sharding import Mesh
from jax.sharding import PartitionSpec as P

GROUP = ("x", "z_lo")
MP = ("z_hi", "y", "core")
SIZES = (4, 4, 4, 4, 2)
N_Z, N_Y = SIZES[2], SIZES[3]

momentum_decay = 0.9
step_size = 0.5

ROWS = 24
BLOCK = 2 * ROWS
SLAB = N_Z * BLOCK
TOKENS = N_Y * SLAB
WIDTH = 256
VALUES = 1024
COLS = VALUES // 2
HALF = TOKENS // 2
PADDED = 32
EXTRA = 16
ROW_SCALE = 1.0 / math.sqrt(WIDTH * N_Z * N_Y * 2)
GRAD_SCALE = 1.0 / math.sqrt(TOKENS)

X2_AT = TOKENS
W_AT = 2 * TOKENS
REC_AT = W_AT + 2 * WIDTH
T_AT = REC_AT + 2 * WIDTH
MESSAGE = T_AT + 4 * PADDED

B16, F32 = jnp.bfloat16, jnp.float32


def f32(value):
    return value.astype(jnp.float32)


def bf16(value):
    return value.astype(jnp.bfloat16)


def dot(a, b, dims=((1,), (0,))):
    return lax.dot_general(a, b, (dims, ((), ())), preferred_element_type=jnp.float32)


def cols_of(core):
    return pl.ds(pl.multiple_of(core * COLS, COLS), COLS)


def half_of(core):
    return pl.ds(pl.multiple_of(core * HALF, 16), HALF)


def own_block():
    return pl.ds(pl.multiple_of(lax.axis_index("z_hi") * BLOCK, 16), BLOCK)


def kept(mix, step):
    return mix[0, step].astype(jnp.float32) * 0.125


def by_y():
    return [((zh * N_Y + y) * BLOCK, (y * N_Z + zh) * BLOCK) for zh in range(N_Z) for y in range(N_Y)]


def first_values(push, x, w, far, own):
    core = lax.axis_index("core")
    for out, side in ((far, 1 - core), (own, core)):
        scaled = bf16(f32(w[:, cols_of(side)]) / push[0])
        part = bf16(dot(x[...], scaled) * ROW_SCALE)
        for at, to in by_y():
            out[to : to + BLOCK] = part[at : at + BLOCK]


def make_message(x, w, rec, targets, velocity, message, velocity_far):
    far = 1 - lax.axis_index("core")
    for step in range(2):
        for at, to in by_y():
            message[step * TOKENS + to : step * TOKENS + to + BLOCK] = x[step, at : at + BLOCK]
    for ref, row in ((w, W_AT), (rec, REC_AT)):
        half = ref[:, cols_of(far)]
        message[row : row + WIDTH] = half[:, :WIDTH]
        message[row + WIDTH : row + 2 * WIDTH] = half[:, WIDTH:]
    spare = jnp.zeros((PADDED - ROWS, COLS), jnp.float32)
    for step in range(2):
        half = bf16(jnp.concatenate([f32(targets[step, :, cols_of(far)]), spare], axis=0))
        row = T_AT + 2 * step * PADDED
        message[row : row + PADDED] = half[:, :WIDTH]
        message[row + PADDED : row + 2 * PADDED] = half[:, WIDTH:]
    velocity_far[...] = velocity[:, cols_of(far)]


def tile(mix, w, rec, velocity, got, velocity_got, k):
    keep = kept(mix, 0)
    if k == 0:
        side = cols_of(lax.axis_index("core"))
        start, arrived, old = w[:, side], rec[:, side], velocity[:, side]
    else:
        start, arrived = (
            jnp.concatenate([got[at : at + WIDTH], got[at + WIDTH : at + 2 * WIDTH]], axis=1)
            for at in (W_AT, REC_AT)
        )
        old = velocity_got[...]
    ahead = f32(start) - (step_size * momentum_decay) * old
    return ahead, keep * ahead + f32(arrived), old


def second_values(push, push_got, mix, w, rec, velocity, targets, velocity_got, mine, got, out, taught):
    core = lax.axis_index("core")
    weight = kept(mix, 0) * push[0] + push_got[0]
    near, far = mine[X2_AT : X2_AT + TOKENS], got[X2_AT : X2_AT + TOKENS]
    scaled = [bf16(tile(mix, w, rec, velocity, got, velocity_got, k)[1] / weight) for k in range(2)]
    out[:, :COLS] = bf16((dot(near, scaled[0]) + dot(far, scaled[1])) * ROW_SCALE)
    rows = half_of(core)
    across = ((1,), (1,))
    out[:, COLS:] = bf16(dot(near, mine[rows], across) + dot(far, got[rows], across))
    for step in range(2):
        own = f32(targets[step, :, cols_of(core)])
        row = T_AT + 2 * step * PADDED
        other = jnp.concatenate(
            [f32(got[row : row + PADDED]), f32(got[row + PADDED : row + 2 * PADDED])], axis=1
        )[:ROWS]
        taught[step, :ROWS] = jnp.where(core == 0, own, other)
        taught[step, ROWS:] = jnp.where(core == 0, other, own)


def sum_over_y(step, parts, taught, slab, own):
    total = f32(parts[0])
    for y in range(1, N_Y):
        total = total + f32(parts[y])
    slab[...] = bf16(total)
    rows = own_block()
    total = f32(parts[0, rows, :COLS])
    for y in range(1, N_Y):
        total = total + f32(parts[y, rows, :COLS])
    own[...] = total
    slab[rows, :COLS] = bf16(total - taught[step])


def add_slab(own, mine, got, out, own_out):
    out[...] = bf16(f32(mine[...]) + f32(got[...]))

    def later():
        own_out[...] = own[...] + f32(got[own_block(), :COLS])

    return later


def add_and_spread(own, mine, got, out, own_out):
    total = bf16(f32(mine[...]) + f32(got[...]))
    for y in range(N_Y):
        out[y] = total

    def later():
        own_out[...] = own[...] + f32(got[own_block()])

    return later


def add_and_part(own, mine, got, out, gram, own_out):
    out[...] = bf16(f32(mine[:, :COLS]) + f32(got[:, :COLS]))
    gram[...] = bf16(f32(mine[:, COLS:]) + f32(got[:, COLS:]))

    def later():
        own_out[...] = own[...] + f32(got[own_block(), :COLS])

    return later


def second_residual(push, push_got, mix, own, all1, gram, gram_got, base, out, own_out, turned):
    core = lax.axis_index("core")
    keep = kept(mix, 0)
    back = step_size * GRAD_SCALE * ROW_SCALE * keep / (keep * push[0] + push_got[0])
    near, far = all1[half_of(core)], all1[half_of(1 - core)]
    turned[...] = (dot(gram[...], near) + dot(gram_got[...], far)) * back
    residual = bf16(f32(base[...]) - turned[...])
    for y in range(N_Y):
        out[y] = residual

    def later():
        own_out[...] = own[...] - turned[own_block()]

    return later


def first_gradient(push, mix, w, rec, velocity, velocity_got, all1, mine, got, near, far, ready):
    keep = kept(mix, 0)
    down = ((0,), (0,))
    for k, x, out in ((0, mine, near), (1, got, far)):
        ahead, base, old = tile(mix, w, rec, velocity, got, velocity_got, k)
        gradient = dot(x[:TOKENS], all1[...], down) * GRAD_SCALE
        out[:WIDTH] = bf16((1.0 - keep) * (ahead - step_size * gradient))
        current = bf16(base - (step_size * keep) * gradient)
        moved = momentum_decay * old + gradient
        ready[k * WIDTH : (k + 1) * WIDTH] = f32(current) - (step_size * momentum_decay) * moved
    near[WIDTH:] = bf16(jnp.full((EXTRA, COLS), (1.0 - keep) * push[0], jnp.float32))


def second_gradient(push, push_got, mix, ready, own1, own2, mine, got, all2, far, near, half, message):
    core = lax.axis_index("core")
    keep = kept(mix, 1)
    down = ((0,), (0,))
    for k, x, out, held in ((1, got, far, message), (0, mine, near, half)):
        gradient = dot(x[X2_AT : X2_AT + TOKENS], all2[...], down) * GRAD_SCALE
        moved = ready[k * WIDTH : (k + 1) * WIDTH] - step_size * gradient
        out[:WIDTH] = bf16((1.0 - keep) * moved)
        held[:WIDTH] = keep * moved
    weight = kept(mix, 0) * push[0] + push_got[0]
    near[WIDTH:] = bf16(jnp.full((EXTRA, COLS), (1.0 - keep) * weight, jnp.float32))
    for step, own in ((0, own1), (1, own2)):
        row = WIDTH + step * ROWS
        message[row : row + ROWS] = jnp.where(core == 0, own[ROWS:], own[:ROWS])


def join_numerator(
    push, push_got, mix, own1, own2, arrived, arrived_far, half, message, out, rows_out, weight
):
    core = lax.axis_index("core")
    out[0, :, cols_of(core)] = bf16(half[...] + f32(arrived[:WIDTH]))
    out[0, :, cols_of(1 - core)] = bf16(message[:WIDTH] + f32(arrived_far[...]))
    for step, own in ((0, own1), (1, own2)):
        row = WIDTH + step * ROWS
        rows_out[step, :, cols_of(core)] = bf16(jnp.where(core == 0, own[:ROWS], own[ROWS:]))
        rows_out[step, :, cols_of(1 - core)] = bf16(message[row : row + ROWS])
    last = kept(mix, 0) * push[0] + push_got[0]
    weight[0] = kept(mix, 1) * last + jnp.max(f32(arrived[WIDTH:]))


def join_received(near, far, out, weight):
    core = lax.axis_index("core")
    out[0, :, cols_of(core)] = near[:WIDTH]
    out[0, :, cols_of(1 - core)] = far[...]
    weight[0] = jnp.max(f32(near[WIDTH:]))


SMEM = pl.BlockSpec(memory_space=pltpu.SMEM)
HBM = pl.BlockSpec(memory_space=pltpu.HBM)
VMEM = pl.BlockSpec(memory_space=pltpu.VMEM)


def call(body, scalars, fetched, late, near, outs, scratch=(), flops=0):
    copied = [f if isinstance(f, tuple) else (f, None) for f in list(fetched) + list(late)]
    n, m, first = len(copied), len(fetched), len(scalars)
    last = first + n + len(near)
    far = [k for k, (_, _, in_hbm) in enumerate(outs) if in_hbm]

    def view(ref, where):
        return ref if where is None else ref.at[where]

    def kernel(*refs):
        out = list(refs[last : last + len(outs)])
        rest = list(refs[last + len(outs) :])
        buffers, out_buffers, rest = rest[:n], rest[n : n + len(far)], rest[n + len(far) :]
        sems = rest.pop(0) if n else None
        out_sems = rest.pop(0) if far else None
        copies = [
            pltpu.make_async_copy(view(refs[first + i], copied[i][1]), buffers[i], sems.at[i])
            for i in range(n)
        ]
        for copy in copies:
            copy.start()
        for copy in copies[:m]:
            copy.wait()
        written = list(out)
        for k, buffer in zip(far, out_buffers):
            written[k] = buffer
        later = body(*refs[:first], *buffers, *refs[first + n : last], *written, *rest)
        for copy in copies[m:]:
            copy.wait()
        if late:
            later()
        copies = [
            pltpu.make_async_copy(buffer, out[k], out_sems.at[i])
            for i, (k, buffer) in enumerate(zip(far, out_buffers))
        ]
        for copy in copies:
            copy.start()
        for copy in copies:
            copy.wait()

    held = [
        pltpu.VMEM(value.shape if where is None else value.shape[1:], value.dtype)
        for value, where in copied
    ]
    held += [pltpu.VMEM(*outs[k][:2]) for k in far]
    held += [pltpu.SemaphoreType.DMA((n,))] if n else []
    held += [pltpu.SemaphoreType.DMA((len(far),))] if far else []
    result, specs = [], []
    for shape, kind, in_hbm in outs:
        result.append(pltpu.HBM(shape, kind) if in_hbm else jax.ShapeDtypeStruct(shape, kind))
        specs.append(HBM if in_hbm else SMEM if shape == (1,) else VMEM)
    arrays = [pltpu.with_memory_space_constraint(value, pltpu.HBM) for value, _ in copied]
    moved = sum(a.size * a.dtype.itemsize for a in arrays + list(near))
    moved += sum(math.prod(shape) * jnp.dtype(kind).itemsize for shape, kind, _ in outs)
    return pl.pallas_call(
        kernel,
        out_shape=result,
        in_specs=[SMEM] * first + [HBM] * n + [VMEM] * len(near),
        out_specs=specs,
        scratch_shapes=held + [pltpu.VMEM(size, kind) for size, kind in scratch],
        compiler_params=pltpu.CompilerParams(vmem_limit_bytes=20 * 2**20),
        cost_estimate=pl.CostEstimate(flops=flops, bytes_accessed=moved, transcendentals=0),
        name=body.func.__name__ if isinstance(body, functools.partial) else body.__name__,
    )(*scalars, *arrays, *near)


def z_pairs(step):
    pairs = []
    for zh in range(N_Z):
        for core in range(2):
            turn = (1, 3)[step ^ core]
            pairs.append((zh * 2 + core, (zh ^ turn) * 2 + core))
    return pairs


def over_z(value, step):
    return lax.ppermute(value, ("z_hi", "core"), z_pairs(step))


def over_y(value):
    return lax.all_to_all(value, "y", 0, 0, tiled=True)


def swap_core(value):
    return lax.ppermute(value, "core", [(0, 1), (1, 0)])


def to_group(value, hop):
    count = SIZES[0] * SIZES[1]
    return lax.ppermute(value, GROUP, [(i, (i + hop) % count) for i in range(count)])


def to_group_other(value, hop):
    count = SIZES[0] * SIZES[1]
    pairs = [(i * 2 + c, (i + hop) % count * 2 + 1 - c) for i in range(count) for c in range(2)]
    return lax.ppermute(value, GROUP + ("core",), pairs)


OWN = ((BLOCK, COLS), F32, True)


def sum_slab(step, parts, taught):
    whole = ((SLAB, parts.shape[2]), B16, False)
    slab, own = call(functools.partial(sum_over_y, step), [], [parts], [], [taught], [whole, OWN])
    return call(add_slab, [], [], [own], [slab, over_z(slab, 0)], [whole, OWN])


def local(inputs, targets, numerator, momentum, received, push_weight, received_weight, mix_share):
    push, push_got, mix = push_weight, received_weight, mix_share
    state = [(numerator, 0), (received, 0), (momentum, 0)]

    part = [((TOKENS, COLS), B16, False)] * 2
    part_far, part_own = call(first_values, [push], [(inputs, 0), (numerator, 0)], [], [], part)
    part1 = bf16(f32(part_own) + f32(swap_core(part_far)))

    targets, part_far = lax.optimization_barrier((targets, part_far))
    mine, velocity_far = call(
        make_message,
        [],
        [inputs] + state[:2] + [targets, state[2]],
        [],
        [],
        [((MESSAGE, WIDTH), B16, False), ((WIDTH, COLS), F32, True)],
    )
    got = swap_core(mine)
    velocity_got = swap_core(velocity_far)

    part2, taught = call(
        second_values,
        [push, push_got, mix],
        state + [targets, velocity_got],
        [],
        [mine, got],
        [((TOKENS, COLS + HALF), B16, True), ((2, BLOCK, COLS), F32, False)],
    )

    spread = ((N_Y, SLAB, COLS), B16, True)
    parts2 = over_y(part2.reshape(N_Y, SLAB, COLS + HALF))
    slab1, own1 = sum_slab(0, over_y(part1.reshape(N_Y, SLAB, COLS)), taught)
    parts2, _ = lax.optimization_barrier((parts2, slab1))
    sent, own1 = call(add_and_spread, [], [], [own1], [slab1, over_z(slab1, 1)], [spread, OWN])
    all1 = over_y(sent).reshape(TOKENS, COLS)

    slab2, own2 = sum_slab(1, parts2, taught)
    near, far, ready = call(
        first_gradient,
        [push, mix],
        state + [velocity_got],
        [],
        [all1, mine, got],
        [
            ((WIDTH + EXTRA, COLS), B16, True),
            ((WIDTH, COLS), B16, True),
            ((2 * WIDTH, COLS), F32, True),
        ],
    )
    slab2_got, _ = lax.optimization_barrier((over_z(slab2, 1), far))
    arrived, arrived_far = to_group(near, 1), to_group_other(far, 1)
    ahead2, gram, own2 = call(
        add_and_part,
        [],
        [],
        [own2],
        [slab2, slab2_got],
        [((SLAB, COLS), B16, False), ((SLAB, HALF), B16, False), OWN],
    )
    gram_got = swap_core(gram)
    sent, own2 = call(
        second_residual,
        [push, push_got, mix],
        [],
        [own2],
        [all1, gram, gram_got, ahead2],
        [spread, OWN],
        [((SLAB, COLS), F32)],
    )
    all2 = over_y(sent).reshape(TOKENS, COLS)
    all2, arrived, arrived_far = lax.optimization_barrier((all2, arrived, arrived_far))

    far, near, half, message = call(
        second_gradient,
        [push, push_got, mix],
        [ready, own1, own2],
        [],
        [mine, got, all2],
        [
            ((WIDTH, COLS), B16, False),
            ((WIDTH + EXTRA, COLS), B16, False),
            ((WIDTH, COLS), F32, False),
            ((WIDTH + 2 * ROWS, COLS), F32, False),
        ],
    )

    sent_far, sent_own = to_group_other(far, 2), to_group(near, 2)
    whole = ((1, WIDTH, VALUES), B16, False)
    number = ((1,), F32, False)
    final_numerator, value_rows, final_weight = call(
        join_numerator,
        [push, push_got, mix],
        [own1, own2, arrived, arrived_far],
        [],
        [half, swap_core(message)],
        [whole, ((2, ROWS, VALUES), B16, False), number],
    )
    sent_far, final_numerator = lax.optimization_barrier((sent_far, final_numerator))
    final_received, got_weight = call(
        join_received, [], [], [], [sent_own, sent_far], [whole, number]
    )
    return final_numerator, final_weight, final_received, got_weight, value_rows


def solution(mesh):
    fine = Mesh(mesh.devices.reshape(SIZES), GROUP + MP)
    placed = (
        P(None, GROUP, MP),
        P(None, GROUP + MP, None),
        P(GROUP, MP, None),
        P(GROUP, MP, None),
        P(GROUP, MP, None),
        P(GROUP),
        P(GROUP),
        P(GROUP, None),
    )
    return jax.shard_map(
        local,
        mesh=fine,
        in_specs=placed,
        out_specs=(
            P(GROUP, MP, None),
            P(GROUP),
            P(GROUP, MP, None),
            P(GROUP),
            P(None, GROUP + MP, None),
        ),
        check_vma=False,
    )
```

time: 188 us -> 184 us (0.979)
  local copies, waits for them, and re-layouts: 25.3 us -> 1.5 us
  Pallas kernels: 17.2 us -> 36.1 us
  waiting for transfers between devices: 62.4 us -> 67.6 us
  starting transfers between devices: 77.9 us -> 74.1 us
    unnamed x78 -> x8, local copies, waits for them, and re-layouts: 25.3 us -> 1.5 us
    pallas_call x14, Pallas kernels: 17.2 us -> 36.1 us  [call(): pl.pallas_call(kernel, out_shape=result, in_specs=[SMEM] * first + [HBM]...]
    all_to_all x4, starting transfers between devices: 21 us -> 17.1 us  [over_y(): return lax.all_to_all(value, 'y', 0, 0, tiled=True)]
    all_to_all x4, waiting for transfers between devices: 0.01 us -> 2.69 us  [over_y(): return lax.all_to_all(value, 'y', 0, 0, tiled=True)]
    ppermute x4, starting transfers between devices: 25.5 us -> 28.1 us  [over_z(): return lax.ppermute(value, ('z_hi', 'core'), z_pairs(step))]
    ppermute x2, starting transfers between devices: 8 us -> 5.83 us  [to_group_other(): return lax.ppermute(value, GROUP + ('core',), pairs)]
  transfers between devices with their start and end apart: 17 -> 17, of which waited for: 7 -> 9; matrix products, arithmetic and copies ran while one was open for 1% -> 1% of each run, Pallas kernels for 6% -> 14%
where the time goes in v6:
time: 184 us; the launch traced here: 183 us
  starting transfers between devices  74.1 us (40%)
  waiting for transfers between devices  67.6 us (37%)
  Pallas kernels  36.1 us (20%)
  between operations  2.2 us (1%)
    pallas_call x14, Pallas kernels, call(): pl.pallas_call(kernel, out_shape=result, in_specs=[SMEM] * first + [HBM]...  36.1 us
    ppermute x2, waiting for transfers between devices, to_group_other(): return lax.ppermute(value, GROUP + ('core',), pairs)  34.5 us
    ppermute x4, waiting for transfers between devices, over_z(): return lax.ppermute(value, ('z_hi', 'core'), z_pairs(step))  28.2 us
    ppermute x4, starting transfers between devices, over_z(): return lax.ppermute(value, ('z_hi', 'core'), z_pairs(step))  28.1 us
    ppermute x5, starting transfers between devices, swap_core(): return lax.ppermute(value, 'core', [(0, 1), (1, 0)])  17.1 us
    all_to_all x4, starting transfers between devices, over_y(): return lax.all_to_all(value, 'y', 0, 0, tiled=True)  17.1 us
    ppermute x2, starting transfers between devices, to_group(): lax.ppermute(value, GROUP, [(i, (i + hop) % count) for i in range(count)])  5.93 us
    ppermute x2, starting transfers between devices, to_group_other(): return lax.ppermute(value, GROUP + ('core',), pairs)  5.83 us
  transfers between devices with their start and end apart: 17, of which 9 were waited for; matrix products, arithmetic and copies ran while one was open for 1% of the time, Pallas kernels for 14%

profile of v6, /device:TPU:1, one launch (start us, length us, event | category | flops | bytes accessed | tf_op | source)
XLA Modules:
  0.0 182.6 jit_solution(4410906436395160135)
XLA Ops:
  3.1 8.8 %collective-permute-start.1 = (bf16[768,512]{1,0:T(8,128)(2,1)S(1)}, bf16[768,512]{1,0:T(8,128)(2,1)S(1)}, u32[]{:S(2)}, u32[]{:S(2)}) collective-permute-start(bf16[768,512]{1,0:T(8,128)(2,1)S(1)} %get-tuple-element.46), channel_id=1, source_target_pairs={{0,1},{1,0},{2,3},{3,2},{4,5},{5,4},{6,7},{7,6},{8,9},{9,8},{10,11... | collective-permute-start | bytes 2359304 | tf_op jit(solution)/shard_map/ppermute | solution.py:333
  11.9 2.7 %make_message.1 = (bf16[2688,256]{1,0:T(8,128)(2,1)S(1)}, f32[256,512]{1,0:T(8,128)}) custom-call(bf16[2,768,256]{2,1,0:T(8,128)(2,1)} %refs_0_.7, bf16[1,256,1024]{2,1,0:T(8,128)(2,1)} %refs_2_.10, bf16[1,256,1024]{2,1,0:T(8,128)(2,1)} %refs_3_.4, bf16[2,24,1024]{2,1,0:T(8,128)(2,1)} %refs_6_, f32[1,256,1024]{2,1,0:T(8,128)} %refs_4_.5), custom_call_target="tpu_custom_call" | custom-call | bytes 4882432 | tf_op jit(solution)/shard_map/make_message/pallas_call | solution.py:303
  17.6 4.3 %all-to-all-start = ((bf16[4,192,512]{2,1,0:T(8,128)(2,1)}), bf16[4,192,512]{2,1,0:T(8,128)(2,1)}, u32[]{:S(2)}, u32[]{:S(2)}) async-start(bf16[4,192,512]{2,1,0:T(8,128)(2,1)} %bitcast), calls=%async_computation | async-start | bytes 1572864 | tf_op jit(solution)/shard_map/all_to_all | solution.py:329
  26.7 4.5 %second_values.1 = (bf16[768,896]{1,0:T(8,128)(2,1)}, f32[2,48,512]{2,1,0:T(8,128)S(1)}) custom-call(f32[1]{0:T(128)S(6)} %copy.13.refs_0_, f32[1]{0:T(128)S(6)} %copy.14.refs_1_, s32[1,2]{1,0:T(1,128)S(1)} %copy-done, bf16[1,256,1024]{2,1,0:T(8,128)(2,1)} %refs_2_.10, bf16[1,256,1024]{2,1,0:T(8,128)(2,1)} %refs_3_.4, f32[1,256,1024]{2,1,0:T(8,128)} %refs_4_.5, ...), custom_call_target="tpu_custom_call" | custom-call | bytes 7045120 | tf_op jit(solution)/shard_map/second_values/pallas_call | solution.py:303
  31.2 2.7 %all-to-all-done.refs_0_ = bf16[4,192,512]{2,1,0:T(8,128)(2,1)} async-done(((bf16[4,192,512]{2,1,0:T(8,128)(2,1)}), bf16[4,192,512]{2,1,0:T(8,128)(2,1)}, u32[]{:S(2)}, u32[]{:S(2)}) %all-to-all-start) | async-done | bytes 786464 | tf_op jit(solution)/shard_map/all_to_all | solution.py:329
  33.9 4.3 %all-to-all-start.2 = ((bf16[4,192,896]{2,1,0:T(8,128)(2,1)}), bf16[4,192,896]{2,1,0:T(8,128)(2,1)}, u32[]{:S(2)}, u32[]{:S(2)}) async-start(bf16[4,192,896]{2,1,0:T(8,128)(2,1)} %bitcast.7), calls=%async_computation.2 | async-start | bytes 2752512 | tf_op jit(solution)/shard_map/all_to_all | solution.py:329
  40.2 6.8 %collective-permute-start.3 = (bf16[192,512]{1,0:T(8,128)(2,1)S(1)}, bf16[192,512]{1,0:T(8,128)(2,1)S(1)}, u32[]{:S(2)}, u32[]{:S(2)}) collective-permute-start(bf16[192,512]{1,0:T(8,128)(2,1)S(1)} %get-tuple-element.53.refs_1_), channel_id=1, source_target_pairs={{0,8},{1,25},{8,0},{9,17},{16,24},{17,9},{24,16},{25,1},{2,10},{3,... | collective-permute-start | bytes 589832 | tf_op jit(solution)/shard_map/ppermute | solution.py:325
  47.0 6.7 %collective-permute-done.3.refs_2_ = bf16[192,512]{1,0:T(8,128)(2,1)S(1)} collective-permute-done((bf16[192,512]{1,0:T(8,128)(2,1)S(1)}, bf16[192,512]{1,0:T(8,128)(2,1)S(1)}, u32[]{:S(2)}, u32[]{:S(2)}) %collective-permute-start.3) | collective-permute-done | bytes 196640 | tf_op jit(solution)/shard_map/ppermute | solution.py:325
  55.2 7.9 %collective-permute-start.4 = (bf16[192,512]{1,0:T(8,128)(2,1)S(1)}, bf16[192,512]{1,0:T(8,128)(2,1)S(1)}, u32[]{:S(2)}, u32[]{:S(2)}) collective-permute-start(bf16[192,512]{1,0:T(8,128)(2,1)S(1)} %get-tuple-element.55.refs_1_), channel_id=1, source_target_pairs={{0,24},{1,9},{8,16},{9,1},{16,8},{17,25},{24,0},{25,17},{2,26},{3,... | collective-permute-start | bytes 589832 | tf_op jit(solution)/shard_map/ppermute | solution.py:325
  63.1 2.8 %sum_over_y.3 = (bf16[192,896]{1,0:T(8,128)(2,1)}, f32[48,512]{1,0:T(8,128)}) custom-call(bf16[4,192,896]{2,1,0:T(8,128)(2,1)} %all-to-all-done.2.refs_0_, f32[2,48,512]{2,1,0:T(8,128)S(1)} %get-tuple-element.51.refs_1_), custom_call_target="tpu_custom_call" | custom-call | bytes 2015232 | tf_op jit(solution)/shard_map/sum_over_y/pallas_call | solution.py:303
  66.0 3.0 %collective-permute-start.5 = (bf16[192,896]{1,0:T(8,128)(2,1)}, bf16[192,896]{1,0:T(8,128)(2,1)}, u32[]{:S(2)}, u32[]{:S(2)}) collective-permute-start(bf16[192,896]{1,0:T(8,128)(2,1)} %get-tuple-element.62.refs_1_), channel_id=1, source_target_pairs={{0,8},{1,25},{8,0},{9,17},{16,24},{17,9},{24,16},{25,1},{2,10},{3,... | collective-permute-start | bytes 1032200 | tf_op jit(solution)/shard_map/ppermute | solution.py:325
  68.9 3.8 %collective-permute-done.4.refs_2_ = bf16[192,512]{1,0:T(8,128)(2,1)S(1)} collective-permute-done((bf16[192,512]{1,0:T(8,128)(2,1)S(1)}, bf16[192,512]{1,0:T(8,128)(2,1)S(1)}, u32[]{:S(2)}, u32[]{:S(2)}) %collective-permute-start.4) | collective-permute-done | bytes 196640 | tf_op jit(solution)/shard_map/ppermute | solution.py:325
  74.6 4.2 %all-to-all-start.1 = ((bf16[4,192,512]{2,1,0:T(8,128)(2,1)}), bf16[4,192,512]{2,1,0:T(8,128)(2,1)S(1)}, u32[]{:S(2)}, u32[]{:S(2)}) async-start(bf16[4,192,512]{2,1,0:T(8,128)(2,1)} %get-tuple-element.56), calls=%async_computation.1 | async-start | bytes 1572864 | tf_op jit(solution)/shard_map/all_to_all | solution.py:329
  78.8 8.6 %collective-permute-done.5.refs_2_ = bf16[192,896]{1,0:T(8,128)(2,1)} collective-permute-done((bf16[192,896]{1,0:T(8,128)(2,1)}, bf16[192,896]{1,0:T(8,128)(2,1)}, u32[]{:S(2)}, u32[]{:S(2)}) %collective-permute-start.5) | collective-permute-done | bytes 344096 | tf_op jit(solution)/shard_map/ppermute | solution.py:325
  87.5 3.4 %add_slab.3 = (bf16[192,896]{1,0:T(8,128)(2,1)}, f32[48,512]{1,0:T(8,128)}) custom-call(f32[48,512]{1,0:T(8,128)} %get-tuple-element.61.refs_0_, bf16[192,896]{1,0:T(8,128)(2,1)} %get-tuple-element.62.refs_1_, bf16[192,896]{1,0:T(8,128)(2,1)} %collective-permute-done.5.refs_2_), custom_call_target="tpu_custom_call" | custom-call | bytes 1228800 | tf_op jit(solution)/shard_map/add_slab/pallas_call | solution.py:303
  90.8 10.4 %collective-permute-start.6 = (bf16[192,896]{1,0:T(8,128)(2,1)}, bf16[192,896]{1,0:T(8,128)(2,1)}, u32[]{:S(2)}, u32[]{:S(2)}) collective-permute-start(bf16[192,896]{1,0:T(8,128)(2,1)} %get-tuple-element.64.refs_1_), channel_id=1, source_target_pairs={{0,24},{1,9},{8,16},{9,1},{16,8},{17,25},{24,0},{25,17},{2,26},{3,... | collective-permute-start | bytes 1032200 | tf_op jit(solution)/shard_map/ppermute | solution.py:325
  101.3 4.4 %first_gradient.1 = (bf16[272,512]{1,0:T(8,128)(2,1)}, bf16[256,512]{1,0:T(8,128)(2,1)}, f32[512,512]{1,0:T(8,128)}) custom-call(f32[1]{0:T(128)S(6)} %copy.13.refs_0_, s32[1,2]{1,0:T(1,128)S(1)} %copy-done, bf16[1,256,1024]{2,1,0:T(8,128)(2,1)} %refs_2_.10, bf16[1,256,1024]{2,1,0:T(8,128)(2,1)} %refs_3_.4, f32[1,256,1024]{2,1,0:T(8,128)} %refs_4_.5, ...), custom_call_target="tpu_custom_call" | custom-call | bytes 7749632 | tf_op jit(solution)/shard_map/first_gradient/pallas_call | solution.py:303
  105.7 9.1 %collective-permute-done.6.refs_2_ = bf16[192,896]{1,0:T(8,128)(2,1)} collective-permute-done((bf16[192,896]{1,0:T(8,128)(2,1)}, bf16[192,896]{1,0:T(8,128)(2,1)}, u32[]{:S(2)}, u32[]{:S(2)}) %collective-permute-start.6) | collective-permute-done | bytes 344096 | tf_op jit(solution)/shard_map/ppermute | solution.py:325
  123.1 4.2 %all-to-all-start.3 = ((bf16[4,192,512]{2,1,0:T(8,128)(2,1)}), bf16[4,192,512]{2,1,0:T(8,128)(2,1)S(1)}, u32[]{:S(2)}, u32[]{:S(2)}) async-start(bf16[4,192,512]{2,1,0:T(8,128)(2,1)} %get-tuple-element.71), calls=%async_computation.3 | async-start | bytes 1572864 | tf_op jit(solution)/shard_map/all_to_all | solution.py:329
  127.4 4.0 %collective-permute-start.8 = (bf16[272,512]{1,0:T(8,128)(2,1)}, bf16[272,512]{1,0:T(8,128)(2,1)}, u32[]{:S(2)}, u32[]{:S(2)}) collective-permute-start(bf16[272,512]{1,0:T(8,128)(2,1)} %get-tuple-element.72), channel_id=1, source_target_pairs={{0,32},{32,64},{64,96},{96,128},{128,160},{160,192},{192,224},{224... | collective-permute-start | bytes 835592 | tf_op jit(solution)/shard_map/ppermute | solution.py:338
  133.6 15.3 %collective-permute-done.9.refs_6_ = bf16[256,512]{1,0:T(8,128)(2,1)S(1)} collective-permute-done((bf16[256,512]{1,0:T(8,128)(2,1)}, bf16[256,512]{1,0:T(8,128)(2,1)S(1)}, u32[]{:S(2)}, u32[]{:S(2)}) %collective-permute-start.9) | collective-permute-done | bytes 262176 | tf_op jit(solution)/shard_map/ppermute | solution.py:344
  156.1 3.7 %collective-permute-start.10 = (bf16[256,512]{1,0:T(8,128)(2,1)S(1)}, bf16[256,512]{1,0:T(8,128)(2,1)S(1)}, u32[]{:S(2)}, u32[]{:S(2)}) collective-permute-start(bf16[256,512]{1,0:T(8,128)(2,1)S(1)} %get-tuple-element.74), channel_id=1, source_target_pairs={{0,65},{1,64},{32,97},{33,96},{64,129},{65,128},{96,161},{97,160},... | collective-permute-start | bytes 786440 | tf_op jit(solution)/shard_map/ppermute | solution.py:344
  159.8 2.7 %join_numerator.1 = (bf16[1,256,1024]{2,1,0:T(8,128)(2,1)}, bf16[2,24,1024]{2,1,0:T(8,128)(2,1)}, f32[1]{0:T(128)}) custom-call(f32[1]{0:T(128)S(6)} %copy.13.refs_0_, f32[1]{0:T(128)S(6)} %copy.14.refs_1_, s32[1,2]{1,0:T(1,128)S(1)} %copy-done, f32[48,512]{1,0:T(8,128)} %get-tuple-element.58.refs_4_.refs_3_, f32[48,512]{1,0:T(8,128)} %get-tuple-element.70.refs_5_.refs_4_, ...), custom_call_target="tpu_custom_call" | custom-call | bytes 2506756 | tf_op jit(solution)/shard_map/join_numerator/pallas_call | solution.py:303
  162.6 19.2 %collective-permute-done.10.refs_1_ = bf16[256,512]{1,0:T(8,128)(2,1)S(1)} collective-permute-done((bf16[256,512]{1,0:T(8,128)(2,1)S(1)}, bf16[256,512]{1,0:T(8,128)(2,1)S(1)}, u32[]{:S(2)}, u32[]{:S(2)}) %collective-permute-start.10) | collective-permute-done | bytes 262176 | tf_op jit(solution)/shard_map/ppermute | solution.py:344
  (33 shorter events, 32.8 us)
Async XLA Ops:
  3.1 13.4 %collective-permute-start.1 = (bf16[768,512]{1,0:T(8,128)(2,1)S(1)}, bf16[768,512]{1,0:T(8,128)(2,1)S(1)}, u32[]{:S(2)}, u32[]{:S(2)}) collective-permute-start(bf16[768,512]{1,0:T(8,128)(2,1)S(1)} %get-tuple-element.46), channel_id=1, source_target_pairs={{0,1},{1,0},{2,3},{3,2},{4,5},{5,4},{6,7},{7,6},{8,9},{9,8},{10,11... | collective-permute-start | bytes 2359304 | tf_op jit(solution)/shard_map/ppermute | solution.py:333
  14.6 11.3 %collective-permute-start.2 = (bf16[2688,256]{1,0:T(8,128)(2,1)S(1)}, bf16[2688,256]{1,0:T(8,128)(2,1)S(1)}, u32[]{:S(2)}, u32[]{:S(2)}) collective-permute-start(bf16[2688,256]{1,0:T(8,128)(2,1)S(1)} %get-tuple-element.50.refs_8_.refs_7_.refs_6_), channel_id=1, source_target_pairs={{0,1},{1,0},{2,3},{3,2},{4,5},{5,4},{6,7},{7,6},{8,9},{9,8},{10,11... | collective-permute-start | bytes 4128776 | tf_op jit(solution)/shard_map/ppermute | solution.py:333
  17.6 4.3 %copy-start.3 = (f32[256,512]{1,0:T(8,128)S(1)}, f32[256,512]{1,0:T(8,128)}, u32[]{:S(2)}) copy-start(f32[256,512]{1,0:T(8,128)} %get-tuple-element.48) | copy-start | bytes 1572868
  17.6 9.1 %copy-start = (s32[1,2]{1,0:T(1,128)S(1)}, s32[1,2]{1,0:T(1,128)}, u32[]{:S(2)}) copy-start(s32[1,2]{1,0:T(1,128)} %refs_2_.13) | copy-start | bytes 28
  17.6 16.3 %all-to-all-start = ((bf16[4,192,512]{2,1,0:T(8,128)(2,1)}), bf16[4,192,512]{2,1,0:T(8,128)(2,1)}, u32[]{:S(2)}, u32[]{:S(2)}) async-start(bf16[4,192,512]{2,1,0:T(8,128)(2,1)} %bitcast), calls=%async_computation | async-start | bytes 1572864 | tf_op jit(solution)/shard_map/all_to_all | solution.py:329
  22.0 3.9 %collective-permute-start = (f32[256,512]{1,0:T(8,128)S(1)}, f32[256,512]{1,0:T(8,128)S(1)}, u32[]{:S(2)}, u32[]{:S(2)}) collective-permute-start(f32[256,512]{1,0:T(8,128)S(1)} %copy-done.3), channel_id=1, source_target_pairs={{0,1},{1,0},{2,3},{3,2},{4,5},{5,4},{6,7},{7,6},{8,9},{9,8},{10,11... | collective-permute-start | bytes 1572872 | tf_op jit(solution)/shard_map/ppermute | solution.py:333
  25.9 0.8 copy-start.1
  33.9 29.2 %all-to-all-start.2 = ((bf16[4,192,896]{2,1,0:T(8,128)(2,1)}), bf16[4,192,896]{2,1,0:T(8,128)(2,1)}, u32[]{:S(2)}, u32[]{:S(2)}) async-start(bf16[4,192,896]{2,1,0:T(8,128)(2,1)} %bitcast.7), calls=%async_computation.2 | async-start | bytes 2752512 | tf_op jit(solution)/shard_map/all_to_all | solution.py:329
  40.2 13.5 %collective-permute-start.3 = (bf16[192,512]{1,0:T(8,128)(2,1)S(1)}, bf16[192,512]{1,0:T(8,128)(2,1)S(1)}, u32[]{:S(2)}, u32[]{:S(2)}) collective-permute-start(bf16[192,512]{1,0:T(8,128)(2,1)S(1)} %get-tuple-element.53.refs_1_), channel_id=1, source_target_pairs={{0,8},{1,25},{8,0},{9,17},{16,24},{17,9},{24,16},{25,1},{2,10},{3,... | collective-permute-start | bytes 589832 | tf_op jit(solution)/shard_map/ppermute | solution.py:325
  55.2 17.5 %collective-permute-start.4 = (bf16[192,512]{1,0:T(8,128)(2,1)S(1)}, bf16[192,512]{1,0:T(8,128)(2,1)S(1)}, u32[]{:S(2)}, u32[]{:S(2)}) collective-permute-start(bf16[192,512]{1,0:T(8,128)(2,1)S(1)} %get-tuple-element.55.refs_1_), channel_id=1, source_target_pairs={{0,24},{1,9},{8,16},{9,1},{16,8},{17,25},{24,0},{25,17},{2,26},{3,... | collective-permute-start | bytes 589832 | tf_op jit(solution)/shard_map/ppermute | solution.py:325
  66.0 21.5 %collective-permute-start.5 = (bf16[192,896]{1,0:T(8,128)(2,1)}, bf16[192,896]{1,0:T(8,128)(2,1)}, u32[]{:S(2)}, u32[]{:S(2)}) collective-permute-start(bf16[192,896]{1,0:T(8,128)(2,1)} %get-tuple-element.62.refs_1_), channel_id=1, source_target_pairs={{0,8},{1,25},{8,0},{9,17},{16,24},{17,9},{24,16},{25,1},{2,10},{3,... | collective-permute-start | bytes 1032200 | tf_op jit(solution)/shard_map/ppermute | solution.py:325
  74.6 26.6 %all-to-all-start.1 = ((bf16[4,192,512]{2,1,0:T(8,128)(2,1)}), bf16[4,192,512]{2,1,0:T(8,128)(2,1)S(1)}, u32[]{:S(2)}, u32[]{:S(2)}) async-start(bf16[4,192,512]{2,1,0:T(8,128)(2,1)} %get-tuple-element.56), calls=%async_computation.1 | async-start | bytes 1572864 | tf_op jit(solution)/shard_map/all_to_all | solution.py:329
  90.8 24.0 %collective-permute-start.6 = (bf16[192,896]{1,0:T(8,128)(2,1)}, bf16[192,896]{1,0:T(8,128)(2,1)}, u32[]{:S(2)}, u32[]{:S(2)}) collective-permute-start(bf16[192,896]{1,0:T(8,128)(2,1)} %get-tuple-element.64.refs_1_), channel_id=1, source_target_pairs={{0,24},{1,9},{8,16},{9,1},{16,8},{17,25},{24,0},{25,17},{2,26},{3,... | collective-permute-start | bytes 1032200 | tf_op jit(solution)/shard_map/ppermute | solution.py:325
  117.5 3.3 %collective-permute-start.7 = (bf16[192,384]{1,0:T(8,128)(2,1)S(1)}, bf16[192,384]{1,0:T(8,128)(2,1)S(1)}, u32[]{:S(2)}, u32[]{:S(2)}) collective-permute-start(bf16[192,384]{1,0:T(8,128)(2,1)S(1)} %get-tuple-element.68.refs_5_), channel_id=1, source_target_pairs={{0,1},{1,0},{2,3},{3,2},{4,5},{5,4},{6,7},{7,6},{8,9},{9,8},{10,11... | collective-permute-start | bytes 442376 | tf_op jit(solution)/shard_map/ppermute | solution.py:333
  123.1 26.5 %all-to-all-start.3 = ((bf16[4,192,512]{2,1,0:T(8,128)(2,1)}), bf16[4,192,512]{2,1,0:T(8,128)(2,1)S(1)}, u32[]{:S(2)}, u32[]{:S(2)}) async-start(bf16[4,192,512]{2,1,0:T(8,128)(2,1)} %get-tuple-element.71), calls=%async_computation.3 | async-start | bytes 1572864 | tf_op jit(solution)/shard_map/all_to_all | solution.py:329
  127.4 22.2 %collective-permute-start.8 = (bf16[272,512]{1,0:T(8,128)(2,1)}, bf16[272,512]{1,0:T(8,128)(2,1)}, u32[]{:S(2)}, u32[]{:S(2)}) collective-permute-start(bf16[272,512]{1,0:T(8,128)(2,1)} %get-tuple-element.72), channel_id=1, source_target_pairs={{0,32},{32,64},{64,96},{96,128},{128,160},{160,192},{192,224},{224... | collective-permute-start | bytes 835592 | tf_op jit(solution)/shard_map/ppermute | solution.py:338
  131.4 17.5 %collective-permute-start.9 = (bf16[256,512]{1,0:T(8,128)(2,1)}, bf16[256,512]{1,0:T(8,128)(2,1)S(1)}, u32[]{:S(2)}, u32[]{:S(2)}) collective-permute-start(bf16[256,512]{1,0:T(8,128)(2,1)} %get-tuple-element.65), channel_id=1, source_target_pairs={{0,33},{1,32},{32,65},{33,64},{64,97},{65,96},{96,129},{97,128},{1... | collective-permute-start | bytes 786440 | tf_op jit(solution)/shard_map/ppermute | solution.py:344
  148.9 0.7 copy-start.2
  152.1 7.7 %collective-permute-start.11 = (f32[304,512]{1,0:T(8,128)S(1)}, f32[304,512]{1,0:T(8,128)S(1)}, u32[]{:S(2)}, u32[]{:S(2)}) collective-permute-start(f32[304,512]{1,0:T(8,128)S(1)} %get-tuple-element.78), channel_id=1, source_target_pairs={{0,1},{1,0},{2,3},{3,2},{4,5},{5,4},{6,7},{7,6},{8,9},{9,8},{10,11... | collective-permute-start | bytes 1867784 | tf_op jit(solution)/shard_map/ppermute | solution.py:333
  154.2 27.5 %collective-permute-start.12 = (bf16[272,512]{1,0:T(8,128)(2,1)S(1)}, bf16[272,512]{1,0:T(8,128)(2,1)S(1)}, u32[]{:S(2)}, u32[]{:S(2)}) collective-permute-start(bf16[272,512]{1,0:T(8,128)(2,1)S(1)} %get-tuple-element.82), channel_id=1, source_target_pairs={{0,64},{32,96},{64,128},{96,160},{128,192},{160,224},{192,256},{22... | collective-permute-start | bytes 835592 | tf_op jit(solution)/shard_map/ppermute | solution.py:338
  156.1 25.6 %collective-permute-start.10 = (bf16[256,512]{1,0:T(8,128)(2,1)S(1)}, bf16[256,512]{1,0:T(8,128)(2,1)S(1)}, u32[]{:S(2)}, u32[]{:S(2)}) collective-permute-start(bf16[256,512]{1,0:T(8,128)(2,1)S(1)} %get-tuple-element.74), channel_id=1, source_target_pairs={{0,65},{1,64},{32,97},{33,96},{64,129},{65,128},{96,161},{97,160},... | collective-permute-start | bytes 786440 | tf_op jit(solution)/shard_map/ppermute | solution.py:344

commit v7 on v6

--- a/solution.py
+++ b/solution.py
@@ -30,11 +30,13 @@
 ROW_SCALE = 1.0 / math.sqrt(WIDTH * N_Z * N_Y * 2)
 GRAD_SCALE = 1.0 / math.sqrt(TOKENS)
 
-X2_AT = TOKENS
+X1_AT = TOKENS
 W_AT = 2 * TOKENS
 REC_AT = W_AT + 2 * WIDTH
-T_AT = REC_AT + 2 * WIDTH
-MESSAGE = T_AT + 4 * PADDED
+M_AT = REC_AT + 2 * WIDTH
+T_AT = M_AT + 4 * WIDTH
+P_AT = T_AT + 4 * PADDED
+MESSAGE = P_AT + 2 * TOKENS
 
 B16, F32 = jnp.bfloat16, jnp.float32
 
@@ -71,55 +73,67 @@
     return [((zh * N_Y + y) * BLOCK, (y * N_Z + zh) * BLOCK) for zh in range(N_Z) for y in range(N_Y)]
 
 
-def first_values(push, x, w, far, own):
-    core = lax.axis_index("core")
-    for out, side in ((far, 1 - core), (own, core)):
+def prepare(push, x, w, rec, velocity, targets, own, message, tokens):
+    core = lax.axis_index("core")
+    for side in (1 - core, core):
         scaled = bf16(f32(w[:, cols_of(side)]) / push[0])
-        part = bf16(dot(x[...], scaled) * ROW_SCALE)
+        part = bf16(dot(x[0], scaled) * ROW_SCALE)
         for at, to in by_y():
-            out[to : to + BLOCK] = part[at : at + BLOCK]
-
-
-def make_message(x, w, rec, targets, velocity, message, velocity_far):
-    far = 1 - lax.axis_index("core")
+            block = part[at : at + BLOCK]
+            if side is core:
+                own[to : to + BLOCK] = block
+            else:
+                message[P_AT + to : P_AT + to + BLOCK] = block[:, :WIDTH]
+                message[P_AT + TOKENS + to : P_AT + TOKENS + to + BLOCK] = block[:, WIDTH:]
+    far = cols_of(1 - core)
     for step in range(2):
         for at, to in by_y():
-            message[step * TOKENS + to : step * TOKENS + to + BLOCK] = x[step, at : at + BLOCK]
-    for ref, row in ((w, W_AT), (rec, REC_AT)):
-        half = ref[:, cols_of(far)]
-        message[row : row + WIDTH] = half[:, :WIDTH]
-        message[row + WIDTH : row + 2 * WIDTH] = half[:, WIDTH:]
+            row = (1 - step) * TOKENS + to
+            message[row : row + BLOCK] = x[step, at : at + BLOCK]
+            tokens[row : row + BLOCK] = x[step, at : at + BLOCK]
+    old = velocity[:, far]
+    high = bf16(old)
     spare = jnp.zeros((PADDED - ROWS, COLS), jnp.float32)
+    halves = [(W_AT, w[:, far]), (REC_AT, rec[:, far]), (M_AT, high)]
+    halves += [(M_AT + 2 * WIDTH, bf16(old - f32(high)))]
     for step in range(2):
-        half = bf16(jnp.concatenate([f32(targets[step, :, cols_of(far)]), spare], axis=0))
-        row = T_AT + 2 * step * PADDED
-        message[row : row + PADDED] = half[:, :WIDTH]
-        message[row + PADDED : row + 2 * PADDED] = half[:, WIDTH:]
-    velocity_far[...] = velocity[:, cols_of(far)]
-
-
-def tile(mix, w, rec, velocity, got, velocity_got, k):
+        padded = jnp.concatenate([f32(targets[step, :, far]), spare], axis=0)
+        halves.append((T_AT + 2 * step * PADDED, bf16(padded)))
+    for row, half in halves:
+        rows = half.shape[0]
+        message[row : row + rows] = half[:, :WIDTH]
+        message[row + rows : row + 2 * rows] = half[:, WIDTH:]
+
+
+def add_parts(got, own, out):
+    for k in range(2):
+        part = slice(k * WIDTH, (k + 1) * WIDTH)
+        at = P_AT + k * TOKENS
+        out[:, part] = bf16(f32(own[:, part]) + f32(got[at : at + TOKENS]))
+
+
+def tile(mix, w, rec, velocity, got, first, k):
     keep = kept(mix, 0)
     if k == 0:
         side = cols_of(lax.axis_index("core"))
         start, arrived, old = w[:, side], rec[:, side], velocity[:, side]
     else:
-        start, arrived = (
+        start, arrived, high, low = (
             jnp.concatenate([got[at : at + WIDTH], got[at + WIDTH : at + 2 * WIDTH]], axis=1)
-            for at in (W_AT, REC_AT)
+            for at in (W_AT - first, REC_AT - first, M_AT - first, M_AT + 2 * WIDTH - first)
         )
-        old = velocity_got[...]
+        old = f32(high) + f32(low)
     ahead = f32(start) - (step_size * momentum_decay) * old
     return ahead, keep * ahead + f32(arrived), old
 
 
-def second_values(push, push_got, mix, w, rec, velocity, targets, velocity_got, mine, got, out, taught):
+def second_values(push, push_got, mix, w, rec, velocity, targets, mine, got, out, taught):
     core = lax.axis_index("core")
     weight = kept(mix, 0) * push[0] + push_got[0]
-    near, far = mine[X2_AT : X2_AT + TOKENS], got[X2_AT : X2_AT + TOKENS]
-    scaled = [bf16(tile(mix, w, rec, velocity, got, velocity_got, k)[1] / weight) for k in range(2)]
+    near, far = mine[:TOKENS], got[:TOKENS]
+    scaled = [bf16(tile(mix, w, rec, velocity, got, 0, k)[1] / weight) for k in range(2)]
     out[:, :COLS] = bf16((dot(near, scaled[0]) + dot(far, scaled[1])) * ROW_SCALE)
-    rows = half_of(core)
+    rows = pl.ds(pl.multiple_of(X1_AT + core * HALF, 16), HALF)
     across = ((1,), (1,))
     out[:, COLS:] = bf16(dot(near, mine[rows], across) + dot(far, got[rows], across))
     for step in range(2):
@@ -147,32 +161,20 @@
 
 def add_slab(own, mine, got, out, own_out):
     out[...] = bf16(f32(mine[...]) + f32(got[...]))
-
-    def later():
-        own_out[...] = own[...] + f32(got[own_block(), :COLS])
-
-    return later
+    own_out[...] = own[...] + f32(got[own_block(), :COLS])
 
 
 def add_and_spread(own, mine, got, out, own_out):
     total = bf16(f32(mine[...]) + f32(got[...]))
     for y in range(N_Y):
         out[y] = total
-
-    def later():
-        own_out[...] = own[...] + f32(got[own_block()])
-
-    return later
+    own_out[...] = own[...] + f32(got[own_block()])
 
 
 def add_and_part(own, mine, got, out, gram, own_out):
     out[...] = bf16(f32(mine[:, :COLS]) + f32(got[:, :COLS]))
     gram[...] = bf16(f32(mine[:, COLS:]) + f32(got[:, COLS:]))
-
-    def later():
-        own_out[...] = own[...] + f32(got[own_block(), :COLS])
-
-    return later
+    own_out[...] = own[...] + f32(got[own_block(), :COLS])
 
 
 def second_residual(push, push_got, mix, own, all1, gram, gram_got, base, out, own_out, turned):
@@ -184,18 +186,14 @@
     residual = bf16(f32(base[...]) - turned[...])
     for y in range(N_Y):
         out[y] = residual
-
-    def later():
-        own_out[...] = own[...] - turned[own_block()]
-
-    return later
-
-
-def first_gradient(push, mix, w, rec, velocity, velocity_got, all1, mine, got, near, far, ready):
+    own_out[...] = own[...] - turned[own_block()]
+
+
+def first_gradient(push, mix, w, rec, velocity, mine, got, all1, near, far, ready):
     keep = kept(mix, 0)
     down = ((0,), (0,))
     for k, x, out in ((0, mine, near), (1, got, far)):
-        ahead, base, old = tile(mix, w, rec, velocity, got, velocity_got, k)
+        ahead, base, old = tile(mix, w, rec, velocity, got, X1_AT, k)
         gradient = dot(x[:TOKENS], all1[...], down) * GRAD_SCALE
         out[:WIDTH] = bf16((1.0 - keep) * (ahead - step_size * gradient))
         current = bf16(base - (step_size * keep) * gradient)
@@ -204,12 +202,12 @@
     near[WIDTH:] = bf16(jnp.full((EXTRA, COLS), (1.0 - keep) * push[0], jnp.float32))
 
 
-def second_gradient(push, push_got, mix, ready, own1, own2, mine, got, all2, far, near, half, message):
+def second_gradient(push, push_got, mix, ready, mine, got, own1, own2, all2, far, near, half, message):
     core = lax.axis_index("core")
     keep = kept(mix, 1)
     down = ((0,), (0,))
     for k, x, out, held in ((1, got, far, message), (0, mine, near, half)):
-        gradient = dot(x[X2_AT : X2_AT + TOKENS], all2[...], down) * GRAD_SCALE
+        gradient = dot(x[...], all2[...], down) * GRAD_SCALE
         moved = ready[k * WIDTH : (k + 1) * WIDTH] - step_size * gradient
         out[:WIDTH] = bf16((1.0 - keep) * moved)
         held[:WIDTH] = keep * moved
@@ -221,7 +219,7 @@
 
 
 def join_numerator(
-    push, push_got, mix, own1, own2, arrived, arrived_far, half, message, out, rows_out, weight
+    push, push_got, mix, arrived, arrived_far, own1, own2, half, message, out, rows_out, weight
 ):
     core = lax.axis_index("core")
     out[0, :, cols_of(core)] = bf16(half[...] + f32(arrived[:WIDTH]))
@@ -250,10 +248,15 @@
     copied = [f if isinstance(f, tuple) else (f, None) for f in list(fetched) + list(late)]
     n, m, first = len(copied), len(fetched), len(scalars)
     last = first + n + len(near)
-    far = [k for k, (_, _, in_hbm) in enumerate(outs) if in_hbm]
+    far = [k for k, (_, _, memory) in enumerate(outs) if memory is pltpu.HBM]
 
     def view(ref, where):
         return ref if where is None else ref.at[where]
+
+    def held_shape(value, where):
+        if where is None:
+            return value.shape
+        return value.shape[1:] if isinstance(where, int) else (where.size,) + value.shape[1:]
 
     def kernel(*refs):
         out = list(refs[last : last + len(outs)])
@@ -286,17 +289,14 @@
         for copy in copies:
             copy.wait()
 
-    held = [
-        pltpu.VMEM(value.shape if where is None else value.shape[1:], value.dtype)
-        for value, where in copied
-    ]
-    held += [pltpu.VMEM(*outs[k][:2]) for k in far]
-    held += [pltpu.SemaphoreType.DMA((n,))] if n else []
-    held += [pltpu.SemaphoreType.DMA((len(far),))] if far else []
+    buffered = [pltpu.VMEM(held_shape(value, where), value.dtype) for value, where in copied]
+    buffered += [pltpu.VMEM(*outs[k][:2]) for k in far]
+    buffered += [pltpu.SemaphoreType.DMA((n,))] if n else []
+    buffered += [pltpu.SemaphoreType.DMA((len(far),))] if far else []
     result, specs = [], []
-    for shape, kind, in_hbm in outs:
-        result.append(pltpu.HBM(shape, kind) if in_hbm else jax.ShapeDtypeStruct(shape, kind))
-        specs.append(HBM if in_hbm else SMEM if shape == (1,) else VMEM)
+    for shape, kind, memory in outs:
+        result.append((memory or jax.ShapeDtypeStruct)(shape, kind))
+        specs.append(HBM if memory is pltpu.HBM else SMEM if shape == (1,) else VMEM)
     arrays = [pltpu.with_memory_space_constraint(value, pltpu.HBM) for value, _ in copied]
     moved = sum(a.size * a.dtype.itemsize for a in arrays + list(near))
     moved += sum(math.prod(shape) * jnp.dtype(kind).itemsize for shape, kind, _ in outs)
@@ -305,11 +305,15 @@
         out_shape=result,
         in_specs=[SMEM] * first + [HBM] * n + [VMEM] * len(near),
         out_specs=specs,
-        scratch_shapes=held + [pltpu.VMEM(size, kind) for size, kind in scratch],
+        scratch_shapes=buffered + [pltpu.VMEM(size, kind) for size, kind in scratch],
         compiler_params=pltpu.CompilerParams(vmem_limit_bytes=20 * 2**20),
         cost_estimate=pl.CostEstimate(flops=flops, bytes_accessed=moved, transcendentals=0),
         name=body.func.__name__ if isinstance(body, functools.partial) else body.__name__,
     )(*scalars, *arrays, *near)
+
+
+def held(value):
+    return pltpu.with_memory_space_constraint(value, pltpu.VMEM)
 
 
 def z_pairs(step):
@@ -344,62 +348,73 @@
     return lax.ppermute(value, GROUP + ("core",), pairs)
 
 
-OWN = ((BLOCK, COLS), F32, True)
+OWN = ((BLOCK, COLS), F32, pltpu.VMEM)
 
 
 def sum_slab(step, parts, taught):
-    whole = ((SLAB, parts.shape[2]), B16, False)
-    slab, own = call(functools.partial(sum_over_y, step), [], [parts], [], [taught], [whole, OWN])
-    return call(add_slab, [], [], [own], [slab, over_z(slab, 0)], [whole, OWN])
+    whole = ((SLAB, parts.shape[2]), B16, pltpu.VMEM)
+    slab, own = call(
+        functools.partial(sum_over_y, step), [], [], [], [held(parts), held(taught)], [whole, OWN]
+    )
+    near = [held(own), held(slab), held(over_z(slab, 0))]
+    return call(add_slab, [], [], [], near, [whole, OWN])
 
 
 def local(inputs, targets, numerator, momentum, received, push_weight, received_weight, mix_share):
     push, push_got, mix = push_weight, received_weight, mix_share
     state = [(numerator, 0), (received, 0), (momentum, 0)]
 
-    part = [((TOKENS, COLS), B16, False)] * 2
-    part_far, part_own = call(first_values, [push], [(inputs, 0), (numerator, 0)], [], [], part)
-    part1 = bf16(f32(part_own) + f32(swap_core(part_far)))
-
-    targets, part_far = lax.optimization_barrier((targets, part_far))
-    mine, velocity_far = call(
-        make_message,
-        [],
-        [inputs] + state[:2] + [targets, state[2]],
-        [],
-        [],
-        [((MESSAGE, WIDTH), B16, False), ((WIDTH, COLS), F32, True)],
-    )
-    got = swap_core(mine)
-    velocity_got = swap_core(velocity_far)
+    part_own, message, mine = call(
+        prepare,
+        [push],
+        [inputs] + state + [targets],
+        [],
+        [],
+        [
+            ((TOKENS, COLS), B16, pltpu.VMEM),
+            ((MESSAGE, WIDTH), B16, pltpu.VMEM),
+            ((2 * TOKENS, WIDTH), B16, pltpu.HBM),
+        ],
+    )
+    got = swap_core(message)
+    (part1,) = call(
+        add_parts,
+        [],
+        [],
+        [],
+        [got, held(part_own)],
+        [((TOKENS, COLS), B16, pltpu.HBM)],
+    )
+    targets, part1 = lax.optimization_barrier((targets, part1))
 
     part2, taught = call(
         second_values,
         [push, push_got, mix],
-        state + [targets, velocity_got],
-        [],
-        [mine, got],
-        [((TOKENS, COLS + HALF), B16, True), ((2, BLOCK, COLS), F32, False)],
-    )
-
-    spread = ((N_Y, SLAB, COLS), B16, True)
+        state + [targets, mine, (got, pl.ds(0, P_AT))],
+        [],
+        [],
+        [((TOKENS, COLS + HALF), B16, pltpu.HBM), ((2, BLOCK, COLS), F32, pltpu.VMEM)],
+    )
+
+    spread = ((N_Y, SLAB, COLS), B16, pltpu.HBM)
     parts2 = over_y(part2.reshape(N_Y, SLAB, COLS + HALF))
     slab1, own1 = sum_slab(0, over_y(part1.reshape(N_Y, SLAB, COLS)), taught)
     parts2, _ = lax.optimization_barrier((parts2, slab1))
-    sent, own1 = call(add_and_spread, [], [], [own1], [slab1, over_z(slab1, 1)], [spread, OWN])
+    near = [held(own1), held(slab1), held(over_z(slab1, 1))]
+    sent, own1 = call(add_and_spread, [], [], [], near, [spread, OWN])
     all1 = over_y(sent).reshape(TOKENS, COLS)
 
     slab2, own2 = sum_slab(1, parts2, taught)
     near, far, ready = call(
         first_gradient,
         [push, mix],
-        state + [velocity_got],
-        [],
-        [all1, mine, got],
+        state + [(mine, pl.ds(X1_AT, TOKENS)), (got, pl.ds(X1_AT, T_AT - X1_AT))],
+        [],
+        [all1],
         [
-            ((WIDTH + EXTRA, COLS), B16, True),
-            ((WIDTH, COLS), B16, True),
-            ((2 * WIDTH, COLS), F32, True),
+            ((WIDTH + EXTRA, COLS), B16, pltpu.HBM),
+            ((WIDTH, COLS), B16, pltpu.HBM),
+            ((2 * WIDTH, COLS), F32, pltpu.HBM),
         ],
     )
     slab2_got, _ = lax.optimization_barrier((over_z(slab2, 1), far))
@@ -408,47 +423,47 @@
         add_and_part,
         [],
         [],
-        [own2],
-        [slab2, slab2_got],
-        [((SLAB, COLS), B16, False), ((SLAB, HALF), B16, False), OWN],
-    )
-    gram_got = swap_core(gram)
+        [],
+        [held(own2), held(slab2), held(slab2_got)],
+        [((SLAB, COLS), B16, pltpu.VMEM), ((SLAB, HALF), B16, pltpu.VMEM), OWN],
+    )
+    gram_got = held(swap_core(gram))
+    gram_got, arrived, arrived_far = lax.optimization_barrier((gram_got, arrived, arrived_far))
     sent, own2 = call(
         second_residual,
         [push, push_got, mix],
         [],
-        [own2],
-        [all1, gram, gram_got, ahead2],
+        [],
+        [held(own2), all1, held(gram), held(gram_got), held(ahead2)],
         [spread, OWN],
         [((SLAB, COLS), F32)],
     )
     all2 = over_y(sent).reshape(TOKENS, COLS)
-    all2, arrived, arrived_far = lax.optimization_barrier((all2, arrived, arrived_far))
 
     far, near, half, message = call(
         second_gradient,
         [push, push_got, mix],
-        [ready, own1, own2],
-        [],
-        [mine, got, all2],
+        [ready, (mine, pl.ds(0, TOKENS)), (got, pl.ds(0, TOKENS))],
+        [],
+        [held(own1), held(own2), all2],
         [
-            ((WIDTH, COLS), B16, False),
-            ((WIDTH + EXTRA, COLS), B16, False),
-            ((WIDTH, COLS), F32, False),
-            ((WIDTH + 2 * ROWS, COLS), F32, False),
+            ((WIDTH, COLS), B16, None),
+            ((WIDTH + EXTRA, COLS), B16, None),
+            ((WIDTH, COLS), F32, None),
+            ((WIDTH + 2 * ROWS, COLS), F32, None),
         ],
     )
 
     sent_far, sent_own = to_group_other(far, 2), to_group(near, 2)
-    whole = ((1, WIDTH, VALUES), B16, False)
-    number = ((1,), F32, False)
+    whole = ((1, WIDTH, VALUES), B16, None)
+    number = ((1,), F32, None)
     final_numerator, value_rows, final_weight = call(
         join_numerator,
         [push, push_got, mix],
-        [own1, own2, arrived, arrived_far],
-        [],
-        [half, swap_core(message)],
-        [whole, ((2, ROWS, VALUES), B16, False), number],
+        [],
+        [],
+        [held(arrived), held(arrived_far), held(own1), held(own2), half, swap_core(message)],
+        [whole, ((2, ROWS, VALUES), B16, None), number],
     )
     sent_far, final_numerator = lax.optimization_barrier((sent_far, final_numerator))
     final_received, got_weight = call(

time: 184 us -> 193 us (1.049)
  blocking collectives: 0 us -> 17.3 us
  Pallas kernels: 36.1 us -> 23.4 us
  starting transfers between devices: 74.1 us -> 79.2 us
  waiting for transfers between devices: 67.6 us -> 69.8 us
    all_to_all x0 -> x1, blocking collectives: none -> 17.3 us  [over_y(): return lax.all_to_all(value, 'y', 0, 0, tiled=True)]
    pallas_call x14, Pallas kernels: 36.1 us -> 23.4 us  [call(): pl.pallas_call(kernel, out_shape=result, in_specs=[SMEM] * first + [HBM]...]
    ppermute x2, starting transfers between devices: 5.83 us -> 13 us  [to_group_other(): return lax.ppermute(value, GROUP + ('core',), pairs)]
    all_to_all x4 -> x3, starting transfers between devices: 17.1 us -> 11.2 us  [over_y(): return lax.all_to_all(value, 'y', 0, 0, tiled=True)]
    ppermute x4, starting transfers between devices: 28.1 us -> 32 us  [over_z(): return lax.ppermute(value, ('z_hi', 'core'), z_pairs(step))]
    all_to_all x4 -> x3, waiting for transfers between devices: 2.69 us -> 6.08 us  [over_y(): return lax.all_to_all(value, 'y', 0, 0, tiled=True)]
    ppermute x5 -> x3, waiting for transfers between devices: 2.21 us -> 4.61 us  [swap_core(): return lax.ppermute(value, 'core', [(0, 1), (1, 0)])]
    ppermute x4, waiting for transfers between devices: 28.2 us -> 26.1 us  [over_z(): return lax.ppermute(value, ('z_hi', 'core'), z_pairs(step))]
  transfers between devices with their start and end apart: 17 -> 14, of which waited for: 9 -> 7; matrix products, arithmetic and copies ran while one was open for 1% -> 0% of each run, Pallas kernels for 14% -> 7%
where the time goes in v7:
time: 193 us; the launch traced here: 192 us
  starting transfers between devices  79.2 us (41%)
  waiting for transfers between devices  69.8 us (36%)
  Pallas kernels  23.4 us (12%)
  blocking collectives  17.3 us (9%)
  between operations  2.16 us (1%)
    ppermute x2, waiting for transfers between devices, to_group_other(): return lax.ppermute(value, GROUP + ('core',), pairs)  33 us
    ppermute x4, starting transfers between devices, over_z(): return lax.ppermute(value, ('z_hi', 'core'), z_pairs(step))  32 us
    ppermute x4, waiting for transfers between devices, over_z(): return lax.ppermute(value, ('z_hi', 'core'), z_pairs(step))  26.1 us
    pallas_call x14, Pallas kernels, call(): pl.pallas_call(kernel, out_shape=result, in_specs=[SMEM] * first + [HBM]...  23.4 us
    ppermute x3, starting transfers between devices, swap_core(): return lax.ppermute(value, 'core', [(0, 1), (1, 0)])  19.2 us
    all_to_all x1, blocking collectives, over_y(): return lax.all_to_all(value, 'y', 0, 0, tiled=True)  17.3 us
    ppermute x2, starting transfers between devices, to_group_other(): return lax.ppermute(value, GROUP + ('core',), pairs)  13 us
    all_to_all x3, starting transfers between devices, over_y(): return lax.all_to_all(value, 'y', 0, 0, tiled=True)  11.2 us
  transfers between devices with their start and end apart: 14, of which 7 were waited for; matrix products, arithmetic and copies ran while one was open for 0% of the time, Pallas kernels for 7%

profile of v7, /device:TPU:1, one launch (start us, length us, event | category | flops | bytes accessed | tf_op | source)
XLA Modules:
  0.0 192.4 jit_solution(12521114208542301258)
XLA Ops:
  1.3 3.5 %prepare.1 = (bf16[768,512]{1,0:T(8,128)(2,1)S(1)}, bf16[5248,256]{1,0:T(8,128)(2,1)S(1)}, bf16[1536,256]{1,0:T(8,128)(2,1)}) custom-call(f32[1]{0:T(128)S(6)} %copy.13.refs_0_, bf16[2,768,256]{2,1,0:T(8,128)(2,1)} %refs_1_.6, bf16[1,256,1024]{2,1,0:T(8,128)(2,1)} %refs_2_.8, bf16[1,256,1024]{2,1,0:T(8,128)(2,1)} %refs_3_.5, f32[1,256,1024]{2,1,0:T(8,128)} %refs_4_.5, ...), custom_call_target="tpu_custom_call" | custom-call | bytes 7241728 | tf_op jit(solution)/shard_map/prepare/pallas_call | solution.py:303
  4.8 8.8 %collective-permute-start = (bf16[5248,256]{1,0:T(8,128)(2,1)S(1)}, bf16[5248,256]{1,0:T(8,128)(2,1)S(1)}, u32[]{:S(2)}, u32[]{:S(2)}) collective-permute-start(bf16[5248,256]{1,0:T(8,128)(2,1)S(1)} %get-tuple-element.47), channel_id=1, source_target_pairs={{0,1},{1,0},{2,3},{3,2},{4,5},{5,4},{6,7},{7,6},{8,9},{9,8},{10,11... | collective-permute-start | bytes 8060936 | tf_op jit(solution)/shard_map/ppermute | solution.py:337
  13.6 4.6 %collective-permute-done.refs_0_.refs_8_.refs_6_.refs_5_ = bf16[5248,256]{1,0:T(8,128)(2,1)S(1)} collective-permute-done((bf16[5248,256]{1,0:T(8,128)(2,1)S(1)}, bf16[5248,256]{1,0:T(8,128)(2,1)S(1)}, u32[]{:S(2)}, u32[]{:S(2)}) %collective-permute-start) | collective-permute-done | bytes 2687008 | tf_op jit(solution)/shard_map/ppermute | solution.py:337
  19.9 3.5 %all-to-all-start = ((bf16[4,192,512]{2,1,0:T(8,128)(2,1)}), bf16[4,192,512]{2,1,0:T(8,128)(2,1)S(1)}, u32[]{:S(2)}, u32[]{:S(2)}) async-start(bf16[4,192,512]{2,1,0:T(8,128)(2,1)} %bitcast.7), calls=%async_computation | async-start | bytes 1572864 | tf_op jit(solution)/shard_map/all_to_all | solution.py:333
  24.1 5.3 %second_values.1 = (bf16[768,896]{1,0:T(8,128)(2,1)}, f32[2,48,512]{2,1,0:T(8,128)S(1)}) custom-call(f32[1]{0:T(128)S(6)} %copy.13.refs_0_, f32[1]{0:T(128)S(6)} %copy.14.refs_1_, s32[1,2]{1,0:T(1,128)S(1)} %copy-done.1, bf16[1,256,1024]{2,1,0:T(8,128)(2,1)} %refs_2_.8, bf16[1,256,1024]{2,1,0:T(8,128)(2,1)} %refs_3_.5, f32[1,256,1024]{2,1,0:T(8,128)} %refs_4_.5, ...), custom_call_target="tpu_custom_call" | custom-call | bytes 7241728 | tf_op jit(solution)/shard_map/second_values/pallas_call | solution.py:303
  29.4 6.1 %all-to-all-done.refs_0_ = bf16[4,192,512]{2,1,0:T(8,128)(2,1)S(1)} async-done(((bf16[4,192,512]{2,1,0:T(8,128)(2,1)}), bf16[4,192,512]{2,1,0:T(8,128)(2,1)S(1)}, u32[]{:S(2)}, u32[]{:S(2)}) %all-to-all-start) | async-done | bytes 786464 | tf_op jit(solution)/shard_map/all_to_all | solution.py:333
  35.4 3.5 %all-to-all-start.2 = ((bf16[4,192,896]{2,1,0:T(8,128)(2,1)}), bf16[4,192,896]{2,1,0:T(8,128)(2,1)S(1)}, u32[]{:S(2)}, u32[]{:S(2)}) async-start(bf16[4,192,896]{2,1,0:T(8,128)(2,1)} %bitcast.8), calls=%async_computation.2 | async-start | bytes 2752512 | tf_op jit(solution)/shard_map/all_to_all | solution.py:333
  39.1 7.5 %collective-permute-start.1 = (bf16[192,512]{1,0:T(8,128)(2,1)S(1)}, bf16[192,512]{1,0:T(8,128)(2,1)S(1)}, u32[]{:S(2)}, u32[]{:S(2)}) collective-permute-start(bf16[192,512]{1,0:T(8,128)(2,1)S(1)} %get-tuple-element.53.refs_1_), channel_id=1, source_target_pairs={{0,8},{1,25},{8,0},{9,17},{16,24},{17,9},{24,16},{25,1},{2,10},{3,... | collective-permute-start | bytes 589832 | tf_op jit(solution)/shard_map/ppermute | solution.py:329
  46.6 6.7 %collective-permute-done.1.refs_2_ = bf16[192,512]{1,0:T(8,128)(2,1)S(1)} collective-permute-done((bf16[192,512]{1,0:T(8,128)(2,1)S(1)}, bf16[192,512]{1,0:T(8,128)(2,1)S(1)}, u32[]{:S(2)}, u32[]{:S(2)}) %collective-permute-start.1) | collective-permute-done | bytes 196640 | tf_op jit(solution)/shard_map/ppermute | solution.py:329
  53.4 7.8 %collective-permute-start.2 = (bf16[192,512]{1,0:T(8,128)(2,1)S(1)}, bf16[192,512]{1,0:T(8,128)(2,1)S(1)}, u32[]{:S(2)}, u32[]{:S(2)}) collective-permute-start(bf16[192,512]{1,0:T(8,128)(2,1)S(1)} %get-tuple-element.55.refs_1_), channel_id=1, source_target_pairs={{0,24},{1,9},{8,16},{9,1},{16,8},{17,25},{24,0},{25,17},{2,26},{3,... | collective-permute-start | bytes 589832 | tf_op jit(solution)/shard_map/ppermute | solution.py:329
  61.2 9.6 %collective-permute-done.2.refs_2_ = bf16[192,512]{1,0:T(8,128)(2,1)S(1)} collective-permute-done((bf16[192,512]{1,0:T(8,128)(2,1)S(1)}, bf16[192,512]{1,0:T(8,128)(2,1)S(1)}, u32[]{:S(2)}, u32[]{:S(2)}) %collective-permute-start.2) | collective-permute-done | bytes 196640 | tf_op jit(solution)/shard_map/ppermute | solution.py:329
  71.8 4.2 %all-to-all-start.1 = ((bf16[4,192,512]{2,1,0:T(8,128)(2,1)}), bf16[4,192,512]{2,1,0:T(8,128)(2,1)S(1)}, u32[]{:S(2)}, u32[]{:S(2)}) async-start(bf16[4,192,512]{2,1,0:T(8,128)(2,1)} %get-tuple-element.56), calls=%async_computation.1 | async-start | bytes 1572864 | tf_op jit(solution)/shard_map/all_to_all | solution.py:333
  76.2 2.3 %collective-permute-start.3 = (bf16[192,896]{1,0:T(8,128)(2,1)S(1)}, bf16[192,896]{1,0:T(8,128)(2,1)S(1)}, u32[]{:S(2)}, u32[]{:S(2)}) collective-permute-start(bf16[192,896]{1,0:T(8,128)(2,1)S(1)} %get-tuple-element.62.refs_1_), channel_id=1, source_target_pairs={{0,8},{1,25},{8,0},{9,17},{16,24},{17,9},{24,16},{25,1},{2,10},{3,... | collective-permute-start | bytes 1032200 | tf_op jit(solution)/shard_map/ppermute | solution.py:329
  78.5 9.8 %collective-permute-done.3.refs_2_ = bf16[192,896]{1,0:T(8,128)(2,1)S(1)} collective-permute-done((bf16[192,896]{1,0:T(8,128)(2,1)S(1)}, bf16[192,896]{1,0:T(8,128)(2,1)S(1)}, u32[]{:S(2)}, u32[]{:S(2)}) %collective-permute-start.3) | collective-permute-done | bytes 344096 | tf_op jit(solution)/shard_map/ppermute | solution.py:329
  88.4 14.3 %collective-permute-start.4 = (bf16[192,896]{1,0:T(8,128)(2,1)S(1)}, bf16[192,896]{1,0:T(8,128)(2,1)S(1)}, u32[]{:S(2)}, u32[]{:S(2)}) collective-permute-start(bf16[192,896]{1,0:T(8,128)(2,1)S(1)} %get-tuple-element.64.refs_1_), channel_id=1, source_target_pairs={{0,24},{1,9},{8,16},{9,1},{16,8},{17,25},{24,0},{25,17},{2,26},{3,... | collective-permute-start | bytes 1032200 | tf_op jit(solution)/shard_map/ppermute | solution.py:329
  102.8 4.9 %first_gradient.1 = (bf16[272,512]{1,0:T(8,128)(2,1)}, bf16[256,512]{1,0:T(8,128)(2,1)}, f32[512,512]{1,0:T(8,128)}) custom-call(f32[1]{0:T(128)S(6)} %copy.13.refs_0_, s32[1,2]{1,0:T(1,128)S(1)} %copy-done.1, bf16[1,256,1024]{2,1,0:T(8,128)(2,1)} %refs_2_.8, bf16[1,256,1024]{2,1,0:T(8,128)(2,1)} %refs_3_.5, f32[1,256,1024]{2,1,0:T(8,128)} %refs_4_.5, ...), custom_call_target="tpu_custom_call" | custom-call | bytes 7946240 | tf_op jit(solution)/shard_map/first_gradient/pallas_call | solution.py:303
  109.6 11.1 %collective-permute-start.7 = (bf16[256,512]{1,0:T(8,128)(2,1)}, bf16[256,512]{1,0:T(8,128)(2,1)S(1)}, u32[]{:S(2)}, u32[]{:S(2)}) collective-permute-start(bf16[256,512]{1,0:T(8,128)(2,1)} %get-tuple-element.65), channel_id=1, source_target_pairs={{0,33},{1,32},{32,65},{33,64},{64,97},{65,96},{96,129},{97,128},{1... | collective-permute-start | bytes 786440 | tf_op jit(solution)/shard_map/ppermute | solution.py:348
  120.8 8.1 %collective-permute-start.5 = (bf16[192,384]{1,0:T(8,128)(2,1)S(1)}, bf16[192,384]{1,0:T(8,128)(2,1)S(1)}, u32[]{:S(2)}, u32[]{:S(2)}) collective-permute-start(bf16[192,384]{1,0:T(8,128)(2,1)S(1)} %get-tuple-element.68.refs_5_), channel_id=1, source_target_pairs={{0,1},{1,0},{2,3},{3,2},{4,5},{5,4},{6,7},{7,6},{8,9},{9,8},{10,11... | collective-permute-start | bytes 442376 | tf_op jit(solution)/shard_map/ppermute | solution.py:337
  128.9 11.2 %collective-permute-done.7.refs_4_ = bf16[256,512]{1,0:T(8,128)(2,1)S(1)} collective-permute-done((bf16[256,512]{1,0:T(8,128)(2,1)}, bf16[256,512]{1,0:T(8,128)(2,1)S(1)}, u32[]{:S(2)}, u32[]{:S(2)}) %collective-permute-start.7) | collective-permute-done | bytes 262176 | tf_op jit(solution)/shard_map/ppermute | solution.py:348
  142.0 17.3 %all_to_all.20 = bf16[4,192,512]{2,1,0:T(8,128)(2,1)S(1)} all-to-all(bf16[4,192,512]{2,1,0:T(8,128)(2,1)} %get-tuple-element.73), channel_id=1, replica_groups=mesh['x'=4,'z_lo'=4,'z_hi'=4,'y'=4,'core'=2] {'y'}, dimensions={0} | all-to-all | bytes 1572864 | tf_op jit(solution)/shard_map/all_to_all | solution.py:333
  159.3 2.6 %second_gradient.1 = (bf16[256,512]{1,0:T(8,128)(2,1)S(1)}, bf16[272,512]{1,0:T(8,128)(2,1)S(1)}, f32[256,512]{1,0:T(8,128)S(1)}, f32[304,512]{1,0:T(8,128)S(1)}) custom-call(f32[1]{0:T(128)S(6)} %copy.13.refs_0_, f32[1]{0:T(128)S(6)} %copy.14.refs_1_, s32[1,2]{1,0:T(1,128)S(1)} %copy-done.1, f32[512,512]{1,0:T(8,128)} %get-tuple-element.57.refs_3_, ...), custom_call_target="tpu_custom_call" | custom-call | bytes 7192576 | tf_op jit(solution)/shard_map/second_gradient/pallas_call | solution.py:303
  162.0 2.3 %collective-permute-start.9 = (f32[304,512]{1,0:T(8,128)S(1)}, f32[304,512]{1,0:T(8,128)S(1)}, u32[]{:S(2)}, u32[]{:S(2)}) collective-permute-start(f32[304,512]{1,0:T(8,128)S(1)} %get-tuple-element.78), channel_id=1, source_target_pairs={{0,1},{1,0},{2,3},{3,2},{4,5},{5,4},{6,7},{7,6},{8,9},{9,8},{10,11... | collective-permute-start | bytes 1867784 | tf_op jit(solution)/shard_map/ppermute | solution.py:337
  164.3 1.9 collective-permute-start.10
  169.7 21.8 %collective-permute-done.8.refs_1_ = bf16[256,512]{1,0:T(8,128)(2,1)S(1)} collective-permute-done((bf16[256,512]{1,0:T(8,128)(2,1)S(1)}, bf16[256,512]{1,0:T(8,128)(2,1)S(1)}, u32[]{:S(2)}, u32[]{:S(2)}) %collective-permute-start.8) | collective-permute-done | bytes 262176 | tf_op jit(solution)/shard_map/ppermute | solution.py:348
  (23 shorter events, 11.4 us)
Async XLA Ops:
  4.8 13.4 %collective-permute-start = (bf16[5248,256]{1,0:T(8,128)(2,1)S(1)}, bf16[5248,256]{1,0:T(8,128)(2,1)S(1)}, u32[]{:S(2)}, u32[]{:S(2)}) collective-permute-start(bf16[5248,256]{1,0:T(8,128)(2,1)S(1)} %get-tuple-element.47), channel_id=1, source_target_pairs={{0,1},{1,0},{2,3},{3,2},{4,5},{5,4},{6,7},{7,6},{8,9},{9,8},{10,11... | collective-permute-start | bytes 8060936 | tf_op jit(solution)/shard_map/ppermute | solution.py:337
  18.2 1.7 copy-start
  18.2 5.9 %copy-start.1 = (s32[1,2]{1,0:T(1,128)S(1)}, s32[1,2]{1,0:T(1,128)}, u32[]{:S(2)}) copy-start(s32[1,2]{1,0:T(1,128)} %refs_2_.11) | copy-start | bytes 28
  19.9 15.5 %all-to-all-start = ((bf16[4,192,512]{2,1,0:T(8,128)(2,1)}), bf16[4,192,512]{2,1,0:T(8,128)(2,1)S(1)}, u32[]{:S(2)}, u32[]{:S(2)}) async-start(bf16[4,192,512]{2,1,0:T(8,128)(2,1)} %bitcast.7), calls=%async_computation | async-start | bytes 1572864 | tf_op jit(solution)/shard_map/all_to_all | solution.py:333
  35.4 36.3 %all-to-all-start.2 = ((bf16[4,192,896]{2,1,0:T(8,128)(2,1)}), bf16[4,192,896]{2,1,0:T(8,128)(2,1)S(1)}, u32[]{:S(2)}, u32[]{:S(2)}) async-start(bf16[4,192,896]{2,1,0:T(8,128)(2,1)} %bitcast.8), calls=%async_computation.2 | async-start | bytes 2752512 | tf_op jit(solution)/shard_map/all_to_all | solution.py:333
  39.1 14.2 %collective-permute-start.1 = (bf16[192,512]{1,0:T(8,128)(2,1)S(1)}, bf16[192,512]{1,0:T(8,128)(2,1)S(1)}, u32[]{:S(2)}, u32[]{:S(2)}) collective-permute-start(bf16[192,512]{1,0:T(8,128)(2,1)S(1)} %get-tuple-element.53.refs_1_), channel_id=1, source_target_pairs={{0,8},{1,25},{8,0},{9,17},{16,24},{17,9},{24,16},{25,1},{2,10},{3,... | collective-permute-start | bytes 589832 | tf_op jit(solution)/shard_map/ppermute | solution.py:329
  53.4 17.4 %collective-permute-start.2 = (bf16[192,512]{1,0:T(8,128)(2,1)S(1)}, bf16[192,512]{1,0:T(8,128)(2,1)S(1)}, u32[]{:S(2)}, u32[]{:S(2)}) collective-permute-start(bf16[192,512]{1,0:T(8,128)(2,1)S(1)} %get-tuple-element.55.refs_1_), channel_id=1, source_target_pairs={{0,24},{1,9},{8,16},{9,1},{16,8},{17,25},{24,0},{25,17},{2,26},{3,... | collective-permute-start | bytes 589832 | tf_op jit(solution)/shard_map/ppermute | solution.py:329
  71.8 31.0 %all-to-all-start.1 = ((bf16[4,192,512]{2,1,0:T(8,128)(2,1)}), bf16[4,192,512]{2,1,0:T(8,128)(2,1)S(1)}, u32[]{:S(2)}, u32[]{:S(2)}) async-start(bf16[4,192,512]{2,1,0:T(8,128)(2,1)} %get-tuple-element.56), calls=%async_computation.1 | async-start | bytes 1572864 | tf_op jit(solution)/shard_map/all_to_all | solution.py:333
  76.2 12.2 %collective-permute-start.3 = (bf16[192,896]{1,0:T(8,128)(2,1)S(1)}, bf16[192,896]{1,0:T(8,128)(2,1)S(1)}, u32[]{:S(2)}, u32[]{:S(2)}) collective-permute-start(bf16[192,896]{1,0:T(8,128)(2,1)S(1)} %get-tuple-element.62.refs_1_), channel_id=1, source_target_pairs={{0,8},{1,25},{8,0},{9,17},{16,24},{17,9},{24,16},{25,1},{2,10},{3,... | collective-permute-start | bytes 1032200 | tf_op jit(solution)/shard_map/ppermute | solution.py:329
  88.4 32.2 %collective-permute-start.4 = (bf16[192,896]{1,0:T(8,128)(2,1)S(1)}, bf16[192,896]{1,0:T(8,128)(2,1)S(1)}, u32[]{:S(2)}, u32[]{:S(2)}) collective-permute-start(bf16[192,896]{1,0:T(8,128)(2,1)S(1)} %get-tuple-element.64.refs_1_), channel_id=1, source_target_pairs={{0,24},{1,9},{8,16},{9,1},{16,8},{17,25},{24,0},{25,17},{2,26},{3,... | collective-permute-start | bytes 1032200 | tf_op jit(solution)/shard_map/ppermute | solution.py:329
  107.7 32.4 %collective-permute-start.6 = (bf16[272,512]{1,0:T(8,128)(2,1)}, bf16[272,512]{1,0:T(8,128)(2,1)S(1)}, u32[]{:S(2)}, u32[]{:S(2)}) collective-permute-start(bf16[272,512]{1,0:T(8,128)(2,1)} %get-tuple-element.69), channel_id=1, source_target_pairs={{0,32},{32,64},{64,96},{96,128},{128,160},{160,192},{192,224},{224... | collective-permute-start | bytes 835592 | tf_op jit(solution)/shard_map/ppermute | solution.py:342
  109.6 30.5 %collective-permute-start.7 = (bf16[256,512]{1,0:T(8,128)(2,1)}, bf16[256,512]{1,0:T(8,128)(2,1)S(1)}, u32[]{:S(2)}, u32[]{:S(2)}) collective-permute-start(bf16[256,512]{1,0:T(8,128)(2,1)} %get-tuple-element.65), channel_id=1, source_target_pairs={{0,33},{1,32},{32,65},{33,64},{64,97},{65,96},{96,129},{97,128},{1... | collective-permute-start | bytes 786440 | tf_op jit(solution)/shard_map/ppermute | solution.py:348
  120.8 19.3 %collective-permute-start.5 = (bf16[192,384]{1,0:T(8,128)(2,1)S(1)}, bf16[192,384]{1,0:T(8,128)(2,1)S(1)}, u32[]{:S(2)}, u32[]{:S(2)}) collective-permute-start(bf16[192,384]{1,0:T(8,128)(2,1)S(1)} %get-tuple-element.68.refs_5_), channel_id=1, source_target_pairs={{0,1},{1,0},{2,3},{3,2},{4,5},{5,4},{6,7},{7,6},{8,9},{9,8},{10,11... | collective-permute-start | bytes 442376 | tf_op jit(solution)/shard_map/ppermute | solution.py:337
  162.0 6.2 %collective-permute-start.9 = (f32[304,512]{1,0:T(8,128)S(1)}, f32[304,512]{1,0:T(8,128)S(1)}, u32[]{:S(2)}, u32[]{:S(2)}) collective-permute-start(f32[304,512]{1,0:T(8,128)S(1)} %get-tuple-element.78), channel_id=1, source_target_pairs={{0,1},{1,0},{2,3},{3,2},{4,5},{5,4},{6,7},{7,6},{8,9},{9,8},{10,11... | collective-permute-start | bytes 1867784 | tf_op jit(solution)/shard_map/ppermute | solution.py:337
  164.3 27.2 %collective-permute-start.10 = (bf16[272,512]{1,0:T(8,128)(2,1)S(1)}, bf16[272,512]{1,0:T(8,128)(2,1)S(1)}, u32[]{:S(2)}, u32[]{:S(2)}) collective-permute-start(bf16[272,512]{1,0:T(8,128)(2,1)S(1)} %get-tuple-element.82), channel_id=1, source_target_pairs={{0,64},{32,96},{64,128},{96,160},{128,192},{160,224},{192,256},{22... | collective-permute-start | bytes 835592 | tf_op jit(solution)/shard_map/ppermute | solution.py:342
  166.2 25.3 %collective-permute-start.8 = (bf16[256,512]{1,0:T(8,128)(2,1)S(1)}, bf16[256,512]{1,0:T(8,128)(2,1)S(1)}, u32[]{:S(2)}, u32[]{:S(2)}) collective-permute-start(bf16[256,512]{1,0:T(8,128)(2,1)S(1)} %get-tuple-element.74), channel_id=1, source_target_pairs={{0,65},{1,64},{32,97},{33,96},{64,129},{65,128},{96,161},{97,160},... | collective-permute-start | bytes 786440 | tf_op jit(solution)/shard_map/ppermute | solution.py:348

commit v8 on v7

--- a/solution.py
+++ b/solution.py
@@ -35,8 +35,7 @@
 REC_AT = W_AT + 2 * WIDTH
 M_AT = REC_AT + 2 * WIDTH
 T_AT = M_AT + 4 * WIDTH
-P_AT = T_AT + 4 * PADDED
-MESSAGE = P_AT + 2 * TOKENS
+MESSAGE = T_AT + 4 * PADDED
 
 B16, F32 = jnp.bfloat16, jnp.float32
 
@@ -73,19 +72,17 @@
     return [((zh * N_Y + y) * BLOCK, (y * N_Z + zh) * BLOCK) for zh in range(N_Z) for y in range(N_Y)]
 
 
-def prepare(push, x, w, rec, velocity, targets, own, message, tokens):
-    core = lax.axis_index("core")
-    for side in (1 - core, core):
+def first_values(push, x, w, far, own):
+    core = lax.axis_index("core")
+    for out, side in ((far, 1 - core), (own, core)):
         scaled = bf16(f32(w[:, cols_of(side)]) / push[0])
-        part = bf16(dot(x[0], scaled) * ROW_SCALE)
+        part = bf16(dot(x[...], scaled) * ROW_SCALE)
         for at, to in by_y():
-            block = part[at : at + BLOCK]
-            if side is core:
-                own[to : to + BLOCK] = block
-            else:
-                message[P_AT + to : P_AT + to + BLOCK] = block[:, :WIDTH]
-                message[P_AT + TOKENS + to : P_AT + TOKENS + to + BLOCK] = block[:, WIDTH:]
-    far = cols_of(1 - core)
+            out[to : to + BLOCK] = part[at : at + BLOCK]
+
+
+def make_message(x, w, rec, velocity, targets, message, tokens):
+    far = cols_of(1 - lax.axis_index("core"))
     for step in range(2):
         for at, to in by_y():
             row = (1 - step) * TOKENS + to
@@ -105,11 +102,8 @@
         message[row + rows : row + 2 * rows] = half[:, WIDTH:]
 
 
-def add_parts(got, own, out):
-    for k in range(2):
-        part = slice(k * WIDTH, (k + 1) * WIDTH)
-        at = P_AT + k * TOKENS
-        out[:, part] = bf16(f32(own[:, part]) + f32(got[at : at + TOKENS]))
+def add_parts(own, got, out):
+    out[...] = bf16(f32(own[...]) + f32(got[...]))
 
 
 def tile(mix, w, rec, velocity, got, first, k):
@@ -127,7 +121,7 @@
     return ahead, keep * ahead + f32(arrived), old
 
 
-def second_values(push, push_got, mix, w, rec, velocity, targets, mine, got, out, taught):
+def second_values(push, push_got, mix, w, rec, velocity, mine, got, out):
     core = lax.axis_index("core")
     weight = kept(mix, 0) * push[0] + push_got[0]
     near, far = mine[:TOKENS], got[:TOKENS]
@@ -136,32 +130,34 @@
     rows = pl.ds(pl.multiple_of(X1_AT + core * HALF, 16), HALF)
     across = ((1,), (1,))
     out[:, COLS:] = bf16(dot(near, mine[rows], across) + dot(far, got[rows], across))
-    for step in range(2):
-        own = f32(targets[step, :, cols_of(core)])
-        row = T_AT + 2 * step * PADDED
-        other = jnp.concatenate(
-            [f32(got[row : row + PADDED]), f32(got[row + PADDED : row + 2 * PADDED])], axis=1
-        )[:ROWS]
-        taught[step, :ROWS] = jnp.where(core == 0, own, other)
-        taught[step, ROWS:] = jnp.where(core == 0, other, own)
-
-
-def sum_over_y(step, parts, taught, slab, own):
+
+
+def sum_over_y(step, targets, targets_got, parts, slab, own, *gram):
+    core = lax.axis_index("core")
     total = f32(parts[0])
     for y in range(1, N_Y):
         total = total + f32(parts[y])
-    slab[...] = bf16(total)
+    slab[...] = bf16(total[:, :COLS])
+    if gram:
+        gram[0][...] = bf16(total[:, COLS:])
     rows = own_block()
     total = f32(parts[0, rows, :COLS])
     for y in range(1, N_Y):
         total = total + f32(parts[y, rows, :COLS])
     own[...] = total
-    slab[rows, :COLS] = bf16(total - taught[step])
+    near = f32(targets[step, :, cols_of(core)])
+    row = 2 * step * PADDED
+    far = jnp.concatenate(
+        [f32(targets_got[row : row + PADDED]), f32(targets_got[row + PADDED : row + 2 * PADDED])],
+        axis=1,
+    )[:ROWS]
+    low, high = jnp.where(core == 0, near, far), jnp.where(core == 0, far, near)
+    slab[rows] = bf16(total - jnp.concatenate([low, high], axis=0))
 
 
 def add_slab(own, mine, got, out, own_out):
     out[...] = bf16(f32(mine[...]) + f32(got[...]))
-    own_out[...] = own[...] + f32(got[own_block(), :COLS])
+    own_out[...] = own[...] + f32(got[own_block()])
 
 
 def add_and_spread(own, mine, got, out, own_out):
@@ -171,21 +167,13 @@
     own_out[...] = own[...] + f32(got[own_block()])
 
 
-def add_and_part(own, mine, got, out, gram, own_out):
-    out[...] = bf16(f32(mine[:, :COLS]) + f32(got[:, :COLS]))
-    gram[...] = bf16(f32(mine[:, COLS:]) + f32(got[:, COLS:]))
-    own_out[...] = own[...] + f32(got[own_block(), :COLS])
-
-
 def second_residual(push, push_got, mix, own, all1, gram, gram_got, base, out, own_out, turned):
     core = lax.axis_index("core")
     keep = kept(mix, 0)
     back = step_size * GRAD_SCALE * ROW_SCALE * keep / (keep * push[0] + push_got[0])
     near, far = all1[half_of(core)], all1[half_of(1 - core)]
     turned[...] = (dot(gram[...], near) + dot(gram_got[...], far)) * back
-    residual = bf16(f32(base[...]) - turned[...])
-    for y in range(N_Y):
-        out[y] = residual
+    out[...] = bf16(f32(base[...]) - turned[...])
     own_out[...] = own[...] - turned[own_block()]
 
 
@@ -351,60 +339,73 @@
 OWN = ((BLOCK, COLS), F32, pltpu.VMEM)
 
 
-def sum_slab(step, parts, taught):
-    whole = ((SLAB, parts.shape[2]), B16, pltpu.VMEM)
-    slab, own = call(
-        functools.partial(sum_over_y, step), [], [], [], [held(parts), held(taught)], [whole, OWN]
-    )
-    near = [held(own), held(slab), held(over_z(slab, 0))]
-    return call(add_slab, [], [], [], near, [whole, OWN])
+WHOLE = ((SLAB, COLS), B16, pltpu.VMEM)
+SPREAD = ((N_Y, SLAB, COLS), B16, pltpu.HBM)
+
+
+def add_z(slab, own, step, body, out, before=None):
+    got = over_z(slab, step)
+    if before is not None:
+        got, _ = lax.optimization_barrier((got, before))
+    return call(body, [], [], [], [held(own), held(slab), held(got)], [out, OWN])
 
 
 def local(inputs, targets, numerator, momentum, received, push_weight, received_weight, mix_share):
     push, push_got, mix = push_weight, received_weight, mix_share
     state = [(numerator, 0), (received, 0), (momentum, 0)]
 
-    part_own, message, mine = call(
-        prepare,
-        [push],
-        [inputs] + state + [targets],
-        [],
-        [],
-        [
-            ((TOKENS, COLS), B16, pltpu.VMEM),
-            ((MESSAGE, WIDTH), B16, pltpu.VMEM),
-            ((2 * TOKENS, WIDTH), B16, pltpu.HBM),
-        ],
+    part = ((TOKENS, COLS), B16, pltpu.VMEM)
+    part_far, part_own = call(
+        first_values, [push], [(inputs, 0), (numerator, 0)], [], [], [part, part]
+    )
+    near = [held(part_own), held(swap_core(part_far))]
+    (part1,) = call(add_parts, [], [], [], near, [((TOKENS, COLS), B16, pltpu.HBM)])
+
+    later, _ = lax.optimization_barrier((targets, part_own))
+    message, mine = call(
+        make_message,
+        [],
+        [inputs] + state + [later],
+        [],
+        [],
+        [((MESSAGE, WIDTH), B16, pltpu.VMEM), ((2 * TOKENS, WIDTH), B16, pltpu.HBM)],
     )
     got = swap_core(message)
-    (part1,) = call(
-        add_parts,
-        [],
-        [],
-        [],
-        [got, held(part_own)],
-        [((TOKENS, COLS), B16, pltpu.HBM)],
-    )
-    targets, part1 = lax.optimization_barrier((targets, part1))
-
-    part2, taught = call(
+    taught = [later, (got, pl.ds(T_AT, 4 * PADDED))]
+
+    parts1 = over_y(part1.reshape(N_Y, SLAB, COLS))
+    slab, own1 = call(
+        functools.partial(sum_over_y, 0), [], taught, [], [held(parts1)], [WHOLE, OWN]
+    )
+
+    mine, _ = lax.optimization_barrier((mine, slab))
+    (part2,) = call(
         second_values,
         [push, push_got, mix],
-        state + [targets, mine, (got, pl.ds(0, P_AT))],
-        [],
-        [],
-        [((TOKENS, COLS + HALF), B16, pltpu.HBM), ((2, BLOCK, COLS), F32, pltpu.VMEM)],
-    )
-
-    spread = ((N_Y, SLAB, COLS), B16, pltpu.HBM)
+        state + [mine, (got, pl.ds(0, T_AT))],
+        [],
+        [],
+        [((TOKENS, COLS + HALF), B16, pltpu.HBM)],
+    )
+    slab, own1 = add_z(slab, own1, 0, add_slab, WHOLE, part2)
+    part2, _ = lax.optimization_barrier((part2, slab))
     parts2 = over_y(part2.reshape(N_Y, SLAB, COLS + HALF))
-    slab1, own1 = sum_slab(0, over_y(part1.reshape(N_Y, SLAB, COLS)), taught)
-    parts2, _ = lax.optimization_barrier((parts2, slab1))
-    near = [held(own1), held(slab1), held(over_z(slab1, 1))]
-    sent, own1 = call(add_and_spread, [], [], [], near, [spread, OWN])
+    sent, own1 = add_z(slab, own1, 1, add_and_spread, SPREAD)
     all1 = over_y(sent).reshape(TOKENS, COLS)
 
-    slab2, own2 = sum_slab(1, parts2, taught)
+    parts2, _ = lax.optimization_barrier((parts2, sent))
+    base, own2, gram = call(
+        functools.partial(sum_over_y, 1),
+        [],
+        taught,
+        [],
+        [held(parts2)],
+        [WHOLE, OWN, ((SLAB, HALF), B16, pltpu.VMEM)],
+    )
+    near = [held(own2), all1, held(gram), held(swap_core(gram)), held(base)]
+    slab, own2 = call(
+        second_residual, [push, push_got, mix], [], [], near, [WHOLE, OWN], [((SLAB, COLS), F32)]
+    )
     near, far, ready = call(
         first_gradient,
         [push, mix],
@@ -412,33 +413,17 @@
         [],
         [all1],
         [
-            ((WIDTH + EXTRA, COLS), B16, pltpu.HBM),
-            ((WIDTH, COLS), B16, pltpu.HBM),
+            ((WIDTH + EXTRA, COLS), B16, pltpu.VMEM),
+            ((WIDTH, COLS), B16, pltpu.VMEM),
             ((2 * WIDTH, COLS), F32, pltpu.HBM),
         ],
     )
-    slab2_got, _ = lax.optimization_barrier((over_z(slab2, 1), far))
+    slab, own2 = add_z(slab, own2, 0, add_slab, WHOLE, far)
+    sent, own2 = add_z(slab, own2, 1, add_and_spread, SPREAD)
+    all2 = over_y(sent).reshape(TOKENS, COLS)
+    near, far, _ = lax.optimization_barrier((near, far, sent))
     arrived, arrived_far = to_group(near, 1), to_group_other(far, 1)
-    ahead2, gram, own2 = call(
-        add_and_part,
-        [],
-        [],
-        [],
-        [held(own2), held(slab2), held(slab2_got)],
-        [((SLAB, COLS), B16, pltpu.VMEM), ((SLAB, HALF), B16, pltpu.VMEM), OWN],
-    )
-    gram_got = held(swap_core(gram))
-    gram_got, arrived, arrived_far = lax.optimization_barrier((gram_got, arrived, arrived_far))
-    sent, own2 = call(
-        second_residual,
-        [push, push_got, mix],
-        [],
-        [],
-        [held(own2), all1, held(gram), held(gram_got), held(ahead2)],
-        [spread, OWN],
-        [((SLAB, COLS), F32)],
-    )
-    all2 = over_y(sent).reshape(TOKENS, COLS)
+    all2, arrived, arrived_far = lax.optimization_barrier((all2, arrived, arrived_far))
 
     far, near, half, message = call(
         second_gradient,

time: 193 us -> 182 us (0.943)
  waiting for transfers between devices: 69.8 us -> 56.1 us
  Pallas kernels: 23.4 us -> 25.7 us
    ppermute x4, waiting for transfers between devices: 26.1 us -> 16.4 us  [over_z(): return lax.ppermute(value, ('z_hi', 'core'), z_pairs(step))]
    ppermute x2, waiting for transfers between devices: 33 us -> 29.1 us  [to_group_other(): return lax.ppermute(value, GROUP + ('core',), pairs)]
    all_to_all x3, starting transfers between devices: 11.2 us -> 14.7 us  [over_y(): return lax.all_to_all(value, 'y', 0, 0, tiled=True)]
    ppermute x3 -> x4, starting transfers between devices: 19.2 us -> 16.1 us  [swap_core(): return lax.ppermute(value, 'core', [(0, 1), (1, 0)])]
    ppermute x4, starting transfers between devices: 32 us -> 29.5 us  [over_z(): return lax.ppermute(value, ('z_hi', 'core'), z_pairs(step))]
    pallas_call x14 -> x15, Pallas kernels: 23.4 us -> 25.7 us  [call(): pl.pallas_call(kernel, out_shape=result, in_specs=[SMEM] * first + [HBM]...]
    ppermute x2, starting transfers between devices: 3.84 us -> 5.8 us  [to_group(): lax.ppermute(value, GROUP, [(i, (i + hop) % count) for i in range(count)])]
    ppermute x3 -> x4, waiting for transfers between devices: 4.61 us -> 2.69 us  [swap_core(): return lax.ppermute(value, 'core', [(0, 1), (1, 0)])]
  transfers between devices with their start and end apart: 14 -> 15, of which waited for: 7 -> 7; matrix products, arithmetic and copies ran while one was open for 0% -> 0% of each run, Pallas kernels for 7% -> 8%
where the time goes in v8:
time: 182 us; the launch traced here: 181 us
  starting transfers between devices  80.6 us (44%)
  waiting for transfers between devices  56.1 us (31%)
  Pallas kernels  25.7 us (14%)
  blocking collectives  15.5 us (9%)
  between operations  2.18 us (1%)
    ppermute x4, starting transfers between devices, over_z(): return lax.ppermute(value, ('z_hi', 'core'), z_pairs(step))  29.5 us
    ppermute x2, waiting for transfers between devices, to_group_other(): return lax.ppermute(value, GROUP + ('core',), pairs)  29.1 us
    pallas_call x15, Pallas kernels, call(): pl.pallas_call(kernel, out_shape=result, in_specs=[SMEM] * first + [HBM]...  25.7 us
    ppermute x4, waiting for transfers between devices, over_z(): return lax.ppermute(value, ('z_hi', 'core'), z_pairs(step))  16.4 us
    ppermute x4, starting transfers between devices, swap_core(): return lax.ppermute(value, 'core', [(0, 1), (1, 0)])  16.1 us
    all_to_all x1, blocking collectives, over_y(): return lax.all_to_all(value, 'y', 0, 0, tiled=True)  15.5 us
    all_to_all x3, starting transfers between devices, over_y(): return lax.all_to_all(value, 'y', 0, 0, tiled=True)  14.7 us
    ppermute x2, starting transfers between devices, to_group_other(): return lax.ppermute(value, GROUP + ('core',), pairs)  14.5 us
  transfers between devices with their start and end apart: 15, of which 7 were waited for; matrix products, arithmetic and copies ran while one was open for 0% of the time, Pallas kernels for 8%

profile of v8, /device:TPU:1, one launch (start us, length us, event | category | flops | bytes accessed | tf_op | source)
XLA Modules:
  0.0 181.4 jit_solution(12754701812332050975)
XLA Ops:
  3.1 2.8 %make_message.1 = (bf16[3712,256]{1,0:T(8,128)(2,1)S(1)}, bf16[1536,256]{1,0:T(8,128)(2,1)}) custom-call(bf16[2,768,256]{2,1,0:T(8,128)(2,1)} %refs_0_.7, bf16[1,256,1024]{2,1,0:T(8,128)(2,1)} %refs_2_.10, bf16[1,256,1024]{2,1,0:T(8,128)(2,1)} %refs_3_.5, f32[1,256,1024]{2,1,0:T(8,128)} %refs_4_.4, bf16[2,24,1024]{2,1,0:T(8,128)(2,1)} %refs_0_.9), custom_call_target="tpu_custom_call" | custom-call | bytes 5668864 | tf_op jit(solution)/shard_map/make_message/pallas_call | solution.py:291
  5.9 8.8 %collective-permute-start = (bf16[3712,256]{1,0:T(8,128)(2,1)S(1)}, bf16[3712,256]{1,0:T(8,128)(2,1)S(1)}, u32[]{:S(2)}, u32[]{:S(2)}) collective-permute-start(bf16[3712,256]{1,0:T(8,128)(2,1)S(1)} %get-tuple-element.52), channel_id=1, source_target_pairs={{0,1},{1,0},{2,3},{3,2},{4,5},{5,4},{6,7},{7,6},{8,9},{9,8},{10,11... | collective-permute-start | bytes 5701640 | tf_op jit(solution)/shard_map/ppermute | solution.py:325
  16.6 2.7 %collective-permute-done.1.refs_1_ = bf16[768,512]{1,0:T(8,128)(2,1)S(1)} collective-permute-done((bf16[768,512]{1,0:T(8,128)(2,1)S(1)}, bf16[768,512]{1,0:T(8,128)(2,1)S(1)}, u32[]{:S(2)}, u32[]{:S(2)}) %collective-permute-start.1) | collective-permute-done | bytes 786464 | tf_op jit(solution)/shard_map/ppermute | solution.py:325
  20.4 15.5 %all_to_all.20.refs_2_ = bf16[4,192,512]{2,1,0:T(8,128)(2,1)S(1)} all-to-all(bf16[4,192,512]{2,1,0:T(8,128)(2,1)} %bitcast.8), channel_id=1, replica_groups=mesh['x'=4,'z_lo'=4,'z_hi'=4,'y'=4,'core'=2] {'y'}, dimensions={0} | all-to-all | bytes 1572864 | tf_op jit(solution)/shard_map/all_to_all | solution.py:321
  38.2 7.2 %collective-permute-start.2 = (bf16[192,512]{1,0:T(8,128)(2,1)S(1)}, bf16[192,512]{1,0:T(8,128)(2,1)S(1)}, u32[]{:S(2)}, u32[]{:S(2)}) collective-permute-start(bf16[192,512]{1,0:T(8,128)(2,1)S(1)} %get-tuple-element.54.refs_1_), channel_id=1, source_target_pairs={{0,8},{1,25},{8,0},{9,17},{16,24},{17,9},{24,16},{25,1},{2,10},{3,... | collective-permute-start | bytes 589832 | tf_op jit(solution)/shard_map/ppermute | solution.py:317
  46.1 5.2 %second_values.1 = bf16[768,896]{1,0:T(8,128)(2,1)} custom-call(f32[1]{0:T(128)S(6)} %copy.13.refs_0_, f32[1]{0:T(128)S(6)} %copy.14.refs_1_, s32[1,2]{1,0:T(1,128)S(1)} %copy-done, bf16[1,256,1024]{2,1,0:T(8,128)(2,1)} %refs_2_.10, bf16[1,256,1024]{2,1,0:T(8,128)(2,1)} %refs_3_.5, f32[1,256,1024]{2,1,0:T(8,128)} %refs_4_.4, ...), custom_call_target="tpu_custom_call" | custom-call | bytes 6160384 | tf_op jit(solution)/shard_map/second_values/pallas_call | solution.py:291
  52.2 3.6 %all-to-all-start.2 = ((bf16[4,192,896]{2,1,0:T(8,128)(2,1)}), bf16[4,192,896]{2,1,0:T(8,128)(2,1)S(1)}, u32[]{:S(2)}, u32[]{:S(2)}) async-start(bf16[4,192,896]{2,1,0:T(8,128)(2,1)} %bitcast.7), calls=%async_computation.2 | async-start | bytes 2752512 | tf_op jit(solution)/shard_map/all_to_all | solution.py:321
  55.8 7.8 %collective-permute-start.3 = (bf16[192,512]{1,0:T(8,128)(2,1)S(1)}, bf16[192,512]{1,0:T(8,128)(2,1)S(1)}, u32[]{:S(2)}, u32[]{:S(2)}) collective-permute-start(bf16[192,512]{1,0:T(8,128)(2,1)S(1)} %get-tuple-element.59.refs_1_), channel_id=1, source_target_pairs={{0,24},{1,9},{8,16},{9,1},{16,8},{17,25},{24,0},{25,17},{2,26},{3,... | collective-permute-start | bytes 589832 | tf_op jit(solution)/shard_map/ppermute | solution.py:317
  63.6 9.6 %collective-permute-done.3.refs_2_ = bf16[192,512]{1,0:T(8,128)(2,1)S(1)} collective-permute-done((bf16[192,512]{1,0:T(8,128)(2,1)S(1)}, bf16[192,512]{1,0:T(8,128)(2,1)S(1)}, u32[]{:S(2)}, u32[]{:S(2)}) %collective-permute-start.3) | collective-permute-done | bytes 196640 | tf_op jit(solution)/shard_map/ppermute | solution.py:317
  74.1 4.2 %all-to-all-start.1 = ((bf16[4,192,512]{2,1,0:T(8,128)(2,1)}), bf16[4,192,512]{2,1,0:T(8,128)(2,1)S(1)}, u32[]{:S(2)}, u32[]{:S(2)}) async-start(bf16[4,192,512]{2,1,0:T(8,128)(2,1)} %get-tuple-element.60), calls=%async_computation.1 | async-start | bytes 1572864 | tf_op jit(solution)/shard_map/all_to_all | solution.py:321
  79.5 2.6 %collective-permute-start.4 = (bf16[192,384]{1,0:T(8,128)(2,1)S(1)}, bf16[192,384]{1,0:T(8,128)(2,1)S(1)}, u32[]{:S(2)}, u32[]{:S(2)}) collective-permute-start(bf16[192,384]{1,0:T(8,128)(2,1)S(1)} %get-tuple-element.66.refs_5_), channel_id=1, source_target_pairs={{0,1},{1,0},{2,3},{3,2},{4,5},{5,4},{6,7},{7,6},{8,9},{9,8},{10,11... | collective-permute-start | bytes 442376 | tf_op jit(solution)/shard_map/ppermute | solution.py:325
  82.1 8.0 %all-to-all-done.1 = bf16[4,192,512]{2,1,0:T(8,128)(2,1)S(1)} async-done(((bf16[4,192,512]{2,1,0:T(8,128)(2,1)}), bf16[4,192,512]{2,1,0:T(8,128)(2,1)S(1)}, u32[]{:S(2)}, u32[]{:S(2)}) %all-to-all-start.1) | async-done | bytes 786464 | tf_op jit(solution)/shard_map/all_to_all | solution.py:321
  91.0 9.0 %collective-permute-start.5 = (bf16[192,512]{1,0:T(8,128)(2,1)S(1)}, bf16[192,512]{1,0:T(8,128)(2,1)S(1)}, u32[]{:S(2)}, u32[]{:S(2)}) collective-permute-start(bf16[192,512]{1,0:T(8,128)(2,1)S(1)} %get-tuple-element.69.refs_1_), channel_id=1, source_target_pairs={{0,8},{1,25},{8,0},{9,17},{16,24},{17,9},{24,16},{25,1},{2,10},{3,... | collective-permute-start | bytes 589832 | tf_op jit(solution)/shard_map/ppermute | solution.py:317
  100.0 4.7 %first_gradient.1 = (bf16[272,512]{1,0:T(8,128)(2,1)S(1)}, bf16[256,512]{1,0:T(8,128)(2,1)S(1)}, f32[512,512]{1,0:T(8,128)}) custom-call(f32[1]{0:T(128)S(6)} %copy.13.refs_0_, s32[1,2]{1,0:T(1,128)S(1)} %copy-done, bf16[1,256,1024]{2,1,0:T(8,128)(2,1)} %refs_2_.10, bf16[1,256,1024]{2,1,0:T(8,128)(2,1)} %refs_3_.5, f32[1,256,1024]{2,1,0:T(8,128)} %refs_4_.4, ...), custom_call_target="tpu_custom_call" | custom-call | bytes 7159808 | tf_op jit(solution)/shard_map/first_gradient/pallas_call | solution.py:291
  104.8 5.5 %collective-permute-start.6 = (bf16[192,512]{1,0:T(8,128)(2,1)S(1)}, bf16[192,512]{1,0:T(8,128)(2,1)S(1)}, u32[]{:S(2)}, u32[]{:S(2)}) collective-permute-start(bf16[192,512]{1,0:T(8,128)(2,1)S(1)} %get-tuple-element.73.refs_1_), channel_id=1, source_target_pairs={{0,24},{1,9},{8,16},{9,1},{16,8},{17,25},{24,0},{25,17},{2,26},{3,... | collective-permute-start | bytes 589832 | tf_op jit(solution)/shard_map/ppermute | solution.py:317
  110.3 6.0 %collective-permute-done.6.refs_2_ = bf16[192,512]{1,0:T(8,128)(2,1)S(1)} collective-permute-done((bf16[192,512]{1,0:T(8,128)(2,1)S(1)}, bf16[192,512]{1,0:T(8,128)(2,1)S(1)}, u32[]{:S(2)}, u32[]{:S(2)}) %collective-permute-start.6) | collective-permute-done | bytes 196640 | tf_op jit(solution)/shard_map/ppermute | solution.py:317
  117.2 6.9 %all-to-all-start.3 = ((bf16[4,192,512]{2,1,0:T(8,128)(2,1)}), bf16[4,192,512]{2,1,0:T(8,128)(2,1)S(1)}, u32[]{:S(2)}, u32[]{:S(2)}) async-start(bf16[4,192,512]{2,1,0:T(8,128)(2,1)} %get-tuple-element.75), calls=%async_computation.3 | async-start | bytes 1572864 | tf_op jit(solution)/shard_map/all_to_all | solution.py:321
  124.1 3.9 %collective-permute-start.7 = (bf16[272,512]{1,0:T(8,128)(2,1)S(1)}, bf16[272,512]{1,0:T(8,128)(2,1)S(1)}, u32[]{:S(2)}, u32[]{:S(2)}) collective-permute-start(bf16[272,512]{1,0:T(8,128)(2,1)S(1)} %get-tuple-element.77), channel_id=1, source_target_pairs={{0,32},{32,64},{64,96},{96,128},{128,160},{160,192},{192,224},{224... | collective-permute-start | bytes 835592 | tf_op jit(solution)/shard_map/ppermute | solution.py:330
  128.0 9.6 %collective-permute-start.8 = (bf16[256,512]{1,0:T(8,128)(2,1)S(1)}, bf16[256,512]{1,0:T(8,128)(2,1)S(1)}, u32[]{:S(2)}, u32[]{:S(2)}) collective-permute-start(bf16[256,512]{1,0:T(8,128)(2,1)S(1)} %get-tuple-element.78), channel_id=1, source_target_pairs={{0,33},{1,32},{32,65},{33,64},{64,97},{65,96},{96,129},{97,128},{1... | collective-permute-start | bytes 786440 | tf_op jit(solution)/shard_map/ppermute | solution.py:336
  137.6 9.1 %collective-permute-done.8.refs_4_ = bf16[256,512]{1,0:T(8,128)(2,1)S(1)} collective-permute-done((bf16[256,512]{1,0:T(8,128)(2,1)S(1)}, bf16[256,512]{1,0:T(8,128)(2,1)S(1)}, u32[]{:S(2)}, u32[]{:S(2)}) %collective-permute-start.8) | collective-permute-done | bytes 262176 | tf_op jit(solution)/shard_map/ppermute | solution.py:336
  146.6 2.6 %second_gradient.1 = (bf16[256,512]{1,0:T(8,128)(2,1)S(1)}, bf16[272,512]{1,0:T(8,128)(2,1)S(1)}, f32[256,512]{1,0:T(8,128)S(1)}, f32[304,512]{1,0:T(8,128)S(1)}) custom-call(f32[1]{0:T(128)S(6)} %copy.13.refs_0_, f32[1]{0:T(128)S(6)} %copy.14.refs_1_, s32[1,2]{1,0:T(1,128)S(1)} %copy-done, f32[512,512]{1,0:T(8,128)} %get-tuple-element.61.refs_3_, ...), custom_call_target="tpu_custom_call" | custom-call | bytes 6406144 | tf_op jit(solution)/shard_map/second_gradient/pallas_call | solution.py:291
  149.3 2.9 %collective-permute-start.10 = (f32[304,512]{1,0:T(8,128)S(1)}, f32[304,512]{1,0:T(8,128)S(1)}, u32[]{:S(2)}, u32[]{:S(2)}) collective-permute-start(f32[304,512]{1,0:T(8,128)S(1)} %get-tuple-element.84), channel_id=1, source_target_pairs={{0,1},{1,0},{2,3},{3,2},{4,5},{5,4},{6,7},{7,6},{8,9},{9,8},{10,11... | collective-permute-start | bytes 1867784 | tf_op jit(solution)/shard_map/ppermute | solution.py:325
  154.1 4.9 %collective-permute-start.9 = (bf16[256,512]{1,0:T(8,128)(2,1)S(1)}, bf16[256,512]{1,0:T(8,128)(2,1)S(1)}, u32[]{:S(2)}, u32[]{:S(2)}) collective-permute-start(bf16[256,512]{1,0:T(8,128)(2,1)S(1)} %get-tuple-element.80), channel_id=1, source_target_pairs={{0,65},{1,64},{32,97},{33,96},{64,129},{65,128},{96,161},{97,160},... | collective-permute-start | bytes 786440 | tf_op jit(solution)/shard_map/ppermute | solution.py:336
  160.5 20.0 %collective-permute-done.9.refs_1_ = bf16[256,512]{1,0:T(8,128)(2,1)S(1)} collective-permute-done((bf16[256,512]{1,0:T(8,128)(2,1)S(1)}, bf16[256,512]{1,0:T(8,128)(2,1)S(1)}, u32[]{:S(2)}, u32[]{:S(2)}) %collective-permute-start.9) | collective-permute-done | bytes 262176 | tf_op jit(solution)/shard_map/ppermute | solution.py:336
  (26 shorter events, 16.3 us)
Async XLA Ops:
  5.9 30.0 %collective-permute-start = (bf16[3712,256]{1,0:T(8,128)(2,1)S(1)}, bf16[3712,256]{1,0:T(8,128)(2,1)S(1)}, u32[]{:S(2)}, u32[]{:S(2)}) collective-permute-start(bf16[3712,256]{1,0:T(8,128)(2,1)S(1)} %get-tuple-element.52), channel_id=1, source_target_pairs={{0,1},{1,0},{2,3},{3,2},{4,5},{5,4},{6,7},{7,6},{8,9},{9,8},{10,11... | collective-permute-start | bytes 5701640 | tf_op jit(solution)/shard_map/ppermute | solution.py:325
  14.7 4.6 %collective-permute-start.1 = (bf16[768,512]{1,0:T(8,128)(2,1)S(1)}, bf16[768,512]{1,0:T(8,128)(2,1)S(1)}, u32[]{:S(2)}, u32[]{:S(2)}) collective-permute-start(bf16[768,512]{1,0:T(8,128)(2,1)S(1)} %get-tuple-element.53), channel_id=1, source_target_pairs={{0,1},{1,0},{2,3},{3,2},{4,5},{5,4},{6,7},{7,6},{8,9},{9,8},{10,11... | collective-permute-start | bytes 2359304 | tf_op jit(solution)/shard_map/ppermute | solution.py:325
  20.4 25.7 %copy-start = (s32[1,2]{1,0:T(1,128)S(1)}, s32[1,2]{1,0:T(1,128)}, u32[]{:S(2)}) copy-start(s32[1,2]{1,0:T(1,128)} %refs_2_.13) | copy-start | bytes 28
  35.9 1.3 copy-start.1
  38.2 13.9 %collective-permute-start.2 = (bf16[192,512]{1,0:T(8,128)(2,1)S(1)}, bf16[192,512]{1,0:T(8,128)(2,1)S(1)}, u32[]{:S(2)}, u32[]{:S(2)}) collective-permute-start(bf16[192,512]{1,0:T(8,128)(2,1)S(1)} %get-tuple-element.54.refs_1_), channel_id=1, source_target_pairs={{0,8},{1,25},{8,0},{9,17},{16,24},{17,9},{24,16},{25,1},{2,10},{3,... | collective-permute-start | bytes 589832 | tf_op jit(solution)/shard_map/ppermute | solution.py:317
  52.2 21.9 %all-to-all-start.2 = ((bf16[4,192,896]{2,1,0:T(8,128)(2,1)}), bf16[4,192,896]{2,1,0:T(8,128)(2,1)S(1)}, u32[]{:S(2)}, u32[]{:S(2)}) async-start(bf16[4,192,896]{2,1,0:T(8,128)(2,1)} %bitcast.7), calls=%async_computation.2 | async-start | bytes 2752512 | tf_op jit(solution)/shard_map/all_to_all | solution.py:321
  55.8 17.4 %collective-permute-start.3 = (bf16[192,512]{1,0:T(8,128)(2,1)S(1)}, bf16[192,512]{1,0:T(8,128)(2,1)S(1)}, u32[]{:S(2)}, u32[]{:S(2)}) collective-permute-start(bf16[192,512]{1,0:T(8,128)(2,1)S(1)} %get-tuple-element.59.refs_1_), channel_id=1, source_target_pairs={{0,24},{1,9},{8,16},{9,1},{16,8},{17,25},{24,0},{25,17},{2,26},{3,... | collective-permute-start | bytes 589832 | tf_op jit(solution)/shard_map/ppermute | solution.py:317
  74.1 15.9 %all-to-all-start.1 = ((bf16[4,192,512]{2,1,0:T(8,128)(2,1)}), bf16[4,192,512]{2,1,0:T(8,128)(2,1)S(1)}, u32[]{:S(2)}, u32[]{:S(2)}) async-start(bf16[4,192,512]{2,1,0:T(8,128)(2,1)} %get-tuple-element.60), calls=%async_computation.1 | async-start | bytes 1572864 | tf_op jit(solution)/shard_map/all_to_all | solution.py:321
  79.5 10.6 %collective-permute-start.4 = (bf16[192,384]{1,0:T(8,128)(2,1)S(1)}, bf16[192,384]{1,0:T(8,128)(2,1)S(1)}, u32[]{:S(2)}, u32[]{:S(2)}) collective-permute-start(bf16[192,384]{1,0:T(8,128)(2,1)S(1)} %get-tuple-element.66.refs_5_), channel_id=1, source_target_pairs={{0,1},{1,0},{2,3},{3,2},{4,5},{5,4},{6,7},{7,6},{8,9},{9,8},{10,11... | collective-permute-start | bytes 442376 | tf_op jit(solution)/shard_map/ppermute | solution.py:325
  91.0 13.7 %collective-permute-start.5 = (bf16[192,512]{1,0:T(8,128)(2,1)S(1)}, bf16[192,512]{1,0:T(8,128)(2,1)S(1)}, u32[]{:S(2)}, u32[]{:S(2)}) collective-permute-start(bf16[192,512]{1,0:T(8,128)(2,1)S(1)} %get-tuple-element.69.refs_1_), channel_id=1, source_target_pairs={{0,8},{1,25},{8,0},{9,17},{16,24},{17,9},{24,16},{25,1},{2,10},{3,... | collective-permute-start | bytes 589832 | tf_op jit(solution)/shard_map/ppermute | solution.py:317
  104.8 11.5 %collective-permute-start.6 = (bf16[192,512]{1,0:T(8,128)(2,1)S(1)}, bf16[192,512]{1,0:T(8,128)(2,1)S(1)}, u32[]{:S(2)}, u32[]{:S(2)}) collective-permute-start(bf16[192,512]{1,0:T(8,128)(2,1)S(1)} %get-tuple-element.73.refs_1_), channel_id=1, source_target_pairs={{0,24},{1,9},{8,16},{9,1},{16,8},{17,25},{24,0},{25,17},{2,26},{3,... | collective-permute-start | bytes 589832 | tf_op jit(solution)/shard_map/ppermute | solution.py:317
  117.2 29.4 %all-to-all-start.3 = ((bf16[4,192,512]{2,1,0:T(8,128)(2,1)}), bf16[4,192,512]{2,1,0:T(8,128)(2,1)S(1)}, u32[]{:S(2)}, u32[]{:S(2)}) async-start(bf16[4,192,512]{2,1,0:T(8,128)(2,1)} %get-tuple-element.75), calls=%async_computation.3 | async-start | bytes 1572864 | tf_op jit(solution)/shard_map/all_to_all | solution.py:321
  124.1 22.5 %collective-permute-start.7 = (bf16[272,512]{1,0:T(8,128)(2,1)S(1)}, bf16[272,512]{1,0:T(8,128)(2,1)S(1)}, u32[]{:S(2)}, u32[]{:S(2)}) collective-permute-start(bf16[272,512]{1,0:T(8,128)(2,1)S(1)} %get-tuple-element.77), channel_id=1, source_target_pairs={{0,32},{32,64},{64,96},{96,128},{128,160},{160,192},{192,224},{224... | collective-permute-start | bytes 835592 | tf_op jit(solution)/shard_map/ppermute | solution.py:330
  128.0 18.7 %collective-permute-start.8 = (bf16[256,512]{1,0:T(8,128)(2,1)S(1)}, bf16[256,512]{1,0:T(8,128)(2,1)S(1)}, u32[]{:S(2)}, u32[]{:S(2)}) collective-permute-start(bf16[256,512]{1,0:T(8,128)(2,1)S(1)} %get-tuple-element.78), channel_id=1, source_target_pairs={{0,33},{1,32},{32,65},{33,64},{64,97},{65,96},{96,129},{97,128},{1... | collective-permute-start | bytes 786440 | tf_op jit(solution)/shard_map/ppermute | solution.py:336
  149.3 9.7 %collective-permute-start.10 = (f32[304,512]{1,0:T(8,128)S(1)}, f32[304,512]{1,0:T(8,128)S(1)}, u32[]{:S(2)}, u32[]{:S(2)}) collective-permute-start(f32[304,512]{1,0:T(8,128)S(1)} %get-tuple-element.84), channel_id=1, source_target_pairs={{0,1},{1,0},{2,3},{3,2},{4,5},{5,4},{6,7},{7,6},{8,9},{9,8},{10,11... | collective-permute-start | bytes 1867784 | tf_op jit(solution)/shard_map/ppermute | solution.py:325
  152.2 28.4 %collective-permute-start.11 = (bf16[272,512]{1,0:T(8,128)(2,1)S(1)}, bf16[272,512]{1,0:T(8,128)(2,1)S(1)}, u32[]{:S(2)}, u32[]{:S(2)}) collective-permute-start(bf16[272,512]{1,0:T(8,128)(2,1)S(1)} %get-tuple-element.88), channel_id=1, source_target_pairs={{0,64},{32,96},{64,128},{96,160},{128,192},{160,224},{192,256},{22... | collective-permute-start | bytes 835592 | tf_op jit(solution)/shard_map/ppermute | solution.py:330
  154.1 26.5 %collective-permute-start.9 = (bf16[256,512]{1,0:T(8,128)(2,1)S(1)}, bf16[256,512]{1,0:T(8,128)(2,1)S(1)}, u32[]{:S(2)}, u32[]{:S(2)}) collective-permute-start(bf16[256,512]{1,0:T(8,128)(2,1)S(1)} %get-tuple-element.80), channel_id=1, source_target_pairs={{0,65},{1,64},{32,97},{33,96},{64,129},{65,128},{96,161},{97,160},... | collective-permute-start | bytes 786440 | tf_op jit(solution)/shard_map/ppermute | solution.py:336

commit v9 on v8

--- a/solution.py
+++ b/solution.py
@@ -34,8 +34,7 @@
 W_AT = 2 * TOKENS
 REC_AT = W_AT + 2 * WIDTH
 M_AT = REC_AT + 2 * WIDTH
-T_AT = M_AT + 4 * WIDTH
-MESSAGE = T_AT + 4 * PADDED
+MESSAGE = M_AT + 4 * WIDTH
 
 B16, F32 = jnp.bfloat16, jnp.float32
 
@@ -72,16 +71,21 @@
     return [((zh * N_Y + y) * BLOCK, (y * N_Z + zh) * BLOCK) for zh in range(N_Z) for y in range(N_Y)]
 
 
-def first_values(push, x, w, far, own):
+def first_values(push, x, w, targets, far, own):
     core = lax.axis_index("core")
     for out, side in ((far, 1 - core), (own, core)):
         scaled = bf16(f32(w[:, cols_of(side)]) / push[0])
         part = bf16(dot(x[...], scaled) * ROW_SCALE)
         for at, to in by_y():
             out[to : to + BLOCK] = part[at : at + BLOCK]
-
-
-def make_message(x, w, rec, velocity, targets, message, tokens):
+    spare = jnp.zeros((PADDED - ROWS, COLS), jnp.float32)
+    for step in range(2):
+        row = TOKENS + step * PADDED
+        half = jnp.concatenate([f32(targets[step, :, cols_of(1 - core)]), spare], axis=0)
+        far[row : row + PADDED] = bf16(half)
+
+
+def make_message(x, w, rec, velocity, message, tokens):
     far = cols_of(1 - lax.axis_index("core"))
     for step in range(2):
         for at, to in by_y():
@@ -90,20 +94,15 @@
             tokens[row : row + BLOCK] = x[step, at : at + BLOCK]
     old = velocity[:, far]
     high = bf16(old)
-    spare = jnp.zeros((PADDED - ROWS, COLS), jnp.float32)
     halves = [(W_AT, w[:, far]), (REC_AT, rec[:, far]), (M_AT, high)]
     halves += [(M_AT + 2 * WIDTH, bf16(old - f32(high)))]
-    for step in range(2):
-        padded = jnp.concatenate([f32(targets[step, :, far]), spare], axis=0)
-        halves.append((T_AT + 2 * step * PADDED, bf16(padded)))
     for row, half in halves:
-        rows = half.shape[0]
-        message[row : row + rows] = half[:, :WIDTH]
-        message[row + rows : row + 2 * rows] = half[:, WIDTH:]
+        message[row : row + WIDTH] = half[:, :WIDTH]
+        message[row + WIDTH : row + 2 * WIDTH] = half[:, WIDTH:]
 
 
 def add_parts(own, got, out):
-    out[...] = bf16(f32(own[...]) + f32(got[...]))
+    out[...] = bf16(f32(own[...]) + f32(got[:TOKENS]))
 
 
 def tile(mix, w, rec, velocity, got, first, k):
@@ -146,11 +145,7 @@
         total = total + f32(parts[y, rows, :COLS])
     own[...] = total
     near = f32(targets[step, :, cols_of(core)])
-    row = 2 * step * PADDED
-    far = jnp.concatenate(
-        [f32(targets_got[row : row + PADDED]), f32(targets_got[row + PADDED : row + 2 * PADDED])],
-        axis=1,
-    )[:ROWS]
+    far = f32(targets_got[step * PADDED : (step + 1) * PADDED])[:ROWS]
     low, high = jnp.where(core == 0, near, far), jnp.where(core == 0, far, near)
     slab[rows] = bf16(total - jnp.concatenate([low, high], axis=0))
 
@@ -354,24 +349,29 @@
     push, push_got, mix = push_weight, received_weight, mix_share
     state = [(numerator, 0), (received, 0), (momentum, 0)]
 
-    part = ((TOKENS, COLS), B16, pltpu.VMEM)
     part_far, part_own = call(
-        first_values, [push], [(inputs, 0), (numerator, 0)], [], [], [part, part]
-    )
-    near = [held(part_own), held(swap_core(part_far))]
+        first_values,
+        [push],
+        [(inputs, 0), (numerator, 0), targets],
+        [],
+        [],
+        [((TOKENS + 2 * PADDED, COLS), B16, pltpu.VMEM), ((TOKENS, COLS), B16, pltpu.VMEM)],
+    )
+    part_got = swap_core(part_far)
+    near = [held(part_own), held(part_got)]
     (part1,) = call(add_parts, [], [], [], near, [((TOKENS, COLS), B16, pltpu.HBM)])
-
-    later, _ = lax.optimization_barrier((targets, part_own))
+    taught = [targets, part_got[TOKENS:]]
+
+    later, _ = lax.optimization_barrier((numerator, part1))
     message, mine = call(
         make_message,
         [],
-        [inputs] + state + [later],
+        [inputs, (later, 0)] + state[1:],
         [],
         [],
         [((MESSAGE, WIDTH), B16, pltpu.VMEM), ((2 * TOKENS, WIDTH), B16, pltpu.HBM)],
     )
     got = swap_core(message)
-    taught = [later, (got, pl.ds(T_AT, 4 * PADDED))]
 
     parts1 = over_y(part1.reshape(N_Y, SLAB, COLS))
     slab, own1 = call(
@@ -382,7 +382,7 @@
     (part2,) = call(
         second_values,
         [push, push_got, mix],
-        state + [mine, (got, pl.ds(0, T_AT))],
+        state + [mine, got],
         [],
         [],
         [((TOKENS, COLS + HALF), B16, pltpu.HBM)],
@@ -409,7 +409,7 @@
     near, far, ready = call(
         first_gradient,
         [push, mix],
-        state + [(mine, pl.ds(X1_AT, TOKENS)), (got, pl.ds(X1_AT, T_AT - X1_AT))],
+        state + [(mine, pl.ds(X1_AT, TOKENS)), (got, pl.ds(X1_AT, MESSAGE - X1_AT))],
         [],
         [all1],
         [
@@ -421,9 +421,9 @@
     slab, own2 = add_z(slab, own2, 0, add_slab, WHOLE, far)
     sent, own2 = add_z(slab, own2, 1, add_and_spread, SPREAD)
     all2 = over_y(sent).reshape(TOKENS, COLS)
-    near, far, _ = lax.optimization_barrier((near, far, sent))
+    near, _ = lax.optimization_barrier((near, sent))
     arrived, arrived_far = to_group(near, 1), to_group_other(far, 1)
-    all2, arrived, arrived_far = lax.optimization_barrier((all2, arrived, arrived_far))
+    all2, arrived = lax.optimization_barrier((all2, arrived))
 
     far, near, half, message = call(
         second_gradient,

time: 182 us -> 183 us (level)
  waiting for transfers between devices: 56.1 us -> 76.5 us
  blocking collectives: 15.5 us -> 0 us
  starting transfers between devices: 80.6 us -> 75.4 us
    all_to_all x1 -> x0, blocking collectives: 15.5 us -> none  [over_y(): return lax.all_to_all(value, 'y', 0, 0, tiled=True)]
    ppermute x2, waiting for transfers between devices: 0.01 us -> 11.2 us  [to_group(): lax.ppermute(value, GROUP, [(i, (i + hop) % count) for i in range(count)])]
    all_to_all x3 -> x4, waiting for transfers between devices: 7.98 us -> 16.9 us  [over_y(): return lax.all_to_all(value, 'y', 0, 0, tiled=True)]
    ppermute x2, starting transfers between devices: 14.5 us -> 6.48 us  [to_group_other(): return lax.ppermute(value, GROUP + ('core',), pairs)]
    ppermute x4, starting transfers between devices: 16.1 us -> 21.6 us  [swap_core(): return lax.ppermute(value, 'core', [(0, 1), (1, 0)])]
    ppermute x4, waiting for transfers between devices: 16.4 us -> 21.8 us  [over_z(): return lax.ppermute(value, ('z_hi', 'core'), z_pairs(step))]
    ppermute x2, waiting for transfers between devices: 29.1 us -> 24.6 us  [to_group_other(): return lax.ppermute(value, GROUP + ('core',), pairs)]
    all_to_all x3 -> x4, starting transfers between devices: 14.7 us -> 14.9 us  [over_y(): return lax.all_to_all(value, 'y', 0, 0, tiled=True)]
  transfers between devices with their start and end apart: 15 -> 16, of which waited for: 7 -> 11; matrix products, arithmetic and copies ran while one was open for 0% -> 0% of each run, Pallas kernels for 8% -> 8%
where the time goes in v9:
time: 183 us; the launch traced here: 182 us
  waiting for transfers between devices  76.5 us (42%)
  starting transfers between devices  75.4 us (41%)
  Pallas kernels  27 us (15%)
  between operations  2.18 us (1%)
    ppermute x4, starting transfers between devices, over_z(): return lax.ppermute(value, ('z_hi', 'core'), z_pairs(step))  28.2 us
    pallas_call x15, Pallas kernels, call(): pl.pallas_call(kernel, out_shape=result, in_specs=[SMEM] * first + [HBM]...  27 us
    ppermute x2, waiting for transfers between devices, to_group_other(): return lax.ppermute(value, GROUP + ('core',), pairs)  24.6 us
    ppermute x4, waiting for transfers between devices, over_z(): return lax.ppermute(value, ('z_hi', 'core'), z_pairs(step))  21.8 us
    ppermute x4, starting transfers between devices, swap_core(): return lax.ppermute(value, 'core', [(0, 1), (1, 0)])  21.6 us
    all_to_all x4, waiting for transfers between devices, over_y(): return lax.all_to_all(value, 'y', 0, 0, tiled=True)  16.9 us
    all_to_all x4, starting transfers between devices, over_y(): return lax.all_to_all(value, 'y', 0, 0, tiled=True)  14.9 us
    ppermute x2, waiting for transfers between devices, to_group(): lax.ppermute(value, GROUP, [(i, (i + hop) % count) for i in range(count)])  11.2 us
  transfers between devices with their start and end apart: 16, of which 11 were waited for; matrix products, arithmetic and copies ran while one was open for 0% of the time, Pallas kernels for 8%

profile of v9, /device:TPU:1, one launch (start us, length us, event | category | flops | bytes accessed | tf_op | source)
XLA Modules:
  0.0 181.8 jit_solution(943953017018443334)
XLA Ops:
  3.1 8.8 %collective-permute-start = (bf16[832,512]{1,0:T(8,128)(2,1)S(1)}, bf16[832,512]{1,0:T(8,128)(2,1)S(1)}, u32[]{:S(2)}, u32[]{:S(2)}) collective-permute-start(bf16[832,512]{1,0:T(8,128)(2,1)S(1)} %get-tuple-element.48), channel_id=1, source_target_pairs={{0,1},{1,0},{2,3},{3,2},{4,5},{5,4},{6,7},{7,6},{8,9},{9,8},{10,11... | collective-permute-start | bytes 2555912 | tf_op jit(solution)/shard_map/ppermute | solution.py:320
  15.0 4.0 %make_message.1 = (bf16[3584,256]{1,0:T(8,128)(2,1)}, bf16[1536,256]{1,0:T(8,128)(2,1)}) custom-call(bf16[2,768,256]{2,1,0:T(8,128)(2,1)} %refs_0_.9, bf16[1,256,1024]{2,1,0:T(8,128)(2,1)} %refs_2_.10, bf16[1,256,1024]{2,1,0:T(8,128)(2,1)} %refs_3_.7, f32[1,256,1024]{2,1,0:T(8,128)} %refs_4_.3), custom_call_target="tpu_custom_call" | custom-call | bytes 5505024 | tf_op jit(solution)/shard_map/make_message/pallas_call | solution.py:286
  21.3 3.5 %all-to-all-start = ((bf16[4,192,512]{2,1,0:T(8,128)(2,1)}), bf16[4,192,512]{2,1,0:T(8,128)(2,1)S(1)}, u32[]{:S(2)}, u32[]{:S(2)}) async-start(bf16[4,192,512]{2,1,0:T(8,128)(2,1)} %bitcast), calls=%async_computation | async-start | bytes 1572864 | tf_op jit(solution)/shard_map/all_to_all | solution.py:316
  25.4 11.6 %all-to-all-done.refs_2_ = bf16[4,192,512]{2,1,0:T(8,128)(2,1)S(1)} async-done(((bf16[4,192,512]{2,1,0:T(8,128)(2,1)}), bf16[4,192,512]{2,1,0:T(8,128)(2,1)S(1)}, u32[]{:S(2)}, u32[]{:S(2)}) %all-to-all-start) | async-done | bytes 786464 | tf_op jit(solution)/shard_map/all_to_all | solution.py:316
  38.1 7.5 %collective-permute-start.2 = (bf16[192,512]{1,0:T(8,128)(2,1)S(1)}, bf16[192,512]{1,0:T(8,128)(2,1)S(1)}, u32[]{:S(2)}, u32[]{:S(2)}) collective-permute-start(bf16[192,512]{1,0:T(8,128)(2,1)S(1)} %get-tuple-element.51.refs_1_), channel_id=1, source_target_pairs={{0,8},{1,25},{8,0},{9,17},{16,24},{17,9},{24,16},{25,1},{2,10},{3,... | collective-permute-start | bytes 589832 | tf_op jit(solution)/shard_map/ppermute | solution.py:312
  46.3 5.2 %second_values.1 = bf16[768,896]{1,0:T(8,128)(2,1)} custom-call(f32[1]{0:T(128)S(6)} %copy.13.refs_0_, f32[1]{0:T(128)S(6)} %copy.14.refs_1_, s32[1,2]{1,0:T(1,128)S(1)} %copy-done, bf16[1,256,1024]{2,1,0:T(8,128)(2,1)} %refs_2_.10, bf16[1,256,1024]{2,1,0:T(8,128)(2,1)} %refs_3_.7, f32[1,256,1024]{2,1,0:T(8,128)} %refs_4_.3, ...), custom_call_target="tpu_custom_call" | custom-call | bytes 6094848 | tf_op jit(solution)/shard_map/second_values/pallas_call | solution.py:286
  53.2 3.6 %all-to-all-start.2 = ((bf16[4,192,896]{2,1,0:T(8,128)(2,1)}), bf16[4,192,896]{2,1,0:T(8,128)(2,1)S(1)}, u32[]{:S(2)}, u32[]{:S(2)}) async-start(bf16[4,192,896]{2,1,0:T(8,128)(2,1)} %bitcast.7), calls=%async_computation.2 | async-start | bytes 2752512 | tf_op jit(solution)/shard_map/all_to_all | solution.py:316
  56.7 7.0 %collective-permute-start.3 = (bf16[192,512]{1,0:T(8,128)(2,1)S(1)}, bf16[192,512]{1,0:T(8,128)(2,1)S(1)}, u32[]{:S(2)}, u32[]{:S(2)}) collective-permute-start(bf16[192,512]{1,0:T(8,128)(2,1)S(1)} %get-tuple-element.57.refs_1_), channel_id=1, source_target_pairs={{0,24},{1,9},{8,16},{9,1},{16,8},{17,25},{24,0},{25,17},{2,26},{3,... | collective-permute-start | bytes 589832 | tf_op jit(solution)/shard_map/ppermute | solution.py:312
  63.8 8.6 %collective-permute-done.3.refs_2_ = bf16[192,512]{1,0:T(8,128)(2,1)S(1)} collective-permute-done((bf16[192,512]{1,0:T(8,128)(2,1)S(1)}, bf16[192,512]{1,0:T(8,128)(2,1)S(1)}, u32[]{:S(2)}, u32[]{:S(2)}) %collective-permute-start.3) | collective-permute-done | bytes 196640 | tf_op jit(solution)/shard_map/ppermute | solution.py:312
  73.5 4.4 %all-to-all-start.1 = ((bf16[4,192,512]{2,1,0:T(8,128)(2,1)}), bf16[4,192,512]{2,1,0:T(8,128)(2,1)S(1)}, u32[]{:S(2)}, u32[]{:S(2)}) async-start(bf16[4,192,512]{2,1,0:T(8,128)(2,1)} %get-tuple-element.58), calls=%async_computation.1 | async-start | bytes 1572864 | tf_op jit(solution)/shard_map/all_to_all | solution.py:316
  79.0 3.8 %collective-permute-start.4 = (bf16[192,384]{1,0:T(8,128)(2,1)S(1)}, bf16[192,384]{1,0:T(8,128)(2,1)S(1)}, u32[]{:S(2)}, u32[]{:S(2)}) collective-permute-start(bf16[192,384]{1,0:T(8,128)(2,1)S(1)} %get-tuple-element.64.refs_5_), channel_id=1, source_target_pairs={{0,1},{1,0},{2,3},{3,2},{4,5},{5,4},{6,7},{7,6},{8,9},{9,8},{10,11... | collective-permute-start | bytes 442376 | tf_op jit(solution)/shard_map/ppermute | solution.py:320
  82.8 5.2 %all-to-all-done.1 = bf16[4,192,512]{2,1,0:T(8,128)(2,1)S(1)} async-done(((bf16[4,192,512]{2,1,0:T(8,128)(2,1)}), bf16[4,192,512]{2,1,0:T(8,128)(2,1)S(1)}, u32[]{:S(2)}, u32[]{:S(2)}) %all-to-all-start.1) | async-done | bytes 786464 | tf_op jit(solution)/shard_map/all_to_all | solution.py:316
  88.9 9.9 %collective-permute-start.5 = (bf16[192,512]{1,0:T(8,128)(2,1)S(1)}, bf16[192,512]{1,0:T(8,128)(2,1)S(1)}, u32[]{:S(2)}, u32[]{:S(2)}) collective-permute-start(bf16[192,512]{1,0:T(8,128)(2,1)S(1)} %get-tuple-element.67.refs_1_), channel_id=1, source_target_pairs={{0,8},{1,25},{8,0},{9,17},{16,24},{17,9},{24,16},{25,1},{2,10},{3,... | collective-permute-start | bytes 589832 | tf_op jit(solution)/shard_map/ppermute | solution.py:312
  98.8 4.7 %first_gradient.1 = (bf16[272,512]{1,0:T(8,128)(2,1)S(1)}, bf16[256,512]{1,0:T(8,128)(2,1)S(1)}, f32[512,512]{1,0:T(8,128)}) custom-call(f32[1]{0:T(128)S(6)} %copy.13.refs_0_, s32[1,2]{1,0:T(1,128)S(1)} %copy-done, bf16[1,256,1024]{2,1,0:T(8,128)(2,1)} %refs_2_.10, bf16[1,256,1024]{2,1,0:T(8,128)(2,1)} %refs_3_.7, f32[1,256,1024]{2,1,0:T(8,128)} %refs_4_.3, ...), custom_call_target="tpu_custom_call" | custom-call | bytes 7094272 | tf_op jit(solution)/shard_map/first_gradient/pallas_call | solution.py:286
  104.1 3.7 %collective-permute-start.6 = (bf16[192,512]{1,0:T(8,128)(2,1)S(1)}, bf16[192,512]{1,0:T(8,128)(2,1)S(1)}, u32[]{:S(2)}, u32[]{:S(2)}) collective-permute-start(bf16[192,512]{1,0:T(8,128)(2,1)S(1)} %get-tuple-element.71.refs_1_), channel_id=1, source_target_pairs={{0,24},{1,9},{8,16},{9,1},{16,8},{17,25},{24,0},{25,17},{2,26},{3,... | collective-permute-start | bytes 589832 | tf_op jit(solution)/shard_map/ppermute | solution.py:312
  107.9 11.1 %collective-permute-done.6.refs_2_ = bf16[192,512]{1,0:T(8,128)(2,1)S(1)} collective-permute-done((bf16[192,512]{1,0:T(8,128)(2,1)S(1)}, bf16[192,512]{1,0:T(8,128)(2,1)S(1)}, u32[]{:S(2)}, u32[]{:S(2)}) %collective-permute-start.6) | collective-permute-done | bytes 196640 | tf_op jit(solution)/shard_map/ppermute | solution.py:312
  119.9 3.5 %all-to-all-start.3 = ((bf16[4,192,512]{2,1,0:T(8,128)(2,1)}), bf16[4,192,512]{2,1,0:T(8,128)(2,1)S(1)}, u32[]{:S(2)}, u32[]{:S(2)}) async-start(bf16[4,192,512]{2,1,0:T(8,128)(2,1)} %get-tuple-element.73), calls=%async_computation.3 | async-start | bytes 1572864 | tf_op jit(solution)/shard_map/all_to_all | solution.py:316
  125.4 11.2 %collective-permute-done.7.refs_3_ = bf16[272,512]{1,0:T(8,128)(2,1)S(1)} collective-permute-done((bf16[272,512]{1,0:T(8,128)(2,1)S(1)}, bf16[272,512]{1,0:T(8,128)(2,1)S(1)}, u32[]{:S(2)}, u32[]{:S(2)}) %collective-permute-start.7) | collective-permute-done | bytes 278560 | tf_op jit(solution)/shard_map/ppermute | solution.py:325
  136.6 2.6 %second_gradient.1 = (bf16[256,512]{1,0:T(8,128)(2,1)S(1)}, bf16[272,512]{1,0:T(8,128)(2,1)S(1)}, f32[256,512]{1,0:T(8,128)S(1)}, f32[304,512]{1,0:T(8,128)S(1)}) custom-call(f32[1]{0:T(128)S(6)} %copy.13.refs_0_, f32[1]{0:T(128)S(6)} %copy.14.refs_1_, s32[1,2]{1,0:T(1,128)S(1)} %copy-done, f32[512,512]{1,0:T(8,128)} %get-tuple-element.59.refs_3_, ...), custom_call_target="tpu_custom_call" | custom-call | bytes 6340608 | tf_op jit(solution)/shard_map/second_gradient/pallas_call | solution.py:286
  139.2 6.7 %collective-permute-start.10 = (f32[304,512]{1,0:T(8,128)S(1)}, f32[304,512]{1,0:T(8,128)S(1)}, u32[]{:S(2)}, u32[]{:S(2)}) collective-permute-start(f32[304,512]{1,0:T(8,128)S(1)} %get-tuple-element.80), channel_id=1, source_target_pairs={{0,1},{1,0},{2,3},{3,2},{4,5},{5,4},{6,7},{7,6},{8,9},{9,8},{10,11... | collective-permute-start | bytes 1867784 | tf_op jit(solution)/shard_map/ppermute | solution.py:320
  145.9 2.3 %collective-permute-start.11 = (bf16[272,512]{1,0:T(8,128)(2,1)S(1)}, bf16[272,512]{1,0:T(8,128)(2,1)S(1)}, u32[]{:S(2)}, u32[]{:S(2)}) collective-permute-start(bf16[272,512]{1,0:T(8,128)(2,1)S(1)} %get-tuple-element.84), channel_id=1, source_target_pairs={{0,64},{32,96},{64,128},{96,160},{128,192},{160,224},{192,256},{22... | collective-permute-start | bytes 835592 | tf_op jit(solution)/shard_map/ppermute | solution.py:325
  150.2 4.6 %collective-permute-start.8 = (bf16[256,512]{1,0:T(8,128)(2,1)S(1)}, bf16[256,512]{1,0:T(8,128)(2,1)S(1)}, u32[]{:S(2)}, u32[]{:S(2)}) collective-permute-start(bf16[256,512]{1,0:T(8,128)(2,1)S(1)} %get-tuple-element.77), channel_id=1, source_target_pairs={{0,65},{1,64},{32,97},{33,96},{64,129},{65,128},{96,161},{97,160},... | collective-permute-start | bytes 786440 | tf_op jit(solution)/shard_map/ppermute | solution.py:331
  154.8 9.0 %collective-permute-done.9.refs_4_ = bf16[256,512]{1,0:T(8,128)(2,1)S(1)} collective-permute-done((bf16[256,512]{1,0:T(8,128)(2,1)S(1)}, bf16[256,512]{1,0:T(8,128)(2,1)S(1)}, u32[]{:S(2)}, u32[]{:S(2)}) %collective-permute-start.9) | collective-permute-done | bytes 262176 | tf_op jit(solution)/shard_map/ppermute | solution.py:331
  165.3 15.6 %collective-permute-done.8.refs_1_ = bf16[256,512]{1,0:T(8,128)(2,1)S(1)} collective-permute-done((bf16[256,512]{1,0:T(8,128)(2,1)S(1)}, bf16[256,512]{1,0:T(8,128)(2,1)S(1)}, u32[]{:S(2)}, u32[]{:S(2)}) %collective-permute-start.8) | collective-permute-done | bytes 262176 | tf_op jit(solution)/shard_map/ppermute | solution.py:331
  (26 shorter events, 21.5 us)
Async XLA Ops:
  3.1 10.8 %collective-permute-start = (bf16[832,512]{1,0:T(8,128)(2,1)S(1)}, bf16[832,512]{1,0:T(8,128)(2,1)S(1)}, u32[]{:S(2)}, u32[]{:S(2)}) collective-permute-start(bf16[832,512]{1,0:T(8,128)(2,1)S(1)} %get-tuple-element.48), channel_id=1, source_target_pairs={{0,1},{1,0},{2,3},{3,2},{4,5},{5,4},{6,7},{7,6},{8,9},{9,8},{10,11... | collective-permute-start | bytes 2555912 | tf_op jit(solution)/shard_map/ppermute | solution.py:320
  19.0 27.3 %copy-start = (s32[1,2]{1,0:T(1,128)S(1)}, s32[1,2]{1,0:T(1,128)}, u32[]{:S(2)}) copy-start(s32[1,2]{1,0:T(1,128)} %refs_2_.13) | copy-start | bytes 28
  19.0 27.2 %collective-permute-start.1 = (bf16[3584,256]{1,0:T(8,128)(2,1)}, bf16[3584,256]{1,0:T(8,128)(2,1)}, u32[]{:S(2)}, u32[]{:S(2)}) collective-permute-start(bf16[3584,256]{1,0:T(8,128)(2,1)} %get-tuple-element.53), channel_id=1, source_target_pairs={{0,1},{1,0},{2,3},{3,2},{4,5},{5,4},{6,7},{7,6},{8,9},{9,8},{10,11... | collective-permute-start | bytes 5505032 | tf_op jit(solution)/shard_map/ppermute | solution.py:320
  21.3 15.8 %all-to-all-start = ((bf16[4,192,512]{2,1,0:T(8,128)(2,1)}), bf16[4,192,512]{2,1,0:T(8,128)(2,1)S(1)}, u32[]{:S(2)}, u32[]{:S(2)}) async-start(bf16[4,192,512]{2,1,0:T(8,128)(2,1)} %bitcast), calls=%async_computation | async-start | bytes 1572864 | tf_op jit(solution)/shard_map/all_to_all | solution.py:316
  38.1 15.0 %collective-permute-start.2 = (bf16[192,512]{1,0:T(8,128)(2,1)S(1)}, bf16[192,512]{1,0:T(8,128)(2,1)S(1)}, u32[]{:S(2)}, u32[]{:S(2)}) collective-permute-start(bf16[192,512]{1,0:T(8,128)(2,1)S(1)} %get-tuple-element.51.refs_1_), channel_id=1, source_target_pairs={{0,8},{1,25},{8,0},{9,17},{16,24},{17,9},{24,16},{25,1},{2,10},{3,... | collective-permute-start | bytes 589832 | tf_op jit(solution)/shard_map/ppermute | solution.py:312
  53.2 20.3 %all-to-all-start.2 = ((bf16[4,192,896]{2,1,0:T(8,128)(2,1)}), bf16[4,192,896]{2,1,0:T(8,128)(2,1)S(1)}, u32[]{:S(2)}, u32[]{:S(2)}) async-start(bf16[4,192,896]{2,1,0:T(8,128)(2,1)} %bitcast.7), calls=%async_computation.2 | async-start | bytes 2752512 | tf_op jit(solution)/shard_map/all_to_all | solution.py:316
  56.7 15.6 %collective-permute-start.3 = (bf16[192,512]{1,0:T(8,128)(2,1)S(1)}, bf16[192,512]{1,0:T(8,128)(2,1)S(1)}, u32[]{:S(2)}, u32[]{:S(2)}) collective-permute-start(bf16[192,512]{1,0:T(8,128)(2,1)S(1)} %get-tuple-element.57.refs_1_), channel_id=1, source_target_pairs={{0,24},{1,9},{8,16},{9,1},{16,8},{17,25},{24,0},{25,17},{2,26},{3,... | collective-permute-start | bytes 589832 | tf_op jit(solution)/shard_map/ppermute | solution.py:312
  73.5 14.5 %all-to-all-start.1 = ((bf16[4,192,512]{2,1,0:T(8,128)(2,1)}), bf16[4,192,512]{2,1,0:T(8,128)(2,1)S(1)}, u32[]{:S(2)}, u32[]{:S(2)}) async-start(bf16[4,192,512]{2,1,0:T(8,128)(2,1)} %get-tuple-element.58), calls=%async_computation.1 | async-start | bytes 1572864 | tf_op jit(solution)/shard_map/all_to_all | solution.py:316
  79.0 9.0 %collective-permute-start.4 = (bf16[192,384]{1,0:T(8,128)(2,1)S(1)}, bf16[192,384]{1,0:T(8,128)(2,1)S(1)}, u32[]{:S(2)}, u32[]{:S(2)}) collective-permute-start(bf16[192,384]{1,0:T(8,128)(2,1)S(1)} %get-tuple-element.64.refs_5_), channel_id=1, source_target_pairs={{0,1},{1,0},{2,3},{3,2},{4,5},{5,4},{6,7},{7,6},{8,9},{9,8},{10,11... | collective-permute-start | bytes 442376 | tf_op jit(solution)/shard_map/ppermute | solution.py:320
  88.9 15.2 %collective-permute-start.5 = (bf16[192,512]{1,0:T(8,128)(2,1)S(1)}, bf16[192,512]{1,0:T(8,128)(2,1)S(1)}, u32[]{:S(2)}, u32[]{:S(2)}) collective-permute-start(bf16[192,512]{1,0:T(8,128)(2,1)S(1)} %get-tuple-element.67.refs_1_), channel_id=1, source_target_pairs={{0,8},{1,25},{8,0},{9,17},{16,24},{17,9},{24,16},{25,1},{2,10},{3,... | collective-permute-start | bytes 589832 | tf_op jit(solution)/shard_map/ppermute | solution.py:312
  104.1 14.8 %collective-permute-start.6 = (bf16[192,512]{1,0:T(8,128)(2,1)S(1)}, bf16[192,512]{1,0:T(8,128)(2,1)S(1)}, u32[]{:S(2)}, u32[]{:S(2)}) collective-permute-start(bf16[192,512]{1,0:T(8,128)(2,1)S(1)} %get-tuple-element.71.refs_1_), channel_id=1, source_target_pairs={{0,24},{1,9},{8,16},{9,1},{16,8},{17,25},{24,0},{25,17},{2,26},{3,... | collective-permute-start | bytes 589832 | tf_op jit(solution)/shard_map/ppermute | solution.py:312
  119.9 16.6 %all-to-all-start.3 = ((bf16[4,192,512]{2,1,0:T(8,128)(2,1)}), bf16[4,192,512]{2,1,0:T(8,128)(2,1)S(1)}, u32[]{:S(2)}, u32[]{:S(2)}) async-start(bf16[4,192,512]{2,1,0:T(8,128)(2,1)} %get-tuple-element.73), calls=%async_computation.3 | async-start | bytes 1572864 | tf_op jit(solution)/shard_map/all_to_all | solution.py:316
  123.5 13.1 %collective-permute-start.7 = (bf16[272,512]{1,0:T(8,128)(2,1)S(1)}, bf16[272,512]{1,0:T(8,128)(2,1)S(1)}, u32[]{:S(2)}, u32[]{:S(2)}) collective-permute-start(bf16[272,512]{1,0:T(8,128)(2,1)S(1)} %get-tuple-element.75), channel_id=1, source_target_pairs={{0,32},{32,64},{64,96},{96,128},{128,160},{160,192},{192,224},{224... | collective-permute-start | bytes 835592 | tf_op jit(solution)/shard_map/ppermute | solution.py:325
  139.2 24.5 %collective-permute-start.10 = (f32[304,512]{1,0:T(8,128)S(1)}, f32[304,512]{1,0:T(8,128)S(1)}, u32[]{:S(2)}, u32[]{:S(2)}) collective-permute-start(f32[304,512]{1,0:T(8,128)S(1)} %get-tuple-element.80), channel_id=1, source_target_pairs={{0,1},{1,0},{2,3},{3,2},{4,5},{5,4},{6,7},{7,6},{8,9},{9,8},{10,11... | collective-permute-start | bytes 1867784 | tf_op jit(solution)/shard_map/ppermute | solution.py:320
  145.9 35.0 %collective-permute-start.11 = (bf16[272,512]{1,0:T(8,128)(2,1)S(1)}, bf16[272,512]{1,0:T(8,128)(2,1)S(1)}, u32[]{:S(2)}, u32[]{:S(2)}) collective-permute-start(bf16[272,512]{1,0:T(8,128)(2,1)S(1)} %get-tuple-element.84), channel_id=1, source_target_pairs={{0,64},{32,96},{64,128},{96,160},{128,192},{160,224},{192,256},{22... | collective-permute-start | bytes 835592 | tf_op jit(solution)/shard_map/ppermute | solution.py:325
  148.3 15.5 %collective-permute-start.9 = (bf16[256,512]{1,0:T(8,128)(2,1)S(1)}, bf16[256,512]{1,0:T(8,128)(2,1)S(1)}, u32[]{:S(2)}, u32[]{:S(2)}) collective-permute-start(bf16[256,512]{1,0:T(8,128)(2,1)S(1)} %get-tuple-element.68), channel_id=1, source_target_pairs={{0,33},{1,32},{32,65},{33,64},{64,97},{65,96},{96,129},{97,128},{1... | collective-permute-start | bytes 786440 | tf_op jit(solution)/shard_map/ppermute | solution.py:331
  150.2 30.7 %collective-permute-start.8 = (bf16[256,512]{1,0:T(8,128)(2,1)S(1)}, bf16[256,512]{1,0:T(8,128)(2,1)S(1)}, u32[]{:S(2)}, u32[]{:S(2)}) collective-permute-start(bf16[256,512]{1,0:T(8,128)(2,1)S(1)} %get-tuple-element.77), channel_id=1, source_target_pairs={{0,65},{1,64},{32,97},{33,96},{64,129},{65,128},{96,161},{97,160},... | collective-permute-start | bytes 786440 | tf_op jit(solution)/shard_map/ppermute | solution.py:331

commit v10 on v9

--- a/solution.py
+++ b/solution.py
@@ -71,30 +71,25 @@
     return [((zh * N_Y + y) * BLOCK, (y * N_Z + zh) * BLOCK) for zh in range(N_Z) for y in range(N_Y)]
 
 
-def first_values(push, x, w, targets, far, own):
+def prepare(push, x, w, rec, velocity, targets, far, own, message, tokens):
     core = lax.axis_index("core")
     for out, side in ((far, 1 - core), (own, core)):
         scaled = bf16(f32(w[:, cols_of(side)]) / push[0])
-        part = bf16(dot(x[...], scaled) * ROW_SCALE)
+        part = bf16(dot(x[0], scaled) * ROW_SCALE)
         for at, to in by_y():
             out[to : to + BLOCK] = part[at : at + BLOCK]
     spare = jnp.zeros((PADDED - ROWS, COLS), jnp.float32)
+    side = cols_of(1 - core)
     for step in range(2):
         row = TOKENS + step * PADDED
-        half = jnp.concatenate([f32(targets[step, :, cols_of(1 - core)]), spare], axis=0)
-        far[row : row + PADDED] = bf16(half)
-
-
-def make_message(x, w, rec, velocity, message, tokens):
-    far = cols_of(1 - lax.axis_index("core"))
-    for step in range(2):
+        far[row : row + PADDED] = bf16(jnp.concatenate([f32(targets[step, :, side]), spare], axis=0))
         for at, to in by_y():
             row = (1 - step) * TOKENS + to
             message[row : row + BLOCK] = x[step, at : at + BLOCK]
             tokens[row : row + BLOCK] = x[step, at : at + BLOCK]
-    old = velocity[:, far]
+    old = velocity[:, side]
     high = bf16(old)
-    halves = [(W_AT, w[:, far]), (REC_AT, rec[:, far]), (M_AT, high)]
+    halves = [(W_AT, w[:, side]), (REC_AT, rec[:, side]), (M_AT, high)]
     halves += [(M_AT + 2 * WIDTH, bf16(old - f32(high)))]
     for row, half in halves:
         message[row : row + WIDTH] = half[:, :WIDTH]
@@ -185,32 +180,42 @@
     near[WIDTH:] = bf16(jnp.full((EXTRA, COLS), (1.0 - keep) * push[0], jnp.float32))
 
 
-def second_gradient(push, push_got, mix, ready, mine, got, own1, own2, all2, far, near, half, message):
+def second_gradient(
+    push, push_got, mix, ready, mine, got, own1, own2, all2, far, near, half, message, message_low
+):
     core = lax.axis_index("core")
     keep = kept(mix, 1)
     down = ((0,), (0,))
-    for k, x, out, held in ((1, got, far, message), (0, mine, near, half)):
-        gradient = dot(x[...], all2[...], down) * GRAD_SCALE
-        moved = ready[k * WIDTH : (k + 1) * WIDTH] - step_size * gradient
-        out[:WIDTH] = bf16((1.0 - keep) * moved)
-        held[:WIDTH] = keep * moved
+    gradient = dot(got[...], all2[...], down) * GRAD_SCALE
+    moved = ready[WIDTH:] - step_size * gradient
+    far[...] = bf16((1.0 - keep) * moved)
+    message[: WIDTH // 2] = bf16(keep * moved[: WIDTH // 2])
+    message_low[...] = bf16(keep * moved[WIDTH // 2 :])
+    gradient = dot(mine[...], all2[...], down) * GRAD_SCALE
+    moved = ready[:WIDTH] - step_size * gradient
+    near[:WIDTH] = bf16((1.0 - keep) * moved)
+    half[...] = keep * moved
     weight = kept(mix, 0) * push[0] + push_got[0]
     near[WIDTH:] = bf16(jnp.full((EXTRA, COLS), (1.0 - keep) * weight, jnp.float32))
+    spare = jnp.zeros((PADDED - ROWS, COLS), jnp.float32)
     for step, own in ((0, own1), (1, own2)):
-        row = WIDTH + step * ROWS
-        message[row : row + ROWS] = jnp.where(core == 0, own[ROWS:], own[:ROWS])
+        row = WIDTH // 2 + step * PADDED
+        block = jnp.where(core == 0, own[ROWS:], own[:ROWS])
+        message[row : row + PADDED] = bf16(jnp.concatenate([block, spare], axis=0))
 
 
 def join_numerator(
-    push, push_got, mix, arrived, arrived_far, own1, own2, half, message, out, rows_out, weight
+    push, push_got, mix, arrived, arrived_far, own1, own2, half, message, message_low, out, rows_out, weight
 ):
     core = lax.axis_index("core")
+    cut = WIDTH // 2
     out[0, :, cols_of(core)] = bf16(half[...] + f32(arrived[:WIDTH]))
-    out[0, :, cols_of(1 - core)] = bf16(message[:WIDTH] + f32(arrived_far[...]))
+    out[0, :cut, cols_of(1 - core)] = bf16(f32(message[:cut]) + f32(arrived_far[:cut]))
+    out[0, cut:, cols_of(1 - core)] = bf16(f32(message_low[...]) + f32(arrived_far[cut:]))
     for step, own in ((0, own1), (1, own2)):
-        row = WIDTH + step * ROWS
+        row = cut + step * PADDED
         rows_out[step, :, cols_of(core)] = bf16(jnp.where(core == 0, own[:ROWS], own[ROWS:]))
-        rows_out[step, :, cols_of(1 - core)] = bf16(message[row : row + ROWS])
+        rows_out[step, :, cols_of(1 - core)] = bf16(f32(message[row : row + PADDED])[:ROWS])
     last = kept(mix, 0) * push[0] + push_got[0]
     weight[0] = kept(mix, 1) * last + jnp.max(f32(arrived[WIDTH:]))
 
@@ -349,28 +354,25 @@
     push, push_got, mix = push_weight, received_weight, mix_share
     state = [(numerator, 0), (received, 0), (momentum, 0)]
 
-    part_far, part_own = call(
-        first_values,
+    part_far, part_own, message, mine = call(
+        prepare,
         [push],
-        [(inputs, 0), (numerator, 0), targets],
-        [],
-        [],
-        [((TOKENS + 2 * PADDED, COLS), B16, pltpu.VMEM), ((TOKENS, COLS), B16, pltpu.VMEM)],
+        [inputs] + state + [targets],
+        [],
+        [],
+        [
+            ((TOKENS + 2 * PADDED, COLS), B16, pltpu.VMEM),
+            ((TOKENS, COLS), B16, pltpu.VMEM),
+            ((MESSAGE, WIDTH), B16, pltpu.VMEM),
+            ((2 * TOKENS, WIDTH), B16, pltpu.HBM),
+        ],
     )
     part_got = swap_core(part_far)
     near = [held(part_own), held(part_got)]
     (part1,) = call(add_parts, [], [], [], near, [((TOKENS, COLS), B16, pltpu.HBM)])
     taught = [targets, part_got[TOKENS:]]
 
-    later, _ = lax.optimization_barrier((numerator, part1))
-    message, mine = call(
-        make_message,
-        [],
-        [inputs, (later, 0)] + state[1:],
-        [],
-        [],
-        [((MESSAGE, WIDTH), B16, pltpu.VMEM), ((2 * TOKENS, WIDTH), B16, pltpu.HBM)],
-    )
+    message, _ = lax.optimization_barrier((message, part1))
     got = swap_core(message)
 
     parts1 = over_y(part1.reshape(N_Y, SLAB, COLS))
@@ -425,7 +427,7 @@
     arrived, arrived_far = to_group(near, 1), to_group_other(far, 1)
     all2, arrived = lax.optimization_barrier((all2, arrived))
 
-    far, near, half, message = call(
+    far, near, half, message, message_low = call(
         second_gradient,
         [push, push_got, mix],
         [ready, (mine, pl.ds(0, TOKENS)), (got, pl.ds(0, TOKENS))],
@@ -435,7 +437,8 @@
             ((WIDTH, COLS), B16, None),
             ((WIDTH + EXTRA, COLS), B16, None),
             ((WIDTH, COLS), F32, None),
-            ((WIDTH + 2 * ROWS, COLS), F32, None),
+            ((WIDTH // 2 + 2 * PADDED, COLS), B16, None),
+            ((WIDTH // 2, COLS), B16, None),
         ],
     )
 
@@ -447,7 +450,15 @@
         [push, push_got, mix],
         [],
         [],
-        [held(arrived), held(arrived_far), held(own1), held(own2), half, swap_core(message)],
+        [
+            held(arrived),
+            held(arrived_far),
+            held(own1),
+            held(own2),
+            half,
+            swap_core(message),
+            swap_core(message_low),
+        ],
         [whole, ((2, ROWS, VALUES), B16, None), number],
     )
     sent_far, final_numerator = lax.optimization_barrier((sent_far, final_numerator))

time: 183 us -> 175 us (0.956)
  waiting for transfers between devices: 76.5 us -> 66.1 us
  starting transfers between devices: 75.4 us -> 79 us
    ppermute x2, waiting for transfers between devices: 24.6 us -> 15.4 us  [to_group_other(): return lax.ppermute(value, GROUP + ('core',), pairs)]
    ppermute x2, starting transfers between devices: 6.48 us -> 12 us  [to_group_other(): return lax.ppermute(value, GROUP + ('core',), pairs)]
    ppermute x4, waiting for transfers between devices: 21.8 us -> 19.8 us  [over_z(): return lax.ppermute(value, ('z_hi', 'core'), z_pairs(step))]
    ppermute x4 -> x5, starting transfers between devices: 21.6 us -> 19.6 us  [swap_core(): return lax.ppermute(value, 'core', [(0, 1), (1, 0)])]
    pallas_call x15 -> x14, Pallas kernels: 27 us -> 25.9 us  [call(): pl.pallas_call(kernel, out_shape=result, in_specs=[SMEM] * first + [HBM]...]
  transfers between devices with their start and end apart: 16 -> 17, of which waited for: 11 -> 12; matrix products, arithmetic and copies ran while one was open for 0% -> 0% of each run, Pallas kernels for 8% -> 8%
where the time goes in v10:
time: 175 us; the launch traced here: 174 us
  starting transfers between devices  79 us (45%)
  waiting for transfers between devices  66.1 us (38%)
  Pallas kernels  25.9 us (15%)
  between operations  2.17 us (1%)
    ppermute x4, starting transfers between devices, over_z(): return lax.ppermute(value, ('z_hi', 'core'), z_pairs(step))  28.4 us
    pallas_call x14, Pallas kernels, call(): pl.pallas_call(kernel, out_shape=result, in_specs=[SMEM] * first + [HBM]...  25.9 us
    ppermute x4, waiting for transfers between devices, over_z(): return lax.ppermute(value, ('z_hi', 'core'), z_pairs(step))  19.8 us
    ppermute x5, starting transfers between devices, swap_core(): return lax.ppermute(value, 'core', [(0, 1), (1, 0)])  19.6 us
    all_to_all x4, waiting for transfers between devices, over_y(): return lax.all_to_all(value, 'y', 0, 0, tiled=True)  16.9 us
    ppermute x2, waiting for transfers between devices, to_group_other(): return lax.ppermute(value, GROUP + ('core',), pairs)  15.4 us
    all_to_all x4, starting transfers between devices, over_y(): return lax.all_to_all(value, 'y', 0, 0, tiled=True)  15.1 us
    ppermute x2, starting transfers between devices, to_group_other(): return lax.ppermute(value, GROUP + ('core',), pairs)  12 us
  transfers between devices with their start and end apart: 17, of which 12 were waited for; matrix products, arithmetic and copies ran while one was open for 0% of the time, Pallas kernels for 8%

profile of v10, /device:TPU:1, one launch (start us, length us, event | category | flops | bytes accessed | tf_op | source)
XLA Modules:
  0.0 173.8 jit_solution(10213257564462014749)
XLA Ops:
  1.3 4.7 %prepare.1 = (bf16[832,512]{1,0:T(8,128)(2,1)S(1)}, bf16[768,512]{1,0:T(8,128)(2,1)S(1)}, bf16[3584,256]{1,0:T(8,128)(2,1)}, bf16[1536,256]{1,0:T(8,128)(2,1)}) custom-call(f32[1]{0:T(128)S(6)} %copy.13.refs_0_, bf16[2,768,256]{2,1,0:T(8,128)(2,1)} %refs_1_.6, bf16[1,256,1024]{2,1,0:T(8,128)(2,1)} %refs_2_.8, bf16[1,256,1024]{2,1,0:T(8,128)(2,1)} %refs_3_.5, ...), custom_call_target="tpu_custom_call" | custom-call | bytes 7241728 | tf_op jit(solution)/shard_map/prepare/pallas_call | solution.py:291
  6.0 8.8 %collective-permute-start = (bf16[832,512]{1,0:T(8,128)(2,1)S(1)}, bf16[832,512]{1,0:T(8,128)(2,1)S(1)}, u32[]{:S(2)}, u32[]{:S(2)}) collective-permute-start(bf16[832,512]{1,0:T(8,128)(2,1)S(1)} %get-tuple-element.49), channel_id=1, source_target_pairs={{0,1},{1,0},{2,3},{3,2},{4,5},{5,4},{6,7},{7,6},{8,9},{9,8},{10,11... | collective-permute-start | bytes 2555912 | tf_op jit(solution)/shard_map/ppermute | solution.py:325
  17.9 2.3 %collective-permute-start.1 = (bf16[3584,256]{1,0:T(8,128)(2,1)}, bf16[3584,256]{1,0:T(8,128)(2,1)}, u32[]{:S(2)}, u32[]{:S(2)}) collective-permute-start(bf16[3584,256]{1,0:T(8,128)(2,1)} %get-tuple-element.54), channel_id=1, source_target_pairs={{0,1},{1,0},{2,3},{3,2},{4,5},{5,4},{6,7},{7,6},{8,9},{9,8},{10,11... | collective-permute-start | bytes 5505032 | tf_op jit(solution)/shard_map/ppermute | solution.py:325
  20.2 3.5 %all-to-all-start = ((bf16[4,192,512]{2,1,0:T(8,128)(2,1)}), bf16[4,192,512]{2,1,0:T(8,128)(2,1)S(1)}, u32[]{:S(2)}, u32[]{:S(2)}) async-start(bf16[4,192,512]{2,1,0:T(8,128)(2,1)} %bitcast.8), calls=%async_computation | async-start | bytes 1572864 | tf_op jit(solution)/shard_map/all_to_all | solution.py:321
  24.3 11.6 %all-to-all-done.refs_2_ = bf16[4,192,512]{2,1,0:T(8,128)(2,1)S(1)} async-done(((bf16[4,192,512]{2,1,0:T(8,128)(2,1)}), bf16[4,192,512]{2,1,0:T(8,128)(2,1)S(1)}, u32[]{:S(2)}, u32[]{:S(2)}) %all-to-all-start) | async-done | bytes 786464 | tf_op jit(solution)/shard_map/all_to_all | solution.py:321
  37.0 7.5 %collective-permute-start.2 = (bf16[192,512]{1,0:T(8,128)(2,1)S(1)}, bf16[192,512]{1,0:T(8,128)(2,1)S(1)}, u32[]{:S(2)}, u32[]{:S(2)}) collective-permute-start(bf16[192,512]{1,0:T(8,128)(2,1)S(1)} %get-tuple-element.51.refs_1_), channel_id=1, source_target_pairs={{0,8},{1,25},{8,0},{9,17},{16,24},{17,9},{24,16},{25,1},{2,10},{3,... | collective-permute-start | bytes 589832 | tf_op jit(solution)/shard_map/ppermute | solution.py:317
  45.2 5.2 %second_values.1 = bf16[768,896]{1,0:T(8,128)(2,1)} custom-call(f32[1]{0:T(128)S(6)} %copy.13.refs_0_, f32[1]{0:T(128)S(6)} %copy.14.refs_1_, s32[1,2]{1,0:T(1,128)S(1)} %copy-done, bf16[1,256,1024]{2,1,0:T(8,128)(2,1)} %refs_2_.8, bf16[1,256,1024]{2,1,0:T(8,128)(2,1)} %refs_3_.5, f32[1,256,1024]{2,1,0:T(8,128)} %refs_4_.5, ...), custom_call_target="tpu_custom_call" | custom-call | bytes 6094848 | tf_op jit(solution)/shard_map/second_values/pallas_call | solution.py:291
  52.1 3.6 %all-to-all-start.2 = ((bf16[4,192,896]{2,1,0:T(8,128)(2,1)}), bf16[4,192,896]{2,1,0:T(8,128)(2,1)S(1)}, u32[]{:S(2)}, u32[]{:S(2)}) async-start(bf16[4,192,896]{2,1,0:T(8,128)(2,1)} %bitcast.7), calls=%async_computation.2 | async-start | bytes 2752512 | tf_op jit(solution)/shard_map/all_to_all | solution.py:321
  55.6 7.0 %collective-permute-start.3 = (bf16[192,512]{1,0:T(8,128)(2,1)S(1)}, bf16[192,512]{1,0:T(8,128)(2,1)S(1)}, u32[]{:S(2)}, u32[]{:S(2)}) collective-permute-start(bf16[192,512]{1,0:T(8,128)(2,1)S(1)} %get-tuple-element.58.refs_1_), channel_id=1, source_target_pairs={{0,24},{1,9},{8,16},{9,1},{16,8},{17,25},{24,0},{25,17},{2,26},{3,... | collective-permute-start | bytes 589832 | tf_op jit(solution)/shard_map/ppermute | solution.py:317
  62.7 8.6 %collective-permute-done.3.refs_2_ = bf16[192,512]{1,0:T(8,128)(2,1)S(1)} collective-permute-done((bf16[192,512]{1,0:T(8,128)(2,1)S(1)}, bf16[192,512]{1,0:T(8,128)(2,1)S(1)}, u32[]{:S(2)}, u32[]{:S(2)}) %collective-permute-start.3) | collective-permute-done | bytes 196640 | tf_op jit(solution)/shard_map/ppermute | solution.py:317
  72.4 4.4 %all-to-all-start.1 = ((bf16[4,192,512]{2,1,0:T(8,128)(2,1)}), bf16[4,192,512]{2,1,0:T(8,128)(2,1)S(1)}, u32[]{:S(2)}, u32[]{:S(2)}) async-start(bf16[4,192,512]{2,1,0:T(8,128)(2,1)} %get-tuple-element.59), calls=%async_computation.1 | async-start | bytes 1572864 | tf_op jit(solution)/shard_map/all_to_all | solution.py:321
  77.9 3.9 %collective-permute-start.4 = (bf16[192,384]{1,0:T(8,128)(2,1)S(1)}, bf16[192,384]{1,0:T(8,128)(2,1)S(1)}, u32[]{:S(2)}, u32[]{:S(2)}) collective-permute-start(bf16[192,384]{1,0:T(8,128)(2,1)S(1)} %get-tuple-element.65.refs_5_), channel_id=1, source_target_pairs={{0,1},{1,0},{2,3},{3,2},{4,5},{5,4},{6,7},{7,6},{8,9},{9,8},{10,11... | collective-permute-start | bytes 442376 | tf_op jit(solution)/shard_map/ppermute | solution.py:325
  81.7 5.1 %all-to-all-done.1 = bf16[4,192,512]{2,1,0:T(8,128)(2,1)S(1)} async-done(((bf16[4,192,512]{2,1,0:T(8,128)(2,1)}), bf16[4,192,512]{2,1,0:T(8,128)(2,1)S(1)}, u32[]{:S(2)}, u32[]{:S(2)}) %all-to-all-start.1) | async-done | bytes 786464 | tf_op jit(solution)/shard_map/all_to_all | solution.py:321
  87.8 10.2 %collective-permute-start.5 = (bf16[192,512]{1,0:T(8,128)(2,1)S(1)}, bf16[192,512]{1,0:T(8,128)(2,1)S(1)}, u32[]{:S(2)}, u32[]{:S(2)}) collective-permute-start(bf16[192,512]{1,0:T(8,128)(2,1)S(1)} %get-tuple-element.68.refs_1_), channel_id=1, source_target_pairs={{0,8},{1,25},{8,0},{9,17},{16,24},{17,9},{24,16},{25,1},{2,10},{3,... | collective-permute-start | bytes 589832 | tf_op jit(solution)/shard_map/ppermute | solution.py:317
  98.0 4.7 %first_gradient.1 = (bf16[272,512]{1,0:T(8,128)(2,1)S(1)}, bf16[256,512]{1,0:T(8,128)(2,1)S(1)}, f32[512,512]{1,0:T(8,128)}) custom-call(f32[1]{0:T(128)S(6)} %copy.13.refs_0_, s32[1,2]{1,0:T(1,128)S(1)} %copy-done, bf16[1,256,1024]{2,1,0:T(8,128)(2,1)} %refs_2_.8, bf16[1,256,1024]{2,1,0:T(8,128)(2,1)} %refs_3_.5, f32[1,256,1024]{2,1,0:T(8,128)} %refs_4_.5, ...), custom_call_target="tpu_custom_call" | custom-call | bytes 7094272 | tf_op jit(solution)/shard_map/first_gradient/pallas_call | solution.py:291
  103.0 3.7 %collective-permute-start.6 = (bf16[192,512]{1,0:T(8,128)(2,1)S(1)}, bf16[192,512]{1,0:T(8,128)(2,1)S(1)}, u32[]{:S(2)}, u32[]{:S(2)}) collective-permute-start(bf16[192,512]{1,0:T(8,128)(2,1)S(1)} %get-tuple-element.72.refs_1_), channel_id=1, source_target_pairs={{0,24},{1,9},{8,16},{9,1},{16,8},{17,25},{24,0},{25,17},{2,26},{3,... | collective-permute-start | bytes 589832 | tf_op jit(solution)/shard_map/ppermute | solution.py:317
  106.8 9.3 %collective-permute-done.6.refs_2_ = bf16[192,512]{1,0:T(8,128)(2,1)S(1)} collective-permute-done((bf16[192,512]{1,0:T(8,128)(2,1)S(1)}, bf16[192,512]{1,0:T(8,128)(2,1)S(1)}, u32[]{:S(2)}, u32[]{:S(2)}) %collective-permute-start.6) | collective-permute-done | bytes 196640 | tf_op jit(solution)/shard_map/ppermute | solution.py:317
  117.0 3.7 %all-to-all-start.3 = ((bf16[4,192,512]{2,1,0:T(8,128)(2,1)}), bf16[4,192,512]{2,1,0:T(8,128)(2,1)S(1)}, u32[]{:S(2)}, u32[]{:S(2)}) async-start(bf16[4,192,512]{2,1,0:T(8,128)(2,1)} %get-tuple-element.74), calls=%async_computation.3 | async-start | bytes 1572864 | tf_op jit(solution)/shard_map/all_to_all | solution.py:321
  122.6 11.9 %collective-permute-done.7.refs_3_ = bf16[272,512]{1,0:T(8,128)(2,1)S(1)} collective-permute-done((bf16[272,512]{1,0:T(8,128)(2,1)S(1)}, bf16[272,512]{1,0:T(8,128)(2,1)S(1)}, u32[]{:S(2)}, u32[]{:S(2)}) %collective-permute-start.7) | collective-permute-done | bytes 278560 | tf_op jit(solution)/shard_map/ppermute | solution.py:330
  134.6 2.7 %second_gradient.1 = (bf16[256,512]{1,0:T(8,128)(2,1)S(1)}, bf16[272,512]{1,0:T(8,128)(2,1)S(1)}, f32[256,512]{1,0:T(8,128)S(1)}, bf16[192,512]{1,0:T(8,128)(2,1)S(1)}, bf16[128,512]{1,0:T(8,128)(2,1)S(1)}) custom-call(f32[1]{0:T(128)S(6)} %copy.13.refs_0_, f32[1]{0:T(128)S(6)} %copy.14.refs_1_, s32[1,2]{1,0:T(1,128)S(1)} %copy-done, ...), custom_call_target="tpu_custom_call" | custom-call | bytes 6045696 | tf_op jit(solution)/shard_map/second_gradient/pallas_call | solution.py:291
  139.2 7.5 %collective-permute-start.9 = (bf16[256,512]{1,0:T(8,128)(2,1)S(1)}, bf16[256,512]{1,0:T(8,128)(2,1)S(1)}, u32[]{:S(2)}, u32[]{:S(2)}) collective-permute-start(bf16[256,512]{1,0:T(8,128)(2,1)S(1)} %get-tuple-element.69), channel_id=1, source_target_pairs={{0,33},{1,32},{32,65},{33,64},{64,97},{65,96},{96,129},{97,128},{1... | collective-permute-start | bytes 786440 | tf_op jit(solution)/shard_map/ppermute | solution.py:336
  146.7 4.5 %collective-permute-start.8 = (bf16[256,512]{1,0:T(8,128)(2,1)S(1)}, bf16[256,512]{1,0:T(8,128)(2,1)S(1)}, u32[]{:S(2)}, u32[]{:S(2)}) collective-permute-start(bf16[256,512]{1,0:T(8,128)(2,1)S(1)} %get-tuple-element.78), channel_id=1, source_target_pairs={{0,65},{1,64},{32,97},{33,96},{64,129},{65,128},{96,161},{97,160},... | collective-permute-start | bytes 786440 | tf_op jit(solution)/shard_map/ppermute | solution.py:336
  151.2 2.8 %collective-permute-start.10 = (bf16[192,512]{1,0:T(8,128)(2,1)S(1)}, bf16[192,512]{1,0:T(8,128)(2,1)S(1)}, u32[]{:S(2)}, u32[]{:S(2)}) collective-permute-start(bf16[192,512]{1,0:T(8,128)(2,1)S(1)} %get-tuple-element.81), channel_id=1, source_target_pairs={{0,1},{1,0},{2,3},{3,2},{4,5},{5,4},{6,7},{7,6},{8,9},{9,8},{10,11... | collective-permute-start | bytes 589832 | tf_op jit(solution)/shard_map/ppermute | solution.py:325
  158.8 14.2 %collective-permute-done.8.refs_1_ = bf16[256,512]{1,0:T(8,128)(2,1)S(1)} collective-permute-done((bf16[256,512]{1,0:T(8,128)(2,1)S(1)}, bf16[256,512]{1,0:T(8,128)(2,1)S(1)}, u32[]{:S(2)}, u32[]{:S(2)}) %collective-permute-start.8) | collective-permute-done | bytes 262176 | tf_op jit(solution)/shard_map/ppermute | solution.py:336
  (27 shorter events, 20.4 us)
Async XLA Ops:
  6.0 10.8 %collective-permute-start = (bf16[832,512]{1,0:T(8,128)(2,1)S(1)}, bf16[832,512]{1,0:T(8,128)(2,1)S(1)}, u32[]{:S(2)}, u32[]{:S(2)}) collective-permute-start(bf16[832,512]{1,0:T(8,128)(2,1)S(1)} %get-tuple-element.49), channel_id=1, source_target_pairs={{0,1},{1,0},{2,3},{3,2},{4,5},{5,4},{6,7},{7,6},{8,9},{9,8},{10,11... | collective-permute-start | bytes 2555912 | tf_op jit(solution)/shard_map/ppermute | solution.py:325
  17.9 27.3 %copy-start = (s32[1,2]{1,0:T(1,128)S(1)}, s32[1,2]{1,0:T(1,128)}, u32[]{:S(2)}) copy-start(s32[1,2]{1,0:T(1,128)} %refs_2_.11) | copy-start | bytes 28
  17.9 27.2 %collective-permute-start.1 = (bf16[3584,256]{1,0:T(8,128)(2,1)}, bf16[3584,256]{1,0:T(8,128)(2,1)}, u32[]{:S(2)}, u32[]{:S(2)}) collective-permute-start(bf16[3584,256]{1,0:T(8,128)(2,1)} %get-tuple-element.54), channel_id=1, source_target_pairs={{0,1},{1,0},{2,3},{3,2},{4,5},{5,4},{6,7},{7,6},{8,9},{9,8},{10,11... | collective-permute-start | bytes 5505032 | tf_op jit(solution)/shard_map/ppermute | solution.py:325
  20.2 15.8 %all-to-all-start = ((bf16[4,192,512]{2,1,0:T(8,128)(2,1)}), bf16[4,192,512]{2,1,0:T(8,128)(2,1)S(1)}, u32[]{:S(2)}, u32[]{:S(2)}) async-start(bf16[4,192,512]{2,1,0:T(8,128)(2,1)} %bitcast.8), calls=%async_computation | async-start | bytes 1572864 | tf_op jit(solution)/shard_map/all_to_all | solution.py:321
  37.0 15.0 %collective-permute-start.2 = (bf16[192,512]{1,0:T(8,128)(2,1)S(1)}, bf16[192,512]{1,0:T(8,128)(2,1)S(1)}, u32[]{:S(2)}, u32[]{:S(2)}) collective-permute-start(bf16[192,512]{1,0:T(8,128)(2,1)S(1)} %get-tuple-element.51.refs_1_), channel_id=1, source_target_pairs={{0,8},{1,25},{8,0},{9,17},{16,24},{17,9},{24,16},{25,1},{2,10},{3,... | collective-permute-start | bytes 589832 | tf_op jit(solution)/shard_map/ppermute | solution.py:317
  52.1 20.3 %all-to-all-start.2 = ((bf16[4,192,896]{2,1,0:T(8,128)(2,1)}), bf16[4,192,896]{2,1,0:T(8,128)(2,1)S(1)}, u32[]{:S(2)}, u32[]{:S(2)}) async-start(bf16[4,192,896]{2,1,0:T(8,128)(2,1)} %bitcast.7), calls=%async_computation.2 | async-start | bytes 2752512 | tf_op jit(solution)/shard_map/all_to_all | solution.py:321
  55.6 15.6 %collective-permute-start.3 = (bf16[192,512]{1,0:T(8,128)(2,1)S(1)}, bf16[192,512]{1,0:T(8,128)(2,1)S(1)}, u32[]{:S(2)}, u32[]{:S(2)}) collective-permute-start(bf16[192,512]{1,0:T(8,128)(2,1)S(1)} %get-tuple-element.58.refs_1_), channel_id=1, source_target_pairs={{0,24},{1,9},{8,16},{9,1},{16,8},{17,25},{24,0},{25,17},{2,26},{3,... | collective-permute-start | bytes 589832 | tf_op jit(solution)/shard_map/ppermute | solution.py:317
  72.4 14.5 %all-to-all-start.1 = ((bf16[4,192,512]{2,1,0:T(8,128)(2,1)}), bf16[4,192,512]{2,1,0:T(8,128)(2,1)S(1)}, u32[]{:S(2)}, u32[]{:S(2)}) async-start(bf16[4,192,512]{2,1,0:T(8,128)(2,1)} %get-tuple-element.59), calls=%async_computation.1 | async-start | bytes 1572864 | tf_op jit(solution)/shard_map/all_to_all | solution.py:321
  77.9 9.0 %collective-permute-start.4 = (bf16[192,384]{1,0:T(8,128)(2,1)S(1)}, bf16[192,384]{1,0:T(8,128)(2,1)S(1)}, u32[]{:S(2)}, u32[]{:S(2)}) collective-permute-start(bf16[192,384]{1,0:T(8,128)(2,1)S(1)} %get-tuple-element.65.refs_5_), channel_id=1, source_target_pairs={{0,1},{1,0},{2,3},{3,2},{4,5},{5,4},{6,7},{7,6},{8,9},{9,8},{10,11... | collective-permute-start | bytes 442376 | tf_op jit(solution)/shard_map/ppermute | solution.py:325
  87.8 15.2 %collective-permute-start.5 = (bf16[192,512]{1,0:T(8,128)(2,1)S(1)}, bf16[192,512]{1,0:T(8,128)(2,1)S(1)}, u32[]{:S(2)}, u32[]{:S(2)}) collective-permute-start(bf16[192,512]{1,0:T(8,128)(2,1)S(1)} %get-tuple-element.68.refs_1_), channel_id=1, source_target_pairs={{0,8},{1,25},{8,0},{9,17},{16,24},{17,9},{24,16},{25,1},{2,10},{3,... | collective-permute-start | bytes 589832 | tf_op jit(solution)/shard_map/ppermute | solution.py:317
  103.0 13.0 %collective-permute-start.6 = (bf16[192,512]{1,0:T(8,128)(2,1)S(1)}, bf16[192,512]{1,0:T(8,128)(2,1)S(1)}, u32[]{:S(2)}, u32[]{:S(2)}) collective-permute-start(bf16[192,512]{1,0:T(8,128)(2,1)S(1)} %get-tuple-element.72.refs_1_), channel_id=1, source_target_pairs={{0,24},{1,9},{8,16},{9,1},{16,8},{17,25},{24,0},{25,17},{2,26},{3,... | collective-permute-start | bytes 589832 | tf_op jit(solution)/shard_map/ppermute | solution.py:317
  117.0 17.5 %all-to-all-start.3 = ((bf16[4,192,512]{2,1,0:T(8,128)(2,1)}), bf16[4,192,512]{2,1,0:T(8,128)(2,1)S(1)}, u32[]{:S(2)}, u32[]{:S(2)}) async-start(bf16[4,192,512]{2,1,0:T(8,128)(2,1)} %get-tuple-element.74), calls=%async_computation.3 | async-start | bytes 1572864 | tf_op jit(solution)/shard_map/all_to_all | solution.py:321
  120.7 13.8 %collective-permute-start.7 = (bf16[272,512]{1,0:T(8,128)(2,1)S(1)}, bf16[272,512]{1,0:T(8,128)(2,1)S(1)}, u32[]{:S(2)}, u32[]{:S(2)}) collective-permute-start(bf16[272,512]{1,0:T(8,128)(2,1)S(1)} %get-tuple-element.76), channel_id=1, source_target_pairs={{0,32},{32,64},{64,96},{96,128},{128,160},{160,192},{192,224},{224... | collective-permute-start | bytes 835592 | tf_op jit(solution)/shard_map/ppermute | solution.py:330
  137.2 35.7 %collective-permute-start.12 = (bf16[272,512]{1,0:T(8,128)(2,1)S(1)}, bf16[272,512]{1,0:T(8,128)(2,1)S(1)}, u32[]{:S(2)}, u32[]{:S(2)}) collective-permute-start(bf16[272,512]{1,0:T(8,128)(2,1)S(1)} %get-tuple-element.86), channel_id=1, source_target_pairs={{0,64},{32,96},{64,128},{96,160},{128,192},{160,224},{192,256},{22... | collective-permute-start | bytes 835592 | tf_op jit(solution)/shard_map/ppermute | solution.py:330
  139.2 17.9 %collective-permute-start.9 = (bf16[256,512]{1,0:T(8,128)(2,1)S(1)}, bf16[256,512]{1,0:T(8,128)(2,1)S(1)}, u32[]{:S(2)}, u32[]{:S(2)}) collective-permute-start(bf16[256,512]{1,0:T(8,128)(2,1)S(1)} %get-tuple-element.69), channel_id=1, source_target_pairs={{0,33},{1,32},{32,65},{33,64},{64,97},{65,96},{96,129},{97,128},{1... | collective-permute-start | bytes 786440 | tf_op jit(solution)/shard_map/ppermute | solution.py:336
  146.7 26.3 %collective-permute-start.8 = (bf16[256,512]{1,0:T(8,128)(2,1)S(1)}, bf16[256,512]{1,0:T(8,128)(2,1)S(1)}, u32[]{:S(2)}, u32[]{:S(2)}) collective-permute-start(bf16[256,512]{1,0:T(8,128)(2,1)S(1)} %get-tuple-element.78), channel_id=1, source_target_pairs={{0,65},{1,64},{32,97},{33,96},{64,129},{65,128},{96,161},{97,160},... | collective-permute-start | bytes 786440 | tf_op jit(solution)/shard_map/ppermute | solution.py:336
  151.2 6.0 %collective-permute-start.10 = (bf16[192,512]{1,0:T(8,128)(2,1)S(1)}, bf16[192,512]{1,0:T(8,128)(2,1)S(1)}, u32[]{:S(2)}, u32[]{:S(2)}) collective-permute-start(bf16[192,512]{1,0:T(8,128)(2,1)S(1)} %get-tuple-element.81), channel_id=1, source_target_pairs={{0,1},{1,0},{2,3},{3,2},{4,5},{5,4},{6,7},{7,6},{8,9},{9,8},{10,11... | collective-permute-start | bytes 589832 | tf_op jit(solution)/shard_map/ppermute | solution.py:325
  153.9 3.2 %collective-permute-start.11 = (bf16[128,512]{1,0:T(8,128)(2,1)S(1)}, bf16[128,512]{1,0:T(8,128)(2,1)S(1)}, u32[]{:S(2)}, u32[]{:S(2)}) collective-permute-start(bf16[128,512]{1,0:T(8,128)(2,1)S(1)} %get-tuple-element.82), channel_id=1, source_target_pairs={{0,1},{1,0},{2,3},{3,2},{4,5},{5,4},{6,7},{7,6},{8,9},{9,8},{10,11... | collective-permute-start | bytes 393224 | tf_op jit(solution)/shard_map/ppermute | solution.py:325

commit v11 on v10

--- a/solution.py
+++ b/solution.py
@@ -71,18 +71,23 @@
     return [((zh * N_Y + y) * BLOCK, (y * N_Z + zh) * BLOCK) for zh in range(N_Z) for y in range(N_Y)]
 
 
-def prepare(push, x, w, rec, velocity, targets, far, own, message, tokens):
+def first_values(push, x, w, targets, far, own):
     core = lax.axis_index("core")
     for out, side in ((far, 1 - core), (own, core)):
         scaled = bf16(f32(w[:, cols_of(side)]) / push[0])
-        part = bf16(dot(x[0], scaled) * ROW_SCALE)
+        part = bf16(dot(x[...], scaled) * ROW_SCALE)
         for at, to in by_y():
             out[to : to + BLOCK] = part[at : at + BLOCK]
     spare = jnp.zeros((PADDED - ROWS, COLS), jnp.float32)
-    side = cols_of(1 - core)
     for step in range(2):
         row = TOKENS + step * PADDED
-        far[row : row + PADDED] = bf16(jnp.concatenate([f32(targets[step, :, side]), spare], axis=0))
+        half = jnp.concatenate([f32(targets[step, :, cols_of(1 - core)]), spare], axis=0)
+        far[row : row + PADDED] = bf16(half)
+
+
+def make_message(x, w, rec, velocity, message, tokens):
+    side = cols_of(1 - lax.axis_index("core"))
+    for step in range(2):
         for at, to in by_y():
             row = (1 - step) * TOKENS + to
             message[row : row + BLOCK] = x[step, at : at + BLOCK]
@@ -354,20 +359,24 @@
     push, push_got, mix = push_weight, received_weight, mix_share
     state = [(numerator, 0), (received, 0), (momentum, 0)]
 
-    part_far, part_own, message, mine = call(
-        prepare,
+    part_far, part_own = call(
+        first_values,
         [push],
-        [inputs] + state + [targets],
-        [],
-        [],
-        [
-            ((TOKENS + 2 * PADDED, COLS), B16, pltpu.VMEM),
-            ((TOKENS, COLS), B16, pltpu.VMEM),
-            ((MESSAGE, WIDTH), B16, pltpu.VMEM),
-            ((2 * TOKENS, WIDTH), B16, pltpu.HBM),
-        ],
-    )
-    part_got = swap_core(part_far)
+        [(inputs, 0), (numerator, 0), targets],
+        [],
+        [],
+        [((TOKENS + 2 * PADDED, COLS), B16, pltpu.VMEM), ((TOKENS, COLS), B16, pltpu.VMEM)],
+    )
+    later, _ = lax.optimization_barrier((numerator, part_own))
+    message, mine = call(
+        make_message,
+        [],
+        [inputs, (later, 0)] + state[1:],
+        [],
+        [],
+        [((MESSAGE, WIDTH), B16, pltpu.VMEM), ((2 * TOKENS, WIDTH), B16, pltpu.HBM)],
+    )
+    part_got, _ = lax.optimization_barrier((swap_core(part_far), mine))
     near = [held(part_own), held(part_got)]
     (part1,) = call(add_parts, [], [], [], near, [((TOKENS, COLS), B16, pltpu.HBM)])
     taught = [targets, part_got[TOKENS:]]
@@ -420,8 +429,8 @@
             ((2 * WIDTH, COLS), F32, pltpu.HBM),
         ],
     )
-    slab, own2 = add_z(slab, own2, 0, add_slab, WHOLE, far)
-    sent, own2 = add_z(slab, own2, 1, add_and_spread, SPREAD)
+    slab, own2 = add_z(slab, own2, 0, add_slab, WHOLE)
+    sent, own2 = add_z(slab, own2, 1, add_and_spread, SPREAD, far)
     all2 = over_y(sent).reshape(TOKENS, COLS)
     near, _ = lax.optimization_barrier((near, sent))
     arrived, arrived_far = to_group(near, 1), to_group_other(far, 1)

time: 175 us -> 175 us (level)
  waiting for transfers between devices: 66.1 us -> 53.4 us
  starting transfers between devices: 79 us -> 89.1 us
    ppermute x2, starting transfers between devices: 12 us -> 19.3 us  [to_group_other(): return lax.ppermute(value, GROUP + ('core',), pairs)]
    ppermute x2, waiting for transfers between devices: 11.9 us -> 5.36 us  [to_group(): lax.ppermute(value, GROUP, [(i, (i + hop) % count) for i in range(count)])]
    ppermute x2, waiting for transfers between devices: 15.4 us -> 10.2 us  [to_group_other(): return lax.ppermute(value, GROUP + ('core',), pairs)]
    ppermute x2, starting transfers between devices: 3.83 us -> 7.74 us  [to_group(): lax.ppermute(value, GROUP, [(i, (i + hop) % count) for i in range(count)])]
    all_to_all x4, waiting for transfers between devices: 16.9 us -> 19.8 us  [over_y(): return lax.all_to_all(value, 'y', 0, 0, tiled=True)]
    ppermute x4, waiting for transfers between devices: 19.8 us -> 17.1 us  [over_z(): return lax.ppermute(value, ('z_hi', 'core'), z_pairs(step))]
    ppermute x5, starting transfers between devices: 19.6 us -> 17.4 us  [swap_core(): return lax.ppermute(value, 'core', [(0, 1), (1, 0)])]
    pallas_call x14 -> x15, Pallas kernels: 25.9 us -> 27.1 us  [call(): pl.pallas_call(kernel, out_shape=result, in_specs=[SMEM] * first + [HBM]...]
  transfers between devices with their start and end apart: 17 -> 17, of which waited for: 12 -> 9; matrix products, arithmetic and copies ran while one was open for 0% -> 0% of each run, Pallas kernels for 8% -> 11%
where the time goes in v11:
time: 175 us; the launch traced here: 172 us
  starting transfers between devices  89.1 us (51%)
  waiting for transfers between devices  53.4 us (31%)
  Pallas kernels  27.1 us (15%)
  between operations  2.2 us (1%)
    ppermute x4, starting transfers between devices, over_z(): return lax.ppermute(value, ('z_hi', 'core'), z_pairs(step))  29.6 us
    pallas_call x15, Pallas kernels, call(): pl.pallas_call(kernel, out_shape=result, in_specs=[SMEM] * first + [HBM]...  27.1 us
    all_to_all x4, waiting for transfers between devices, over_y(): return lax.all_to_all(value, 'y', 0, 0, tiled=True)  19.8 us
    ppermute x2, starting transfers between devices, to_group_other(): return lax.ppermute(value, GROUP + ('core',), pairs)  19.3 us
    ppermute x5, starting transfers between devices, swap_core(): return lax.ppermute(value, 'core', [(0, 1), (1, 0)])  17.4 us
    ppermute x4, waiting for transfers between devices, over_z(): return lax.ppermute(value, ('z_hi', 'core'), z_pairs(step))  17.1 us
    all_to_all x4, starting transfers between devices, over_y(): return lax.all_to_all(value, 'y', 0, 0, tiled=True)  15.2 us
    ppermute x2, waiting for transfers between devices, to_group_other(): return lax.ppermute(value, GROUP + ('core',), pairs)  10.2 us
  transfers between devices with their start and end apart: 17, of which 9 were waited for; matrix products, arithmetic and copies ran while one was open for 0% of the time, Pallas kernels for 11%

profile of v11, /device:TPU:1, one launch (start us, length us, event | category | flops | bytes accessed | tf_op | source)
XLA Modules:
  0.0 172.4 jit_solution(1115473309440208663)
XLA Ops:
  3.1 8.8 %collective-permute-start = (bf16[832,512]{1,0:T(8,128)(2,1)S(1)}, bf16[832,512]{1,0:T(8,128)(2,1)S(1)}, u32[]{:S(2)}, u32[]{:S(2)}) collective-permute-start(bf16[832,512]{1,0:T(8,128)(2,1)S(1)} %get-tuple-element.53), channel_id=1, source_target_pairs={{0,1},{1,0},{2,3},{3,2},{4,5},{5,4},{6,7},{7,6},{8,9},{9,8},{10,11... | collective-permute-start | bytes 2555912 | tf_op jit(solution)/shard_map/ppermute | solution.py:330
  11.9 4.0 %make_message.1 = (bf16[3584,256]{1,0:T(8,128)(2,1)}, bf16[1536,256]{1,0:T(8,128)(2,1)}) custom-call(bf16[2,768,256]{2,1,0:T(8,128)(2,1)} %refs_0_.9, bf16[1,256,1024]{2,1,0:T(8,128)(2,1)} %refs_2_.10, bf16[1,256,1024]{2,1,0:T(8,128)(2,1)} %refs_3_.7, f32[1,256,1024]{2,1,0:T(8,128)} %refs_4_.3), custom_call_target="tpu_custom_call" | custom-call | bytes 5505024 | tf_op jit(solution)/shard_map/make_message/pallas_call | solution.py:296
  19.0 3.5 %all-to-all-start = ((bf16[4,192,512]{2,1,0:T(8,128)(2,1)}), bf16[4,192,512]{2,1,0:T(8,128)(2,1)S(1)}, u32[]{:S(2)}, u32[]{:S(2)}) async-start(bf16[4,192,512]{2,1,0:T(8,128)(2,1)} %bitcast.8), calls=%async_computation | async-start | bytes 1572864 | tf_op jit(solution)/shard_map/all_to_all | solution.py:326
  23.1 11.2 %all-to-all-done.refs_2_ = bf16[4,192,512]{2,1,0:T(8,128)(2,1)S(1)} async-done(((bf16[4,192,512]{2,1,0:T(8,128)(2,1)}), bf16[4,192,512]{2,1,0:T(8,128)(2,1)S(1)}, u32[]{:S(2)}, u32[]{:S(2)}) %all-to-all-start) | async-done | bytes 786464 | tf_op jit(solution)/shard_map/all_to_all | solution.py:326
  35.4 7.5 %collective-permute-start.2 = (bf16[192,512]{1,0:T(8,128)(2,1)S(1)}, bf16[192,512]{1,0:T(8,128)(2,1)S(1)}, u32[]{:S(2)}, u32[]{:S(2)}) collective-permute-start(bf16[192,512]{1,0:T(8,128)(2,1)S(1)} %get-tuple-element.55.refs_1_), channel_id=1, source_target_pairs={{0,8},{1,25},{8,0},{9,17},{16,24},{17,9},{24,16},{25,1},{2,10},{3,... | collective-permute-start | bytes 589832 | tf_op jit(solution)/shard_map/ppermute | solution.py:322
  43.6 5.2 %second_values.1 = bf16[768,896]{1,0:T(8,128)(2,1)} custom-call(f32[1]{0:T(128)S(6)} %copy.13.refs_0_, f32[1]{0:T(128)S(6)} %copy.14.refs_1_, s32[1,2]{1,0:T(1,128)S(1)} %copy-done, bf16[1,256,1024]{2,1,0:T(8,128)(2,1)} %refs_2_.10, bf16[1,256,1024]{2,1,0:T(8,128)(2,1)} %refs_3_.7, f32[1,256,1024]{2,1,0:T(8,128)} %refs_4_.3, ...), custom_call_target="tpu_custom_call" | custom-call | bytes 6094848 | tf_op jit(solution)/shard_map/second_values/pallas_call | solution.py:296
  49.7 3.6 %all-to-all-start.2 = ((bf16[4,192,896]{2,1,0:T(8,128)(2,1)}), bf16[4,192,896]{2,1,0:T(8,128)(2,1)S(1)}, u32[]{:S(2)}, u32[]{:S(2)}) async-start(bf16[4,192,896]{2,1,0:T(8,128)(2,1)} %bitcast.7), calls=%async_computation.2 | async-start | bytes 2752512 | tf_op jit(solution)/shard_map/all_to_all | solution.py:326
  53.2 7.8 %collective-permute-start.3 = (bf16[192,512]{1,0:T(8,128)(2,1)S(1)}, bf16[192,512]{1,0:T(8,128)(2,1)S(1)}, u32[]{:S(2)}, u32[]{:S(2)}) collective-permute-start(bf16[192,512]{1,0:T(8,128)(2,1)S(1)} %get-tuple-element.62.refs_1_), channel_id=1, source_target_pairs={{0,24},{1,9},{8,16},{9,1},{16,8},{17,25},{24,0},{25,17},{2,26},{3,... | collective-permute-start | bytes 589832 | tf_op jit(solution)/shard_map/ppermute | solution.py:322
  61.1 9.6 %collective-permute-done.3.refs_2_ = bf16[192,512]{1,0:T(8,128)(2,1)S(1)} collective-permute-done((bf16[192,512]{1,0:T(8,128)(2,1)S(1)}, bf16[192,512]{1,0:T(8,128)(2,1)S(1)}, u32[]{:S(2)}, u32[]{:S(2)}) %collective-permute-start.3) | collective-permute-done | bytes 196640 | tf_op jit(solution)/shard_map/ppermute | solution.py:322
  71.7 4.2 %all-to-all-start.1 = ((bf16[4,192,512]{2,1,0:T(8,128)(2,1)}), bf16[4,192,512]{2,1,0:T(8,128)(2,1)S(1)}, u32[]{:S(2)}, u32[]{:S(2)}) async-start(bf16[4,192,512]{2,1,0:T(8,128)(2,1)} %get-tuple-element.63), calls=%async_computation.1 | async-start | bytes 1572864 | tf_op jit(solution)/shard_map/all_to_all | solution.py:326
  77.0 2.3 %collective-permute-start.4 = (bf16[192,384]{1,0:T(8,128)(2,1)S(1)}, bf16[192,384]{1,0:T(8,128)(2,1)S(1)}, u32[]{:S(2)}, u32[]{:S(2)}) collective-permute-start(bf16[192,384]{1,0:T(8,128)(2,1)S(1)} %get-tuple-element.69.refs_5_), channel_id=1, source_target_pairs={{0,1},{1,0},{2,3},{3,2},{4,5},{5,4},{6,7},{7,6},{8,9},{9,8},{10,11... | collective-permute-start | bytes 442376 | tf_op jit(solution)/shard_map/ppermute | solution.py:330
  79.3 8.6 %all-to-all-done.1 = bf16[4,192,512]{2,1,0:T(8,128)(2,1)S(1)} async-done(((bf16[4,192,512]{2,1,0:T(8,128)(2,1)}), bf16[4,192,512]{2,1,0:T(8,128)(2,1)S(1)}, u32[]{:S(2)}, u32[]{:S(2)}) %all-to-all-start.1) | async-done | bytes 786464 | tf_op jit(solution)/shard_map/all_to_all | solution.py:326
  88.8 8.7 %collective-permute-start.5 = (bf16[192,512]{1,0:T(8,128)(2,1)S(1)}, bf16[192,512]{1,0:T(8,128)(2,1)S(1)}, u32[]{:S(2)}, u32[]{:S(2)}) collective-permute-start(bf16[192,512]{1,0:T(8,128)(2,1)S(1)} %get-tuple-element.72.refs_1_), channel_id=1, source_target_pairs={{0,8},{1,25},{8,0},{9,17},{16,24},{17,9},{24,16},{25,1},{2,10},{3,... | collective-permute-start | bytes 589832 | tf_op jit(solution)/shard_map/ppermute | solution.py:322
  97.5 4.5 %collective-permute-done.5.refs_2_ = bf16[192,512]{1,0:T(8,128)(2,1)S(1)} collective-permute-done((bf16[192,512]{1,0:T(8,128)(2,1)S(1)}, bf16[192,512]{1,0:T(8,128)(2,1)S(1)}, u32[]{:S(2)}, u32[]{:S(2)}) %collective-permute-start.5) | collective-permute-done | bytes 196640 | tf_op jit(solution)/shard_map/ppermute | solution.py:322
  102.1 5.5 %collective-permute-start.6 = (bf16[192,512]{1,0:T(8,128)(2,1)S(1)}, bf16[192,512]{1,0:T(8,128)(2,1)S(1)}, u32[]{:S(2)}, u32[]{:S(2)}) collective-permute-start(bf16[192,512]{1,0:T(8,128)(2,1)S(1)} %get-tuple-element.74.refs_1_), channel_id=1, source_target_pairs={{0,24},{1,9},{8,16},{9,1},{16,8},{17,25},{24,0},{25,17},{2,26},{3,... | collective-permute-start | bytes 589832 | tf_op jit(solution)/shard_map/ppermute | solution.py:322
  107.6 4.7 %first_gradient.1 = (bf16[272,512]{1,0:T(8,128)(2,1)S(1)}, bf16[256,512]{1,0:T(8,128)(2,1)S(1)}, f32[512,512]{1,0:T(8,128)}) custom-call(f32[1]{0:T(128)S(6)} %copy.13.refs_0_, s32[1,2]{1,0:T(1,128)S(1)} %copy-done, bf16[1,256,1024]{2,1,0:T(8,128)(2,1)} %refs_2_.10, bf16[1,256,1024]{2,1,0:T(8,128)(2,1)} %refs_3_.7, f32[1,256,1024]{2,1,0:T(8,128)} %refs_4_.3, ...), custom_call_target="tpu_custom_call" | custom-call | bytes 7094272 | tf_op jit(solution)/shard_map/first_gradient/pallas_call | solution.py:296
  115.5 3.9 %all-to-all-start.3 = ((bf16[4,192,512]{2,1,0:T(8,128)(2,1)}), bf16[4,192,512]{2,1,0:T(8,128)(2,1)S(1)}, u32[]{:S(2)}, u32[]{:S(2)}) async-start(bf16[4,192,512]{2,1,0:T(8,128)(2,1)} %get-tuple-element.78), calls=%async_computation.3 | async-start | bytes 1572864 | tf_op jit(solution)/shard_map/all_to_all | solution.py:326
  119.4 5.8 %collective-permute-start.7 = (bf16[272,512]{1,0:T(8,128)(2,1)S(1)}, bf16[272,512]{1,0:T(8,128)(2,1)S(1)}, u32[]{:S(2)}, u32[]{:S(2)}) collective-permute-start(bf16[272,512]{1,0:T(8,128)(2,1)S(1)} %get-tuple-element.80), channel_id=1, source_target_pairs={{0,32},{32,64},{64,96},{96,128},{128,160},{160,192},{192,224},{224... | collective-permute-start | bytes 835592 | tf_op jit(solution)/shard_map/ppermute | solution.py:335
  125.3 5.4 %collective-permute-done.7.refs_3_ = bf16[272,512]{1,0:T(8,128)(2,1)S(1)} collective-permute-done((bf16[272,512]{1,0:T(8,128)(2,1)S(1)}, bf16[272,512]{1,0:T(8,128)(2,1)S(1)}, u32[]{:S(2)}, u32[]{:S(2)}) %collective-permute-start.7) | collective-permute-done | bytes 278560 | tf_op jit(solution)/shard_map/ppermute | solution.py:335
  130.6 2.7 %second_gradient.1 = (bf16[256,512]{1,0:T(8,128)(2,1)S(1)}, bf16[272,512]{1,0:T(8,128)(2,1)S(1)}, f32[256,512]{1,0:T(8,128)S(1)}, bf16[192,512]{1,0:T(8,128)(2,1)S(1)}, bf16[128,512]{1,0:T(8,128)(2,1)S(1)}) custom-call(f32[1]{0:T(128)S(6)} %copy.13.refs_0_, f32[1]{0:T(128)S(6)} %copy.14.refs_1_, s32[1,2]{1,0:T(1,128)S(1)} %copy-done, ...), custom_call_target="tpu_custom_call" | custom-call | bytes 6045696 | tf_op jit(solution)/shard_map/second_gradient/pallas_call | solution.py:296
  135.2 13.6 %collective-permute-start.9 = (bf16[256,512]{1,0:T(8,128)(2,1)S(1)}, bf16[256,512]{1,0:T(8,128)(2,1)S(1)}, u32[]{:S(2)}, u32[]{:S(2)}) collective-permute-start(bf16[256,512]{1,0:T(8,128)(2,1)S(1)} %get-tuple-element.75), channel_id=1, source_target_pairs={{0,33},{1,32},{32,65},{33,64},{64,97},{65,96},{96,129},{97,128},{1... | collective-permute-start | bytes 786440 | tf_op jit(solution)/shard_map/ppermute | solution.py:341
  148.9 5.7 %collective-permute-start.8 = (bf16[256,512]{1,0:T(8,128)(2,1)S(1)}, bf16[256,512]{1,0:T(8,128)(2,1)S(1)}, u32[]{:S(2)}, u32[]{:S(2)}) collective-permute-start(bf16[256,512]{1,0:T(8,128)(2,1)S(1)} %get-tuple-element.82), channel_id=1, source_target_pairs={{0,65},{1,64},{32,97},{33,96},{64,129},{65,128},{96,161},{97,160},... | collective-permute-start | bytes 786440 | tf_op jit(solution)/shard_map/ppermute | solution.py:341
  156.5 2.4 %collective-permute-start.11 = (bf16[128,512]{1,0:T(8,128)(2,1)S(1)}, bf16[128,512]{1,0:T(8,128)(2,1)S(1)}, u32[]{:S(2)}, u32[]{:S(2)}) collective-permute-start(bf16[128,512]{1,0:T(8,128)(2,1)S(1)} %get-tuple-element.86), channel_id=1, source_target_pairs={{0,1},{1,0},{2,3},{3,2},{4,5},{5,4},{6,7},{7,6},{8,9},{9,8},{10,11... | collective-permute-start | bytes 393224 | tf_op jit(solution)/shard_map/ppermute | solution.py:330
  161.4 10.2 %collective-permute-done.8.refs_1_ = bf16[256,512]{1,0:T(8,128)(2,1)S(1)} collective-permute-done((bf16[256,512]{1,0:T(8,128)(2,1)S(1)}, bf16[256,512]{1,0:T(8,128)(2,1)S(1)}, u32[]{:S(2)}, u32[]{:S(2)}) %collective-permute-start.8) | collective-permute-done | bytes 262176 | tf_op jit(solution)/shard_map/ppermute | solution.py:341
  (28 shorter events, 20.9 us)
Async XLA Ops:
  3.1 12.8 %collective-permute-start = (bf16[832,512]{1,0:T(8,128)(2,1)S(1)}, bf16[832,512]{1,0:T(8,128)(2,1)S(1)}, u32[]{:S(2)}, u32[]{:S(2)}) collective-permute-start(bf16[832,512]{1,0:T(8,128)(2,1)S(1)} %get-tuple-element.53), channel_id=1, source_target_pairs={{0,1},{1,0},{2,3},{3,2},{4,5},{5,4},{6,7},{7,6},{8,9},{9,8},{10,11... | collective-permute-start | bytes 2555912 | tf_op jit(solution)/shard_map/ppermute | solution.py:330
  17.1 26.5 %copy-start = (s32[1,2]{1,0:T(1,128)S(1)}, s32[1,2]{1,0:T(1,128)}, u32[]{:S(2)}) copy-start(s32[1,2]{1,0:T(1,128)} %refs_2_.13) | copy-start | bytes 28
  17.1 26.5 %collective-permute-start.1 = (bf16[3584,256]{1,0:T(8,128)(2,1)}, bf16[3584,256]{1,0:T(8,128)(2,1)}, u32[]{:S(2)}, u32[]{:S(2)}) collective-permute-start(bf16[3584,256]{1,0:T(8,128)(2,1)} %get-tuple-element.58), channel_id=1, source_target_pairs={{0,1},{1,0},{2,3},{3,2},{4,5},{5,4},{6,7},{7,6},{8,9},{9,8},{10,11... | collective-permute-start | bytes 5505032 | tf_op jit(solution)/shard_map/ppermute | solution.py:330
  19.0 15.4 %all-to-all-start = ((bf16[4,192,512]{2,1,0:T(8,128)(2,1)}), bf16[4,192,512]{2,1,0:T(8,128)(2,1)S(1)}, u32[]{:S(2)}, u32[]{:S(2)}) async-start(bf16[4,192,512]{2,1,0:T(8,128)(2,1)} %bitcast.8), calls=%async_computation | async-start | bytes 1572864 | tf_op jit(solution)/shard_map/all_to_all | solution.py:326
  35.4 14.2 %collective-permute-start.2 = (bf16[192,512]{1,0:T(8,128)(2,1)S(1)}, bf16[192,512]{1,0:T(8,128)(2,1)S(1)}, u32[]{:S(2)}, u32[]{:S(2)}) collective-permute-start(bf16[192,512]{1,0:T(8,128)(2,1)S(1)} %get-tuple-element.55.refs_1_), channel_id=1, source_target_pairs={{0,8},{1,25},{8,0},{9,17},{16,24},{17,9},{24,16},{25,1},{2,10},{3,... | collective-permute-start | bytes 589832 | tf_op jit(solution)/shard_map/ppermute | solution.py:322
  49.7 22.0 %all-to-all-start.2 = ((bf16[4,192,896]{2,1,0:T(8,128)(2,1)}), bf16[4,192,896]{2,1,0:T(8,128)(2,1)S(1)}, u32[]{:S(2)}, u32[]{:S(2)}) async-start(bf16[4,192,896]{2,1,0:T(8,128)(2,1)} %bitcast.7), calls=%async_computation.2 | async-start | bytes 2752512 | tf_op jit(solution)/shard_map/all_to_all | solution.py:326
  53.2 17.4 %collective-permute-start.3 = (bf16[192,512]{1,0:T(8,128)(2,1)S(1)}, bf16[192,512]{1,0:T(8,128)(2,1)S(1)}, u32[]{:S(2)}, u32[]{:S(2)}) collective-permute-start(bf16[192,512]{1,0:T(8,128)(2,1)S(1)} %get-tuple-element.62.refs_1_), channel_id=1, source_target_pairs={{0,24},{1,9},{8,16},{9,1},{16,8},{17,25},{24,0},{25,17},{2,26},{3,... | collective-permute-start | bytes 589832 | tf_op jit(solution)/shard_map/ppermute | solution.py:322
  71.7 16.2 %all-to-all-start.1 = ((bf16[4,192,512]{2,1,0:T(8,128)(2,1)}), bf16[4,192,512]{2,1,0:T(8,128)(2,1)S(1)}, u32[]{:S(2)}, u32[]{:S(2)}) async-start(bf16[4,192,512]{2,1,0:T(8,128)(2,1)} %get-tuple-element.63), calls=%async_computation.1 | async-start | bytes 1572864 | tf_op jit(solution)/shard_map/all_to_all | solution.py:326
  77.0 10.9 %collective-permute-start.4 = (bf16[192,384]{1,0:T(8,128)(2,1)S(1)}, bf16[192,384]{1,0:T(8,128)(2,1)S(1)}, u32[]{:S(2)}, u32[]{:S(2)}) collective-permute-start(bf16[192,384]{1,0:T(8,128)(2,1)S(1)} %get-tuple-element.69.refs_5_), channel_id=1, source_target_pairs={{0,1},{1,0},{2,3},{3,2},{4,5},{5,4},{6,7},{7,6},{8,9},{9,8},{10,11... | collective-permute-start | bytes 442376 | tf_op jit(solution)/shard_map/ppermute | solution.py:330
  88.8 13.2 %collective-permute-start.5 = (bf16[192,512]{1,0:T(8,128)(2,1)S(1)}, bf16[192,512]{1,0:T(8,128)(2,1)S(1)}, u32[]{:S(2)}, u32[]{:S(2)}) collective-permute-start(bf16[192,512]{1,0:T(8,128)(2,1)S(1)} %get-tuple-element.72.refs_1_), channel_id=1, source_target_pairs={{0,8},{1,25},{8,0},{9,17},{16,24},{17,9},{24,16},{25,1},{2,10},{3,... | collective-permute-start | bytes 589832 | tf_op jit(solution)/shard_map/ppermute | solution.py:322
  102.1 12.5 %collective-permute-start.6 = (bf16[192,512]{1,0:T(8,128)(2,1)S(1)}, bf16[192,512]{1,0:T(8,128)(2,1)S(1)}, u32[]{:S(2)}, u32[]{:S(2)}) collective-permute-start(bf16[192,512]{1,0:T(8,128)(2,1)S(1)} %get-tuple-element.74.refs_1_), channel_id=1, source_target_pairs={{0,24},{1,9},{8,16},{9,1},{16,8},{17,25},{24,0},{25,17},{2,26},{3,... | collective-permute-start | bytes 589832 | tf_op jit(solution)/shard_map/ppermute | solution.py:322
  115.5 15.1 %all-to-all-start.3 = ((bf16[4,192,512]{2,1,0:T(8,128)(2,1)}), bf16[4,192,512]{2,1,0:T(8,128)(2,1)S(1)}, u32[]{:S(2)}, u32[]{:S(2)}) async-start(bf16[4,192,512]{2,1,0:T(8,128)(2,1)} %get-tuple-element.78), calls=%async_computation.3 | async-start | bytes 1572864 | tf_op jit(solution)/shard_map/all_to_all | solution.py:326
  119.4 11.2 %collective-permute-start.7 = (bf16[272,512]{1,0:T(8,128)(2,1)S(1)}, bf16[272,512]{1,0:T(8,128)(2,1)S(1)}, u32[]{:S(2)}, u32[]{:S(2)}) collective-permute-start(bf16[272,512]{1,0:T(8,128)(2,1)S(1)} %get-tuple-element.80), channel_id=1, source_target_pairs={{0,32},{32,64},{64,96},{96,128},{128,160},{160,192},{192,224},{224... | collective-permute-start | bytes 835592 | tf_op jit(solution)/shard_map/ppermute | solution.py:335
  133.3 38.3 %collective-permute-start.12 = (bf16[272,512]{1,0:T(8,128)(2,1)S(1)}, bf16[272,512]{1,0:T(8,128)(2,1)S(1)}, u32[]{:S(2)}, u32[]{:S(2)}) collective-permute-start(bf16[272,512]{1,0:T(8,128)(2,1)S(1)} %get-tuple-element.90), channel_id=1, source_target_pairs={{0,64},{32,96},{64,128},{96,160},{128,192},{160,224},{192,256},{22... | collective-permute-start | bytes 835592 | tf_op jit(solution)/shard_map/ppermute | solution.py:335
  135.2 23.7 %collective-permute-start.9 = (bf16[256,512]{1,0:T(8,128)(2,1)S(1)}, bf16[256,512]{1,0:T(8,128)(2,1)S(1)}, u32[]{:S(2)}, u32[]{:S(2)}) collective-permute-start(bf16[256,512]{1,0:T(8,128)(2,1)S(1)} %get-tuple-element.75), channel_id=1, source_target_pairs={{0,33},{1,32},{32,65},{33,64},{64,97},{65,96},{96,129},{97,128},{1... | collective-permute-start | bytes 786440 | tf_op jit(solution)/shard_map/ppermute | solution.py:341
  148.9 22.7 %collective-permute-start.8 = (bf16[256,512]{1,0:T(8,128)(2,1)S(1)}, bf16[256,512]{1,0:T(8,128)(2,1)S(1)}, u32[]{:S(2)}, u32[]{:S(2)}) collective-permute-start(bf16[256,512]{1,0:T(8,128)(2,1)S(1)} %get-tuple-element.82), channel_id=1, source_target_pairs={{0,65},{1,64},{32,97},{33,96},{64,129},{65,128},{96,161},{97,160},... | collective-permute-start | bytes 786440 | tf_op jit(solution)/shard_map/ppermute | solution.py:341
  154.6 5.3 %collective-permute-start.10 = (bf16[192,512]{1,0:T(8,128)(2,1)S(1)}, bf16[192,512]{1,0:T(8,128)(2,1)S(1)}, u32[]{:S(2)}, u32[]{:S(2)}) collective-permute-start(bf16[192,512]{1,0:T(8,128)(2,1)S(1)} %get-tuple-element.85), channel_id=1, source_target_pairs={{0,1},{1,0},{2,3},{3,2},{4,5},{5,4},{6,7},{7,6},{8,9},{9,8},{10,11... | collective-permute-start | bytes 589832 | tf_op jit(solution)/shard_map/ppermute | solution.py:330
  156.5 3.4 %collective-permute-start.11 = (bf16[128,512]{1,0:T(8,128)(2,1)S(1)}, bf16[128,512]{1,0:T(8,128)(2,1)S(1)}, u32[]{:S(2)}, u32[]{:S(2)}) collective-permute-start(bf16[128,512]{1,0:T(8,128)(2,1)S(1)} %get-tuple-element.86), channel_id=1, source_target_pairs={{0,1},{1,0},{2,3},{3,2},{4,5},{5,4},{6,7},{7,6},{8,9},{9,8},{10,11... | collective-permute-start | bytes 393224 | tf_op jit(solution)/shard_map/ppermute | solution.py:330

commit v12 on v11

--- a/solution.py
+++ b/solution.py
@@ -31,10 +31,6 @@
 GRAD_SCALE = 1.0 / math.sqrt(TOKENS)
 
 X1_AT = TOKENS
-W_AT = 2 * TOKENS
-REC_AT = W_AT + 2 * WIDTH
-M_AT = REC_AT + 2 * WIDTH
-MESSAGE = M_AT + 4 * WIDTH
 
 B16, F32 = jnp.bfloat16, jnp.float32
 
@@ -85,27 +81,27 @@
         far[row : row + PADDED] = bf16(half)
 
 
-def make_message(x, w, rec, velocity, message, tokens):
+def make_message(x, w, rec, velocity, second, first, state, moving, tokens):
     side = cols_of(1 - lax.axis_index("core"))
-    for step in range(2):
+    for step, out in ((0, first), (1, second)):
         for at, to in by_y():
             row = (1 - step) * TOKENS + to
-            message[row : row + BLOCK] = x[step, at : at + BLOCK]
+            out[to : to + BLOCK] = x[step, at : at + BLOCK]
             tokens[row : row + BLOCK] = x[step, at : at + BLOCK]
     old = velocity[:, side]
     high = bf16(old)
-    halves = [(W_AT, w[:, side]), (REC_AT, rec[:, side]), (M_AT, high)]
-    halves += [(M_AT + 2 * WIDTH, bf16(old - f32(high)))]
-    for row, half in halves:
-        message[row : row + WIDTH] = half[:, :WIDTH]
-        message[row + WIDTH : row + 2 * WIDTH] = half[:, WIDTH:]
+    halves = [(state, 0, w[:, side]), (state, 2 * WIDTH, rec[:, side])]
+    halves += [(moving, 0, high), (moving, 2 * WIDTH, bf16(old - f32(high)))]
+    for out, row, half in halves:
+        out[row : row + WIDTH] = half[:, :WIDTH]
+        out[row + WIDTH : row + 2 * WIDTH] = half[:, WIDTH:]
 
 
 def add_parts(own, got, out):
     out[...] = bf16(f32(own[...]) + f32(got[:TOKENS]))
 
 
-def tile(mix, w, rec, velocity, got, first, k):
+def tile(mix, w, rec, velocity, state, moving, k):
     keep = kept(mix, 0)
     if k == 0:
         side = cols_of(lax.axis_index("core"))
@@ -113,22 +109,24 @@
     else:
         start, arrived, high, low = (
             jnp.concatenate([got[at : at + WIDTH], got[at + WIDTH : at + 2 * WIDTH]], axis=1)
-            for at in (W_AT - first, REC_AT - first, M_AT - first, M_AT + 2 * WIDTH - first)
+            for got in (state, moving)
+            for at in (0, 2 * WIDTH)
         )
         old = f32(high) + f32(low)
     ahead = f32(start) - (step_size * momentum_decay) * old
     return ahead, keep * ahead + f32(arrived), old
 
 
-def second_values(push, push_got, mix, w, rec, velocity, mine, got, out):
+def second_values(push, push_got, mix, w, rec, velocity, mine, got2, got1, state, moving, out):
     core = lax.axis_index("core")
     weight = kept(mix, 0) * push[0] + push_got[0]
-    near, far = mine[:TOKENS], got[:TOKENS]
-    scaled = [bf16(tile(mix, w, rec, velocity, got, 0, k)[1] / weight) for k in range(2)]
+    near, far = mine[:TOKENS], got2[...]
+    scaled = [bf16(tile(mix, w, rec, velocity, state, moving, k)[1] / weight) for k in range(2)]
     out[:, :COLS] = bf16((dot(near, scaled[0]) + dot(far, scaled[1])) * ROW_SCALE)
     rows = pl.ds(pl.multiple_of(X1_AT + core * HALF, 16), HALF)
+    rows_got = half_of(core)
     across = ((1,), (1,))
-    out[:, COLS:] = bf16(dot(near, mine[rows], across) + dot(far, got[rows], across))
+    out[:, COLS:] = bf16(dot(near, mine[rows], across) + dot(far, got1[rows_got], across))
 
 
 def sum_over_y(step, targets, targets_got, parts, slab, own, *gram):
@@ -172,11 +170,11 @@
     own_out[...] = own[...] - turned[own_block()]
 
 
-def first_gradient(push, mix, w, rec, velocity, mine, got, all1, near, far, ready):
+def first_gradient(push, mix, w, rec, velocity, mine, got, state, moving, all1, near, far, ready):
     keep = kept(mix, 0)
     down = ((0,), (0,))
     for k, x, out in ((0, mine, near), (1, got, far)):
-        ahead, base, old = tile(mix, w, rec, velocity, got, X1_AT, k)
+        ahead, base, old = tile(mix, w, rec, velocity, state, moving, k)
         gradient = dot(x[:TOKENS], all1[...], down) * GRAD_SCALE
         out[:WIDTH] = bf16((1.0 - keep) * (ahead - step_size * gradient))
         current = bf16(base - (step_size * keep) * gradient)
@@ -368,13 +366,15 @@
         [((TOKENS + 2 * PADDED, COLS), B16, pltpu.VMEM), ((TOKENS, COLS), B16, pltpu.VMEM)],
     )
     later, _ = lax.optimization_barrier((numerator, part_own))
-    message, mine = call(
+    *message, mine = call(
         make_message,
         [],
         [inputs, (later, 0)] + state[1:],
         [],
         [],
-        [((MESSAGE, WIDTH), B16, pltpu.VMEM), ((2 * TOKENS, WIDTH), B16, pltpu.HBM)],
+        [((TOKENS, WIDTH), B16, pltpu.VMEM)] * 2
+        + [((4 * WIDTH, WIDTH), B16, pltpu.VMEM)] * 2
+        + [((2 * TOKENS, WIDTH), B16, pltpu.HBM)],
     )
     part_got, _ = lax.optimization_barrier((swap_core(part_far), mine))
     near = [held(part_own), held(part_got)]
@@ -382,7 +382,7 @@
     taught = [targets, part_got[TOKENS:]]
 
     message, _ = lax.optimization_barrier((message, part1))
-    got = swap_core(message)
+    got2, got1, state_got, moving_got = [swap_core(value) for value in message]
 
     parts1 = over_y(part1.reshape(N_Y, SLAB, COLS))
     slab, own1 = call(
@@ -393,7 +393,7 @@
     (part2,) = call(
         second_values,
         [push, push_got, mix],
-        state + [mine, got],
+        state + [mine, got2, got1, state_got, moving_got],
         [],
         [],
         [((TOKENS, COLS + HALF), B16, pltpu.HBM)],
@@ -420,7 +420,7 @@
     near, far, ready = call(
         first_gradient,
         [push, mix],
-        state + [(mine, pl.ds(X1_AT, TOKENS)), (got, pl.ds(X1_AT, MESSAGE - X1_AT))],
+        state + [(mine, pl.ds(X1_AT, TOKENS)), got1, state_got, moving_got],
         [],
         [all1],
         [
@@ -439,7 +439,7 @@
     far, near, half, message, message_low = call(
         second_gradient,
         [push, push_got, mix],
-        [ready, (mine, pl.ds(0, TOKENS)), (got, pl.ds(0, TOKENS))],
+        [ready, (mine, pl.ds(0, TOKENS)), got2],
         [],
         [held(own1), held(own2), all2],
         [

time: 175 us -> 172 us (0.983); the launches traced: 172 us -> 171 us
  starting transfers between devices: 89.1 us -> 97.3 us
  waiting for transfers between devices: 53.4 us -> 45.5 us
    all_to_all x4, waiting for transfers between devices: 19.8 us -> 7.62 us  [over_y(): return lax.all_to_all(value, 'y', 0, 0, tiled=True)]
    ppermute x5 -> x8, starting transfers between devices: 17.4 us -> 26.3 us  [swap_core(): return lax.ppermute(value, 'core', [(0, 1), (1, 0)])]
    ppermute x2, waiting for transfers between devices: 10.2 us -> 17.5 us  [to_group_other(): return lax.ppermute(value, GROUP + ('core',), pairs)]
    ppermute x2, starting transfers between devices: 19.3 us -> 13.9 us  [to_group_other(): return lax.ppermute(value, GROUP + ('core',), pairs)]
    all_to_all x4, starting transfers between devices: 15.2 us -> 20.3 us  [over_y(): return lax.all_to_all(value, 'y', 0, 0, tiled=True)]
    ppermute x4, waiting for transfers between devices: 17.1 us -> 12.6 us  [over_z(): return lax.ppermute(value, ('z_hi', 'core'), z_pairs(step))]
    ppermute x2, starting transfers between devices: 7.74 us -> 5.34 us  [to_group(): lax.ppermute(value, GROUP, [(i, (i + hop) % count) for i in range(count)])]
    ppermute x2, waiting for transfers between devices: 5.36 us -> 7.76 us  [to_group(): lax.ppermute(value, GROUP, [(i, (i + hop) % count) for i in range(count)])]
  transfers between devices with their start and end apart: 17 -> 20, of which waited for: 9 -> 10; matrix products, arithmetic and copies ran while one was open for 0% -> 0% of each run, Pallas kernels for 11% -> 10%
where the time goes in v12:
time: 172 us; the launch traced here: 171 us
  starting transfers between devices  97.3 us (57%)
  waiting for transfers between devices  45.5 us (26%)
  Pallas kernels  25.7 us (15%)
  between operations  2.23 us (1%)
    ppermute x4, starting transfers between devices, over_z(): return lax.ppermute(value, ('z_hi', 'core'), z_pairs(step))  31.4 us
    ppermute x8, starting transfers between devices, swap_core(): return lax.ppermute(value, 'core', [(0, 1), (1, 0)])  26.3 us
    pallas_call x15, Pallas kernels, call(): pl.pallas_call(kernel, out_shape=result, in_specs=[SMEM] * first + [HBM]...  25.7 us
    all_to_all x4, starting transfers between devices, over_y(): return lax.all_to_all(value, 'y', 0, 0, tiled=True)  20.3 us
    ppermute x2, waiting for transfers between devices, to_group_other(): return lax.ppermute(value, GROUP + ('core',), pairs)  17.5 us
    ppermute x2, starting transfers between devices, to_group_other(): return lax.ppermute(value, GROUP + ('core',), pairs)  13.9 us
    ppermute x4, waiting for transfers between devices, over_z(): return lax.ppermute(value, ('z_hi', 'core'), z_pairs(step))  12.6 us
    ppermute x2, waiting for transfers between devices, to_group(): lax.ppermute(value, GROUP, [(i, (i + hop) % count) for i in range(count)])  7.76 us
  transfers between devices with their start and end apart: 20, of which 10 were waited for; matrix products, arithmetic and copies ran while one was open for 0% of the time, Pallas kernels for 10%

profile of v12, /device:TPU:1, one launch (start us, length us, event | category | flops | bytes accessed | tf_op | source)
XLA Modules:
  0.0 171.4 jit_solution(4811205012304105225)
XLA Ops:
  3.1 8.8 %collective-permute-start = (bf16[832,512]{1,0:T(8,128)(2,1)S(1)}, bf16[832,512]{1,0:T(8,128)(2,1)S(1)}, u32[]{:S(2)}, u32[]{:S(2)}) collective-permute-start(bf16[832,512]{1,0:T(8,128)(2,1)S(1)} %get-tuple-element.59), channel_id=1, source_target_pairs={{0,1},{1,0},{2,3},{3,2},{4,5},{5,4},{6,7},{7,6},{8,9},{9,8},{10,11... | collective-permute-start | bytes 2555912 | tf_op jit(solution)/shard_map/ppermute | solution.py:328
  11.9 2.8 %make_message.1 = (bf16[768,256]{1,0:T(8,128)(2,1)S(1)}, bf16[768,256]{1,0:T(8,128)(2,1)S(1)}, bf16[1024,256]{1,0:T(8,128)(2,1)S(1)}, bf16[1024,256]{1,0:T(8,128)(2,1)S(1)}, bf16[1536,256]{1,0:T(8,128)(2,1)}) custom-call(bf16[2,768,256]{2,1,0:T(8,128)(2,1)} %refs_0_.9, bf16[1,256,1024]{2,1,0:T(8,128)(2,1)} %refs_2_.10, bf16[1,256,1024]{2,1,0:T(8,128)(2,1)} %refs_3_.7, ...), custom_call_target="tpu_custom_call" | custom-call | bytes 5505024 | tf_op jit(solution)/shard_map/make_message/pallas_call | solution.py:294
  15.8 3.5 %all-to-all-start = ((bf16[4,192,512]{2,1,0:T(8,128)(2,1)}), bf16[4,192,512]{2,1,0:T(8,128)(2,1)S(1)}, u32[]{:S(2)}, u32[]{:S(2)}) async-start(bf16[4,192,512]{2,1,0:T(8,128)(2,1)} %bitcast.8), calls=%async_computation | async-start | bytes 1572864 | tf_op jit(solution)/shard_map/all_to_all | solution.py:324
  28.6 3.1 %all-to-all-done.refs_2_ = bf16[4,192,512]{2,1,0:T(8,128)(2,1)S(1)} async-done(((bf16[4,192,512]{2,1,0:T(8,128)(2,1)}), bf16[4,192,512]{2,1,0:T(8,128)(2,1)S(1)}, u32[]{:S(2)}, u32[]{:S(2)}) %all-to-all-start) | async-done | bytes 786464 | tf_op jit(solution)/shard_map/all_to_all | solution.py:324
  32.8 7.5 %collective-permute-start.4 = (bf16[192,512]{1,0:T(8,128)(2,1)S(1)}, bf16[192,512]{1,0:T(8,128)(2,1)S(1)}, u32[]{:S(2)}, u32[]{:S(2)}) collective-permute-start(bf16[192,512]{1,0:T(8,128)(2,1)S(1)} %get-tuple-element.61.refs_1_), channel_id=1, source_target_pairs={{0,8},{1,25},{8,0},{9,17},{16,24},{17,9},{24,16},{25,1},{2,10},{3,... | collective-permute-start | bytes 589832 | tf_op jit(solution)/shard_map/ppermute | solution.py:320
  41.0 5.2 %second_values.1 = bf16[768,896]{1,0:T(8,128)(2,1)} custom-call(f32[1]{0:T(128)S(6)} %copy.13.refs_0_, f32[1]{0:T(128)S(6)} %copy.14.refs_1_, s32[1,2]{1,0:T(1,128)S(1)} %copy-done, bf16[1,256,1024]{2,1,0:T(8,128)(2,1)} %refs_2_.10, bf16[1,256,1024]{2,1,0:T(8,128)(2,1)} %refs_3_.7, f32[1,256,1024]{2,1,0:T(8,128)} %refs_4_.3, ...), custom_call_target="tpu_custom_call" | custom-call | bytes 6094848 | tf_op jit(solution)/shard_map/second_values/pallas_call | solution.py:294
  47.7 3.6 %all-to-all-start.2 = ((bf16[4,192,896]{2,1,0:T(8,128)(2,1)}), bf16[4,192,896]{2,1,0:T(8,128)(2,1)S(1)}, u32[]{:S(2)}, u32[]{:S(2)}) async-start(bf16[4,192,896]{2,1,0:T(8,128)(2,1)} %bitcast.7), calls=%async_computation.2 | async-start | bytes 2752512 | tf_op jit(solution)/shard_map/all_to_all | solution.py:324
  51.2 7.2 %collective-permute-start.6 = (bf16[192,512]{1,0:T(8,128)(2,1)S(1)}, bf16[192,512]{1,0:T(8,128)(2,1)S(1)}, u32[]{:S(2)}, u32[]{:S(2)}) collective-permute-start(bf16[192,512]{1,0:T(8,128)(2,1)S(1)} %get-tuple-element.74.refs_1_), channel_id=1, source_target_pairs={{0,24},{1,9},{8,16},{9,1},{16,8},{17,25},{24,0},{25,17},{2,26},{3,... | collective-permute-start | bytes 589832 | tf_op jit(solution)/shard_map/ppermute | solution.py:320
  58.4 7.7 %collective-permute-done.6.refs_2_ = bf16[192,512]{1,0:T(8,128)(2,1)S(1)} collective-permute-done((bf16[192,512]{1,0:T(8,128)(2,1)S(1)}, bf16[192,512]{1,0:T(8,128)(2,1)S(1)}, u32[]{:S(2)}, u32[]{:S(2)}) %collective-permute-start.6) | collective-permute-done | bytes 196640 | tf_op jit(solution)/shard_map/ppermute | solution.py:320
  68.0 3.6 %all-to-all-start.1 = ((bf16[4,192,512]{2,1,0:T(8,128)(2,1)}), bf16[4,192,512]{2,1,0:T(8,128)(2,1)S(1)}, u32[]{:S(2)}, u32[]{:S(2)}) async-start(bf16[4,192,512]{2,1,0:T(8,128)(2,1)} %get-tuple-element.75), calls=%async_computation.1 | async-start | bytes 1572864 | tf_op jit(solution)/shard_map/all_to_all | solution.py:324
  72.7 4.6 %collective-permute-start.7 = (bf16[192,384]{1,0:T(8,128)(2,1)S(1)}, bf16[192,384]{1,0:T(8,128)(2,1)S(1)}, u32[]{:S(2)}, u32[]{:S(2)}) collective-permute-start(bf16[192,384]{1,0:T(8,128)(2,1)S(1)} %get-tuple-element.81.refs_5_), channel_id=1, source_target_pairs={{0,1},{1,0},{2,3},{3,2},{4,5},{5,4},{6,7},{7,6},{8,9},{9,8},{10,11... | collective-permute-start | bytes 442376 | tf_op jit(solution)/shard_map/ppermute | solution.py:328
  77.3 3.7 %all-to-all-done.1 = bf16[4,192,512]{2,1,0:T(8,128)(2,1)S(1)} async-done(((bf16[4,192,512]{2,1,0:T(8,128)(2,1)}), bf16[4,192,512]{2,1,0:T(8,128)(2,1)S(1)}, u32[]{:S(2)}, u32[]{:S(2)}) %all-to-all-start.1) | async-done | bytes 786464 | tf_op jit(solution)/shard_map/all_to_all | solution.py:324
  82.0 11.2 %collective-permute-start.8 = (bf16[192,512]{1,0:T(8,128)(2,1)S(1)}, bf16[192,512]{1,0:T(8,128)(2,1)S(1)}, u32[]{:S(2)}, u32[]{:S(2)}) collective-permute-start(bf16[192,512]{1,0:T(8,128)(2,1)S(1)} %get-tuple-element.84.refs_1_), channel_id=1, source_target_pairs={{0,8},{1,25},{8,0},{9,17},{16,24},{17,9},{24,16},{25,1},{2,10},{3,... | collective-permute-start | bytes 589832 | tf_op jit(solution)/shard_map/ppermute | solution.py:320
  93.2 3.3 %collective-permute-done.8.refs_2_ = bf16[192,512]{1,0:T(8,128)(2,1)S(1)} collective-permute-done((bf16[192,512]{1,0:T(8,128)(2,1)S(1)}, bf16[192,512]{1,0:T(8,128)(2,1)S(1)}, u32[]{:S(2)}, u32[]{:S(2)}) %collective-permute-start.8) | collective-permute-done | bytes 196640 | tf_op jit(solution)/shard_map/ppermute | solution.py:320
  96.5 5.5 %collective-permute-start.9 = (bf16[192,512]{1,0:T(8,128)(2,1)S(1)}, bf16[192,512]{1,0:T(8,128)(2,1)S(1)}, u32[]{:S(2)}, u32[]{:S(2)}) collective-permute-start(bf16[192,512]{1,0:T(8,128)(2,1)S(1)} %get-tuple-element.86.refs_1_), channel_id=1, source_target_pairs={{0,24},{1,9},{8,16},{9,1},{16,8},{17,25},{24,0},{25,17},{2,26},{3,... | collective-permute-start | bytes 589832 | tf_op jit(solution)/shard_map/ppermute | solution.py:320
  102.1 4.7 %first_gradient.1 = (bf16[272,512]{1,0:T(8,128)(2,1)S(1)}, bf16[256,512]{1,0:T(8,128)(2,1)S(1)}, f32[512,512]{1,0:T(8,128)}) custom-call(f32[1]{0:T(128)S(6)} %copy.13.refs_0_, s32[1,2]{1,0:T(1,128)S(1)} %copy-done, bf16[1,256,1024]{2,1,0:T(8,128)(2,1)} %refs_2_.10, bf16[1,256,1024]{2,1,0:T(8,128)(2,1)} %refs_3_.7, f32[1,256,1024]{2,1,0:T(8,128)} %refs_4_.3, ...), custom_call_target="tpu_custom_call" | custom-call | bytes 6701056 | tf_op jit(solution)/shard_map/first_gradient/pallas_call | solution.py:294
  107.8 9.6 %all-to-all-start.3 = ((bf16[4,192,512]{2,1,0:T(8,128)(2,1)}), bf16[4,192,512]{2,1,0:T(8,128)(2,1)S(1)}, u32[]{:S(2)}, u32[]{:S(2)}) async-start(bf16[4,192,512]{2,1,0:T(8,128)(2,1)} %get-tuple-element.90), calls=%async_computation.3 | async-start | bytes 1572864 | tf_op jit(solution)/shard_map/all_to_all | solution.py:324
  117.4 3.4 %collective-permute-start.10 = (bf16[272,512]{1,0:T(8,128)(2,1)S(1)}, bf16[272,512]{1,0:T(8,128)(2,1)S(1)}, u32[]{:S(2)}, u32[]{:S(2)}) collective-permute-start(bf16[272,512]{1,0:T(8,128)(2,1)S(1)} %get-tuple-element.92), channel_id=1, source_target_pairs={{0,32},{32,64},{64,96},{96,128},{128,160},{160,192},{192,224},{224... | collective-permute-start | bytes 835592 | tf_op jit(solution)/shard_map/ppermute | solution.py:333
  120.9 7.8 %collective-permute-done.10.refs_3_ = bf16[272,512]{1,0:T(8,128)(2,1)S(1)} collective-permute-done((bf16[272,512]{1,0:T(8,128)(2,1)S(1)}, bf16[272,512]{1,0:T(8,128)(2,1)S(1)}, u32[]{:S(2)}, u32[]{:S(2)}) %collective-permute-start.10) | collective-permute-done | bytes 278560 | tf_op jit(solution)/shard_map/ppermute | solution.py:333
  128.6 2.6 %second_gradient.1 = (bf16[256,512]{1,0:T(8,128)(2,1)S(1)}, bf16[272,512]{1,0:T(8,128)(2,1)S(1)}, f32[256,512]{1,0:T(8,128)S(1)}, bf16[192,512]{1,0:T(8,128)(2,1)S(1)}, bf16[128,512]{1,0:T(8,128)(2,1)S(1)}) custom-call(f32[1]{0:T(128)S(6)} %copy.13.refs_0_, f32[1]{0:T(128)S(6)} %copy.14.refs_1_, s32[1,2]{1,0:T(1,128)S(1)} %copy-done, ...), custom_call_target="tpu_custom_call" | custom-call | bytes 4603904 | tf_op jit(solution)/shard_map/second_gradient/pallas_call | solution.py:294
  133.2 10.8 %collective-permute-start.12 = (bf16[256,512]{1,0:T(8,128)(2,1)S(1)}, bf16[256,512]{1,0:T(8,128)(2,1)S(1)}, u32[]{:S(2)}, u32[]{:S(2)}) collective-permute-start(bf16[256,512]{1,0:T(8,128)(2,1)S(1)} %get-tuple-element.87), channel_id=1, source_target_pairs={{0,33},{1,32},{32,65},{33,64},{64,97},{65,96},{96,129},{97,128},{1... | collective-permute-start | bytes 786440 | tf_op jit(solution)/shard_map/ppermute | solution.py:339
  144.0 3.1 %collective-permute-start.11 = (bf16[256,512]{1,0:T(8,128)(2,1)S(1)}, bf16[256,512]{1,0:T(8,128)(2,1)S(1)}, u32[]{:S(2)}, u32[]{:S(2)}) collective-permute-start(bf16[256,512]{1,0:T(8,128)(2,1)S(1)} %get-tuple-element.94), channel_id=1, source_target_pairs={{0,65},{1,64},{32,97},{33,96},{64,129},{65,128},{96,161},{97,160},... | collective-permute-start | bytes 786440 | tf_op jit(solution)/shard_map/ppermute | solution.py:339
  151.5 5.7 %collective-permute-done.12.refs_4_ = bf16[256,512]{1,0:T(8,128)(2,1)S(1)} collective-permute-done((bf16[256,512]{1,0:T(8,128)(2,1)S(1)}, bf16[256,512]{1,0:T(8,128)(2,1)S(1)}, u32[]{:S(2)}, u32[]{:S(2)}) %collective-permute-start.12) | collective-permute-done | bytes 262176 | tf_op jit(solution)/shard_map/ppermute | solution.py:339
  158.8 11.7 %collective-permute-done.11.refs_1_ = bf16[256,512]{1,0:T(8,128)(2,1)S(1)} collective-permute-done((bf16[256,512]{1,0:T(8,128)(2,1)S(1)}, bf16[256,512]{1,0:T(8,128)(2,1)S(1)}, u32[]{:S(2)}, u32[]{:S(2)}) %collective-permute-start.11) | collective-permute-done | bytes 262176 | tf_op jit(solution)/shard_map/ppermute | solution.py:339
  (34 shorter events, 28.4 us)
Async XLA Ops:
  3.1 11.6 %collective-permute-start = (bf16[832,512]{1,0:T(8,128)(2,1)S(1)}, bf16[832,512]{1,0:T(8,128)(2,1)S(1)}, u32[]{:S(2)}, u32[]{:S(2)}) collective-permute-start(bf16[832,512]{1,0:T(8,128)(2,1)S(1)} %get-tuple-element.59), channel_id=1, source_target_pairs={{0,1},{1,0},{2,3},{3,2},{4,5},{5,4},{6,7},{7,6},{8,9},{9,8},{10,11... | collective-permute-start | bytes 2555912 | tf_op jit(solution)/shard_map/ppermute | solution.py:328
  15.8 25.2 %copy-start = (s32[1,2]{1,0:T(1,128)S(1)}, s32[1,2]{1,0:T(1,128)}, u32[]{:S(2)}) copy-start(s32[1,2]{1,0:T(1,128)} %refs_2_.13) | copy-start | bytes 28
  15.8 15.9 %all-to-all-start = ((bf16[4,192,512]{2,1,0:T(8,128)(2,1)}), bf16[4,192,512]{2,1,0:T(8,128)(2,1)S(1)}, u32[]{:S(2)}, u32[]{:S(2)}) async-start(bf16[4,192,512]{2,1,0:T(8,128)(2,1)} %bitcast.8), calls=%async_computation | async-start | bytes 1572864 | tf_op jit(solution)/shard_map/all_to_all | solution.py:324
  19.3 21.6 %collective-permute-start.2 = (bf16[1024,256]{1,0:T(8,128)(2,1)S(1)}, bf16[1024,256]{1,0:T(8,128)(2,1)}, u32[]{:S(2)}, u32[]{:S(2)}) collective-permute-start(bf16[1024,256]{1,0:T(8,128)(2,1)S(1)} %get-tuple-element.68), channel_id=1, source_target_pairs={{0,1},{1,0},{2,3},{3,2},{4,5},{5,4},{6,7},{7,6},{8,9},{9,8},{10,11... | collective-permute-start | bytes 1572872 | tf_op jit(solution)/shard_map/ppermute | solution.py:328
  21.2 19.7 %collective-permute-start.3 = (bf16[1024,256]{1,0:T(8,128)(2,1)S(1)}, bf16[1024,256]{1,0:T(8,128)(2,1)}, u32[]{:S(2)}, u32[]{:S(2)}) collective-permute-start(bf16[1024,256]{1,0:T(8,128)(2,1)S(1)} %get-tuple-element.69), channel_id=1, source_target_pairs={{0,1},{1,0},{2,3},{3,2},{4,5},{5,4},{6,7},{7,6},{8,9},{9,8},{10,11... | collective-permute-start | bytes 1572872 | tf_op jit(solution)/shard_map/ppermute | solution.py:328
  23.7 17.3 %collective-permute-start.1 = (bf16[768,256]{1,0:T(8,128)(2,1)S(1)}, bf16[768,256]{1,0:T(8,128)(2,1)}, u32[]{:S(2)}, u32[]{:S(2)}) collective-permute-start(bf16[768,256]{1,0:T(8,128)(2,1)S(1)} %get-tuple-element.67), channel_id=1, source_target_pairs={{0,1},{1,0},{2,3},{3,2},{4,5},{5,4},{6,7},{7,6},{8,9},{9,8},{10,11... | collective-permute-start | bytes 1179656 | tf_op jit(solution)/shard_map/ppermute | solution.py:328
  25.6 15.3 %collective-permute-start.5 = (bf16[768,256]{1,0:T(8,128)(2,1)S(1)}, bf16[768,256]{1,0:T(8,128)(2,1)}, u32[]{:S(2)}, u32[]{:S(2)}) collective-permute-start(bf16[768,256]{1,0:T(8,128)(2,1)S(1)} %get-tuple-element.71), channel_id=1, source_target_pairs={{0,1},{1,0},{2,3},{3,2},{4,5},{5,4},{6,7},{7,6},{8,9},{9,8},{10,11... | collective-permute-start | bytes 1179656 | tf_op jit(solution)/shard_map/ppermute | solution.py:328
  32.8 14.8 %collective-permute-start.4 = (bf16[192,512]{1,0:T(8,128)(2,1)S(1)}, bf16[192,512]{1,0:T(8,128)(2,1)S(1)}, u32[]{:S(2)}, u32[]{:S(2)}) collective-permute-start(bf16[192,512]{1,0:T(8,128)(2,1)S(1)} %get-tuple-element.61.refs_1_), channel_id=1, source_target_pairs={{0,8},{1,25},{8,0},{9,17},{16,24},{17,9},{24,16},{25,1},{2,10},{3,... | collective-permute-start | bytes 589832 | tf_op jit(solution)/shard_map/ppermute | solution.py:320
  47.7 20.3 %all-to-all-start.2 = ((bf16[4,192,896]{2,1,0:T(8,128)(2,1)}), bf16[4,192,896]{2,1,0:T(8,128)(2,1)S(1)}, u32[]{:S(2)}, u32[]{:S(2)}) async-start(bf16[4,192,896]{2,1,0:T(8,128)(2,1)} %bitcast.7), calls=%async_computation.2 | async-start | bytes 2752512 | tf_op jit(solution)/shard_map/all_to_all | solution.py:324
  51.2 14.9 %collective-permute-start.6 = (bf16[192,512]{1,0:T(8,128)(2,1)S(1)}, bf16[192,512]{1,0:T(8,128)(2,1)S(1)}, u32[]{:S(2)}, u32[]{:S(2)}) collective-permute-start(bf16[192,512]{1,0:T(8,128)(2,1)S(1)} %get-tuple-element.74.refs_1_), channel_id=1, source_target_pairs={{0,24},{1,9},{8,16},{9,1},{16,8},{17,25},{24,0},{25,17},{2,26},{3,... | collective-permute-start | bytes 589832 | tf_op jit(solution)/shard_map/ppermute | solution.py:320
  68.0 13.0 %all-to-all-start.1 = ((bf16[4,192,512]{2,1,0:T(8,128)(2,1)}), bf16[4,192,512]{2,1,0:T(8,128)(2,1)S(1)}, u32[]{:S(2)}, u32[]{:S(2)}) async-start(bf16[4,192,512]{2,1,0:T(8,128)(2,1)} %get-tuple-element.75), calls=%async_computation.1 | async-start | bytes 1572864 | tf_op jit(solution)/shard_map/all_to_all | solution.py:324
  72.7 8.3 %collective-permute-start.7 = (bf16[192,384]{1,0:T(8,128)(2,1)S(1)}, bf16[192,384]{1,0:T(8,128)(2,1)S(1)}, u32[]{:S(2)}, u32[]{:S(2)}) collective-permute-start(bf16[192,384]{1,0:T(8,128)(2,1)S(1)} %get-tuple-element.81.refs_5_), channel_id=1, source_target_pairs={{0,1},{1,0},{2,3},{3,2},{4,5},{5,4},{6,7},{7,6},{8,9},{9,8},{10,11... | collective-permute-start | bytes 442376 | tf_op jit(solution)/shard_map/ppermute | solution.py:328
  82.0 14.5 %collective-permute-start.8 = (bf16[192,512]{1,0:T(8,128)(2,1)S(1)}, bf16[192,512]{1,0:T(8,128)(2,1)S(1)}, u32[]{:S(2)}, u32[]{:S(2)}) collective-permute-start(bf16[192,512]{1,0:T(8,128)(2,1)S(1)} %get-tuple-element.84.refs_1_), channel_id=1, source_target_pairs={{0,8},{1,25},{8,0},{9,17},{16,24},{17,9},{24,16},{25,1},{2,10},{3,... | collective-permute-start | bytes 589832 | tf_op jit(solution)/shard_map/ppermute | solution.py:320
  96.5 10.3 %collective-permute-start.9 = (bf16[192,512]{1,0:T(8,128)(2,1)S(1)}, bf16[192,512]{1,0:T(8,128)(2,1)S(1)}, u32[]{:S(2)}, u32[]{:S(2)}) collective-permute-start(bf16[192,512]{1,0:T(8,128)(2,1)S(1)} %get-tuple-element.86.refs_1_), channel_id=1, source_target_pairs={{0,24},{1,9},{8,16},{9,1},{16,8},{17,25},{24,0},{25,17},{2,26},{3,... | collective-permute-start | bytes 589832 | tf_op jit(solution)/shard_map/ppermute | solution.py:320
  107.8 20.8 %all-to-all-start.3 = ((bf16[4,192,512]{2,1,0:T(8,128)(2,1)}), bf16[4,192,512]{2,1,0:T(8,128)(2,1)S(1)}, u32[]{:S(2)}, u32[]{:S(2)}) async-start(bf16[4,192,512]{2,1,0:T(8,128)(2,1)} %get-tuple-element.90), calls=%async_computation.3 | async-start | bytes 1572864 | tf_op jit(solution)/shard_map/all_to_all | solution.py:324
  117.4 11.2 %collective-permute-start.10 = (bf16[272,512]{1,0:T(8,128)(2,1)S(1)}, bf16[272,512]{1,0:T(8,128)(2,1)S(1)}, u32[]{:S(2)}, u32[]{:S(2)}) collective-permute-start(bf16[272,512]{1,0:T(8,128)(2,1)S(1)} %get-tuple-element.92), channel_id=1, source_target_pairs={{0,32},{32,64},{64,96},{96,128},{128,160},{160,192},{192,224},{224... | collective-permute-start | bytes 835592 | tf_op jit(solution)/shard_map/ppermute | solution.py:333
  131.3 39.3 %collective-permute-start.15 = (bf16[272,512]{1,0:T(8,128)(2,1)S(1)}, bf16[272,512]{1,0:T(8,128)(2,1)S(1)}, u32[]{:S(2)}, u32[]{:S(2)}) collective-permute-start(bf16[272,512]{1,0:T(8,128)(2,1)S(1)} %get-tuple-element.102), channel_id=1, source_target_pairs={{0,64},{32,96},{64,128},{96,160},{128,192},{160,224},{192,256},{22... | collective-permute-start | bytes 835592 | tf_op jit(solution)/shard_map/ppermute | solution.py:333
  133.2 24.0 %collective-permute-start.12 = (bf16[256,512]{1,0:T(8,128)(2,1)S(1)}, bf16[256,512]{1,0:T(8,128)(2,1)S(1)}, u32[]{:S(2)}, u32[]{:S(2)}) collective-permute-start(bf16[256,512]{1,0:T(8,128)(2,1)S(1)} %get-tuple-element.87), channel_id=1, source_target_pairs={{0,33},{1,32},{32,65},{33,64},{64,97},{65,96},{96,129},{97,128},{1... | collective-permute-start | bytes 786440 | tf_op jit(solution)/shard_map/ppermute | solution.py:339
  144.0 26.5 %collective-permute-start.11 = (bf16[256,512]{1,0:T(8,128)(2,1)S(1)}, bf16[256,512]{1,0:T(8,128)(2,1)S(1)}, u32[]{:S(2)}, u32[]{:S(2)}) collective-permute-start(bf16[256,512]{1,0:T(8,128)(2,1)S(1)} %get-tuple-element.94), channel_id=1, source_target_pairs={{0,65},{1,64},{32,97},{33,96},{64,129},{65,128},{96,161},{97,160},... | collective-permute-start | bytes 786440 | tf_op jit(solution)/shard_map/ppermute | solution.py:339
  147.2 10.1 %collective-permute-start.13 = (bf16[192,512]{1,0:T(8,128)(2,1)S(1)}, bf16[192,512]{1,0:T(8,128)(2,1)S(1)}, u32[]{:S(2)}, u32[]{:S(2)}) collective-permute-start(bf16[192,512]{1,0:T(8,128)(2,1)S(1)} %get-tuple-element.97), channel_id=1, source_target_pairs={{0,1},{1,0},{2,3},{3,2},{4,5},{5,4},{6,7},{7,6},{8,9},{9,8},{10,11... | collective-permute-start | bytes 589832 | tf_op jit(solution)/shard_map/ppermute | solution.py:328
  149.6 7.7 %collective-permute-start.14 = (bf16[128,512]{1,0:T(8,128)(2,1)S(1)}, bf16[128,512]{1,0:T(8,128)(2,1)S(1)}, u32[]{:S(2)}, u32[]{:S(2)}) collective-permute-start(bf16[128,512]{1,0:T(8,128)(2,1)S(1)} %get-tuple-element.98), channel_id=1, source_target_pairs={{0,1},{1,0},{2,3},{3,2},{4,5},{5,4},{6,7},{7,6},{8,9},{9,8},{10,11... | collective-permute-start | bytes 393224 | tf_op jit(solution)/shard_map/ppermute | solution.py:328
